TPU v7x, 32 devices: a whole 2x2x4 slice. The times are simulated.
32 devices in a mesh: seq: 16 (over z, y, core), pool: 2 (over x).
Axes of the slice: x: 2, y: 2, z: 4, core: 2. Of those that a mesh axis runs over, the one named last changes fastest.
Arguments:
- query_rows: bfloat16 [8192, 4096], P('seq', 'pool'), may hold values from -6 to 6
- key_rows: bfloat16 [8192, 4096], P('seq', 'pool'), may hold values from -6 to 6
- value_rows: bfloat16 [8192, 4096], P('seq', 'pool'), may hold values from -6 to 6
- log_decay: float32 [32, 8192], P('pool', 'seq'), may hold values from -0.7 to 0
- residual: bfloat16 [8192, 4096], P(('seq', 'pool')), may hold values from -6 to 6
- out_weight: bfloat16 [4096, 4096], P('pool', 'seq'), may hold values from -0.09375 to 0.09375
- norm_gain: float32 [4096], replicated, may hold values from 0.5 to 1.5
- kv_weight: bfloat16 [4096, 1024], P('seq'), may hold values from -0.09375 to 0.09375
- block_table: int32 [64, 2], P(('seq', 'pool')), may hold values from 0 to 3, as said below
Outputs:
- page_cache: bfloat16 [16, 2, 4, 128, 1024], P('seq', 'pool')
Inputs may be any that keep to these rules, and one draw needn't show every extreme that they name: `block_table`: column 0 is a page's pool device, column 1 its slot there. The pages of one index of seq go to pool devices of that same index, no two to the same device and slot; one pool device receives exactly 4 of them, each other at most 4, and all 2 pages of some device go to that one.
All inputs are finite; a program needn't handle non-finite values.
Results may differ from a plain program's by a relative error of at most 0.0056.
Values may be sent and summed in bfloat16 or wider, within the bound.
No kernel may reach another device: no remote copies, remote signals or barrier semaphores. Data moves between devices by JAX's collectives and lax.ppermute only.
A program may use at most 128 MiB of HBM per device.

v0:
```python
import jax
import jax.numpy as jnp
from jax import lax
from jax.sharding import PartitionSpec as P

HD = 128
PAGE = 128
BLK = 512


def entering(part, axis, combine, identity):
    place = lax.axis_index(axis)
    gathered = jax.tree.map(lambda a: lax.all_gather(a, axis), part)
    state = jax.tree.map(lambda a, e: jnp.zeros_like(a) + jnp.asarray(e, a.dtype), part, identity)

    def one(hop, state):
        return combine(
            state, jax.tree.map(lambda a: lax.dynamic_index_in_dim(a, hop, 0, False), gathered)
        )

    return lax.fori_loop(0, place, one, state)


def head_major(matrix, head_count):
    return matrix.reshape(BLK, head_count, HD).transpose(1, 0, 2)


def combine_states(earlier, later):
    return (earlier[0] + later[0], jnp.exp(later[0])[:, None, None] * earlier[1] + later[1])


def on_device(
    query_rows,
    key_rows,
    value_rows,
    log_decay,
    residual,
    out_weight,
    norm_gain,
    kv_weight,
    block_table,
):
    head_count = query_rows.shape[1] // HD
    lower_mask = jnp.tril(jnp.ones((BLK, BLK), dtype=bool))
    query_blk = head_major(query_rows, head_count)
    key_blk = head_major(key_rows, head_count)
    value_blk = head_major(value_rows, head_count)
    cumulative = jnp.cumsum(log_decay, axis=1)
    block_total = cumulative[:, -1]
    log_gap = jnp.where(lower_mask[None], cumulative[:, :, None] - cumulative[:, None, :], 0.0)
    products = jnp.einsum("hid,hjd->hij", query_blk, key_blk, preferred_element_type=jnp.float32)
    scores = jnp.where(lower_mask[None], products * jnp.exp(log_gap), 0.0).astype(jnp.bfloat16)
    inner = jnp.einsum("hij,hjd->hid", scores, value_blk, preferred_element_type=jnp.float32)
    weighted = (
        key_blk.astype(jnp.float32) * jnp.exp(block_total[:, None] - cumulative)[:, :, None]
    ).astype(jnp.bfloat16)
    update = jnp.einsum("hjd,hje->hde", weighted, value_blk, preferred_element_type=jnp.float32)
    query_list = [query_blk]
    inner_list = [inner]
    update_list = [update]
    cumul_list = [cumulative]
    total_list = [block_total]
    state_sum = jnp.zeros((head_count, HD, HD), jnp.float32)
    block_index = 0
    state_sum = (
        jnp.exp(total_list[block_index])[:, None, None] * state_sum + update_list[block_index]
    )
    log_sum = total_list[block_index]
    incoming = entering(
        (log_sum, state_sum),
        "seq",
        combine_states,
        (jnp.zeros_like(log_sum), jnp.zeros_like(state_sum)),
    )
    carried = incoming[1]
    block_index = 0
    outer = (
        jnp.einsum(
            "hid,hde->hie",
            query_list[block_index].astype(jnp.float32),
            carried,
            precision=lax.Precision.HIGHEST,
        )
        * jnp.exp(cumul_list[block_index])[:, :, None]
    )
    retained = inner_list[block_index] + outer
    scaled = retained * lax.rsqrt(jnp.mean(retained * retained, axis=-1, keepdims=True) + 1e-05)
    mixed_list = scaled.transpose(1, 0, 2).reshape(BLK, head_count * HD).astype(jnp.bfloat16)
    partial_value = jnp.dot(
        mixed_list,
        lax.all_gather(out_weight, "seq", axis=1, tiled=True),
        preferred_element_type=jnp.float32,
    )
    summed = lax.psum_scatter(partial_value, "pool", scatter_dimension=0, tiled=True)
    hidden = residual.astype(jnp.float32) + summed
    normed = (
        hidden * lax.rsqrt(jnp.mean(hidden * hidden, axis=-1, keepdims=True) + 1e-05) * norm_gain
    ).astype(jnp.bfloat16)
    pool_count = lax.axis_size("pool")
    pages_here = block_table.shape[0]
    slot_count = 2 * pages_here
    cache_width = kv_weight.shape[1]
    owner_ids = jnp.arange(pool_count, dtype=jnp.int32)
    slot_ids = jnp.arange(slot_count, dtype=jnp.int32)
    owner_match = block_table[:, 0][:, None] == owner_ids[None, :]
    slot_match = block_table[:, 1][:, None] == slot_ids[None, :]
    placed = jnp.logical_and(owner_match[:, :, None], slot_match[:, None, :]).astype(jnp.bfloat16)
    cache_rows = jnp.dot(
        normed,
        lax.all_gather(kv_weight, "seq", axis=0, tiled=True),
        preferred_element_type=jnp.float32,
    ).astype(jnp.bfloat16)
    own_pages = cache_rows.reshape(pages_here, PAGE, cache_width)
    outgoing = jnp.where(
        owner_match.T[:, :, None, None], own_pages[None], jnp.zeros((), jnp.bfloat16)
    )
    slot_tags = placed.transpose(1, 0, 2)
    arrived, arrived_tags = (
        lax.all_to_all(outgoing, "pool", split_axis=0, concat_axis=0, tiled=True),
        lax.all_to_all(slot_tags, "pool", split_axis=0, concat_axis=0, tiled=True),
    )
    page_cache = jnp.einsum(
        "ips,ipqc->sqc", arrived_tags, arrived, preferred_element_type=jnp.float32
    ).astype(jnp.bfloat16)
    return page_cache.reshape(1, 1, slot_count, PAGE, cache_width)


def solution(mesh):
    placed = (
        P("seq", "pool"),
        P("seq", "pool"),
        P("seq", "pool"),
        P("pool", "seq"),
        P(("seq", "pool"), None),
        P("pool", "seq"),
        P(),
        P("seq", None),
        P(("seq", "pool"), None),
    )
    return jax.shard_map(
        on_device,
        mesh=mesh,
        in_specs=placed,
        out_specs=P("seq", "pool", None, None, None),
        check_vma=False,
    )
```

profile of v0, /device:TPU:0, one launch (start us, length us, event | category | flops | bytes accessed | tf_op | source)
XLA Modules:
  0.0 502.0 jit_solution(6680977372593971796)
XLA Ops:
  6.5 0.0 copy-start
  6.5 0.0 all-gather.10.cloned.1.call-start
  6.5 0.9 copy_bitcast_fusion.1
  7.4 1.1 reduce-window.6
  8.6 0.2 slice_reduce_fusion
  8.8 0.1 copy_bitcast_fusion
  8.9 0.2 slice_reduce_fusion.1
  9.1 0.1 exponential_bitcast_fusion.1
  9.2 3.9 copy.57
  13.1 0.0 copy-start.5
  13.1 4.0 fusion.18
  17.1 0.0 all-gather.10.cloned.1.call-update
  17.2 0.0 all-gather.6.cloned.1.call-start
  17.2 0.7 all-gather.6.cloned.1.call-update
  17.9 0.0 reduce-scatter.2.cloned.1.call-start
  18.0 0.0 copy-done.5
  18.0 0.6 dynamic-slice
  19.2 0.2 dynamic-update-slice
  19.4 36.0 %all-reduce = f32[256]{0:T(256)S(1)} all-reduce(f32[256]{0:T(256)S(1)} %dynamic-update-slice), channel_id=2, replica_groups=mesh['seq'=16,'pool'=2] {'seq'}, use_global_device_ids=true, to_apply=%add | all-reduce | flops 256 | bytes 2048
  55.4 0.1 reshape.180
  55.5 3.6 copy.64
  59.1 0.1 iota_compare_fusion
  59.1 88.0 %all-gather.10.cloned.1.call-done = f32[256,128,128]{2,1,0:T(8,128)} async-done(((f32[16,128,128]{2,1,0:T(8,128)}), f32[256,128,128]{2,1,0:T(8,128)}) %all-gather.10.cloned.1.call-update) | async-done | bytes 16777232 | tf_op jit(solution)/shard_map/all_gather | solution.py:13
  147.2 0.1 broadcast.99
  147.3 0.2 while.12
  147.5 0.0 copy-done
  147.5 3.8 fusion.8
  151.3 11.2 %fusion.1 = (f32[16,512]{1,0:T(8,128)S(1)}, f32[16,512,128]{1,2,0:T(8,128)}) fusion(f32[16,128,512]{2,1,0:T(8,128)} %fusion.8, f32[16,512]{1,0:T(8,128)S(1)} %get-tuple-element.63, bf16[16,512,128]{2,0,1:T(8,128)(2,1)} %bitcast.118, bf16[16,512,128]{1,2,0:T(8,128)(2,1)} %bitcast.117, f32[16,512]{1,0:T(8,128)S(1)} %copy_bitcast_fusion, ...), kind=kOutput, calls=%fused_computation.5 | convolution fusion | flops 2172641280 | bytes 15040512 | tf_op jit(solution)/shard_map/hij,hjd->hid/dot_general | solution.py:53
  162.5 4.7 fusion.4
  167.2 110.7 %all-gather.6.cloned.1.call-done = bf16[2048,4096]{1,0:T(8,128)(2,1)} async-done(((bf16[2048,256]{1,0:T(8,128)(2,1)}), bf16[2048,4096]{1,0:T(8,128)(2,1)}) %all-gather.6.cloned.1.call-update) | async-done | bytes 16777232 | tf_op jit(solution)/shard_map/all_gather | solution.py:91
  277.9 14.6 %fusion.23 = f32[512,4096]{1,0:T(8,128)} fusion(bf16[512,2048]{0,1:T(8,128)(2,1)S(1)} %bitcast.114, bf16[2048,4096]{1,0:T(8,128)(2,1)} %all-gather.6.cloned.1.call-done), kind=kOutput, calls=%fused_computation.51 | convolution fusion | flops 8589934592 | bytes 27262976 | tf_op jit(solution)/shard_map/dot_general | solution.py:89
  292.4 0.0 copy-start.3
  292.4 0.0 copy-start.2
  292.4 0.0 reduce-scatter.2.cloned.1.call-update
  292.5 0.0 copy-start.4
  292.5 0.0 all-gather.8.cloned.1.call-start
  292.5 0.5 all-gather.8.cloned.1.call-update
  293.0 0.1 copy-done.3
  293.1 0.2 slice_reduce_fusion.2
  293.3 0.1 iota_compare_fusion.1
  293.4 0.6 and_convert_fusion
  294.0 3.4 all-to-all-start
  297.4 92.7 %reduce-scatter.2.cloned.1.call-done = f32[256,4096]{1,0:T(8,128)} async-done(((f32[512,4096]{1,0:T(8,128)}), f32[256,4096]{1,0:T(8,128)}) %reduce-scatter.2.cloned.1.call-update) | async-done | bytes 4194320 | tf_op jit(solution)/shard_map/reduce_scatter | solution.py:94
  390.1 0.0 copy-done.2
  390.1 2.8 multiply_reduce_fusion
  392.9 74.4 %all-gather.8.cloned.1.call-done = bf16[4096,1024]{1,0:T(8,128)(2,1)} async-done(((bf16[256,1024]{1,0:T(8,128)(2,1)}), bf16[4096,1024]{1,0:T(8,128)(2,1)}) %all-gather.8.cloned.1.call-update) | async-done | bytes 8388624 | tf_op jit(solution)/shard_map/all_gather | solution.py:110
  467.3 0.0 copy-done.4
  467.3 7.0 %fusion.19 = bf16[256,1024]{1,0:T(8,128)(2,1)S(1)} fusion(bf16[4096,1024]{1,0:T(8,128)(2,1)} %all-gather.8.cloned.1.call-done, f32[256,4096]{1,0:T(8,128)} %reduce-scatter.2.cloned.1.call-done, bf16[256,4096]{1,0:T(8,128)(2,1)S(1)} %copy-done.2, f32[4096]{0:T(1024)S(1)} %copy-done.4, f32[256]{0:T(256)S(1)} %add_rsqrt_fusion), kind=kOutput, calls=%fused_computation.31 | convolution fusion | flops 2152988672 | bytes 15221760 | tf_op jit(solution)/shard_map/dot_general | solution.py:108
  474.3 0.5 copy.50
  474.9 0.0 copy-start.1
  474.9 0.9 broadcast_select_fusion
  475.8 0.0 all-to-all-done
  475.8 16.8 %all_to_all.10 = bf16[2,2,128,1024]{3,1,2,0:T(2,128)(2,1)S(1)} all-to-all(bf16[2,2,128,1024]{3,1,2,0:T(2,128)(2,1)S(1)} %broadcast_select_fusion), channel_id=1, replica_groups=mesh['seq'=16,'pool'=2] {'pool'}, dimensions={0} | all-to-all | bytes 2097152 | tf_op jit(solution)/shard_map/all_to_all | solution.py:119
  492.5 1.7 fusion.17
  494.2 1.3 copy.52
  495.5 0.0 copy-done.1
  (7 shorter events, 0.1 us)
Async XLA Ops:
  6.5 140.9 %copy-start = (bf16[512,2048]{1,0:T(8,128)(2,1)S(1)}, bf16[512,2048]{1,0:T(8,128)(2,1)}, u32[]{:S(2)}) copy-start(bf16[512,2048]{1,0:T(8,128)(2,1)} %param.11) | copy-start | bytes 6291460
  6.5 140.6 %all-gather.10.cloned.1.call-start = ((), (), s32[]{:S(2)}) async-start(), calls=%async_computation.6 | async-start | bytes 17825792 | tf_op jit(solution)/shard_map/all_gather | solution.py:13
  13.1 4.9 copy-start.5
  17.2 260.7 %all-gather.6.cloned.1.call-start = ((), (), s32[]{:S(2)}) async-start(), calls=%async_computation.3 | async-start | bytes 17825792 | tf_op jit(solution)/shard_map/all_gather | solution.py:91
  17.9 372.2 %reduce-scatter.2.cloned.1.call-start = ((), (), s32[]{:S(2)}) async-start(), calls=%async_computation.4 | async-start | bytes 12582912 | tf_op jit(solution)/shard_map/reduce_scatter | solution.py:94
  292.4 0.7 copy-start.3
  292.4 97.7 %copy-start.2 = (bf16[256,4096]{1,0:T(8,128)(2,1)S(1)}, bf16[256,4096]{1,0:T(8,128)(2,1)}, u32[]{:S(2)}) copy-start(bf16[256,4096]{1,0:T(8,128)(2,1)} %param.15) | copy-start | bytes 6291460
  292.5 174.8 %copy-start.4 = (f32[4096]{0:T(1024)S(1)}, f32[4096]{0:T(1024)}, u32[]{:S(2)}) copy-start(f32[4096]{0:T(1024)} %param.17) | copy-start | bytes 49156
  292.5 174.8 %all-gather.8.cloned.1.call-start = ((), (), s32[]{:S(2)}) async-start(), calls=%async_computation.5 | async-start | bytes 8912896 | tf_op jit(solution)/shard_map/all_gather | solution.py:110
  294.0 181.8 %all-to-all-start = ((bf16[2,2,4]{2,1,0:T(2,128)(2,1)}), bf16[2,2,4]{2,1,0:T(2,128)(2,1)S(1)}, u32[]{:S(2)}, u32[]{:S(2)}) async-start(bf16[2,2,4]{2,1,0:T(2,128)(2,1)} %and_convert_fusion), calls=%async_computation | async-start | bytes 2048 | tf_op jit(solution)/shard_map/all_to_all | solution.py:120
  474.9 20.6 %copy-start.1 = (bf16[512,2048]{1,0:T(8,128)(2,1)S(1)}, bf16[512,2048]{1,0:T(8,128)(2,1)}, u32[]{:S(2)}) copy-start(bf16[512,2048]{1,0:T(8,128)(2,1)} %param.11) | copy-start | bytes 6291460
Sparse Core Ops, SparseCore 0:
  17.3 129.8 all-gather.9
  149.3 128.5 all-gather.5
  292.6 97.4 reduce-scatter.1
  392.3 74.8 all-gather.7
where the time goes:
time: 503 us; the launch traced here: 502 us
  waiting for transfers between devices  367 us (73%)
  blocking collectives  52.7 us (10%)
  matrix products  42.3 us (8%)
  between operations  13.9 us (3%)
  local copies, waits for them, and re-layouts  11.9 us (2%)
  other arithmetic  10.5 us (2%)
    all_gather x1, waiting for transfers between devices, on_device(): lax.all_gather(out_weight, 'seq', axis=1, tiled=True)  111 us
    reduce_scatter x1, waiting for transfers between devices, on_device(): lax.psum_scatter(partial_value, 'pool', scatter_dimension=0, tiled=True)  92.7 us
    all_gather x1, waiting for transfers between devices, entering(): gathered = jax.tree.map(lambda a: lax.all_gather(a, axis), part)  88 us
    all_gather x1, waiting for transfers between devices, on_device(): lax.all_gather(kv_weight, 'seq', axis=0, tiled=True)  74.4 us
    unnamed x1, blocking collectives  36 us
    all_to_all x1, blocking collectives, on_device(): lax.all_to_all(outgoing, 'pool', split_axis=0, concat_axis=0, tiled=True)  16.8 us
    dot_general x1, matrix products, on_device(): jnp.dot(mixed_list, lax.all_gather(out_weight, 'seq', axis=1, tiled=True)...  14.6 us
    dot_general x1, matrix products, on_device(): jnp.einsum('hij,hjd->hid', scores, value_blk, preferred_element_type=jnp....  11.2 us
  transfers between devices with their start and end apart: 5, of which 4 were waited for; matrix products, arithmetic and copies ran while one was open for 7% of the time, Pallas kernels for 0%

commit v1 on v0

v1 whole, which is shorter than its diff:
```python
import jax
import jax.numpy as jnp
from jax import lax
from jax.sharding import PartitionSpec as P

HD = 128
PAGE = 128
INNER = 4
BF16 = jnp.bfloat16
F32 = jnp.float32


def hop(value, axis, pairs):
    return lax.ppermute(value, axis, pairs)


def seq_xor(value, seq_count, bits):
    return hop(value, "seq", [(j, j ^ bits) for j in range(seq_count)])


def seq_shift(value, seq_count, planes):
    step = planes * INNER
    pairs = [(j, j + step) for j in range(seq_count) if 0 <= j + step < seq_count]
    return hop(value, "seq", pairs)


def pool_shift(value, pool_count, by):
    return hop(value, "pool", [(i, (i + by) % pool_count) for i in range(pool_count)])


def plane_chain(own, seq_count, plane):
    planes = seq_count // INNER
    up, down = [own], [own]
    for _ in range(planes - 1):
        up.append(seq_shift(up[-1], seq_count, 1))
        down.append(seq_shift(down[-1], seq_count, -1))
    blocks = [own]
    for d in range(1, planes):
        blocks.append(jnp.where(plane >= d, up[d], down[planes - d]))
    return blocks


def gathered_totals(totals, seq_count, place, plane):
    planes = seq_count // INNER
    near = jnp.stack([totals] + [seq_xor(totals, seq_count, r) for r in range(1, INNER)])
    order = place ^ jnp.arange(INNER)
    in_plane = near[order]
    parts = [in_plane] + [
        hop(in_plane, "seq", [(j, (j + d * INNER) % seq_count) for j in range(seq_count)])
        for d in range(1, planes)
    ]
    stacked = jnp.stack(parts)
    return stacked[(plane - jnp.arange(planes)) % planes].reshape(seq_count, -1)


def entering_state(update, totals, seq_count, place, plane):
    planes = seq_count // INNER
    heads = update.shape[0]
    share = heads // INNER
    everyone = gathered_totals(totals, seq_count, place, plane)
    pieces = update.astype(BF16).reshape(INNER, share, HD, HD)

    def piece(at):
        return lax.dynamic_index_in_dim(pieces, at, 0, False)

    got = [piece(place)] + [
        seq_xor(piece(place ^ r), seq_count, r) for r in range(1, INNER)
    ]
    got = jnp.stack(got)
    mine = lax.dynamic_slice_in_dim(everyone, place * share, share, 1)
    here = lax.dynamic_slice_in_dim(mine, plane * INNER, INNER, 0)
    by_plane = mine.reshape(planes, INNER, share).sum(1)
    inner_updates = [
        lax.dynamic_index_in_dim(got, place ^ i, 0, False).astype(F32) for i in range(INNER)
    ]
    within = [jnp.zeros_like(inner_updates[0])]
    for i in range(INNER):
        within.append(jnp.exp(here[i])[:, None, None] * within[-1] + inner_updates[i])
    plane_total = within[-1].astype(BF16)
    prefix = jnp.zeros_like(inner_updates[0])
    gap = jnp.zeros((share,), F32)
    for d in range(1, planes):
        arrived = seq_shift(plane_total, seq_count, d).astype(F32)
        prefix = prefix + jnp.exp(gap)[:, None, None] * arrived
        behind = lax.dynamic_index_in_dim(by_plane, jnp.maximum(plane - d, 0), 0, False)
        gap = gap + behind
    outgoing = []
    decay = jnp.zeros((share,), F32)
    for i in range(INNER):
        outgoing.append(
            (within[i] + jnp.exp(decay)[:, None, None] * prefix).astype(BF16)
        )
        decay = decay + here[i]
    outgoing = jnp.stack(outgoing)

    def leaving(at):
        return lax.dynamic_index_in_dim(outgoing, at, 0, False)

    back = [leaving(place)] + [
        seq_xor(leaving(place ^ r), seq_count, r) for r in range(1, INNER)
    ]
    back = jnp.stack(back)
    return jnp.concatenate(
        [lax.dynamic_index_in_dim(back, place ^ h, 0, False) for h in range(INNER)]
    )


def head_major(matrix, head_count):
    return matrix.reshape(matrix.shape[0], head_count, HD).transpose(1, 0, 2)


def retention(query_rows, key_rows, value_rows, log_decay, seq_count, place, plane):
    rows = query_rows.shape[0]
    head_count = query_rows.shape[1] // HD
    lower_mask = jnp.tril(jnp.ones((rows, rows), dtype=bool))
    query_blk = head_major(query_rows, head_count)
    key_blk = head_major(key_rows, head_count)
    value_blk = head_major(value_rows, head_count)
    cumulative = jnp.cumsum(log_decay, axis=1)
    block_total = cumulative[:, -1]
    weighted = (
        key_blk.astype(F32) * jnp.exp(block_total[:, None] - cumulative)[:, :, None]
    ).astype(BF16)
    update = jnp.einsum("hjd,hje->hde", weighted, value_blk, preferred_element_type=F32)
    carried = entering_state(update, block_total, seq_count, place, plane)
    log_gap = jnp.where(lower_mask[None], cumulative[:, :, None] - cumulative[:, None, :], 0.0)
    products = jnp.einsum("hid,hjd->hij", query_blk, key_blk, preferred_element_type=F32)
    scores = jnp.where(lower_mask[None], products * jnp.exp(log_gap), 0.0).astype(BF16)
    inner = jnp.einsum("hij,hjd->hid", scores, value_blk, preferred_element_type=F32)
    outer = (
        jnp.einsum("hid,hde->hie", query_blk, carried, preferred_element_type=F32)
        * jnp.exp(cumulative)[:, :, None]
    )
    retained = inner + outer
    scaled = retained * lax.rsqrt(jnp.mean(retained * retained, axis=-1, keepdims=True) + 1e-05)
    return scaled.transpose(1, 0, 2).reshape(rows, head_count * HD).astype(BF16)


def on_device(
    query_rows,
    key_rows,
    value_rows,
    log_decay,
    residual,
    out_weight,
    norm_gain,
    kv_weight,
    block_table,
):
    seq_count = lax.axis_size("seq")
    pool_count = lax.axis_size("pool")
    planes = seq_count // INNER
    index = lax.axis_index("seq")
    me = lax.axis_index("pool")
    place = index % INNER
    plane = index // INNER
    width = out_weight.shape[1]
    rows_here = residual.shape[0]
    cache_width = kv_weight.shape[1]
    pages_here = block_table.shape[0]
    slot_count = 2 * pages_here

    columns = []
    for block in plane_chain(out_weight, seq_count, plane):
        other = seq_xor(block, seq_count, 2)
        columns.append([block, seq_xor(block, seq_count, 1), other, seq_xor(other, seq_count, 1)])

    kv_share = kv_weight.shape[0] // pool_count
    kv_own = lax.dynamic_slice_in_dim(kv_weight, me * kv_share, kv_share, 0)
    kv_pair = jnp.stack([kv_own, seq_xor(kv_own, seq_count, 2)])
    kv_blocks = []
    for pair in plane_chain(kv_pair, seq_count, plane):
        shares = jnp.stack([pair] + [pool_shift(pair, pool_count, r) for r in range(1, pool_count)])
        shares = shares[(me - jnp.arange(pool_count)) % pool_count]
        whole = shares.transpose(1, 0, 2, 3).reshape(2, kv_weight.shape[0], cache_width)
        swapped = seq_xor(whole, seq_count, 1)
        kv_blocks += [whole[0], swapped[0], whole[1], swapped[1]]

    table_parts = jnp.stack(
        [block_table] + [pool_shift(block_table, pool_count, r) for r in range(1, pool_count)]
    )

    mixed = retention(
        query_rows, key_rows, value_rows, log_decay, seq_count, place, plane
    )

    def rows_of(at):
        return lax.dynamic_slice_in_dim(mixed, at * rows_here, rows_here, 0)

    mixed_mine = rows_of(me)
    mixed_away = [rows_of((me + r) % pool_count) for r in range(1, pool_count)]
    hidden = []
    gains = []
    for d in range(planes):
        total = jnp.concatenate(
            [jnp.dot(mixed_mine, w, preferred_element_type=F32) for w in columns[d]], axis=1
        )
        for r in range(1, pool_count):
            away = jnp.concatenate(
                [
                    jnp.dot(mixed_away[r - 1], w, preferred_element_type=F32).astype(BF16)
                    for w in columns[d]
                ],
                axis=1,
            )
            total = total + pool_shift(away, pool_count, r).astype(F32)
        origin = ((plane - d) % planes) * INNER
        starts = [(origin + (place ^ bits)) * width for bits in range(INNER)]
        total = total + jnp.concatenate(
            [lax.dynamic_slice_in_dim(residual, s, width, 1) for s in starts], axis=1
        ).astype(F32)
        gains += [lax.dynamic_slice_in_dim(norm_gain, s, width, 0) for s in starts]
        hidden.append(total)
    square = sum(jnp.sum(h * h, axis=-1, keepdims=True) for h in hidden)
    scale = lax.rsqrt(square / (width * seq_count) + 1e-05)
    normed = (jnp.concatenate(hidden, axis=1) * scale * jnp.concatenate(gains)).astype(BF16)
    cache_rows = jnp.dot(
        normed, jnp.concatenate(kv_blocks, axis=0), preferred_element_type=F32
    ).astype(BF16)

    own_pages = cache_rows.reshape(pages_here, PAGE, cache_width)
    page_cache = jnp.zeros((slot_count, PAGE, cache_width), BF16)
    slot_ids = jnp.arange(slot_count, dtype=jnp.int32)
    for r in range(pool_count):
        pages = own_pages if r == 0 else pool_shift(own_pages, pool_count, r)
        for p in range(pages_here):
            entry = table_parts[r, p]
            here = jnp.logical_and(entry[0] == me, entry[1] == slot_ids)
            page_cache = jnp.where(here[:, None, None], pages[p][None], page_cache)
    return page_cache.reshape(1, 1, slot_count, PAGE, cache_width)


def solution(mesh):
    placed = (
        P("seq", "pool"),
        P("seq", "pool"),
        P("seq", "pool"),
        P("pool", "seq"),
        P(("seq", "pool"), None),
        P("pool", "seq"),
        P(),
        P("seq", None),
        P(("seq", "pool"), None),
    )
    return jax.shard_map(
        on_device,
        mesh=mesh,
        in_specs=placed,
        out_specs=P("seq", "pool", None, None, None),
        check_vma=False,
    )
```

time: 503 us -> 398 us (0.79); the launches traced: 502 us -> 390 us
  waiting for transfers between devices: 367 us -> 135 us
  starting transfers between devices: 3.55 us -> 76.1 us
  local copies, waits for them, and re-layouts: 11.9 us -> 82.7 us
  blocking collectives: 52.7 us -> 0 us
  other arithmetic: 10.5 us -> 35.7 us
  matrix products: 42.3 us -> 56.5 us
  between operations: 13.9 us -> 4.27 us
    all_gather x3 -> x0, waiting for transfers between devices: 273 us -> none  [the longest x1 111 us: on_device(): lax.all_gather(out_weight, 'seq', axis=1, tiled=True)]
    ppermute x0 -> x54, waiting for transfers between devices: none -> 135 us  [hop(): return lax.ppermute(value, axis, pairs)]
    reduce_scatter x1 -> x0, waiting for transfers between devices: 92.7 us -> none  [on_device(): lax.psum_scatter(partial_value, 'pool', scatter_dimension=0, tiled=True)]
    ppermute x0 -> x54, starting transfers between devices: none -> 76.1 us  [hop(): return lax.ppermute(value, axis, pairs)]
    unnamed x16 -> x151, local copies, waits for them, and re-layouts: 4.51 us -> 52.1 us
    unnamed x1 -> x0, blocking collectives: 36 us -> none
    all_to_all x1 -> x0, blocking collectives: 16.8 us -> none  [on_device(): lax.all_to_all(outgoing, 'pool', split_axis=0, concat_axis=0, tiled=True)]
    dot_general x6 -> x36, matrix products: 42.3 us -> 56.5 us  [the longest x16 17.7 us: on_device(): jnp.dot(mixed_mine, w, preferred_element_type=F32)]
  transfers between devices with their start and end apart: 5 -> 54, of which waited for: 4 -> 18; matrix products, arithmetic and copies ran while one was open for 7% -> 43% of each run, Pallas kernels for 0% -> 0%
where the time goes in v1:
time: 398 us; the launch traced here: 390 us
  waiting for transfers between devices  135 us (34%)
  local copies, waits for them, and re-layouts  82.7 us (21%)
  starting transfers between devices  76.1 us (19%)
  matrix products  56.5 us (14%)
  other arithmetic  35.7 us (9%)
  between operations  4.27 us (1%)
    ppermute x54, waiting for transfers between devices, hop(): return lax.ppermute(value, axis, pairs)  135 us
    ppermute x54, starting transfers between devices, hop(): return lax.ppermute(value, axis, pairs)  76.1 us
    unnamed x151, local copies, waits for them, and re-layouts  52.1 us
    dot_general x16, matrix products, on_device(): jnp.dot(mixed_mine, w, preferred_element_type=F32)  17.7 us
    dot_general x16, matrix products, on_device(): jnp.dot(mixed_away[r - 1], w, preferred_element_type=F32).astype(BF16)  16.4 us
    dot_general x1, matrix products, retention(): jnp.einsum('hij,hjd->hid', scores, value_blk, preferred_element_type=F32)  12.2 us
  transfers between devices with their start and end apart: 54, of which 18 were waited for; matrix products, arithmetic and copies ran while one was open for 43% of the time, Pallas kernels for 0%

profile of v1, /device:TPU:0, one launch (start us, length us, event | category | flops | bytes accessed | tf_op | source)
XLA Modules:
  0.0 390.4 jit_solution(8215566582924431085)
XLA Ops:
  3.7 3.0 collective-permute-start.2
  8.2 3.9 %copy.166 = bf16[512,2048]{0,1:T(8,128)(2,1)} copy(bf16[512,2048]{1,0:T(8,128)(2,1)} %param.10) | data formatting | bytes 4194304 | tf_op jit(solution)/shard_map/reshape | solution.py:109
  12.1 3.1 fusion.23
  16.5 1.7 collective-permute-start.8
  41.5 2.8 constant_dynamic-slice_fusion.16
  45.6 1.6 collective-permute-start.4
  47.2 2.6 collective-permute-start.5
  58.7 1.5 fusion.43
  60.2 3.0 collective-permute-start.10
  63.2 4.2 %collective-permute-start.11 = (bf16[4,128,128]{2,1,0:T(8,128)(2,1)}, bf16[4,128,128]{2,1,0:T(8,128)(2,1)}, u32[]{:S(2)}, u32[]{:S(2)}) collective-permute-start(bf16[4,128,128]{2,1,0:T(8,128)(2,1)} %fusion.43), channel_id=1, source_target_pairs={{0,16},{2,18},{4,20},{6,22},{8,24},{10,26},{12,28},{14,30},{1,17},... | collective-permute-start | bytes 393224 | tf_op jit(solution)/shard_map/ppermute | solution.py:14
  67.4 1.9 collective-permute-start.12
  74.2 1.5 fusion.47
  76.6 1.5 collective-permute-start.14
  79.8 3.6 copy.193
  83.5 1.7 copy.173
  85.2 1.7 copy.174
  86.8 1.7 copy.175
  90.4 1.7 copy.179
  92.0 1.7 copy.180
  93.7 1.7 copy.181
  101.7 1.8 fusion.59
  103.6 1.5 collective-permute-start.39
  106.4 5.5 %collective-permute-start.41 = (bf16[2,128,1024]{2,1,0:T(8,128)(2,1)}, bf16[2,128,1024]{2,1,0:T(8,128)(2,1)}, u32[]{:S(2)}, u32[]{:S(2)}) collective-permute-start(bf16[2,128,1024]{2,1,0:T(8,128)(2,1)} %get-tuple-element.59), channel_id=1, source_target_pairs={{0,8},{2,10},{4,12},{6,14},{8,16},{10,18},{12,20},{14,22},{16,24},... | collective-permute-start | bytes 1572872 | tf_op jit(solution)/shard_map/ppermute | solution.py:14
  113.9 1.6 copy.140
  115.5 1.7 copy.141
  117.2 1.7 copy.142
  118.9 1.7 copy.143
  120.5 3.8 fusion.11
  124.4 12.2 %fusion.3 = (f32[16,512]{1,0:T(8,128)}, f32[16,512,128]{1,2,0:T(8,128)}) fusion(f32[16,128,512]{2,1,0:T(8,128)} %fusion.11, f32[16,512]{1,0:T(8,128)} %get-tuple-element.62, bf16[16,512,128]{2,0,1:T(8,128)(2,1)} %bitcast.323, bf16[16,512,128]{1,2,0:T(8,128)(2,1)} %bitcast.322, f32[16,512]{1,0:T(8,128)} %copy-done.43, ...), kind=kOutput, calls=%fused_computation.12 | convolution fusion | flops 2172641280 | bytes 15040512 | tf_op jit(solution)/shard_map/hij,hjd->hid/dot_general | solution.py:129
  137.4 4.7 %fusion.6 = bf16[512,16,128]{0,2,1:T(8,128)(2,1)S(1)} fusion(f32[16,128,512]{2,1,0:T(8,128)} %fusion.11, f32[16,512,128]{1,2,0:T(8,128)} %get-tuple-element.81, f32[512,16]{0,1:T(8,128)S(1)} %rsqrt_bitcast_fusion, f32[512,16]{0,1:T(8,128)} %get-tuple-element.61), kind=kLoop, calls=%fused_computation.16 | loop fusion | flops 4194304 | bytes 10551296 | tf_op jit(solution)/shard_map/convert_element_type | solution.py:136
  142.1 3.2 fusion.75
  145.3 2.4 convolution_convert_fusion.15
  150.8 5.7 %collective-permute-start.20 = (bf16[2048,256]{1,0:T(8,128)(2,1)}, bf16[2048,256]{1,0:T(8,128)(2,1)}, u32[]{:S(2)}, u32[]{:S(2)}) collective-permute-start(bf16[2048,256]{1,0:T(8,128)(2,1)} %param.14), channel_id=1, source_target_pairs={{0,8},{2,10},{4,12},{6,14},{8,16},{10,18},{12,20},{14,22},{16,24},... | collective-permute-start | bytes 3145736 | tf_op jit(solution)/shard_map/ppermute | solution.py:14
  157.8 4.6 %collective-permute-start.47 = (bf16[2,128,1024]{2,1,0:T(8,128)(2,1)}, bf16[2,128,1024]{2,1,0:T(8,128)(2,1)S(1)}, u32[]{:S(2)}, u32[]{:S(2)}) collective-permute-start(bf16[2,128,1024]{2,1,0:T(8,128)(2,1)} %collective-permute-done.41), channel_id=1, source_target_pairs={{0,8},{2,10},{4,12},{6,14},{8,16},{10,18},{12,20},{14,22},{16,24},... | collective-permute-start | bytes 1572872 | tf_op jit(solution)/shard_map/ppermute | solution.py:14
  164.1 2.4 convolution_convert_fusion.13
  166.5 19.1 %collective-permute-done.43 = bf16[2,128,1024]{2,1,0:T(8,128)(2,1)} collective-permute-done((bf16[2,128,1024]{2,1,0:T(8,128)(2,1)}, bf16[2,128,1024]{2,1,0:T(8,128)(2,1)}, u32[]{:S(2)}, u32[]{:S(2)}) %collective-permute-start.43) | collective-permute-done | bytes 524320 | tf_op jit(solution)/shard_map/ppermute | solution.py:14
  185.6 3.1 collective-permute-done.47
  190.6 2.4 convolution_convert_fusion.14
  194.3 5.9 %collective-permute-start.28 = (bf16[2048,256]{1,0:T(8,128)(2,1)}, bf16[2048,256]{1,0:T(8,128)(2,1)}, u32[]{:S(2)}, u32[]{:S(2)}) collective-permute-start(bf16[2048,256]{1,0:T(8,128)(2,1)} %collective-permute-done.20), channel_id=1, source_target_pairs={{0,8},{2,10},{4,12},{6,14},{8,16},{10,18},{12,20},{14,22},{16,24},... | collective-permute-start | bytes 3145736 | tf_op jit(solution)/shard_map/ppermute | solution.py:14
  200.3 2.5 fusion.73
  202.7 2.5 fusion.74
  208.4 4.6 %collective-permute-start.50 = (bf16[2,128,1024]{2,1,0:T(8,128)(2,1)S(1)}, bf16[2,128,1024]{2,1,0:T(8,128)(2,1)S(1)}, u32[]{:S(2)}, u32[]{:S(2)}) collective-permute-start(bf16[2,128,1024]{2,1,0:T(8,128)(2,1)S(1)} %copy-done.31), channel_id=1, source_target_pairs={{0,8},{2,10},{4,12},{6,14},{8,16},{10,18},{12,20},{14,22},{16,24},... | collective-permute-start | bytes 1572872 | tf_op jit(solution)/shard_map/ppermute | solution.py:14
  216.5 15.7 %collective-permute-done.44 = bf16[2,128,1024]{2,1,0:T(8,128)(2,1)} collective-permute-done((bf16[2,128,1024]{2,1,0:T(8,128)(2,1)}, bf16[2,128,1024]{2,1,0:T(8,128)(2,1)}, u32[]{:S(2)}, u32[]{:S(2)}) %collective-permute-start.44) | collective-permute-done | bytes 524320 | tf_op jit(solution)/shard_map/ppermute | solution.py:14
  232.2 1.5 collective-permute-start
  236.7 1.8 convolution_convert_fusion.12
  239.4 1.4 collective-permute-start.51
  245.2 2.5 fusion.72
  247.7 2.1 collective-permute-done.45
  251.8 9.3 %collective-permute-done.51 = bf16[2,128,1024]{2,1,0:T(8,128)(2,1)} collective-permute-done((bf16[2,128,1024]{2,1,0:T(8,128)(2,1)S(1)}, bf16[2,128,1024]{2,1,0:T(8,128)(2,1)}, u32[]{:S(2)}, u32[]{:S(2)}) %collective-permute-start.51) | collective-permute-done | bytes 524320 | tf_op jit(solution)/shard_map/ppermute | solution.py:14
  261.1 4.8 %collective-permute-start.33 = (bf16[2048,256]{1,0:T(8,128)(2,1)}, bf16[2048,256]{1,0:T(8,128)(2,1)}, u32[]{:S(2)}, u32[]{:S(2)}) collective-permute-start(bf16[2048,256]{1,0:T(8,128)(2,1)} %collective-permute-done.28), channel_id=1, source_target_pairs={{0,8},{2,10},{4,12},{6,14},{8,16},{10,18},{12,20},{14,22},{16,24},... | collective-permute-start | bytes 3145736 | tf_op jit(solution)/shard_map/ppermute | solution.py:14
  269.0 1.5 collective-permute-done.19
  270.5 1.5 collective-permute-start.30
  273.4 1.4 collective-permute-done.23
  276.8 6.7 %collective-permute-done.33 = bf16[2048,256]{1,0:T(8,128)(2,1)} collective-permute-done((bf16[2048,256]{1,0:T(8,128)(2,1)}, bf16[2048,256]{1,0:T(8,128)(2,1)}, u32[]{:S(2)}, u32[]{:S(2)}) %collective-permute-start.33) | collective-permute-done | bytes 1048608 | tf_op jit(solution)/shard_map/ppermute | solution.py:14
  285.9 8.0 %collective-permute-done.30 = bf16[2048,256]{1,0:T(8,128)(2,1)S(1)} collective-permute-done((bf16[2048,256]{1,0:T(8,128)(2,1)S(1)}, bf16[2048,256]{1,0:T(8,128)(2,1)S(1)}, u32[]{:S(2)}, u32[]{:S(2)}) %collective-permute-start.30) | collective-permute-done | bytes 1048608 | tf_op jit(solution)/shard_map/ppermute | solution.py:14
  295.5 1.6 collective-permute-start.25
  303.6 18.0 %collective-permute-done.25 = bf16[2048,256]{1,0:T(8,128)(2,1)S(1)} collective-permute-done((bf16[2048,256]{1,0:T(8,128)(2,1)S(1)}, bf16[2048,256]{1,0:T(8,128)(2,1)S(1)}, u32[]{:S(2)}, u32[]{:S(2)}) %collective-permute-start.25) | collective-permute-done | bytes 1048608 | tf_op jit(solution)/shard_map/ppermute | solution.py:14
  326.0 17.6 %collective-permute-done.35 = bf16[2048,256]{1,0:T(8,128)(2,1)S(1)} collective-permute-done((bf16[2048,256]{1,0:T(8,128)(2,1)S(1)}, bf16[2048,256]{1,0:T(8,128)(2,1)S(1)}, u32[]{:S(2)}, u32[]{:S(2)}) %collective-permute-start.35) | collective-permute-done | bytes 1048608 | tf_op jit(solution)/shard_map/ppermute | solution.py:14
  347.1 1.5 collective-permute-start.37
  349.8 10.9 %collective-permute-done.27 = bf16[256,1024]{0,1:T(8,128)(2,1)S(1)} collective-permute-done((bf16[256,1024]{0,1:T(8,128)(2,1)S(1)}, bf16[256,1024]{0,1:T(8,128)(2,1)S(1)}, u32[]{:S(2)}, u32[]{:S(2)}) %collective-permute-start.27) | collective-permute-done | bytes 524320 | tf_op jit(solution)/shard_map/ppermute | solution.py:14
  360.9 10.6 %collective-permute-done.37 = bf16[256,1024]{0,1:T(8,128)(2,1)S(1)} collective-permute-done((bf16[256,1024]{0,1:T(8,128)(2,1)S(1)}, bf16[256,1024]{0,1:T(8,128)(2,1)S(1)}, u32[]{:S(2)}, u32[]{:S(2)}) %collective-permute-start.37) | collective-permute-done | bytes 524320 | tf_op jit(solution)/shard_map/ppermute | solution.py:14
  371.8 3.2 fusion.20
  378.9 1.4 compare_and_fusion.2
  380.4 8.3 %collective-permute-done.53 = bf16[2,128,1024]{2,1,0:T(8,128)(2,1)S(1)} collective-permute-done((bf16[2,128,1024]{2,1,0:T(8,128)(2,1)S(1)}, bf16[2,128,1024]{2,1,0:T(8,128)(2,1)S(1)}, u32[]{:S(2)}, u32[]{:S(2)}) %collective-permute-start.53) | collective-permute-done | bytes 524320 | tf_op jit(solution)/shard_map/ppermute | solution.py:14
  (318 shorter events, 114.1 us)
Async XLA Ops:
  0.0 120.5 %copy-start = (bf16[512,2048]{1,0:T(8,128)(2,1)S(1)}, bf16[512,2048]{1,0:T(8,128)(2,1)}, u32[]{:S(2)}) copy-start(bf16[512,2048]{1,0:T(8,128)(2,1)} %param.9) | copy-start | bytes 6291460
  3.7 40.6 %collective-permute-start.2 = (f32[16]{0:T(128)}, f32[16]{0:T(128)}, u32[]{:S(2)}, u32[]{:S(2)}) collective-permute-start(f32[16]{0:T(128)} %slice_reduce_fusion.1), channel_id=1, source_target_pairs={{0,4},{2,6},{4,0},{6,2},{8,12},{10,14},{12,8},{14,10},{16,20},{18,... | collective-permute-start | bytes 200 | tf_op jit(solution)/shard_map/ppermute | solution.py:14
  6.7 37.6 %collective-permute-start.3 = (f32[16]{0:T(128)}, f32[16]{0:T(128)}, u32[]{:S(2)}, u32[]{:S(2)}) collective-permute-start(f32[16]{0:T(128)} %slice_reduce_fusion.1), channel_id=1, source_target_pairs={{0,6},{2,4},{4,2},{6,0},{8,14},{10,12},{12,10},{14,8},{16,22},{18,... | collective-permute-start | bytes 200 | tf_op jit(solution)/shard_map/ppermute | solution.py:14
  6.7 37.6 %collective-permute-start.1 = (f32[16]{0:T(128)}, f32[16]{0:T(128)}, u32[]{:S(2)}, u32[]{:S(2)}) collective-permute-start(f32[16]{0:T(128)} %slice_reduce_fusion.1), channel_id=1, source_target_pairs={{0,2},{2,0},{4,6},{6,4},{8,10},{10,8},{12,14},{14,12},{16,18},{18,... | collective-permute-start | bytes 200 | tf_op jit(solution)/shard_map/ppermute | solution.py:14
  16.1 39.7 %collective-permute-start.7 = (bf16[4,128,128]{2,1,0:T(8,128)(2,1)}, bf16[4,128,128]{2,1,0:T(8,128)(2,1)}, u32[]{:S(2)}, u32[]{:S(2)}) collective-permute-start(bf16[4,128,128]{2,1,0:T(8,128)(2,1)} %get-tuple-element.57), channel_id=1, source_target_pairs={{0,2},{2,0},{4,6},{6,4},{8,10},{10,8},{12,14},{14,12},{16,18},{18,... | collective-permute-start | bytes 393224 | tf_op jit(solution)/shard_map/ppermute | solution.py:14
  16.5 39.4 %collective-permute-start.8 = (bf16[4,128,128]{2,1,0:T(8,128)(2,1)}, bf16[4,128,128]{2,1,0:T(8,128)(2,1)}, u32[]{:S(2)}, u32[]{:S(2)}) collective-permute-start(bf16[4,128,128]{2,1,0:T(8,128)(2,1)} %get-tuple-element.56), channel_id=1, source_target_pairs={{0,4},{2,6},{4,0},{6,2},{8,12},{10,14},{12,8},{14,10},{16,20},{18,... | collective-permute-start | bytes 393224 | tf_op jit(solution)/shard_map/ppermute | solution.py:14
  45.6 5.6 %collective-permute-start.4 = (f32[4,16]{1,0:T(4,128)S(1)}, f32[4,16]{1,0:T(4,128)S(1)}, u32[]{:S(2)}, u32[]{:S(2)}) collective-permute-start(f32[4,16]{1,0:T(4,128)S(1)} %gather_fusion), channel_id=1, source_target_pairs={{0,8},{2,10},{4,12},{6,14},{8,16},{10,18},{12,20},{14,22},{16,24},... | collective-permute-start | bytes 776 | tf_op jit(solution)/shard_map/ppermute | solution.py:14
  47.2 4.5 %collective-permute-start.5 = (f32[4,16]{1,0:T(4,128)S(1)}, f32[4,16]{1,0:T(4,128)S(1)}, u32[]{:S(2)}, u32[]{:S(2)}) collective-permute-start(f32[4,16]{1,0:T(4,128)S(1)} %gather_fusion), channel_id=1, source_target_pairs={{0,16},{2,18},{4,20},{6,22},{8,24},{10,26},{12,28},{14,30},{16,0},... | collective-permute-start | bytes 776 | tf_op jit(solution)/shard_map/ppermute | solution.py:14
  49.8 3.6 collective-permute-start.6
  51.2 5.7 %collective-permute-start.9 = (bf16[4,128,128]{2,1,0:T(8,128)(2,1)S(1)}, bf16[4,128,128]{2,1,0:T(8,128)(2,1)S(1)}, u32[]{:S(2)}, u32[]{:S(2)}) collective-permute-start(bf16[4,128,128]{2,1,0:T(8,128)(2,1)S(1)} %copy-done.37), channel_id=1, source_target_pairs={{0,6},{2,4},{4,2},{6,0},{8,14},{10,12},{12,10},{14,8},{16,22},{18,... | collective-permute-start | bytes 393224 | tf_op jit(solution)/shard_map/ppermute | solution.py:14
  51.7 106.1 %collective-permute-start.17 = (bf16[2048,256]{1,0:T(8,128)(2,1)}, bf16[2048,256]{1,0:T(8,128)(2,1)}, u32[]{:S(2)}, u32[]{:S(2)}) collective-permute-start(bf16[2048,256]{1,0:T(8,128)(2,1)} %param.14), channel_id=1, source_target_pairs={{0,4},{2,6},{4,0},{6,2},{8,12},{10,14},{12,8},{14,10},{16,20},{18,... | collective-permute-start | bytes 3145736 | tf_op jit(solution)/shard_map/ppermute | solution.py:14
  53.4 48.0 %collective-permute-start.38 = (bf16[128,1024]{1,0:T(8,128)(2,1)}, bf16[128,1024]{1,0:T(8,128)(2,1)}, u32[]{:S(2)}, u32[]{:S(2)}) collective-permute-start(bf16[128,1024]{1,0:T(8,128)(2,1)} %constant_dynamic-slice_fusion), channel_id=1, source_target_pairs={{0,4},{2,6},{4,0},{6,2},{8,12},{10,14},{12,8},{14,10},{16,20},{18,... | collective-permute-start | bytes 786440 | tf_op jit(solution)/shard_map/ppermute | solution.py:14
  60.2 14.0 %collective-permute-start.10 = (bf16[4,128,128]{2,1,0:T(8,128)(2,1)}, bf16[4,128,128]{2,1,0:T(8,128)(2,1)}, u32[]{:S(2)}, u32[]{:S(2)}) collective-permute-start(bf16[4,128,128]{2,1,0:T(8,128)(2,1)} %fusion.43), channel_id=1, source_target_pairs={{0,8},{2,10},{4,12},{6,14},{8,16},{10,18},{12,20},{14,22},{16,24},... | collective-permute-start | bytes 393224 | tf_op jit(solution)/shard_map/ppermute | solution.py:14
  63.2 11.0 %collective-permute-start.11 = (bf16[4,128,128]{2,1,0:T(8,128)(2,1)}, bf16[4,128,128]{2,1,0:T(8,128)(2,1)}, u32[]{:S(2)}, u32[]{:S(2)}) collective-permute-start(bf16[4,128,128]{2,1,0:T(8,128)(2,1)} %fusion.43), channel_id=1, source_target_pairs={{0,16},{2,18},{4,20},{6,22},{8,24},{10,26},{12,28},{14,30},{1,17},... | collective-permute-start | bytes 393224 | tf_op jit(solution)/shard_map/ppermute | solution.py:14
  67.4 6.8 %collective-permute-start.12 = (bf16[4,128,128]{2,1,0:T(8,128)(2,1)}, bf16[4,128,128]{2,1,0:T(8,128)(2,1)}, u32[]{:S(2)}, u32[]{:S(2)}) collective-permute-start(bf16[4,128,128]{2,1,0:T(8,128)(2,1)} %fusion.43), channel_id=1, source_target_pairs={{0,24},{2,26},{4,28},{6,30},{1,25},{3,27},{5,29},{7,31}} | collective-permute-start | bytes 393224 | tf_op jit(solution)/shard_map/ppermute | solution.py:14
  76.6 27.0 %collective-permute-start.13 = (bf16[4,128,128]{2,1,0:T(8,128)(2,1)}, bf16[4,128,128]{2,1,0:T(8,128)(2,1)}, u32[]{:S(2)}, u32[]{:S(2)}) collective-permute-start(bf16[4,128,128]{2,1,0:T(8,128)(2,1)} %get-tuple-element.53), channel_id=1, source_target_pairs={{0,2},{2,0},{4,6},{6,4},{8,10},{10,8},{12,14},{14,12},{16,18},{18,... | collective-permute-start | bytes 393224 | tf_op jit(solution)/shard_map/ppermute | solution.py:14
  76.6 28.5 %collective-permute-start.14 = (bf16[4,128,128]{2,1,0:T(8,128)(2,1)}, bf16[4,128,128]{2,1,0:T(8,128)(2,1)}, u32[]{:S(2)}, u32[]{:S(2)}) collective-permute-start(bf16[4,128,128]{2,1,0:T(8,128)(2,1)} %get-tuple-element.52), channel_id=1, source_target_pairs={{0,4},{2,6},{4,0},{6,2},{8,12},{10,14},{12,8},{14,10},{16,20},{18,... | collective-permute-start | bytes 393224 | tf_op jit(solution)/shard_map/ppermute | solution.py:14
  78.1 28.2 %collective-permute-start.15 = (bf16[4,128,128]{2,1,0:T(8,128)(2,1)}, bf16[4,128,128]{2,1,0:T(8,128)(2,1)}, u32[]{:S(2)}, u32[]{:S(2)}) collective-permute-start(bf16[4,128,128]{2,1,0:T(8,128)(2,1)} %get-tuple-element.51), channel_id=1, source_target_pairs={{0,6},{2,4},{4,2},{6,0},{8,14},{10,12},{12,10},{14,8},{16,22},{18,... | collective-permute-start | bytes 393224 | tf_op jit(solution)/shard_map/ppermute | solution.py:14
  101.4 88.6 %collective-permute-start.16 = (bf16[2048,256]{1,0:T(8,128)(2,1)}, bf16[2048,256]{1,0:T(8,128)(2,1)}, u32[]{:S(2)}, u32[]{:S(2)}) collective-permute-start(bf16[2048,256]{1,0:T(8,128)(2,1)} %param.14), channel_id=1, source_target_pairs={{0,2},{2,0},{4,6},{6,4},{8,10},{10,8},{12,14},{14,12},{16,18},{18,... | collective-permute-start | bytes 3145736 | tf_op jit(solution)/shard_map/ppermute | solution.py:14
  103.6 44.1 %collective-permute-start.39 = (bf16[2,128,1024]{2,1,0:T(8,128)(2,1)}, bf16[2,128,1024]{2,1,0:T(8,128)(2,1)S(1)}, u32[]{:S(2)}, u32[]{:S(2)}) collective-permute-start(bf16[2,128,1024]{2,1,0:T(8,128)(2,1)} %get-tuple-element.59), channel_id=1, source_target_pairs={{0,1},{1,0},{2,3},{3,2},{4,5},{5,4},{6,7},{7,6},{8,9},{9,8},{10,11... | collective-permute-start | bytes 1572872 | tf_op jit(solution)/shard_map/ppermute | solution.py:14
  105.1 45.7 %collective-permute-start.42 = (bf16[2,128,1024]{2,1,0:T(8,128)(2,1)}, bf16[2,128,1024]{2,1,0:T(8,128)(2,1)}, u32[]{:S(2)}, u32[]{:S(2)}) collective-permute-start(bf16[2,128,1024]{2,1,0:T(8,128)(2,1)} %get-tuple-element.59), channel_id=1, source_target_pairs={{8,0},{10,2},{12,4},{14,6},{16,8},{18,10},{20,12},{22,14},{24,16},... | collective-permute-start | bytes 1572872 | tf_op jit(solution)/shard_map/ppermute | solution.py:14
  106.4 50.1 %collective-permute-start.41 = (bf16[2,128,1024]{2,1,0:T(8,128)(2,1)}, bf16[2,128,1024]{2,1,0:T(8,128)(2,1)}, u32[]{:S(2)}, u32[]{:S(2)}) collective-permute-start(bf16[2,128,1024]{2,1,0:T(8,128)(2,1)} %get-tuple-element.59), channel_id=1, source_target_pairs={{0,8},{2,10},{4,12},{6,14},{8,16},{10,18},{12,20},{14,22},{16,24},... | collective-permute-start | bytes 1572872 | tf_op jit(solution)/shard_map/ppermute | solution.py:14
  147.7 45.3 %collective-permute-start.21 = (bf16[2048,256]{1,0:T(8,128)(2,1)}, bf16[2048,256]{1,0:T(8,128)(2,1)}, u32[]{:S(2)}, u32[]{:S(2)}) collective-permute-start(bf16[2048,256]{1,0:T(8,128)(2,1)} %param.14), channel_id=1, source_target_pairs={{8,0},{10,2},{12,4},{14,6},{16,8},{18,10},{20,12},{22,14},{24,16},... | collective-permute-start | bytes 3145736 | tf_op jit(solution)/shard_map/ppermute | solution.py:14
  150.8 43.5 %collective-permute-start.20 = (bf16[2048,256]{1,0:T(8,128)(2,1)}, bf16[2048,256]{1,0:T(8,128)(2,1)}, u32[]{:S(2)}, u32[]{:S(2)}) collective-permute-start(bf16[2048,256]{1,0:T(8,128)(2,1)} %param.14), channel_id=1, source_target_pairs={{0,8},{2,10},{4,12},{6,14},{8,16},{10,18},{12,20},{14,22},{16,24},... | collective-permute-start | bytes 3145736 | tf_op jit(solution)/shard_map/ppermute | solution.py:14
  156.5 29.1 %collective-permute-start.43 = (bf16[2,128,1024]{2,1,0:T(8,128)(2,1)}, bf16[2,128,1024]{2,1,0:T(8,128)(2,1)}, u32[]{:S(2)}, u32[]{:S(2)}) collective-permute-start(bf16[2,128,1024]{2,1,0:T(8,128)(2,1)} %collective-permute-done.42), channel_id=1, source_target_pairs={{8,0},{10,2},{12,4},{14,6},{16,8},{18,10},{20,12},{22,14},{24,16},... | collective-permute-start | bytes 1572872 | tf_op jit(solution)/shard_map/ppermute | solution.py:14
  157.8 30.9 %collective-permute-start.47 = (bf16[2,128,1024]{2,1,0:T(8,128)(2,1)}, bf16[2,128,1024]{2,1,0:T(8,128)(2,1)S(1)}, u32[]{:S(2)}, u32[]{:S(2)}) collective-permute-start(bf16[2,128,1024]{2,1,0:T(8,128)(2,1)} %collective-permute-done.41), channel_id=1, source_target_pairs={{0,8},{2,10},{4,12},{6,14},{8,16},{10,18},{12,20},{14,22},{16,24},... | collective-permute-start | bytes 1572872 | tf_op jit(solution)/shard_map/ppermute | solution.py:14
  185.6 22.7 %collective-permute-start.40 = (bf16[2,256,1024]{2,1,0:T(8,128)(2,1)}, bf16[2,256,1024]{2,1,0:T(8,128)(2,1)S(1)}, u32[]{:S(2)}, u32[]{:S(2)}) collective-permute-start(bf16[2,256,1024]{2,1,0:T(8,128)(2,1)} %bitcast.64), channel_id=1, source_target_pairs={{0,2},{2,0},{4,6},{6,4},{8,10},{10,8},{12,14},{14,12},{16,18},{18,... | collective-permute-start | bytes 3145736 | tf_op jit(solution)/shard_map/ppermute | solution.py:14
  188.7 47.9 %collective-permute-start.18 = (bf16[2048,256]{1,0:T(8,128)(2,1)}, bf16[2048,256]{1,0:T(8,128)(2,1)}, u32[]{:S(2)}, u32[]{:S(2)}) collective-permute-start(bf16[2048,256]{1,0:T(8,128)(2,1)} %collective-permute-done.17), channel_id=1, source_target_pairs={{0,2},{2,0},{4,6},{6,4},{8,10},{10,8},{12,14},{14,12},{16,18},{18,... | collective-permute-start | bytes 3145736 | tf_op jit(solution)/shard_map/ppermute | solution.py:14
  190.0 15.2 %collective-permute-start.48 = (bf16[2,128,1024]{2,1,0:T(8,128)(2,1)S(1)}, bf16[2,128,1024]{2,1,0:T(8,128)(2,1)S(1)}, u32[]{:S(2)}, u32[]{:S(2)}) collective-permute-start(bf16[2,128,1024]{2,1,0:T(8,128)(2,1)S(1)} %broadcast_select_fusion.4), channel_id=1, source_target_pairs={{0,1},{1,0},{2,3},{3,2},{4,5},{5,4},{6,7},{7,6},{8,9},{9,8},{10,11... | collective-permute-start | bytes 1572872 | tf_op jit(solution)/shard_map/ppermute | solution.py:14
  193.0 46.4 %collective-permute-start.22 = (bf16[2048,256]{1,0:T(8,128)(2,1)}, bf16[2048,256]{1,0:T(8,128)(2,1)}, u32[]{:S(2)}, u32[]{:S(2)}) collective-permute-start(bf16[2048,256]{1,0:T(8,128)(2,1)} %collective-permute-done.21), channel_id=1, source_target_pairs={{8,0},{10,2},{12,4},{14,6},{16,8},{18,10},{20,12},{22,14},{24,16},... | collective-permute-start | bytes 3145736 | tf_op jit(solution)/shard_map/ppermute | solution.py:14
  194.3 46.5 %collective-permute-start.28 = (bf16[2048,256]{1,0:T(8,128)(2,1)}, bf16[2048,256]{1,0:T(8,128)(2,1)}, u32[]{:S(2)}, u32[]{:S(2)}) collective-permute-start(bf16[2048,256]{1,0:T(8,128)(2,1)} %collective-permute-done.20), channel_id=1, source_target_pairs={{0,8},{2,10},{4,12},{6,14},{8,16},{10,18},{12,20},{14,22},{16,24},... | collective-permute-start | bytes 3145736 | tf_op jit(solution)/shard_map/ppermute | solution.py:14
  205.2 27.0 %collective-permute-start.44 = (bf16[2,128,1024]{2,1,0:T(8,128)(2,1)}, bf16[2,128,1024]{2,1,0:T(8,128)(2,1)}, u32[]{:S(2)}, u32[]{:S(2)}) collective-permute-start(bf16[2,128,1024]{2,1,0:T(8,128)(2,1)} %collective-permute-done.43), channel_id=1, source_target_pairs={{8,0},{10,2},{12,4},{14,6},{16,8},{18,10},{20,12},{22,14},{24,16},... | collective-permute-start | bytes 1572872 | tf_op jit(solution)/shard_map/ppermute | solution.py:14
  208.4 26.4 %collective-permute-start.50 = (bf16[2,128,1024]{2,1,0:T(8,128)(2,1)S(1)}, bf16[2,128,1024]{2,1,0:T(8,128)(2,1)S(1)}, u32[]{:S(2)}, u32[]{:S(2)}) collective-permute-start(bf16[2,128,1024]{2,1,0:T(8,128)(2,1)S(1)} %copy-done.31), channel_id=1, source_target_pairs={{0,8},{2,10},{4,12},{6,14},{8,16},{10,18},{12,20},{14,22},{16,24},... | collective-permute-start | bytes 1572872 | tf_op jit(solution)/shard_map/ppermute | solution.py:14
  215.7 21.0 %copy-start.4 = (bf16[512,16,128]{0,2,1:T(8,128)(2,1)S(1)}, bf16[512,16,128]{0,2,1:T(8,128)(2,1)}, u32[]{:S(2)}) copy-start(bf16[512,16,128]{0,2,1:T(8,128)(2,1)} %copy-done.2) | copy-start | bytes 6291460
  232.2 144.7 %collective-permute-start = (s32[2,2]{1,0:T(2,128)S(1)}, s32[2,2]{1,0:T(2,128)S(1)}, u32[]{:S(2)}, u32[]{:S(2)}) collective-permute-start(s32[2,2]{1,0:T(2,128)S(1)} %copy-done.47), channel_id=1, source_target_pairs={{0,1},{1,0},{2,3},{3,2},{4,5},{5,4},{6,7},{7,6},{8,9},{9,8},{10,11... | collective-permute-start | bytes 56 | tf_op jit(solution)/shard_map/ppermute | solution.py:14
  234.8 14.9 %collective-permute-start.45 = (bf16[2,128,1024]{2,1,0:T(8,128)(2,1)S(1)}, bf16[2,128,1024]{2,1,0:T(8,128)(2,1)S(1)}, u32[]{:S(2)}, u32[]{:S(2)}) collective-permute-start(bf16[2,128,1024]{2,1,0:T(8,128)(2,1)S(1)} %broadcast_select_fusion.5), channel_id=1, source_target_pairs={{0,1},{1,0},{2,3},{3,2},{4,5},{5,4},{6,7},{7,6},{8,9},{9,8},{10,11... | collective-permute-start | bytes 1572872 | tf_op jit(solution)/shard_map/ppermute | solution.py:14
  236.6 62.7 %collective-permute-start.49 = (bf16[2,256,1024]{2,1,0:T(8,128)(2,1)}, bf16[2,256,1024]{2,1,0:T(8,128)(2,1)}, u32[]{:S(2)}, u32[]{:S(2)}) collective-permute-start(bf16[2,256,1024]{2,1,0:T(8,128)(2,1)} %bitcast.80), channel_id=1, source_target_pairs={{0,2},{2,0},{4,6},{6,4},{8,10},{10,8},{12,14},{14,12},{16,18},{18,... | collective-permute-start | bytes 3145736 | tf_op jit(solution)/shard_map/ppermute | solution.py:14
  239.4 21.7 %collective-permute-start.51 = (bf16[2,128,1024]{2,1,0:T(8,128)(2,1)S(1)}, bf16[2,128,1024]{2,1,0:T(8,128)(2,1)}, u32[]{:S(2)}, u32[]{:S(2)}) collective-permute-start(bf16[2,128,1024]{2,1,0:T(8,128)(2,1)S(1)} %broadcast_select_fusion.3), channel_id=1, source_target_pairs={{0,1},{1,0},{2,3},{3,2},{4,5},{5,4},{6,7},{7,6},{8,9},{9,8},{10,11... | collective-permute-start | bytes 1572872 | tf_op jit(solution)/shard_map/ppermute | solution.py:14
  240.9 29.7 %collective-permute-start.19 = (bf16[256,1024]{0,1:T(8,128)(2,1)}, bf16[256,1024]{0,1:T(8,128)(2,1)}, u32[]{:S(2)}, u32[]{:S(2)}) collective-permute-start(bf16[256,1024]{0,1:T(8,128)(2,1)} %pad_maximum_fusion.7), channel_id=1, source_target_pairs={{0,1},{1,0},{2,3},{3,2},{4,5},{5,4},{6,7},{7,6},{8,9},{9,8},{10,11... | collective-permute-start | bytes 1572872 | tf_op jit(solution)/shard_map/ppermute | solution.py:14
  249.7 25.1 %collective-permute-start.23 = (bf16[2048,256]{1,0:T(8,128)(2,1)}, bf16[2048,256]{1,0:T(8,128)(2,1)}, u32[]{:S(2)}, u32[]{:S(2)}) collective-permute-start(bf16[2048,256]{1,0:T(8,128)(2,1)} %collective-permute-done.22), channel_id=1, source_target_pairs={{8,0},{10,2},{12,4},{14,6},{16,8},{18,10},{20,12},{22,14},{24,16},... | collective-permute-start | bytes 3145736 | tf_op jit(solution)/shard_map/ppermute | solution.py:14
  261.1 22.4 %collective-permute-start.33 = (bf16[2048,256]{1,0:T(8,128)(2,1)}, bf16[2048,256]{1,0:T(8,128)(2,1)}, u32[]{:S(2)}, u32[]{:S(2)}) collective-permute-start(bf16[2048,256]{1,0:T(8,128)(2,1)} %collective-permute-done.28), channel_id=1, source_target_pairs={{0,8},{2,10},{4,12},{6,14},{8,16},{10,18},{12,20},{14,22},{16,24},... | collective-permute-start | bytes 3145736 | tf_op jit(solution)/shard_map/ppermute | solution.py:14
  270.5 23.4 %collective-permute-start.30 = (bf16[2048,256]{1,0:T(8,128)(2,1)S(1)}, bf16[2048,256]{1,0:T(8,128)(2,1)S(1)}, u32[]{:S(2)}, u32[]{:S(2)}) collective-permute-start(bf16[2048,256]{1,0:T(8,128)(2,1)S(1)} %copy-done.11), channel_id=1, source_target_pairs={{0,4},{2,6},{4,0},{6,2},{8,12},{10,14},{12,8},{14,10},{16,20},{18,... | collective-permute-start | bytes 3145736 | tf_op jit(solution)/shard_map/ppermute | solution.py:14
  274.9 20.7 %collective-permute-start.29 = (bf16[2048,256]{1,0:T(8,128)(2,1)S(1)}, bf16[2048,256]{1,0:T(8,128)(2,1)S(1)}, u32[]{:S(2)}, u32[]{:S(2)}) collective-permute-start(bf16[2048,256]{1,0:T(8,128)(2,1)S(1)} %copy-done.11), channel_id=1, source_target_pairs={{0,2},{2,0},{4,6},{6,4},{8,10},{10,8},{12,14},{14,12},{16,18},{18,... | collective-permute-start | bytes 3145736 | tf_op jit(solution)/shard_map/ppermute | solution.py:14
  283.5 14.8 %collective-permute-start.46 = (bf16[2,256,1024]{2,1,0:T(8,128)(2,1)S(1)}, bf16[2,256,1024]{2,1,0:T(8,128)(2,1)S(1)}, u32[]{:S(2)}, u32[]{:S(2)}) collective-permute-start(bf16[2,256,1024]{2,1,0:T(8,128)(2,1)S(1)} %bitcast.336), channel_id=1, source_target_pairs={{0,2},{2,0},{4,6},{6,4},{8,10},{10,8},{12,14},{14,12},{16,18},{18,... | collective-permute-start | bytes 3145736 | tf_op jit(solution)/shard_map/ppermute | solution.py:14
  293.9 8.0 %collective-permute-start.52 = (bf16[2,256,1024]{2,1,0:T(8,128)(2,1)S(1)}, bf16[2,256,1024]{2,1,0:T(8,128)(2,1)S(1)}, u32[]{:S(2)}, u32[]{:S(2)}) collective-permute-start(bf16[2,256,1024]{2,1,0:T(8,128)(2,1)S(1)} %bitcast.335), channel_id=1, source_target_pairs={{0,2},{2,0},{4,6},{6,4},{8,10},{10,8},{12,14},{14,12},{16,18},{18,... | collective-permute-start | bytes 3145736 | tf_op jit(solution)/shard_map/ppermute | solution.py:14
  295.5 26.0 %collective-permute-start.25 = (bf16[2048,256]{1,0:T(8,128)(2,1)S(1)}, bf16[2048,256]{1,0:T(8,128)(2,1)S(1)}, u32[]{:S(2)}, u32[]{:S(2)}) collective-permute-start(bf16[2048,256]{1,0:T(8,128)(2,1)S(1)} %broadcast_select_fusion.2), channel_id=1, source_target_pairs={{0,4},{2,6},{4,0},{6,2},{8,12},{10,14},{12,8},{14,10},{16,20},{18,... | collective-permute-start | bytes 3145736 | tf_op jit(solution)/shard_map/ppermute | solution.py:14
  298.2 24.4 %collective-permute-start.24 = (bf16[2048,256]{1,0:T(8,128)(2,1)S(1)}, bf16[2048,256]{1,0:T(8,128)(2,1)S(1)}, u32[]{:S(2)}, u32[]{:S(2)}) collective-permute-start(bf16[2048,256]{1,0:T(8,128)(2,1)S(1)} %broadcast_select_fusion.2), channel_id=1, source_target_pairs={{0,2},{2,0},{4,6},{6,4},{8,10},{10,8},{12,14},{14,12},{16,18},{18,... | collective-permute-start | bytes 3145736 | tf_op jit(solution)/shard_map/ppermute | solution.py:14
  299.3 3.2 collective-permute-start.31
  301.9 22.5 %collective-permute-start.34 = (bf16[2048,256]{1,0:T(8,128)(2,1)S(1)}, bf16[2048,256]{1,0:T(8,128)(2,1)S(1)}, u32[]{:S(2)}, u32[]{:S(2)}) collective-permute-start(bf16[2048,256]{1,0:T(8,128)(2,1)S(1)} %broadcast_select_fusion), channel_id=1, source_target_pairs={{0,2},{2,0},{4,6},{6,4},{8,10},{10,8},{12,14},{14,12},{16,18},{18,... | collective-permute-start | bytes 3145736 | tf_op jit(solution)/shard_map/ppermute | solution.py:14
  302.5 41.2 %collective-permute-start.35 = (bf16[2048,256]{1,0:T(8,128)(2,1)S(1)}, bf16[2048,256]{1,0:T(8,128)(2,1)S(1)}, u32[]{:S(2)}, u32[]{:S(2)}) collective-permute-start(bf16[2048,256]{1,0:T(8,128)(2,1)S(1)} %broadcast_select_fusion), channel_id=1, source_target_pairs={{0,4},{2,6},{4,0},{6,2},{8,12},{10,14},{12,8},{14,10},{16,20},{18,... | collective-permute-start | bytes 3145736 | tf_op jit(solution)/shard_map/ppermute | solution.py:14
  321.6 23.2 %collective-permute-start.32 = (bf16[256,1024]{0,1:T(8,128)(2,1)S(1)}, bf16[256,1024]{0,1:T(8,128)(2,1)S(1)}, u32[]{:S(2)}, u32[]{:S(2)}) collective-permute-start(bf16[256,1024]{0,1:T(8,128)(2,1)S(1)} %pad_maximum_fusion.9), channel_id=1, source_target_pairs={{0,1},{1,0},{2,3},{3,2},{4,5},{5,4},{6,7},{7,6},{8,9},{9,8},{10,11... | collective-permute-start | bytes 1572872 | tf_op jit(solution)/shard_map/ppermute | solution.py:14
  322.7 22.4 %collective-permute-start.26 = (bf16[2048,256]{1,0:T(8,128)(2,1)S(1)}, bf16[2048,256]{1,0:T(8,128)(2,1)S(1)}, u32[]{:S(2)}, u32[]{:S(2)}) collective-permute-start(bf16[2048,256]{1,0:T(8,128)(2,1)S(1)} %collective-permute-done.25), channel_id=1, source_target_pairs={{0,2},{2,0},{4,6},{6,4},{8,10},{10,8},{12,14},{14,12},{16,18},{18,... | collective-permute-start | bytes 3145736 | tf_op jit(solution)/shard_map/ppermute | solution.py:14
  326.0 18.7 %copy-start.18 = (bf16[256,256]{0,1:T(8,128)(2,1)S(1)}, bf16[256,256]{0,1:T(8,128)(2,1)}, u32[]{:S(2)}) copy-start(bf16[256,256]{0,1:T(8,128)(2,1)} %copy.181) | copy-start | bytes 393220
  326.0 18.7 %copy-start.19 = (bf16[256,256]{0,1:T(8,128)(2,1)S(1)}, bf16[256,256]{0,1:T(8,128)(2,1)}, u32[]{:S(2)}) copy-start(bf16[256,256]{0,1:T(8,128)(2,1)} %copy.182) | copy-start | bytes 393220
  326.0 18.7 %copy-start.20 = (bf16[256,256]{0,1:T(8,128)(2,1)S(1)}, bf16[256,256]{0,1:T(8,128)(2,1)}, u32[]{:S(2)}) copy-start(bf16[256,256]{0,1:T(8,128)(2,1)} %copy.183) | copy-start | bytes 393220
  326.0 18.7 %copy-start.21 = (bf16[256,256]{0,1:T(8,128)(2,1)S(1)}, bf16[256,256]{0,1:T(8,128)(2,1)}, u32[]{:S(2)}) copy-start(bf16[256,256]{0,1:T(8,128)(2,1)} %copy.184) | copy-start | bytes 393220
  326.0 18.7 %copy-start.32 = (f32[256,256]{0,1:T(8,128)S(1)}, f32[256,256]{0,1:T(8,128)}, u32[]{:S(2)}) copy-start(f32[256,256]{0,1:T(8,128)} %fusion.67) | copy-start | bytes 786436
  343.7 2.9 collective-permute-start.36
  345.9 14.8 %collective-permute-start.27 = (bf16[256,1024]{0,1:T(8,128)(2,1)S(1)}, bf16[256,1024]{0,1:T(8,128)(2,1)S(1)}, u32[]{:S(2)}, u32[]{:S(2)}) collective-permute-start(bf16[256,1024]{0,1:T(8,128)(2,1)S(1)} %pad_maximum_fusion.8), channel_id=1, source_target_pairs={{0,1},{1,0},{2,3},{3,2},{4,5},{5,4},{6,7},{7,6},{8,9},{9,8},{10,11... | collective-permute-start | bytes 1572872 | tf_op jit(solution)/shard_map/ppermute | solution.py:14
  347.1 24.4 %collective-permute-start.37 = (bf16[256,1024]{0,1:T(8,128)(2,1)S(1)}, bf16[256,1024]{0,1:T(8,128)(2,1)S(1)}, u32[]{:S(2)}, u32[]{:S(2)}) collective-permute-start(bf16[256,1024]{0,1:T(8,128)(2,1)S(1)} %pad_maximum_fusion.10), channel_id=1, source_target_pairs={{0,1},{1,0},{2,3},{3,2},{4,5},{5,4},{6,7},{7,6},{8,9},{9,8},{10,11... | collective-permute-start | bytes 1572872 | tf_op jit(solution)/shard_map/ppermute | solution.py:14
  349.7 21.8 %copy-start.13 = (bf16[256,256]{0,1:T(8,128)(2,1)S(1)}, bf16[256,256]{0,1:T(8,128)(2,1)}, u32[]{:S(2)}) copy-start(bf16[256,256]{0,1:T(8,128)(2,1)} %copy.186) | copy-start | bytes 393220
  349.7 21.8 %copy-start.15 = (bf16[256,256]{0,1:T(8,128)(2,1)S(1)}, bf16[256,256]{0,1:T(8,128)(2,1)}, u32[]{:S(2)}) copy-start(bf16[256,256]{0,1:T(8,128)(2,1)} %copy.187) | copy-start | bytes 393220
  349.7 21.8 %copy-start.17 = (bf16[256,256]{0,1:T(8,128)(2,1)S(1)}, bf16[256,256]{0,1:T(8,128)(2,1)}, u32[]{:S(2)}) copy-start(bf16[256,256]{0,1:T(8,128)(2,1)} %copy.188) | copy-start | bytes 393220
  375.0 13.6 %collective-permute-start.53 = (bf16[2,128,1024]{2,1,0:T(8,128)(2,1)S(1)}, bf16[2,128,1024]{2,1,0:T(8,128)(2,1)S(1)}, u32[]{:S(2)}, u32[]{:S(2)}) collective-permute-start(bf16[2,128,1024]{2,1,0:T(8,128)(2,1)S(1)} %bitcast.337), channel_id=1, source_target_pairs={{0,1},{1,0},{2,3},{3,2},{4,5},{5,4},{6,7},{7,6},{8,9},{9,8},{10,11... | collective-permute-start | bytes 1572872 | tf_op jit(solution)/shard_map/ppermute | solution.py:14
  (41 other events, 258.5 us)

commit v2 on v0

v2 whole, which is shorter than its diff:
```python
import functools

import jax
import jax.numpy as jnp
from jax import lax
from jax.experimental import pallas as pl
from jax.experimental.pallas import tpu as pltpu
from jax.sharding import PartitionSpec as P

HD = 128
PAGE = 128
INNER = 4
TAG = 16
EPS = 1e-05
BF16 = jnp.bfloat16
F32 = jnp.float32
SMEM = pl.BlockSpec(memory_space=pltpu.SMEM)
VMEM = pl.BlockSpec(memory_space=pltpu.VMEM)
LIGHT = pl.CostEstimate(flops=1, bytes_accessed=1, transcendentals=0)


def params(mib):
    return pltpu.CompilerParams(vmem_limit_bytes=mib * 2**20)


def call(body, name, out_shape, args, scratch=(), mib=40):
    return pl.pallas_call(
        body,
        name=name,
        out_shape=out_shape,
        in_specs=[SMEM if a.dtype == jnp.int32 else VMEM for a in args],
        out_specs=jax.tree.map(lambda _: VMEM, out_shape),
        scratch_shapes=list(scratch),
        cost_estimate=LIGHT,
        compiler_params=params(mib),
    )(*args)


def shape(dims, dtype):
    return jax.ShapeDtypeStruct(dims, dtype)


def seq_xor(value, seq_count, bits):
    return lax.ppermute(value, "seq", [(j, j ^ bits) for j in range(seq_count)])


def seq_up(value, seq_count, planes):
    step = planes * INNER
    return lax.ppermute(value, "seq", [(j, j + step) for j in range(seq_count - step)])


def pool_shift(value, pool_count, by):
    return lax.ppermute(value, "pool", [(i, (i + by) % pool_count) for i in range(pool_count)])


def ring_chip(spot, planes):
    if isinstance(spot, int):
        return spot * 2 if spot < planes else (2 * planes - 1 - spot) * 2 + 1
    return jnp.where(spot < planes, spot * 2, (2 * planes - 1 - spot) * 2 + 1)


def ring_step(value, seq_count, by):
    planes = seq_count // INNER
    length = 2 * planes
    pairs = []
    for spot in range(length):
        source, target = ring_chip(spot, planes), ring_chip((spot + by) % length, planes)
        pairs += [(source * 2 + core, target * 2 + core) for core in range(2)]
    return lax.ppermute(value, "seq", pairs)


def column(row):
    return jnp.broadcast_to(row, (8, row.shape[1])).T[:, :1]


def update_kernel(meta, key, value, decay, cumul, *outs):
    *pieces, held = outs
    heads, rows = decay.shape
    share = heads // INNER
    before = lax.broadcasted_iota(jnp.int32, (rows, rows), 0)
    after = lax.broadcasted_iota(jnp.int32, (rows, rows), 1)
    ones = (before <= after).astype(F32)
    total = jnp.dot(
        decay[...], ones, precision=lax.Precision.HIGHEST, preferred_element_type=F32
    )
    cumul[...] = total
    upright = total.T
    term = lax.broadcasted_iota(jnp.int32, (TAG, HD), 0)
    place = meta[0]
    for h in range(heads):
        lane = slice(h * HD, (h + 1) * HD)
        last = total[h : h + 1, rows - 1 : rows]
        weight = jnp.exp(last - upright[:, h : h + 1])
        weighted = (key[:, lane].astype(F32) * weight).astype(BF16)
        update = lax.dot_general(
            weighted, value[:, lane], (((0,), (0,)), ((), ())), preferred_element_type=F32
        )
        high = last.astype(BF16).astype(F32)
        middle = (last - high).astype(BF16).astype(F32)
        low = last - high - middle
        tag = jnp.where(
            term == 0, high, jnp.where(term == 1, middle, jnp.where(term == 2, low, 0.0))
        )
        spot = (h // share) ^ place
        held[spot, h % share, :HD, :] = update.astype(BF16)
        held[spot, h % share, HD:, :] = tag.astype(BF16)
    for r in range(INNER):
        pieces[r][...] = held[r]


def state_of(ref, i):
    return ref[i, :HD, :].astype(F32)


def total_of(ref, i):
    return jnp.sum(ref[i, HD:, :].astype(F32), axis=0, keepdims=True)


def stack_in_order(place, got, held):
    for r in range(INNER):
        held[r] = got[r][...]
    return [held.at[place ^ i] for i in range(INNER)]


def plane_kernel(meta, *refs):
    *got, out, held = refs
    parts = stack_in_order(meta[0], got, held)
    term = lax.broadcasted_iota(jnp.int32, (TAG, HD), 0)
    for i in range(out.shape[0]):
        state = jnp.zeros((HD, HD), F32)
        total = jnp.zeros((1, HD), F32)
        for part in parts:
            one = total_of(part, i)
            state = jnp.exp(one) * state + state_of(part, i)
            total = total + one
        high = total.astype(BF16).astype(F32)
        middle = (total - high).astype(BF16).astype(F32)
        low = total - high - middle
        tag = jnp.where(
            term == 0, high, jnp.where(term == 1, middle, jnp.where(term == 2, low, 0.0))
        )
        out[i, :HD, :] = state.astype(BF16)
        out[i, HD:, :] = tag.astype(BF16)


def entering_kernel(meta, *refs):
    held, leaving = refs[-2:]
    outs = refs[-2 - INNER : -2]
    got = refs[:INNER]
    earlier = refs[INNER : -2 - INNER]
    place = meta[0]
    parts = stack_in_order(place, got, held)
    for i in range(leaving.shape[1]):
        state = jnp.zeros((HD, HD), F32)
        gap = jnp.zeros((1, HD), F32)
        for plane in earlier:
            state = state + jnp.exp(gap) * state_of(plane, i)
            gap = gap + total_of(plane, i)
        for spot, part in enumerate(parts):
            leaving[place ^ spot, i] = state.astype(BF16)
            state = jnp.exp(total_of(part, i)) * state + state_of(part, i)
    for r in range(INNER):
        outs[r][...] = leaving[r]


def inner_kernel(query, key, value, cumul, out):
    rows = query.shape[0]
    half = min(256, rows)
    line = cumul[0]
    upright = column(line)
    lower = lax.broadcasted_iota(jnp.int32, (half, half), 0) >= lax.broadcasted_iota(
        jnp.int32, (half, half), 1
    )
    for at in range(0, rows, half):
        here = pl.ds(at, half)
        total = jnp.zeros((half, HD), F32)
        for start in range(0, at + half, half):
            there = pl.ds(start, half)
            products = lax.dot_general(
                query[here, :], key[there, :], (((1,), (1,)), ((), ())), preferred_element_type=F32
            )
            gap = upright[at : at + half] - line[:, start : start + half]
            if start == at:
                scores = jnp.where(lower, products * jnp.exp(jnp.where(lower, gap, 0.0)), 0.0)
            else:
                scores = products * jnp.exp(gap)
            total = total + jnp.dot(
                scores.astype(BF16), value[there, :], preferred_element_type=F32
            )
        out[here, :] = total


def mixed_kernel(meta, query, inner, cumul, *refs):
    *states, out, held = refs
    pool_count, rows, _ = out.shape
    place, me = meta[0], meta[2]
    source = pl.program_id(0) ^ place
    share = cumul.shape[0]
    for i in range(share):
        lane = slice(i * HD, (i + 1) * HD)
        state = states[0][i]
        for r in range(1, INNER):
            state = jnp.where(source == r, states[r][i], state)
        outer = jnp.dot(query[:, lane], state, preferred_element_type=F32)
        retained = inner[:, lane] + outer * jnp.exp(column(cumul[i]))
        mean = jnp.mean(retained * retained, axis=-1, keepdims=True)
        held[:, lane] = (retained * lax.rsqrt(mean + EPS)).astype(BF16)
    for r in range(pool_count):
        start = pl.multiple_of(lax.rem(me + r, pool_count) * rows, rows)
        out[r] = held[pl.ds(start, rows), :]


def project_kernel(parts, splits, *refs):
    own, other = refs[:2]
    weights = refs[2 : 2 + parts]
    mine, *away = refs[2 + parts :]
    pool_count, rows, depth = own.shape
    for r in list(range(1, pool_count)) + [0]:
        for core, mixed in enumerate((own, other)):
            here = pl.ds(core * rows, rows)
            at = 0
            for start in range(0, parts, splits):
                width = weights[start].shape[1]
                total = None
                for s in range(splits):
                    deep = depth // splits
                    part = jnp.dot(
                        mixed[r, :, s * deep : (s + 1) * deep],
                        weights[start + s][...],
                        preferred_element_type=F32,
                    )
                    total = part if total is None else total + part
                if r == 0:
                    mine[here, at : at + width] = total
                else:
                    away[r - 1][here, at : at + width] = total.astype(BF16)
                at += width


def cache_kernel(first, parts, shares, meta, mine, residual, gain, *refs):
    pool_count = shares
    arrived = refs[: pool_count - 1]
    refs = refs[pool_count - 1 :]
    kv = refs[: parts * pool_count]
    refs = refs[parts * pool_count :]
    if not first:
        old_total, old_square = refs[:2]
        refs = refs[2:]
    total, square, held = refs
    me = meta[2]
    depth = kv[0].shape[0]
    for p in range(parts):
        for r in range(pool_count):
            share = lax.rem(me + pool_count - r, pool_count)
            start = pl.multiple_of(p * depth * pool_count + share * depth, depth)
            held[pl.ds(start, depth), :] = kv[p * pool_count + r][...]
    hidden = mine[...] + residual[...].astype(F32)
    for part in arrived:
        hidden = hidden + part[...].astype(F32)
    squares = jnp.sum(hidden * hidden, axis=-1, keepdims=True)
    scaled = (hidden * gain[...]).astype(BF16)
    product = jnp.dot(scaled, held[...], preferred_element_type=F32)
    if first:
        square[...] = jnp.broadcast_to(squares, square.shape)
        total[...] = product
    else:
        square[...] = old_square[...] + squares
        total[...] = old_total[...] + product


def finish_kernel(features, total, square, total_in, square_in, out):
    rows = out.shape[0]
    mean = (square[:rows, :1] + square_in[:, :1]) / features
    out[...] = ((total[:rows, :] + total_in[...]) * lax.rsqrt(mean + EPS)).astype(BF16)


def place_kernel(meta, tables, *refs):
    *pages, out = refs
    me = meta[2]
    out[...] = jnp.zeros(out.shape, out.dtype)
    for r, part in enumerate(pages):
        for p in range(part.shape[0] // PAGE):
            owner, slot = tables[r, 2 * p], tables[r, 2 * p + 1]

            @pl.when(owner == me)
            def _():
                out[slot] = part[p * PAGE : (p + 1) * PAGE, :]


def entering_states(pieces, meta, seq_count):
    planes = seq_count // INNER
    share = pieces[0].shape[0]
    got = [pieces[0]] + [seq_xor(pieces[r], seq_count, r) for r in range(1, INNER)]
    tagged = (share, HD + TAG, HD)
    plane_total = call(
        plane_kernel,
        "plane_state",
        shape(tagged, BF16),
        [meta, *got],
        [pltpu.VMEM((INNER, *tagged), BF16)],
    )
    earlier = [seq_up(plane_total, seq_count, d) for d in range(1, planes)]
    leaving = call(
        entering_kernel,
        "entering_state",
        [shape((share, HD, HD), BF16)] * INNER,
        [meta, *got, *earlier],
        [pltpu.VMEM((INNER, *tagged), BF16), pltpu.VMEM((INNER, share, HD, HD), BF16)],
    )
    return [leaving[0]] + [seq_xor(leaving[r], seq_count, r) for r in range(1, INNER)]


def retention(query_rows, key_rows, value_rows, log_decay, meta, seq_count, pool_count):
    rows, wide = query_rows.shape
    heads = wide // HD
    share = heads // INNER
    tagged = (share, HD + TAG, HD)
    cumul, *pieces = call(
        update_kernel,
        "update",
        [shape(log_decay.shape, F32)] + [shape(tagged, BF16)] * INNER,
        [meta, key_rows, value_rows, log_decay],
        [pltpu.VMEM((INNER, *tagged), BF16)],
    )
    cumul = cumul.reshape(heads, 1, rows)
    states = entering_states(pieces, meta, seq_count)
    by_head = pl.BlockSpec((rows, HD), lambda h: (0, h))
    inner = pl.pallas_call(
        inner_kernel,
        name="inner",
        grid=(heads,),
        out_shape=shape((rows, wide), F32),
        in_specs=[by_head, by_head, by_head, pl.BlockSpec((1, 1, rows), lambda h: (h, 0, 0))],
        out_specs=by_head,
        cost_estimate=LIGHT,
        compiler_params=params(24),
    )(query_rows, key_rows, value_rows, cumul)
    by_share = pl.BlockSpec((rows, share * HD), lambda g: (0, g))
    return pl.pallas_call(
        mixed_kernel,
        name="mixed",
        grid=(INNER,),
        out_shape=shape((pool_count, rows // pool_count, wide), BF16),
        in_specs=[
            SMEM,
            by_share,
            by_share,
            pl.BlockSpec((share, 1, rows), lambda g: (g, 0, 0)),
            *[VMEM] * INNER,
        ],
        out_specs=pl.BlockSpec(
            (pool_count, rows // pool_count, share * HD), lambda g: (0, 0, g)
        ),
        scratch_shapes=[pltpu.VMEM((rows, share * HD), BF16)],
        cost_estimate=LIGHT,
        compiler_params=params(24),
    )(meta, query_rows, inner, cumul, *states)


def ring(own, seq_count):
    length = seq_count // 2
    groups = [([0], [own])]
    ahead, behind = own, own
    for d in range(1, length // 2):
        ahead, behind = ring_step(ahead, seq_count, 1), ring_step(behind, seq_count, -1)
        groups.append(([d, length - d], [ahead, behind]))
    half = own.shape[0] // 2
    groups.append(
        (
            [length // 2],
            [ring_step(ahead[:half], seq_count, 1), ring_step(behind[half:], seq_count, -1)],
        )
    )
    return groups


def on_device(
    query_rows,
    key_rows,
    value_rows,
    log_decay,
    residual,
    out_weight,
    norm_gain,
    kv_weight,
    block_table,
):
    seq_count = lax.axis_size("seq")
    pool_count = lax.axis_size("pool")
    planes = seq_count // INNER
    length = 2 * planes
    index = lax.axis_index("seq")
    me = lax.axis_index("pool")
    place = index % INNER
    plane = index // INNER
    core = index % 2
    spot = jnp.where(place < 2, plane, length - 1 - plane)
    meta = jnp.stack([place, plane, me]).astype(jnp.int32)
    width = out_weight.shape[1]
    rows_here = residual.shape[0]
    cache_width = kv_weight.shape[1]
    pages_here = block_table.shape[0]
    slot_count = 2 * pages_here
    chip_rows = 2 * rows_here

    weight_groups = ring(out_weight, seq_count)
    kv_share = kv_weight.shape[0] // pool_count
    kv_own = lax.dynamic_slice_in_dim(kv_weight, me * kv_share, kv_share, 0)
    kv_groups = []
    for distances, blocks in ring(kv_own, seq_count):
        if len(blocks) > len(distances):
            blocks = [jnp.concatenate(blocks)]
        kv_groups.append(
            [[b] + [pool_shift(b, pool_count, r) for r in range(1, pool_count)] for b in blocks]
        )
    tables = jnp.stack(
        [block_table] + [pool_shift(block_table, pool_count, r) for r in range(1, pool_count)]
    ).reshape(pool_count, 2 * pages_here)
    residual_pair = [residual, seq_xor(residual, seq_count, 1)]

    mixed = retention(
        query_rows, key_rows, value_rows, log_decay, meta, seq_count, pool_count
    )
    mixed_other = seq_xor(mixed, seq_count, 1)

    total = square = None
    for (distances, blocks), kv_parts in zip(weight_groups, kv_groups):
        count = len(distances)
        splits = len(blocks) // count
        wide = count * width
        mine, *away = call(
            functools.partial(project_kernel, len(blocks), splits),
            "project",
            [shape((chip_rows, wide), F32)] + [shape((chip_rows, wide), BF16)] * (pool_count - 1),
            [mixed, mixed_other, *blocks],
        )
        arrived = [pool_shift(away[r - 1], pool_count, r) for r in range(1, pool_count)]
        starts = [
            (ring_chip((spot + length - d) % length, planes) * 2 + core) * width
            for d in distances
        ]
        residual_part = jnp.concatenate(
            [
                jnp.concatenate([lax.dynamic_slice_in_dim(rows, s, width, 1) for s in starts], 1)
                for rows in residual_pair
            ]
        )
        gain_part = jnp.concatenate(
            [lax.dynamic_slice_in_dim(norm_gain, s, width, 0) for s in starts]
        ).reshape(1, wide)
        first = total is None
        total, square = call(
            functools.partial(cache_kernel, first, count, pool_count),
            "cache",
            [shape((chip_rows, cache_width), F32), shape((chip_rows, HD), F32)],
            [meta, mine, residual_part, gain_part, *arrived]
            + [piece for part in kv_parts for piece in part]
            + ([] if first else [total, square]),
            [pltpu.VMEM((wide, cache_width), BF16)],
        )
    features = width * seq_count
    cache_rows = call(
        functools.partial(finish_kernel, features),
        "finish",
        shape((rows_here, cache_width), BF16),
        [
            total,
            square,
            seq_xor(total[rows_here:], seq_count, 1),
            seq_xor(square[rows_here:], seq_count, 1),
        ],
    )
    pages = [cache_rows] + [pool_shift(cache_rows, pool_count, r) for r in range(1, pool_count)]
    page_cache = call(
        place_kernel,
        "place",
        shape((slot_count, PAGE, cache_width), BF16),
        [meta, tables, *pages],
    )
    return page_cache.reshape(1, 1, slot_count, PAGE, cache_width)


def solution(mesh):
    placed = (
        P("seq", "pool"),
        P("seq", "pool"),
        P("seq", "pool"),
        P("pool", "seq"),
        P(("seq", "pool"), None),
        P("pool", "seq"),
        P(),
        P("seq", None),
        P(("seq", "pool"), None),
    )
    return jax.shard_map(
        on_device,
        mesh=mesh,
        in_specs=placed,
        out_specs=P("seq", "pool", None, None, None),
        check_vma=False,
    )
```

time: 503 us -> 262 us (0.52)
  waiting for transfers between devices: 367 us -> 138 us
  Pallas kernels: 0 us -> 55.2 us
  blocking collectives: 52.7 us -> 0 us
  starting transfers between devices: 3.55 us -> 50.2 us
  matrix products: 42.3 us -> 0 us
  between operations: 13.9 us -> 0.51 us
  other arithmetic: 10.5 us -> 0.25 us
  local copies, waits for them, and re-layouts: 11.9 us -> 17.6 us
    all_gather x3 -> x0, waiting for transfers between devices: 273 us -> none  [the longest x1 111 us: on_device(): lax.all_gather(out_weight, 'seq', axis=1, tiled=True)]
    ppermute x0 -> x44, waiting for transfers between devices: none -> 138 us  [the longest x16 58.7 us: ring_step(): return lax.ppermute(value, 'seq', pairs)]
    reduce_scatter x1 -> x0, waiting for transfers between devices: 92.7 us -> none  [on_device(): lax.psum_scatter(partial_value, 'pool', scatter_dimension=0, tiled=True)]
    pallas_call x0 -> x17, Pallas kernels: none -> 55.2 us  [the longest x15 35.5 us: call(): pl.pallas_call(body, name=name, out_shape=out_shape, in_specs=[SMEM if a....]
    ppermute x0 -> x44, starting transfers between devices: none -> 50.2 us  [the longest x16 21 us: ring_step(): return lax.ppermute(value, 'seq', pairs)]
    dot_general x6 -> x0, matrix products: 42.3 us -> none  [the longest x1 14.6 us: on_device(): jnp.dot(mixed_list, lax.all_gather(out_weight, 'seq', axis=1, tiled=True)...]
    unnamed x1 -> x0, blocking collectives: 36 us -> none
    all_to_all x1 -> x0, blocking collectives: 16.8 us -> none  [on_device(): lax.all_to_all(outgoing, 'pool', split_axis=0, concat_axis=0, tiled=True)]
  transfers between devices with their start and end apart: 5 -> 44, of which waited for: 4 -> 21; matrix products, arithmetic and copies ran while one was open for 7% -> 2% of each run, Pallas kernels for 0% -> 20%
where the time goes in v2:
time: 262 us; the launch traced here: 261 us
  waiting for transfers between devices  138 us (53%)
  Pallas kernels  55.2 us (21%)
  starting transfers between devices  50.2 us (19%)
  local copies, waits for them, and re-layouts  17.6 us (7%)
    ppermute x16, waiting for transfers between devices, ring_step(): return lax.ppermute(value, 'seq', pairs)  58.7 us
    ppermute x15, waiting for transfers between devices, pool_shift(): lax.ppermute(value, 'pool', [(i, (i + by) % pool_count) for i in range(po...  56.6 us
    pallas_call x15, Pallas kernels, call(): pl.pallas_call(body, name=name, out_shape=out_shape, in_specs=[SMEM if a....  35.5 us
    ppermute x16, starting transfers between devices, ring_step(): return lax.ppermute(value, 'seq', pairs)  21 us
    ppermute x3, waiting for transfers between devices, seq_up(): lax.ppermute(value, 'seq', [(j, j + step) for j in range(seq_count - step)])  16.4 us
    ppermute x15, starting transfers between devices, pool_shift(): lax.ppermute(value, 'pool', [(i, (i + by) % pool_count) for i in range(po...  14.1 us
    pallas_call x1, Pallas kernels, retention(): pl.pallas_call(inner_kernel, name='inner', grid=(heads,), out_shape=shape...  13.4 us
    unnamed x49, local copies, waits for them, and re-layouts  11.5 us
  transfers between devices with their start and end apart: 44, of which 21 were waited for; matrix products, arithmetic and copies ran while one was open for 2% of the time, Pallas kernels for 20%

profile of v2, /device:TPU:0, one launch (start us, length us, event | category | flops | bytes accessed | tf_op | source)
XLA Modules:
  0.0 261.5 jit_solution(6969238680254741333)
XLA Ops:
  0.0 3.0 %collective-permute-start.11 = (bf16[2048,256]{1,0:T(8,128)(2,1)}, bf16[2048,256]{1,0:T(8,128)(2,1)}, u32[]{:S(2)}, u32[]{:S(2)}) collective-permute-start(bf16[2048,256]{1,0:T(8,128)(2,1)} %refs_2_.1), channel_id=1, source_target_pairs={{0,8},{2,10},{8,16},{10,18},{16,24},{18,26},{24,28},{26,30},{28,20... | collective-permute-start | bytes 3145736 | tf_op jit(solution)/shard_map/ppermute | solution.py:69
  3.1 1.6 copy-done.3
  4.7 1.6 copy-done.5
  7.0 5.5 %update.1 = (f32[16,512]{1,0:T(8,128)S(1)}, bf16[4,144,128]{2,1,0:T(8,128)(2,1)S(1)}, bf16[4,144,128]{2,1,0:T(8,128)(2,1)S(1)}, bf16[4,144,128]{2,1,0:T(8,128)(2,1)S(1)}, bf16[4,144,128]{2,1,0:T(8,128)(2,1)S(1)}) custom-call(s32[3]{0:T(128)S(1)} %pad_add_fusion.1.meta, bf16[512,2048]{1,0:T(8,128)(2,1)S(1)} %copy-done.3, bf16[512,2048]{1,0:T(8,128)(2,1)S(1)} %copy-done.5, ...), custom_call_target="tpu_custom_call" | custom-call | flops 1 | bytes 1 | tf_op jit(solution)/shard_map/update/pallas_call | solution.py:27
  12.6 2.0 collective-permute-start.2
  14.7 12.6 %collective-permute-done.11.refs_2_ = bf16[2048,256]{1,0:T(8,128)(2,1)} collective-permute-done((bf16[2048,256]{1,0:T(8,128)(2,1)}, bf16[2048,256]{1,0:T(8,128)(2,1)}, u32[]{:S(2)}, u32[]{:S(2)}) %collective-permute-start.11) | collective-permute-done | bytes 1048608 | tf_op jit(solution)/shard_map/ppermute | solution.py:69
  27.3 1.0 collective-permute-start.12
  28.2 2.1 collective-permute-done.2.refs_2_
  30.3 1.7 collective-permute-done.3.refs_3_
  32.7 1.3 collective-permute-start.4
  34.0 7.7 %collective-permute-start.5 = (bf16[4,144,128]{2,1,0:T(8,128)(2,1)S(1)}, bf16[4,144,128]{2,1,0:T(8,128)(2,1)S(1)}, u32[]{:S(2)}, u32[]{:S(2)}) collective-permute-start(bf16[4,144,128]{2,1,0:T(8,128)(2,1)S(1)} %plane_state.1), channel_id=1, source_target_pairs={{0,16},{2,18},{4,20},{6,22},{8,24},{10,26},{12,28},{14,30},{1,17},... | collective-permute-start | bytes 442376 | tf_op jit(solution)/shard_map/ppermute | solution.py:49
  41.8 1.3 collective-permute-start.6
  43.1 12.1 %collective-permute-done.4.refs_4_ = bf16[4,144,128]{2,1,0:T(8,128)(2,1)S(1)} collective-permute-done((bf16[4,144,128]{2,1,0:T(8,128)(2,1)S(1)}, bf16[4,144,128]{2,1,0:T(8,128)(2,1)S(1)}, u32[]{:S(2)}, u32[]{:S(2)}) %collective-permute-start.4) | collective-permute-done | bytes 147488 | tf_op jit(solution)/shard_map/ppermute | solution.py:49
  55.2 2.7 %collective-permute-done.5.refs_5_ = bf16[4,144,128]{2,1,0:T(8,128)(2,1)S(1)} collective-permute-done((bf16[4,144,128]{2,1,0:T(8,128)(2,1)S(1)}, bf16[4,144,128]{2,1,0:T(8,128)(2,1)S(1)}, u32[]{:S(2)}, u32[]{:S(2)}) %collective-permute-start.5) | collective-permute-done | bytes 147488 | tf_op jit(solution)/shard_map/ppermute | solution.py:49
  57.9 1.6 collective-permute-done.6.refs_6_
  59.5 1.5 entering_state.1
  62.3 1.9 collective-permute-start.9
  64.5 1.6 collective-permute-start.40
  66.1 1.6 copy-done.4
  67.7 1.6 copy-done.6
  69.3 13.4 %inner.1 = f32[512,2048]{1,0:T(8,128)S(1)} custom-call(bf16[512,2048]{1,0:T(8,128)(2,1)S(1)} %copy-done.1, bf16[512,2048]{1,0:T(8,128)(2,1)S(1)} %copy-done.4, bf16[512,2048]{1,0:T(8,128)(2,1)S(1)} %copy-done.6, f32[16,1,512]{2,1,0:T(1,128)S(1)} %reshape.26.cumul), custom_call_target="tpu_custom_call" | custom-call | flops 1 | bytes 1 | tf_op jit(solution)/shard_map/inner/pallas_call | solution.py:328
  83.6 6.3 %mixed.1.refs_0_ = bf16[2,256,2048]{2,1,0:T(8,128)(2,1)S(1)} custom-call(s32[3]{0:T(128)S(1)} %pad_add_fusion.1.meta, bf16[512,2048]{1,0:T(8,128)(2,1)S(1)} %copy-done.2, f32[512,2048]{1,0:T(8,128)S(1)} %inner.1, f32[16,1,512]{2,1,0:T(1,128)S(1)} %reshape.26.cumul, bf16[4,128,128]{2,1,0:T(8,128)(2,1)S(1)} %get-tuple-element.39.refs_0_, ...), custom_call_target="tpu_custom_call" | custom-call | flops 1 | bytes 1 | tf_op jit(solution)/shard_map/mixed/pallas_call | solution.py:339
  90.0 4.5 %collective-permute-start.21 = (bf16[128,1024]{1,0:T(8,128)(2,1)S(1)}, bf16[128,1024]{1,0:T(8,128)(2,1)S(1)}, u32[]{:S(2)}, u32[]{:S(2)}) collective-permute-start(bf16[128,1024]{1,0:T(8,128)(2,1)S(1)} %constant_dynamic-slice_fusion.14.refs_1_), channel_id=1, source_target_pairs={{0,8},{2,10},{8,16},{10,18},{16,24},{18,26},{24,28},{26,30},{28,20... | collective-permute-start | bytes 786440 | tf_op jit(solution)/shard_map/ppermute | solution.py:69
  95.5 6.2 %collective-permute-done.21.refs_1_ = bf16[128,1024]{1,0:T(8,128)(2,1)S(1)} collective-permute-done((bf16[128,1024]{1,0:T(8,128)(2,1)S(1)}, bf16[128,1024]{1,0:T(8,128)(2,1)S(1)}, u32[]{:S(2)}, u32[]{:S(2)}) %collective-permute-start.21) | collective-permute-done | bytes 262176 | tf_op jit(solution)/shard_map/ppermute | solution.py:69
  102.2 1.6 collective-permute-done.25.refs_3_
  103.8 5.9 %collective-permute-done.37.refs_2_ = bf16[128,1024]{1,0:T(8,128)(2,1)S(1)} collective-permute-done((bf16[128,1024]{1,0:T(8,128)(2,1)S(1)}, bf16[128,1024]{1,0:T(8,128)(2,1)S(1)}, u32[]{:S(2)}, u32[]{:S(2)}) %collective-permute-start.37) | collective-permute-done | bytes 262176 | tf_op jit(solution)/shard_map/ppermute | solution.py:53
  110.5 1.2 collective-permute-start.22
  112.4 2.0 collective-permute-start.13
  114.5 5.3 %collective-permute-done.22.refs_1_ = bf16[128,1024]{1,0:T(8,128)(2,1)S(1)} collective-permute-done((bf16[128,1024]{1,0:T(8,128)(2,1)S(1)}, bf16[128,1024]{1,0:T(8,128)(2,1)S(1)}, u32[]{:S(2)}, u32[]{:S(2)}) %collective-permute-start.22) | collective-permute-done | bytes 262176 | tf_op jit(solution)/shard_map/ppermute | solution.py:69
  119.7 1.9 collective-permute-start.26
  121.6 22.2 %collective-permute-done.26.refs_3_ = bf16[128,1024]{1,0:T(8,128)(2,1)} collective-permute-done((bf16[128,1024]{1,0:T(8,128)(2,1)S(1)}, bf16[128,1024]{1,0:T(8,128)(2,1)}, u32[]{:S(2)}, u32[]{:S(2)}) %collective-permute-start.26) | collective-permute-done | bytes 262176 | tf_op jit(solution)/shard_map/ppermute | solution.py:69
  143.8 2.0 collective-permute-start.23
  145.8 4.4 %collective-permute-done.23.refs_1_ = bf16[128,1024]{1,0:T(8,128)(2,1)S(1)} collective-permute-done((bf16[128,1024]{1,0:T(8,128)(2,1)S(1)}, bf16[128,1024]{1,0:T(8,128)(2,1)S(1)}, u32[]{:S(2)}, u32[]{:S(2)}) %collective-permute-start.23) | collective-permute-done | bytes 262176 | tf_op jit(solution)/shard_map/ppermute | solution.py:69
  150.3 6.5 %collective-permute-done.27.refs_3_ = bf16[128,1024]{1,0:T(8,128)(2,1)S(1)} collective-permute-done((bf16[128,1024]{1,0:T(8,128)(2,1)}, bf16[128,1024]{1,0:T(8,128)(2,1)S(1)}, u32[]{:S(2)}, u32[]{:S(2)}) %collective-permute-start.27) | collective-permute-done | bytes 262176 | tf_op jit(solution)/shard_map/ppermute | solution.py:69
  157.3 1.5 collective-permute-start.34
  159.7 1.4 constant_dynamic-slice_fusion.1
  161.1 1.1 slice.24
  162.2 2.1 collective-permute-start.14
  164.3 1.1 slice.25
  165.4 1.8 collective-permute-start.24
  167.9 4.5 %project.8 = (f32[512,512]{1,0:T(8,128)S(1)}, bf16[512,512]{1,0:T(8,128)(2,1)S(1)}) custom-call(bf16[2,256,2048]{2,1,0:T(8,128)(2,1)S(1)} %mixed.1.refs_0_, bf16[2,256,2048]{2,1,0:T(8,128)(2,1)} %collective-permute-done.10.refs_1_, bf16[2048,256]{1,0:T(8,128)(2,1)} %collective-permute-done.11.refs_2_, bf16[2048,256]{1,0:T(8,128)(2,1)} %collective-permute-done.15.refs_3_), custom_call_target="tpu_custom_call" | custom-call | flops 1 | bytes 1 | tf_op jit(solution)/shard_map/project/pallas_call | solution.py:27
  172.5 4.6 %project.7 = (f32[512,512]{1,0:T(8,128)S(1)}, bf16[512,512]{1,0:T(8,128)(2,1)S(1)}) custom-call(bf16[2,256,2048]{2,1,0:T(8,128)(2,1)S(1)} %mixed.1.refs_0_, bf16[2,256,2048]{2,1,0:T(8,128)(2,1)} %collective-permute-done.10.refs_1_, bf16[2048,256]{1,0:T(8,128)(2,1)} %collective-permute-done.12.refs_2_, bf16[2048,256]{1,0:T(8,128)(2,1)} %collective-permute-done.16.refs_3_), custom_call_target="tpu_custom_call" | custom-call | flops 1 | bytes 1 | tf_op jit(solution)/shard_map/project/pallas_call | solution.py:27
  177.7 1.5 collective-permute-start.33
  179.2 2.9 %project.9 = (f32[512,256]{1,0:T(8,128)S(1)}, bf16[512,256]{1,0:T(8,128)(2,1)S(1)}) custom-call(bf16[2,256,2048]{2,1,0:T(8,128)(2,1)S(1)} %mixed.1.refs_0_, bf16[2,256,2048]{2,1,0:T(8,128)(2,1)} %collective-permute-done.10.refs_1_, bf16[2048,256]{1,0:T(8,128)(2,1)S(1)} %copy-done.7), custom_call_target="tpu_custom_call" | custom-call | flops 1 | bytes 1 | tf_op jit(solution)/shard_map/project/pallas_call | solution.py:27
  182.8 1.5 collective-permute-start.39
  184.2 1.4 constant_dynamic-slice_fusion
  185.6 4.5 %project.6 = (f32[512,512]{1,0:T(8,128)S(1)}, bf16[512,512]{1,0:T(8,128)(2,1)S(1)}) custom-call(bf16[2,256,2048]{2,1,0:T(8,128)(2,1)S(1)} %mixed.1.refs_0_, bf16[2,256,2048]{2,1,0:T(8,128)(2,1)} %collective-permute-done.10.refs_1_, bf16[2048,256]{1,0:T(8,128)(2,1)} %collective-permute-done.13.refs_2_, bf16[2048,256]{1,0:T(8,128)(2,1)} %collective-permute-done.17.refs_3_), custom_call_target="tpu_custom_call" | custom-call | flops 1 | bytes 1 | tf_op jit(solution)/shard_map/project/pallas_call | solution.py:27
  190.8 2.9 %project.5 = (f32[512,256]{1,0:T(8,128)S(1)}, bf16[512,256]{1,0:T(8,128)(2,1)S(1)}) custom-call(bf16[2,256,2048]{2,1,0:T(8,128)(2,1)S(1)} %mixed.1.refs_0_, bf16[2,256,2048]{2,1,0:T(8,128)(2,1)} %collective-permute-done.10.refs_1_, bf16[1024,256]{1,0:T(8,128)(2,1)S(1)} %collective-permute-done.14.refs_2_, bf16[1024,256]{1,0:T(8,128)(2,1)S(1)} %collective-permute-done.18.refs_3_), custom_call_target="tpu_custom_call" | custom-call | flops 1 | bytes 1 | tf_op jit(solution)/shard_map/project/pallas_call | solution.py:27
  193.7 15.2 %collective-permute-done.35.refs_4_ = bf16[128,1024]{1,0:T(8,128)(2,1)S(1)} collective-permute-done((bf16[128,1024]{1,0:T(8,128)(2,1)}, bf16[128,1024]{1,0:T(8,128)(2,1)S(1)}, u32[]{:S(2)}, u32[]{:S(2)}) %collective-permute-start.35) | collective-permute-done | bytes 262176 | tf_op jit(solution)/shard_map/ppermute | solution.py:53
  209.4 5.1 %collective-permute-done.39.refs_0_ = bf16[512,256]{1,0:T(8,128)(2,1)S(1)} collective-permute-done((bf16[512,256]{1,0:T(8,128)(2,1)S(1)}, bf16[512,256]{1,0:T(8,128)(2,1)S(1)}, u32[]{:S(2)}, u32[]{:S(2)}) %collective-permute-start.39) | collective-permute-done | bytes 262176 | tf_op jit(solution)/shard_map/ppermute | solution.py:53
  215.0 1.5 collective-permute-start.29
  217.2 1.1 cache.5
  218.3 1.4 cache.6
  219.7 1.8 cache.7
  221.5 9.9 %collective-permute-done.31.refs_2_ = bf16[128,1024]{1,0:T(8,128)(2,1)S(1)} collective-permute-done((bf16[128,1024]{1,0:T(8,128)(2,1)S(1)}, bf16[128,1024]{1,0:T(8,128)(2,1)S(1)}, u32[]{:S(2)}, u32[]{:S(2)}) %collective-permute-start.31) | collective-permute-done | bytes 262176 | tf_op jit(solution)/shard_map/ppermute | solution.py:53
  231.4 4.4 %collective-permute-done.32.refs_4_ = bf16[128,1024]{1,0:T(8,128)(2,1)S(1)} collective-permute-done((bf16[128,1024]{1,0:T(8,128)(2,1)S(1)}, bf16[128,1024]{1,0:T(8,128)(2,1)S(1)}, u32[]{:S(2)}, u32[]{:S(2)}) %collective-permute-start.32) | collective-permute-done | bytes 262176 | tf_op jit(solution)/shard_map/ppermute | solution.py:53
  235.8 1.4 cache.8
  237.2 1.4 collective-permute-done.29.refs_2_
  238.6 2.8 %collective-permute-done.20.refs_0_ = bf16[512,256]{1,0:T(8,128)(2,1)S(1)} collective-permute-done((bf16[512,256]{1,0:T(8,128)(2,1)S(1)}, bf16[512,256]{1,0:T(8,128)(2,1)S(1)}, u32[]{:S(2)}, u32[]{:S(2)}) %collective-permute-start.20) | collective-permute-done | bytes 262176 | tf_op jit(solution)/shard_map/ppermute | solution.py:53
  241.4 1.1 cache.9
  243.3 2.2 collective-permute-done.42.square_in
  246.3 1.5 collective-permute-start
  247.9 11.9 %collective-permute-done = s32[2,2]{1,0:T(2,128)S(1)} collective-permute-done((s32[2,2]{1,0:T(2,128)S(1)}, s32[2,2]{1,0:T(2,128)S(1)}, u32[]{:S(2)}, u32[]{:S(2)}) %collective-permute-start) | collective-permute-done | bytes 48 | tf_op jit(solution)/shard_map/ppermute | solution.py:53
  259.9 1.6 place.1
  (114 shorter events, 15.0 us)
Async XLA Ops:
  0.0 64.5 %copy-start = (bf16[256,1024]{1,0:T(8,128)(2,1)S(1)}, bf16[256,1024]{1,0:T(8,128)(2,1)}, u32[]{:S(2)}) copy-start(bf16[256,1024]{1,0:T(8,128)(2,1)} %param.16) | copy-start | bytes 1572868
  0.0 27.3 %collective-permute-start.11 = (bf16[2048,256]{1,0:T(8,128)(2,1)}, bf16[2048,256]{1,0:T(8,128)(2,1)}, u32[]{:S(2)}, u32[]{:S(2)}) collective-permute-start(bf16[2048,256]{1,0:T(8,128)(2,1)} %refs_2_.1), channel_id=1, source_target_pairs={{0,8},{2,10},{8,16},{10,18},{16,24},{18,26},{24,28},{26,30},{28,20... | collective-permute-start | bytes 3145736 | tf_op jit(solution)/shard_map/ppermute | solution.py:69
  3.0 61.1 %collective-permute-start.15 = (bf16[2048,256]{1,0:T(8,128)(2,1)}, bf16[2048,256]{1,0:T(8,128)(2,1)}, u32[]{:S(2)}, u32[]{:S(2)}) collective-permute-start(bf16[2048,256]{1,0:T(8,128)(2,1)} %refs_2_.1), channel_id=1, source_target_pairs={{0,4},{2,6},{8,0},{10,2},{16,8},{18,10},{24,16},{26,18},{28,24},{3... | collective-permute-start | bytes 3145736 | tf_op jit(solution)/shard_map/ppermute | solution.py:69
  3.1 1.6 copy-start.3
  4.7 1.6 copy-start.5
  6.3 0.8 copy-start.20
  12.5 53.6 %copy-start.1 = (bf16[512,2048]{1,0:T(8,128)(2,1)S(1)}, bf16[512,2048]{1,0:T(8,128)(2,1)}, u32[]{:S(2)}) copy-start(bf16[512,2048]{1,0:T(8,128)(2,1)} %query.3) | copy-start | bytes 6291460
  12.5 15.7 %collective-permute-start.1 = (bf16[4,144,128]{2,1,0:T(8,128)(2,1)S(1)}, bf16[4,144,128]{2,1,0:T(8,128)(2,1)S(1)}, u32[]{:S(2)}, u32[]{:S(2)}) collective-permute-start(bf16[4,144,128]{2,1,0:T(8,128)(2,1)S(1)} %get-tuple-element.36), channel_id=1, source_target_pairs={{0,2},{2,0},{4,6},{6,4},{8,10},{10,8},{12,14},{14,12},{16,18},{18,... | collective-permute-start | bytes 442376 | tf_op jit(solution)/shard_map/ppermute | solution.py:44
  12.6 17.7 %collective-permute-start.2 = (bf16[4,144,128]{2,1,0:T(8,128)(2,1)S(1)}, bf16[4,144,128]{2,1,0:T(8,128)(2,1)S(1)}, u32[]{:S(2)}, u32[]{:S(2)}) collective-permute-start(bf16[4,144,128]{2,1,0:T(8,128)(2,1)S(1)} %get-tuple-element.37), channel_id=1, source_target_pairs={{0,4},{2,6},{4,0},{6,2},{8,12},{10,14},{12,8},{14,10},{16,20},{18,... | collective-permute-start | bytes 442376 | tf_op jit(solution)/shard_map/ppermute | solution.py:44
  14.6 17.4 %collective-permute-start.3 = (bf16[4,144,128]{2,1,0:T(8,128)(2,1)S(1)}, bf16[4,144,128]{2,1,0:T(8,128)(2,1)S(1)}, u32[]{:S(2)}, u32[]{:S(2)}) collective-permute-start(bf16[4,144,128]{2,1,0:T(8,128)(2,1)S(1)} %get-tuple-element.38), channel_id=1, source_target_pairs={{0,6},{2,4},{4,2},{6,0},{8,14},{10,12},{12,10},{14,8},{16,22},{18,... | collective-permute-start | bytes 442376 | tf_op jit(solution)/shard_map/ppermute | solution.py:44
  27.3 85.2 %collective-permute-start.12 = (bf16[2048,256]{1,0:T(8,128)(2,1)}, bf16[2048,256]{1,0:T(8,128)(2,1)}, u32[]{:S(2)}, u32[]{:S(2)}) collective-permute-start(bf16[2048,256]{1,0:T(8,128)(2,1)} %collective-permute-done.11.refs_2_), channel_id=1, source_target_pairs={{0,8},{2,10},{8,16},{10,18},{16,24},{18,26},{24,28},{26,30},{28,20... | collective-permute-start | bytes 3145736 | tf_op jit(solution)/shard_map/ppermute | solution.py:69
  32.7 22.5 %collective-permute-start.4 = (bf16[4,144,128]{2,1,0:T(8,128)(2,1)S(1)}, bf16[4,144,128]{2,1,0:T(8,128)(2,1)S(1)}, u32[]{:S(2)}, u32[]{:S(2)}) collective-permute-start(bf16[4,144,128]{2,1,0:T(8,128)(2,1)S(1)} %plane_state.1), channel_id=1, source_target_pairs={{0,8},{2,10},{4,12},{6,14},{8,16},{10,18},{12,20},{14,22},{16,24},... | collective-permute-start | bytes 442376 | tf_op jit(solution)/shard_map/ppermute | solution.py:49
  34.0 23.9 %collective-permute-start.5 = (bf16[4,144,128]{2,1,0:T(8,128)(2,1)S(1)}, bf16[4,144,128]{2,1,0:T(8,128)(2,1)S(1)}, u32[]{:S(2)}, u32[]{:S(2)}) collective-permute-start(bf16[4,144,128]{2,1,0:T(8,128)(2,1)S(1)} %plane_state.1), channel_id=1, source_target_pairs={{0,16},{2,18},{4,20},{6,22},{8,24},{10,26},{12,28},{14,30},{1,17},... | collective-permute-start | bytes 442376 | tf_op jit(solution)/shard_map/ppermute | solution.py:49
  41.8 17.7 %collective-permute-start.6 = (bf16[4,144,128]{2,1,0:T(8,128)(2,1)S(1)}, bf16[4,144,128]{2,1,0:T(8,128)(2,1)S(1)}, u32[]{:S(2)}, u32[]{:S(2)}) collective-permute-start(bf16[4,144,128]{2,1,0:T(8,128)(2,1)S(1)} %plane_state.1), channel_id=1, source_target_pairs={{0,24},{2,26},{4,28},{6,30},{1,25},{3,27},{5,29},{7,31}} | collective-permute-start | bytes 442376 | tf_op jit(solution)/shard_map/ppermute | solution.py:49
  62.3 2.2 collective-permute-start.7
  62.3 20.4 %collective-permute-start.8 = (bf16[4,128,128]{2,1,0:T(8,128)(2,1)}, bf16[4,128,128]{2,1,0:T(8,128)(2,1)S(1)}, u32[]{:S(2)}, u32[]{:S(2)}) collective-permute-start(bf16[4,128,128]{2,1,0:T(8,128)(2,1)} %copy-done.22), channel_id=1, source_target_pairs={{0,4},{2,6},{4,0},{6,2},{8,12},{10,14},{12,8},{14,10},{16,20},{18,... | collective-permute-start | bytes 393224 | tf_op jit(solution)/shard_map/ppermute | solution.py:44
  62.3 20.4 %collective-permute-start.9 = (bf16[4,128,128]{2,1,0:T(8,128)(2,1)}, bf16[4,128,128]{2,1,0:T(8,128)(2,1)S(1)}, u32[]{:S(2)}, u32[]{:S(2)}) collective-permute-start(bf16[4,128,128]{2,1,0:T(8,128)(2,1)} %copy-done.21), channel_id=1, source_target_pairs={{0,6},{2,4},{4,2},{6,0},{8,14},{10,12},{12,10},{14,8},{16,22},{18,... | collective-permute-start | bytes 393224 | tf_op jit(solution)/shard_map/ppermute | solution.py:44
  64.1 50.3 %collective-permute-start.16 = (bf16[2048,256]{1,0:T(8,128)(2,1)}, bf16[2048,256]{1,0:T(8,128)(2,1)}, u32[]{:S(2)}, u32[]{:S(2)}) collective-permute-start(bf16[2048,256]{1,0:T(8,128)(2,1)} %collective-permute-done.15.refs_3_), channel_id=1, source_target_pairs={{0,4},{2,6},{8,0},{10,2},{16,8},{18,10},{24,16},{26,18},{28,24},{3... | collective-permute-start | bytes 3145736 | tf_op jit(solution)/shard_map/ppermute | solution.py:69
  64.5 18.2 %copy-start.18 = (bf16[4,128,128]{2,1,0:T(8,128)(2,1)}, bf16[4,128,128]{2,1,0:T(8,128)(2,1)S(1)}, u32[]{:S(2)}) copy-start(bf16[4,128,128]{2,1,0:T(8,128)(2,1)S(1)} %collective-permute-done.7.refs_1_) | copy-start | bytes 393220
  64.5 30.0 %collective-permute-start.40 = (bf16[128,1024]{1,0:T(8,128)(2,1)S(1)}, bf16[128,1024]{1,0:T(8,128)(2,1)S(1)}, u32[]{:S(2)}, u32[]{:S(2)}) collective-permute-start(bf16[128,1024]{1,0:T(8,128)(2,1)S(1)} %constant_dynamic-slice_fusion.14.refs_1_), channel_id=1, source_target_pairs={{0,1},{1,0},{2,3},{3,2},{4,5},{5,4},{6,7},{7,6},{8,9},{9,8},{10,11... | collective-permute-start | bytes 786440 | tf_op jit(solution)/shard_map/ppermute | solution.py:53
  66.1 1.6 copy-start.4
  67.7 1.6 copy-start.6
  69.3 13.4 %copy-start.2 = (bf16[512,2048]{1,0:T(8,128)(2,1)S(1)}, bf16[512,2048]{1,0:T(8,128)(2,1)}, u32[]{:S(2)}) copy-start(bf16[512,2048]{1,0:T(8,128)(2,1)} %query.3) | copy-start | bytes 6291460
  82.7 0.9 copy-start.19
  89.9 77.5 %collective-permute-start.10 = (bf16[2,256,2048]{2,1,0:T(8,128)(2,1)S(1)}, bf16[2,256,2048]{2,1,0:T(8,128)(2,1)}, u32[]{:S(2)}, u32[]{:S(2)}) collective-permute-start(bf16[2,256,2048]{2,1,0:T(8,128)(2,1)S(1)} %mixed.1.refs_0_), channel_id=1, source_target_pairs={{0,2},{2,0},{4,6},{6,4},{8,10},{10,8},{12,14},{14,12},{16,18},{18,... | collective-permute-start | bytes 6291464 | tf_op jit(solution)/shard_map/ppermute | solution.py:44
  90.0 11.7 %collective-permute-start.21 = (bf16[128,1024]{1,0:T(8,128)(2,1)S(1)}, bf16[128,1024]{1,0:T(8,128)(2,1)S(1)}, u32[]{:S(2)}, u32[]{:S(2)}) collective-permute-start(bf16[128,1024]{1,0:T(8,128)(2,1)S(1)} %constant_dynamic-slice_fusion.14.refs_1_), channel_id=1, source_target_pairs={{0,8},{2,10},{8,16},{10,18},{16,24},{18,26},{24,28},{26,30},{28,20... | collective-permute-start | bytes 786440 | tf_op jit(solution)/shard_map/ppermute | solution.py:69
  95.2 8.6 %collective-permute-start.25 = (bf16[128,1024]{1,0:T(8,128)(2,1)S(1)}, bf16[128,1024]{1,0:T(8,128)(2,1)S(1)}, u32[]{:S(2)}, u32[]{:S(2)}) collective-permute-start(bf16[128,1024]{1,0:T(8,128)(2,1)S(1)} %constant_dynamic-slice_fusion.14.refs_1_), channel_id=1, source_target_pairs={{0,4},{2,6},{8,0},{10,2},{16,8},{18,10},{24,16},{26,18},{28,24},{3... | collective-permute-start | bytes 786440 | tf_op jit(solution)/shard_map/ppermute | solution.py:69
  101.7 8.1 %collective-permute-start.37 = (bf16[128,1024]{1,0:T(8,128)(2,1)S(1)}, bf16[128,1024]{1,0:T(8,128)(2,1)S(1)}, u32[]{:S(2)}, u32[]{:S(2)}) collective-permute-start(bf16[128,1024]{1,0:T(8,128)(2,1)S(1)} %collective-permute-done.21.refs_1_), channel_id=1, source_target_pairs={{0,1},{1,0},{2,3},{3,2},{4,5},{5,4},{6,7},{7,6},{8,9},{9,8},{10,11... | collective-permute-start | bytes 786440 | tf_op jit(solution)/shard_map/ppermute | solution.py:53
  103.8 42.0 %copy-start.12 = (bf16[128,1024]{1,0:T(8,128)(2,1)}, bf16[128,1024]{1,0:T(8,128)(2,1)S(1)}, u32[]{:S(2)}) copy-start(bf16[128,1024]{1,0:T(8,128)(2,1)S(1)} %collective-permute-done.25.refs_3_) | copy-start | bytes 786436
  103.8 78.3 %collective-permute-start.19 = (bf16[256,4096]{1,0:T(8,128)(2,1)}, bf16[256,4096]{1,0:T(8,128)(2,1)}, u32[]{:S(2)}, u32[]{:S(2)}) collective-permute-start(bf16[256,4096]{1,0:T(8,128)(2,1)} %param.13), channel_id=1, source_target_pairs={{0,2},{2,0},{4,6},{6,4},{8,10},{10,8},{12,14},{14,12},{16,18},{18,... | collective-permute-start | bytes 6291464 | tf_op jit(solution)/shard_map/ppermute | solution.py:44
  110.5 9.2 %collective-permute-start.22 = (bf16[128,1024]{1,0:T(8,128)(2,1)S(1)}, bf16[128,1024]{1,0:T(8,128)(2,1)S(1)}, u32[]{:S(2)}, u32[]{:S(2)}) collective-permute-start(bf16[128,1024]{1,0:T(8,128)(2,1)S(1)} %collective-permute-done.21.refs_1_), channel_id=1, source_target_pairs={{0,8},{2,10},{8,16},{10,18},{16,24},{18,26},{24,28},{26,30},{28,20... | collective-permute-start | bytes 786440 | tf_op jit(solution)/shard_map/ppermute | solution.py:69
  111.7 0.7 copy-start.10
  112.4 44.9 %collective-permute-start.13 = (bf16[2048,256]{1,0:T(8,128)(2,1)}, bf16[2048,256]{1,0:T(8,128)(2,1)}, u32[]{:S(2)}, u32[]{:S(2)}) collective-permute-start(bf16[2048,256]{1,0:T(8,128)(2,1)} %collective-permute-done.12.refs_2_), channel_id=1, source_target_pairs={{0,8},{2,10},{8,16},{10,18},{16,24},{18,26},{24,28},{26,30},{28,20... | collective-permute-start | bytes 3145736 | tf_op jit(solution)/shard_map/ppermute | solution.py:69
  114.4 47.7 %collective-permute-start.17 = (bf16[2048,256]{1,0:T(8,128)(2,1)}, bf16[2048,256]{1,0:T(8,128)(2,1)}, u32[]{:S(2)}, u32[]{:S(2)}) collective-permute-start(bf16[2048,256]{1,0:T(8,128)(2,1)} %collective-permute-done.16.refs_3_), channel_id=1, source_target_pairs={{0,4},{2,6},{8,0},{10,2},{16,8},{18,10},{24,16},{26,18},{28,24},{3... | collective-permute-start | bytes 3145736 | tf_op jit(solution)/shard_map/ppermute | solution.py:69
  119.7 30.5 %copy-start.16 = (bf16[128,1024]{1,0:T(8,128)(2,1)}, bf16[128,1024]{1,0:T(8,128)(2,1)S(1)}, u32[]{:S(2)}) copy-start(bf16[128,1024]{1,0:T(8,128)(2,1)S(1)} %collective-permute-done.22.refs_1_) | copy-start | bytes 786436
  119.7 24.1 %collective-permute-start.26 = (bf16[128,1024]{1,0:T(8,128)(2,1)S(1)}, bf16[128,1024]{1,0:T(8,128)(2,1)}, u32[]{:S(2)}, u32[]{:S(2)}) collective-permute-start(bf16[128,1024]{1,0:T(8,128)(2,1)S(1)} %collective-permute-done.25.refs_3_), channel_id=1, source_target_pairs={{0,4},{2,6},{8,0},{10,2},{16,8},{18,10},{24,16},{26,18},{28,24},{3... | collective-permute-start | bytes 786440 | tf_op jit(solution)/shard_map/ppermute | solution.py:69
  143.8 6.4 %collective-permute-start.23 = (bf16[128,1024]{1,0:T(8,128)(2,1)S(1)}, bf16[128,1024]{1,0:T(8,128)(2,1)S(1)}, u32[]{:S(2)}, u32[]{:S(2)}) collective-permute-start(bf16[128,1024]{1,0:T(8,128)(2,1)S(1)} %collective-permute-done.22.refs_1_), channel_id=1, source_target_pairs={{0,8},{2,10},{8,16},{10,18},{16,24},{18,26},{24,28},{26,30},{28,20... | collective-permute-start | bytes 786440 | tf_op jit(solution)/shard_map/ppermute | solution.py:69
  150.2 6.6 %collective-permute-start.27 = (bf16[128,1024]{1,0:T(8,128)(2,1)}, bf16[128,1024]{1,0:T(8,128)(2,1)S(1)}, u32[]{:S(2)}, u32[]{:S(2)}) collective-permute-start(bf16[128,1024]{1,0:T(8,128)(2,1)} %collective-permute-done.26.refs_3_), channel_id=1, source_target_pairs={{0,4},{2,6},{8,0},{10,2},{16,8},{18,10},{24,16},{26,18},{28,24},{3... | collective-permute-start | bytes 786440 | tf_op jit(solution)/shard_map/ppermute | solution.py:69
  156.8 8.6 %collective-permute-start.38 = (bf16[128,1024]{1,0:T(8,128)(2,1)}, bf16[128,1024]{1,0:T(8,128)(2,1)S(1)}, u32[]{:S(2)}, u32[]{:S(2)}) collective-permute-start(bf16[128,1024]{1,0:T(8,128)(2,1)} %copy-done.12), channel_id=1, source_target_pairs={{0,1},{1,0},{2,3},{3,2},{4,5},{5,4},{6,7},{7,6},{8,9},{9,8},{10,11... | collective-permute-start | bytes 786440 | tf_op jit(solution)/shard_map/ppermute | solution.py:53
  157.3 9.8 %collective-permute-start.34 = (bf16[128,1024]{1,0:T(8,128)(2,1)}, bf16[128,1024]{1,0:T(8,128)(2,1)S(1)}, u32[]{:S(2)}, u32[]{:S(2)}) collective-permute-start(bf16[128,1024]{1,0:T(8,128)(2,1)} %copy-done.16), channel_id=1, source_target_pairs={{0,1},{1,0},{2,3},{3,2},{4,5},{5,4},{6,7},{7,6},{8,9},{9,8},{10,11... | collective-permute-start | bytes 786440 | tf_op jit(solution)/shard_map/ppermute | solution.py:53
  162.2 20.6 %collective-permute-start.14 = (bf16[1024,256]{1,0:T(8,128)(2,1)S(1)}, bf16[1024,256]{1,0:T(8,128)(2,1)S(1)}, u32[]{:S(2)}, u32[]{:S(2)}) collective-permute-start(bf16[1024,256]{1,0:T(8,128)(2,1)S(1)} %slice.24), channel_id=1, source_target_pairs={{0,8},{2,10},{8,16},{10,18},{16,24},{18,26},{24,28},{26,30},{28,20... | collective-permute-start | bytes 1572872 | tf_op jit(solution)/shard_map/ppermute | solution.py:69
  165.4 11.7 %collective-permute-start.24 = (bf16[64,1024]{1,0:T(8,128)(2,1)S(1)}, bf16[64,1024]{1,0:T(8,128)(2,1)S(1)}, u32[]{:S(2)}, u32[]{:S(2)}) collective-permute-start(bf16[64,1024]{1,0:T(8,128)(2,1)S(1)} %slice.26), channel_id=1, source_target_pairs={{0,8},{2,10},{8,16},{10,18},{16,24},{18,26},{24,28},{26,30},{28,20... | collective-permute-start | bytes 393224 | tf_op jit(solution)/shard_map/ppermute | solution.py:69
  167.2 10.6 %collective-permute-start.28 = (bf16[64,1024]{1,0:T(8,128)(2,1)S(1)}, bf16[64,1024]{1,0:T(8,128)(2,1)S(1)}, u32[]{:S(2)}, u32[]{:S(2)}) collective-permute-start(bf16[64,1024]{1,0:T(8,128)(2,1)S(1)} %slice.27), channel_id=1, source_target_pairs={{0,4},{2,6},{8,0},{10,2},{16,8},{18,10},{24,16},{26,18},{28,24},{3... | collective-permute-start | bytes 393224 | tf_op jit(solution)/shard_map/ppermute | solution.py:69
  167.4 22.7 %collective-permute-start.18 = (bf16[1024,256]{1,0:T(8,128)(2,1)S(1)}, bf16[1024,256]{1,0:T(8,128)(2,1)S(1)}, u32[]{:S(2)}, u32[]{:S(2)}) collective-permute-start(bf16[1024,256]{1,0:T(8,128)(2,1)S(1)} %slice.25), channel_id=1, source_target_pairs={{0,4},{2,6},{8,0},{10,2},{16,8},{18,10},{24,16},{26,18},{28,24},{3... | collective-permute-start | bytes 1572872 | tf_op jit(solution)/shard_map/ppermute | solution.py:69
  172.5 6.8 %copy-start.7 = (bf16[2048,256]{1,0:T(8,128)(2,1)S(1)}, bf16[2048,256]{1,0:T(8,128)(2,1)}, u32[]{:S(2)}) copy-start(bf16[2048,256]{1,0:T(8,128)(2,1)} %refs_2_.1) | copy-start | bytes 3145732
  177.1 37.9 %collective-permute-start.36 = (bf16[512,512]{1,0:T(8,128)(2,1)S(1)}, bf16[512,512]{1,0:T(8,128)(2,1)S(1)}, u32[]{:S(2)}, u32[]{:S(2)}) collective-permute-start(bf16[512,512]{1,0:T(8,128)(2,1)S(1)} %get-tuple-element.50), channel_id=1, source_target_pairs={{0,1},{1,0},{2,3},{3,2},{4,5},{5,4},{6,7},{7,6},{8,9},{9,8},{10,11... | collective-permute-start | bytes 1572872 | tf_op jit(solution)/shard_map/ppermute | solution.py:53
  177.7 38.8 %collective-permute-start.33 = (bf16[512,512]{1,0:T(8,128)(2,1)S(1)}, bf16[512,512]{1,0:T(8,128)(2,1)S(1)}, u32[]{:S(2)}, u32[]{:S(2)}) collective-permute-start(bf16[512,512]{1,0:T(8,128)(2,1)S(1)} %get-tuple-element.48), channel_id=1, source_target_pairs={{0,1},{1,0},{2,3},{3,2},{4,5},{5,4},{6,7},{7,6},{8,9},{9,8},{10,11... | collective-permute-start | bytes 1572872 | tf_op jit(solution)/shard_map/ppermute | solution.py:53
  182.1 26.7 %collective-permute-start.35 = (bf16[128,1024]{1,0:T(8,128)(2,1)}, bf16[128,1024]{1,0:T(8,128)(2,1)S(1)}, u32[]{:S(2)}, u32[]{:S(2)}) collective-permute-start(bf16[128,1024]{1,0:T(8,128)(2,1)} %collective-permute-done.26.refs_3_), channel_id=1, source_target_pairs={{0,1},{1,0},{2,3},{3,2},{4,5},{5,4},{6,7},{7,6},{8,9},{9,8},{10,11... | collective-permute-start | bytes 786440 | tf_op jit(solution)/shard_map/ppermute | solution.py:53
  182.8 31.7 %collective-permute-start.39 = (bf16[512,256]{1,0:T(8,128)(2,1)S(1)}, bf16[512,256]{1,0:T(8,128)(2,1)S(1)}, u32[]{:S(2)}, u32[]{:S(2)}) collective-permute-start(bf16[512,256]{1,0:T(8,128)(2,1)S(1)} %get-tuple-element.52), channel_id=1, source_target_pairs={{0,1},{1,0},{2,3},{3,2},{4,5},{5,4},{6,7},{7,6},{8,9},{9,8},{10,11... | collective-permute-start | bytes 786440 | tf_op jit(solution)/shard_map/ppermute | solution.py:53
  190.2 45.7 %collective-permute-start.30 = (bf16[512,512]{1,0:T(8,128)(2,1)S(1)}, bf16[512,512]{1,0:T(8,128)(2,1)S(1)}, u32[]{:S(2)}, u32[]{:S(2)}) collective-permute-start(bf16[512,512]{1,0:T(8,128)(2,1)S(1)} %get-tuple-element.46), channel_id=1, source_target_pairs={{0,1},{1,0},{2,3},{3,2},{4,5},{5,4},{6,7},{7,6},{8,9},{9,8},{10,11... | collective-permute-start | bytes 1572872 | tf_op jit(solution)/shard_map/ppermute | solution.py:53
  193.7 23.5 %copy-start.9 = (bf16[128,1024]{1,0:T(8,128)(2,1)S(1)}, bf16[128,1024]{1,0:T(8,128)(2,1)}, u32[]{:S(2)}) copy-start(bf16[128,1024]{1,0:T(8,128)(2,1)} %copy-done.8) | copy-start | bytes 786436
  208.9 22.5 %collective-permute-start.31 = (bf16[128,1024]{1,0:T(8,128)(2,1)S(1)}, bf16[128,1024]{1,0:T(8,128)(2,1)S(1)}, u32[]{:S(2)}, u32[]{:S(2)}) collective-permute-start(bf16[128,1024]{1,0:T(8,128)(2,1)S(1)} %collective-permute-done.23.refs_1_), channel_id=1, source_target_pairs={{0,1},{1,0},{2,3},{3,2},{4,5},{5,4},{6,7},{7,6},{8,9},{9,8},{10,11... | collective-permute-start | bytes 786440 | tf_op jit(solution)/shard_map/ppermute | solution.py:53
  214.5 21.3 %collective-permute-start.32 = (bf16[128,1024]{1,0:T(8,128)(2,1)S(1)}, bf16[128,1024]{1,0:T(8,128)(2,1)S(1)}, u32[]{:S(2)}, u32[]{:S(2)}) collective-permute-start(bf16[128,1024]{1,0:T(8,128)(2,1)S(1)} %collective-permute-done.27.refs_3_), channel_id=1, source_target_pairs={{0,1},{1,0},{2,3},{3,2},{4,5},{5,4},{6,7},{7,6},{8,9},{9,8},{10,11... | collective-permute-start | bytes 786440 | tf_op jit(solution)/shard_map/ppermute | solution.py:53
  215.0 23.6 %collective-permute-start.29 = (bf16[128,1024]{1,0:T(8,128)(2,1)S(1)}, bf16[128,1024]{1,0:T(8,128)(2,1)S(1)}, u32[]{:S(2)}, u32[]{:S(2)}) collective-permute-start(bf16[128,1024]{1,0:T(8,128)(2,1)S(1)} %constant_dynamic-update-slice_fusion.refs_1_), channel_id=1, source_target_pairs={{0,1},{1,0},{2,3},{3,2},{4,5},{5,4},{6,7},{7,6},{8,9},{9,8},{10,11... | collective-permute-start | bytes 786440 | tf_op jit(solution)/shard_map/ppermute | solution.py:53
  216.5 24.9 %collective-permute-start.20 = (bf16[512,256]{1,0:T(8,128)(2,1)S(1)}, bf16[512,256]{1,0:T(8,128)(2,1)S(1)}, u32[]{:S(2)}, u32[]{:S(2)}) collective-permute-start(bf16[512,256]{1,0:T(8,128)(2,1)S(1)} %get-tuple-element.44), channel_id=1, source_target_pairs={{0,1},{1,0},{2,3},{3,2},{4,5},{5,4},{6,7},{7,6},{8,9},{9,8},{10,11... | collective-permute-start | bytes 786440 | tf_op jit(solution)/shard_map/ppermute | solution.py:53
  217.1 1.2 copy-start.11
  217.1 1.2 copy-start.13
  217.1 1.2 copy-start.15
  218.3 1.4 copy-start.17
  242.6 2.9 %collective-permute-start.41 = (f32[256,1024]{1,0:T(8,128)S(1)}, f32[256,1024]{1,0:T(8,128)S(1)}, u32[]{:S(2)}, u32[]{:S(2)}) collective-permute-start(f32[256,1024]{1,0:T(8,128)S(1)} %slice.22), channel_id=1, source_target_pairs={{0,2},{2,0},{4,6},{6,4},{8,10},{10,8},{12,14},{14,12},{16,18},{18,... | collective-permute-start | bytes 3145736 | tf_op jit(solution)/shard_map/ppermute | solution.py:44
  242.7 3.6 %copy-start.23 = (s32[2,2]{1,0:T(2,128)S(1)}, s32[2,2]{1,0:T(2,128)}, u32[]{:S(2)}) copy-start(s32[2,2]{1,0:T(2,128)} %param.17) | copy-start | bytes 52
  242.7 2.8 %collective-permute-start.42 = (f32[256,128]{1,0:T(8,128)S(1)}, f32[256,128]{1,0:T(8,128)S(1)}, u32[]{:S(2)}, u32[]{:S(2)}) collective-permute-start(f32[256,128]{1,0:T(8,128)S(1)} %slice.23), channel_id=1, source_target_pairs={{0,2},{2,0},{4,6},{6,4},{8,10},{10,8},{12,14},{14,12},{16,18},{18,... | collective-permute-start | bytes 393224 | tf_op jit(solution)/shard_map/ppermute | solution.py:44
  245.7 14.2 %collective-permute-start.43 = (bf16[256,1024]{1,0:T(8,128)(2,1)S(1)}, bf16[256,1024]{1,0:T(8,128)(2,1)S(1)}, u32[]{:S(2)}, u32[]{:S(2)}) collective-permute-start(bf16[256,1024]{1,0:T(8,128)(2,1)S(1)} %finish.1.refs_0_), channel_id=1, source_target_pairs={{0,1},{1,0},{2,3},{3,2},{4,5},{5,4},{6,7},{7,6},{8,9},{9,8},{10,11... | collective-permute-start | bytes 1572872 | tf_op jit(solution)/shard_map/ppermute | solution.py:53
  246.3 13.5 %collective-permute-start = (s32[2,2]{1,0:T(2,128)S(1)}, s32[2,2]{1,0:T(2,128)S(1)}, u32[]{:S(2)}, u32[]{:S(2)}) collective-permute-start(s32[2,2]{1,0:T(2,128)S(1)} %copy-done.23), channel_id=1, source_target_pairs={{0,1},{1,0},{2,3},{3,2},{4,5},{5,4},{6,7},{7,6},{8,9},{9,8},{10,11... | collective-permute-start | bytes 56 | tf_op jit(solution)/shard_map/ppermute | solution.py:53
  (4 other events, 2.7 us)

commit v3 on v0

v3 whole, which is shorter than its diff:
```python
import functools

import jax
import jax.numpy as jnp
from jax import lax
from jax.experimental import pallas as pl
from jax.experimental.pallas import tpu as pltpu
from jax.sharding import PartitionSpec as P

HD = 128
PAGE = 128
INNER = 4
TAG = 16
EPS = 1e-05
BF16 = jnp.bfloat16
F32 = jnp.float32
SMEM = pl.BlockSpec(memory_space=pltpu.SMEM)
VMEM = pl.BlockSpec(memory_space=pltpu.VMEM)
FAR = pl.BlockSpec(memory_space=pltpu.HBM)
LIGHT = pl.CostEstimate(flops=1, bytes_accessed=1, transcendentals=0)


def params(mib):
    return pltpu.CompilerParams(vmem_limit_bytes=mib * 2**20)


def call(body, name, out_shape, args, scratch=(), mib=8, far=()):
    return pl.pallas_call(
        body,
        name=name,
        out_shape=out_shape,
        in_specs=[
            SMEM if a.dtype == jnp.int32 else FAR if n in far else VMEM
            for n, a in enumerate(args)
        ],
        out_specs=jax.tree.map(lambda _: VMEM, out_shape),
        scratch_shapes=list(scratch),
        cost_estimate=LIGHT,
        compiler_params=params(mib),
    )(*[in_hbm(a) if n in far else a for n, a in enumerate(args)])


def after(value, *first):
    return lax.optimization_barrier((value, *first))[0]


def in_hbm(value):
    return pltpu.with_memory_space_constraint(value, pltpu.HBM)


def shape(dims, dtype):
    return jax.ShapeDtypeStruct(dims, dtype)


def seq_xor(value, seq_count, bits):
    return lax.ppermute(value, "seq", [(j, j ^ bits) for j in range(seq_count)])


def seq_up(value, seq_count, planes):
    step = planes * INNER
    return lax.ppermute(value, "seq", [(j, j + step) for j in range(seq_count - step)])


def pool_shift(value, pool_count, by):
    return lax.ppermute(value, "pool", [(i, (i + by) % pool_count) for i in range(pool_count)])


def ring_chip(spot, planes):
    if isinstance(spot, int):
        return spot * 2 if spot < planes else (2 * planes - 1 - spot) * 2 + 1
    return jnp.where(spot < planes, spot * 2, (2 * planes - 1 - spot) * 2 + 1)


def ring_step(value, seq_count):
    planes = seq_count // INNER
    length = 2 * planes
    pairs = []
    for spot in range(length):
        for core, by in ((0, 1), (1, -1)):
            source, target = ring_chip(spot, planes), ring_chip((spot + by) % length, planes)
            pairs.append((source * 2 + core, target * 2 + core))
    return lax.ppermute(value, "seq", pairs)


def columns(lines):
    repeat = -(-8 // lines.shape[0])
    return jnp.concatenate([lines] * repeat).T


def tag_of(total):
    term = lax.broadcasted_iota(jnp.int32, (TAG, HD), 0)
    high = total.astype(BF16).astype(F32)
    middle = (total - high).astype(BF16).astype(F32)
    low = total - high - middle
    terms = jnp.where(
        term == 0, high, jnp.where(term == 1, middle, jnp.where(term == 2, low, 0.0))
    )
    return terms.astype(BF16)


def update_kernel(meta, key, value, decay, cumul, *outs):
    *pieces, held = outs
    _, share, rows = cumul.shape
    step = pl.program_id(0)

    @pl.when(step == 0)
    def _():
        before = lax.broadcasted_iota(jnp.int32, (rows, rows), 0)
        upto = lax.broadcasted_iota(jnp.int32, (rows, rows), 1)
        ones = (before <= upto).astype(F32)
        total = jnp.dot(
            decay[...], ones, precision=lax.Precision.HIGHEST, preferred_element_type=F32
        )
        for n in range(INNER):
            cumul[n] = total[n * share : (n + 1) * share]

    lines = cumul[step]
    weights = columns(jnp.exp(lines[:, rows - 1 :] - lines))
    for i in range(share):
        lane = slice(i * HD, (i + 1) * HD)
        weighted = (key[:, lane].astype(F32) * weights[:, i : i + 1]).astype(BF16)
        update = lax.dot_general(
            weighted, value[:, lane], (((0,), (0,)), ((), ())), preferred_element_type=F32
        )
        spot = step ^ meta[0]
        held[spot, i, :HD, :] = update.astype(BF16)
        held[spot, i, HD:, :] = tag_of(lines[i : i + 1, rows - 1 :])

    @pl.when(step == INNER - 1)
    def _():
        for r in range(INNER):
            pieces[r][...] = held[r]


def state_of(ref, i):
    return ref[i, :HD, :].astype(F32)


def total_of(ref, i):
    return jnp.sum(ref[i, HD:, :].astype(F32), axis=0, keepdims=True)


def stack_in_order(place, got, held):
    for r in range(INNER):
        held[r] = got[r][...]
    return [held.at[place ^ i] for i in range(INNER)]


def plane_kernel(meta, *refs):
    *got, out, held = refs
    parts = stack_in_order(meta[0], got, held)
    for i in range(out.shape[0]):
        state = jnp.zeros((HD, HD), F32)
        total = jnp.zeros((1, HD), F32)
        for part in parts:
            one = total_of(part, i)
            state = jnp.exp(one) * state + state_of(part, i)
            total = total + one
        out[i, :HD, :] = state.astype(BF16)
        out[i, HD:, :] = tag_of(total)


def entering_kernel(meta, *refs):
    held, leaving = refs[-2:]
    outs = refs[-2 - INNER : -2]
    got = refs[:INNER]
    earlier = refs[INNER : -2 - INNER]
    place = meta[0]
    parts = stack_in_order(place, got, held)
    for i in range(leaving.shape[1]):
        state = jnp.zeros((HD, HD), F32)
        gap = jnp.zeros((1, HD), F32)
        for plane in earlier:
            state = state + jnp.exp(gap) * state_of(plane, i)
            gap = gap + total_of(plane, i)
        for spot, part in enumerate(parts):
            leaving[place ^ spot, i] = state.astype(BF16)
            state = jnp.exp(total_of(part, i)) * state + state_of(part, i)
    for r in range(INNER):
        outs[r][...] = leaving[r]


def inner_kernel(query, key, value, cumul, out):
    rows = query.shape[0]
    half = min(256, rows)
    lines = cumul[0]
    upright = columns(lines)
    row = lax.broadcasted_iota(jnp.int32, (half, half), 0)
    col = lax.broadcasted_iota(jnp.int32, (half, half), 1)
    bar = jnp.where(row >= col, 0.0, -1e30)
    for i in range(lines.shape[0]):
        lane = slice(i * HD, (i + 1) * HD)
        for at in range(0, rows, half):
            here = slice(at, at + half)
            total = None
            for start in range(0, at + half, half):
                there = slice(start, start + half)
                products = lax.dot_general(
                    query[here, lane],
                    key[there, lane],
                    (((1,), (1,)), ((), ())),
                    preferred_element_type=F32,
                )
                gap = upright[here, i : i + 1] - lines[i : i + 1, there]
                if start == at:
                    gap = gap + bar
                scores = (products * jnp.exp(gap)).astype(BF16)
                part = jnp.dot(scores, value[there, lane], preferred_element_type=F32)
                total = part if total is None else total + part
            out[here, lane] = total


def mixed_kernel(meta, query, *refs):
    inners = refs[:2]
    cumul, *refs = refs[2:]
    *states, out, held = refs
    pool_count, rows, _ = out.shape
    step = pl.program_id(0)
    place, me = meta[0], meta[2]
    lines = cumul[0]
    grown = columns(jnp.exp(lines))
    for i in range(lines.shape[0]):
        lane = slice(i * HD, (i + 1) * HD)
        state = states[0][i]
        for r in range(1, INNER):
            state = jnp.where(step ^ place == r, states[r][i], state)
        outer = jnp.dot(query[:, lane], state, preferred_element_type=F32)
        held[:, lane] = outer * grown[:, i : i + 1]
    for n in range(INNER):

        @pl.when(step == n)
        def _():
            part = n % (INNER // 2) * held.shape[1]
            held[...] = held[...] + inners[n // (INNER // 2)][:, part : part + held.shape[1]]

    for r in range(pool_count):
        start = pl.multiple_of(lax.rem(me + r, pool_count) * rows, rows)
        for i in range(lines.shape[0]):
            lane = slice(i * HD, (i + 1) * HD)
            retained = held[pl.ds(start, rows), lane]
            mean = jnp.mean(retained * retained, axis=-1, keepdims=True)
            out[r, :, lane] = (retained * lax.rsqrt(mean + EPS)).astype(BF16)


def pack_kernel(weight, kv, out):
    depth, width = weight.shape
    rows = kv.shape[0]
    out[:depth, :] = weight[...]
    for c in range(kv.shape[1] // width):
        here = slice(c * width, (c + 1) * width)
        out[depth + c * rows : depth + (c + 1) * rows, :] = kv[:, here]


def project_kernel(joins, parts, *refs):
    if joins:
        own, other = refs[:2]
        both = refs[-1]
        refs = refs[2:-1]
        rows = own.shape[1]
        both[:, :rows, :] = own[...]
        both[:, rows:, :] = other[...]
    else:
        both = refs[0]
        refs = refs[1:]
    blocks = refs[:parts]
    kv, mine, *away = refs[parts:]
    pool_count, _, depth = both.shape
    width = blocks[0].shape[1]
    rows = kv.shape[0] // parts
    for r in list(range(1, pool_count)) + [0]:
        for p in range(parts):
            here = slice(p * width, (p + 1) * width)
            total = jnp.dot(both[r], blocks[p][:depth, :], preferred_element_type=F32)
            if r == 0:
                mine[:, here] = total
            else:
                away[r - 1][:, here] = total.astype(BF16)
    for p in range(parts):
        for c in range(kv.shape[1] // width):
            below = slice(depth + c * rows, depth + (c + 1) * rows)
            kv[p * rows : (p + 1) * rows, c * width : (c + 1) * width] = blocks[p][below, :]


def cache_kernel(first, parts, width, at, meta, mine, *refs):
    own_rows, other_rows, kv, gain, *refs = refs
    *arrived, scaled, near, sems = refs
    arrived, sums = arrived[:-4], arrived[-4:]
    if not first:
        arrived, old = arrived[:-4], arrived[-4:]
    rows = own_rows.shape[0]
    whole = own_rows.shape[1] == parts * width
    copies = []
    for p in range(parts if not whole else 0):
        here = slice(p * width, (p + 1) * width)
        there = pl.ds(pl.multiple_of(meta[at + p], width), width)
        for n, source in enumerate((own_rows, other_rows)):
            target = near.at[n * rows : (n + 1) * rows, here]
            copies.append(
                pltpu.make_async_copy(source.at[:, there], target, sems.at[2 * p + n])
            )
            copies[-1].start()
    for copy in copies:
        copy.wait()
    if whole:
        near[:rows, :] = own_rows[...]
        near[rows:, :] = other_rows[...]
    squares = 0.0
    for p in range(parts):
        here = slice(p * width, (p + 1) * width)
        there = here if whole else pl.ds(pl.multiple_of(meta[at + p], width), width)
        values = near[:, here].astype(F32) + mine[:, here]
        for part in arrived:
            values = values + part[:, here].astype(F32)
        squares = squares + jnp.sum(values * values, axis=-1, keepdims=True)
        scaled[:, here] = (values * gain[:, there]).astype(BF16)
    for n in range(2):
        here = slice(n * rows, (n + 1) * rows)
        product = jnp.dot(scaled[here, :], kv[...], preferred_element_type=F32)
        if first:
            sums[n][...] = product
            sums[2 + n][...] = jnp.broadcast_to(squares[here], (rows, HD))
        else:
            sums[n][...] = old[n][...] + product
            sums[2 + n][...] = old[2 + n][...] + squares[here]


def finish_kernel(features, total, square, total_in, square_in, out):
    mean = (square[:, :1] + square_in[:, :1]) / features
    out[...] = ((total[...] + total_in[...]) * lax.rsqrt(mean + EPS)).astype(BF16)


def place_kernel(pool_count, meta, *refs):
    tables = refs[:pool_count]
    *pages, out = refs[pool_count:]
    me = meta[2]
    out[...] = jnp.zeros(out.shape, out.dtype)
    for table, part in zip(tables, pages):
        for p in range(part.shape[0] // PAGE):
            owner, slot = table[p, 0], table[p, 1]

            @pl.when(owner == me)
            def _():
                out[slot] = part[p * PAGE : (p + 1) * PAGE, :]


def inner_part(n, count, query_rows, key_rows, value_rows, cumul):
    rows = query_rows.shape[0]
    _, share, _ = cumul.shape
    there = pl.BlockSpec((rows, share * HD), lambda i: (0, i + n))
    return pl.pallas_call(
        inner_kernel,
        name="inner",
        grid=(count,),
        out_shape=shape((rows, count * share * HD), F32),
        in_specs=[there] * 3 + [pl.BlockSpec((1, share, rows), lambda i: (i + n, 0, 0))],
        out_specs=pl.BlockSpec((rows, share * HD), lambda i: (0, i)),
        cost_estimate=LIGHT,
        compiler_params=params(12),
    )(in_hbm(query_rows), in_hbm(key_rows), in_hbm(value_rows), cumul)


def on_device(
    query_rows,
    key_rows,
    value_rows,
    log_decay,
    residual,
    out_weight,
    norm_gain,
    kv_weight,
    block_table,
):
    seq_count = lax.axis_size("seq")
    pool_count = lax.axis_size("pool")
    planes = seq_count // INNER
    length = 2 * planes
    index = lax.axis_index("seq")
    me = lax.axis_index("pool")
    place = index % INNER
    plane = index // INNER
    core = index % 2
    spot = jnp.where(place < 2, plane, length - 1 - plane)
    width = out_weight.shape[1]
    steps = length // 2
    starts = []
    for g in range(steps + 1):
        chip = ring_chip((spot + length + jnp.where(core == 0, -g, g)) % length, planes)
        cores = [core] if g in (0, steps) else [core, 1 - core]
        starts.append([(chip * 2 + c) * width for c in cores])
    meta = jnp.stack([place, plane, me] + sum(starts, [])).astype(jnp.int32)
    rows, wide = query_rows.shape
    heads = wide // HD
    share = heads // INNER
    rows_here = residual.shape[0]
    cache_width = kv_weight.shape[1]
    pages_here = block_table.shape[0]
    slot_count = 2 * pages_here
    chip_rows = 2 * rows_here
    tagged = (share, HD + TAG, HD)

    packed = shape(
        (out_weight.shape[0] + kv_weight.shape[0] * cache_width // width, width), BF16
    )
    weights = call(pack_kernel, "pack", packed, [out_weight, kv_weight])
    last = 2 * steps - 1
    come = {-1: weights, 0: seq_xor(weights, seq_count, 1)}

    def serve(n, *first):
        come[n] = ring_step(after(come[n - 2], *first) if first else come[n - 2], seq_count)
        return come[n]

    def arrivals(g):
        if g == 0:
            return [come[-1]]
        if g == steps:
            return [come[last]]
        return [come[2 * g - 1], come[2 * g]]

    serve(1)
    tables = [block_table] + [pool_shift(block_table, pool_count, r) for r in range(1, pool_count)]
    residual_other = seq_xor(residual, seq_count, 1)

    by_share = pl.BlockSpec((rows, share * HD), lambda g: (0, g))
    cumul, *pieces = pl.pallas_call(
        update_kernel,
        name="update",
        grid=(INNER,),
        out_shape=[shape((INNER, share, rows), F32)] + [shape(tagged, BF16)] * INNER,
        in_specs=[SMEM, by_share, by_share, pl.BlockSpec((heads, rows), lambda g: (0, 0))],
        out_specs=[pl.BlockSpec((INNER, share, rows), lambda g: (0, 0, 0))]
        + [pl.BlockSpec(tagged, lambda g: (0, 0, 0))] * INNER,
        scratch_shapes=[pltpu.VMEM((INNER, *tagged), BF16)],
        cost_estimate=LIGHT,
        compiler_params=params(12),
    )(meta, in_hbm(key_rows), in_hbm(value_rows), log_decay)
    pieces[1] = after(pieces[1], residual_other, *tables)
    got = [pieces[0]] + [seq_xor(pieces[r], seq_count, r) for r in range(1, INNER)]

    inners = [inner_part(0, INNER // 2, query_rows, key_rows, value_rows, cumul)]
    serve(2, got[1])
    got[1] = after(got[1], inners[0])
    plane_total = call(
        plane_kernel,
        "plane_state",
        shape(tagged, BF16),
        [meta, *got],
        [pltpu.VMEM((INNER, *tagged), BF16)],
    )
    earlier = [seq_up(plane_total, seq_count, d) for d in range(1, planes)]
    inners.append(
        inner_part(
            INNER // 2, INNER // 2, after(query_rows, plane_total), key_rows, value_rows, cumul
        )
    )
    serve(3, earlier[0])
    earlier[1] = after(earlier[1], inners[1], come[1], come[2])
    leaving = call(
        entering_kernel,
        "entering_state",
        [shape((share, HD, HD), BF16)] * INNER,
        [meta, *got, *earlier],
        [pltpu.VMEM((INNER, *tagged), BF16), pltpu.VMEM((INNER, share, HD, HD), BF16)],
    )
    states = [leaving[0]] + [seq_xor(leaving[r], seq_count, r) for r in range(1, INNER)]
    serve(4, states[1])
    states[2] = after(states[2], come[3])

    mixed = pl.pallas_call(
        mixed_kernel,
        name="mixed",
        grid=(INNER,),
        out_shape=shape((pool_count, rows_here, wide), BF16),
        in_specs=[SMEM, by_share]
        + [VMEM] * 2
        + [pl.BlockSpec((1, share, rows), lambda g: (g, 0, 0))]
        + [VMEM] * INNER,
        out_specs=pl.BlockSpec((pool_count, rows_here, share * HD), lambda g: (0, 0, g)),
        scratch_shapes=[pltpu.VMEM((rows, share * HD), F32)],
        cost_estimate=LIGHT,
        compiler_params=params(12),
    )(meta, in_hbm(query_rows), *inners, cumul, *states)
    mixed_other = seq_xor(mixed, seq_count, 1)
    serve(5, mixed)
    both = []

    def project(g, *first):
        blocks = arrivals(g)
        count = len(blocks)
        out_wide = count * width
        joins = not both
        sources = [after(both[0], *first)] if both else [mixed, mixed_other]
        joined = [shape((pool_count, chip_rows, wide), BF16)] if joins else []
        kv, mine, *away = call(
            functools.partial(project_kernel, joins, count),
            "project",
            [shape((out_wide, cache_width), BF16), shape((chip_rows, out_wide), F32)]
            + [shape((chip_rows, out_wide), BF16)] * (pool_count - 1)
            + joined,
            [*sources, *blocks],
            mib=12,
        )
        if joins:
            both.append(away.pop())
        arrived = [pool_shift(away[r - 1], pool_count, r) for r in range(1, pool_count)]
        return mine, kv, arrived

    def cache(g, projected, sums, *first):
        mine, kv, arrived = projected
        count = len(starts[g])
        out_wide = count * width
        around = [residual, residual_other, norm_gain.reshape(1, -1)]
        if width % HD:
            around = [
                jnp.concatenate([lax.dynamic_slice_in_dim(a, s, width, 1) for s in starts[g]], 1)
                for a in around
            ]
        return call(
            functools.partial(
                cache_kernel, not sums, count, width, 3 + sum(len(x) for x in starts[:g])
            ),
            "cache",
            [shape((rows_here, cache_width), F32)] * 2 + [shape((rows_here, HD), F32)] * 2,
            [
                meta,
                after(mine, *first),
                *around[:2],
                kv,
                around[2],
                *arrived,
                *sums,
            ],
            [
                pltpu.VMEM((chip_rows, out_wide), BF16),
                pltpu.VMEM((chip_rows, out_wide), BF16),
                pltpu.SemaphoreType.DMA((2 * count,)),
            ],
            mib=12,
            far=() if width % HD else (2, 3),
        )

    projected = {0: project(0)}
    done = (projected[0][0],)
    sums = ()
    cached = 0

    def reduce_one():
        nonlocal sums, done, cached
        sums = cache(cached, projected[cached], sums, *done)
        done = (sums[2],)
        cached += 1

    for g in range(1, steps + 1):
        if g >= 2:
            for n in (2 * g - 1, 2 * g):
                if n <= last:
                    if 5 < n + 2 <= last:
                        serve(n + 2, come[n], *done)
                    done = (*done, come[n])
        projected[g] = project(g, *done)
        done = (projected[g][0],)
        if 2 <= g < steps:
            reduce_one()
    while cached <= steps:
        reduce_one()
    own_total, other_total, own_square, other_square = sums
    cache_rows = call(
        functools.partial(finish_kernel, width * seq_count),
        "finish",
        shape((rows_here, cache_width), BF16),
        [
            own_total,
            own_square,
            seq_xor(other_total, seq_count, 1),
            seq_xor(other_square, seq_count, 1),
        ],
    )
    pages = [cache_rows] + [pool_shift(cache_rows, pool_count, r) for r in range(1, pool_count)]
    page_cache = call(
        functools.partial(place_kernel, pool_count),
        "place",
        shape((slot_count, PAGE, cache_width), BF16),
        [meta, *tables, *pages],
    )
    return page_cache.reshape(1, 1, slot_count, PAGE, cache_width)


def solution(mesh):
    placed = (
        P("seq", "pool"),
        P("seq", "pool"),
        P("seq", "pool"),
        P("pool", "seq"),
        P(("seq", "pool"), None),
        P("pool", "seq"),
        P(),
        P("seq", None),
        P(("seq", "pool"), None),
    )
    return jax.shard_map(
        on_device,
        mesh=mesh,
        in_specs=placed,
        out_specs=P("seq", "pool", None, None, None),
        check_vma=False,
    )
```

time: 503 us -> 195 us (0.39)
  waiting for transfers between devices: 367 us -> 101 us
  blocking collectives: 52.7 us -> 0 us
  Pallas kernels: 0 us -> 46.5 us
  matrix products: 42.3 us -> 0 us
  starting transfers between devices: 3.55 us -> 44.8 us
  between operations: 13.9 us -> 0.29 us
  other arithmetic: 10.5 us -> 0 us
  local copies, waits for them, and re-layouts: 11.9 us -> 2.36 us
    all_gather x3 -> x0, waiting for transfers between devices: 273 us -> none  [the longest x1 111 us: on_device(): lax.all_gather(out_weight, 'seq', axis=1, tiled=True)]
    ppermute x0 -> x28, waiting for transfers between devices: none -> 101 us  [the longest x7 45.3 us: ring_step(): return lax.ppermute(value, 'seq', pairs)]
    reduce_scatter x1 -> x0, waiting for transfers between devices: 92.7 us -> none  [on_device(): lax.psum_scatter(partial_value, 'pool', scatter_dimension=0, tiled=True)]
    pallas_call x0 -> x19, Pallas kernels: none -> 46.5 us  [the longest x15 24.7 us: call(): pl.pallas_call(body, name=name, out_shape=out_shape, in_specs=[SMEM if a....]
    ppermute x0 -> x28, starting transfers between devices: none -> 44.8 us  [the longest x7 18.1 us: ring_step(): return lax.ppermute(value, 'seq', pairs)]
    dot_general x6 -> x0, matrix products: 42.3 us -> none  [the longest x1 14.6 us: on_device(): jnp.dot(mixed_list, lax.all_gather(out_weight, 'seq', axis=1, tiled=True)...]
    unnamed x1 -> x0, blocking collectives: 36 us -> none
    all_to_all x1 -> x0, blocking collectives: 16.8 us -> none  [on_device(): lax.all_to_all(outgoing, 'pool', split_axis=0, concat_axis=0, tiled=True)]
  transfers between devices with their start and end apart: 5 -> 28, of which waited for: 4 -> 12; matrix products, arithmetic and copies ran while one was open for 7% -> 0% of each run, Pallas kernels for 0% -> 19%
where the time goes in v3:
time: 195 us
  waiting for transfers between devices  101 us (52%)
  Pallas kernels  46.5 us (24%)
  starting transfers between devices  44.8 us (23%)
  local copies, waits for them, and re-layouts  2.36 us (1%)
    ppermute x7, waiting for transfers between devices, ring_step(): return lax.ppermute(value, 'seq', pairs)  45.3 us
    ppermute x3, waiting for transfers between devices, seq_up(): lax.ppermute(value, 'seq', [(j, j + step) for j in range(seq_count - step)])  26.6 us
    pallas_call x15, Pallas kernels, call(): pl.pallas_call(body, name=name, out_shape=out_shape, in_specs=[SMEM if a....  24.7 us
    ppermute x7, starting transfers between devices, ring_step(): return lax.ppermute(value, 'seq', pairs)  18.1 us
    ppermute x11, waiting for transfers between devices, seq_xor(): return lax.ppermute(value, 'seq', [(j, j ^ bits) for j in range(seq_count)])  14.8 us
    ppermute x7, waiting for transfers between devices, pool_shift(): lax.ppermute(value, 'pool', [(i, (i + by) % pool_count) for i in range(po...  14.2 us
    pallas_call x2, Pallas kernels, inner_part(): pl.pallas_call(inner_kernel, name='inner', grid=(count,), out_shape=shape...  10.6 us
    ppermute x3, starting transfers between devices, seq_up(): lax.ppermute(value, 'seq', [(j, j + step) for j in range(seq_count - step)])  10.5 us
  transfers between devices with their start and end apart: 28, of which 12 were waited for; matrix products, arithmetic and copies ran while one was open for 0% of the time, Pallas kernels for 19%

profile of v3, /device:TPU:0, one launch (start us, length us, event | category | flops | bytes accessed | tf_op | source)
XLA Modules:
  0.0 194.9 jit_solution(5321488549814619503)
XLA Ops:
  0.0 0.5 collective-permute-start.1
  0.5 1.2 copy-done
  1.7 1.0 copy-done.1
  2.7 0.1 pack.1.refs_2_
  2.8 0.1 collective-permute-start.8
  3.0 3.0 %collective-permute-start.7 = (bf16[3072,256]{1,0:T(8,128)(2,1)S(1)}, bf16[3072,256]{1,0:T(8,128)(2,1)S(1)}, u32[]{:S(2)}, u32[]{:S(2)}) collective-permute-start(bf16[3072,256]{1,0:T(8,128)(2,1)S(1)} %pack.1.refs_2_), channel_id=1, source_target_pairs={{0,8},{2,6},{8,16},{10,2},{16,24},{18,10},{24,28},{26,18},{28,20},... | collective-permute-start | bytes 4718600 | tf_op jit(solution)/shard_map/ppermute | solution.py:82
  6.0 1.5 collective-permute-start
  7.5 0.1 stack.47.meta
  7.6 5.8 %update.1 = (f32[4,4,512]{2,1,0:T(4,128)S(1)}, bf16[4,144,128]{2,1,0:T(8,128)(2,1)S(1)}, bf16[4,144,128]{2,1,0:T(8,128)(2,1)S(1)}, bf16[4,144,128]{2,1,0:T(8,128)(2,1)S(1)}, bf16[4,144,128]{2,1,0:T(8,128)(2,1)S(1)}) custom-call(s32[11]{0:T(128)S(1)} %stack.47.meta, bf16[512,2048]{1,0:T(8,128)(2,1)} %key.5, bf16[512,2048]{1,0:T(8,128)(2,1)} %value.5, ...), custom_call_target="tpu_custom_call" | custom-call | flops 1 | bytes 1 | tf_op jit(solution)/shard_map/update/pallas_call | solution.py:424
  13.4 0.0 collective-permute-done.1.refs_1_
  13.4 0.1 collective-permute-start.2
  13.5 1.0 collective-permute-start.3
  14.5 0.8 collective-permute-start.4
  15.4 5.3 %inner.2.refs_0_ = f32[512,1024]{1,0:T(8,128)S(1)} custom-call(bf16[512,2048]{1,0:T(8,128)(2,1)} %query.4, bf16[512,2048]{1,0:T(8,128)(2,1)} %key.5, bf16[512,2048]{1,0:T(8,128)(2,1)} %value.5, f32[4,4,512]{2,1,0:T(4,128)S(1)} %get-tuple-element.70.cumul.refs_2_), custom_call_target="tpu_custom_call" | custom-call | flops 1 | bytes 1 | tf_op jit(solution)/shard_map/inner/pallas_call | solution.py:350
  20.7 0.0 collective-permute-done.2.refs_1_
  20.7 8.4 %collective-permute-done.3.refs_2_ = bf16[4,144,128]{2,1,0:T(8,128)(2,1)S(1)} collective-permute-done((bf16[4,144,128]{2,1,0:T(8,128)(2,1)S(1)}, bf16[4,144,128]{2,1,0:T(8,128)(2,1)S(1)}, u32[]{:S(2)}, u32[]{:S(2)}) %collective-permute-start.3) | collective-permute-done | bytes 147488 | tf_op jit(solution)/shard_map/ppermute | solution.py:56
  29.1 0.7 plane_state.1
  29.8 1.3 collective-permute-start.5
  31.1 0.1 collective-permute-start.9
  31.2 3.5 %collective-permute-done.5.refs_4_ = bf16[4,144,128]{2,1,0:T(8,128)(2,1)S(1)} collective-permute-done((bf16[4,144,128]{2,1,0:T(8,128)(2,1)S(1)}, bf16[4,144,128]{2,1,0:T(8,128)(2,1)S(1)}, u32[]{:S(2)}, u32[]{:S(2)}) %collective-permute-start.5) | collective-permute-done | bytes 147488 | tf_op jit(solution)/shard_map/ppermute | solution.py:61
  34.6 3.0 %collective-permute-start.13 = (bf16[3072,256]{1,0:T(8,128)(2,1)S(1)}, bf16[3072,256]{1,0:T(8,128)(2,1)S(1)}, u32[]{:S(2)}, u32[]{:S(2)}) collective-permute-start(bf16[3072,256]{1,0:T(8,128)(2,1)S(1)} %collective-permute-done.7.refs_1_), channel_id=1, source_target_pairs={{0,8},{2,6},{8,16},{10,2},{16,24},{18,10},{24,28},{26,18},{28,20},... | collective-permute-start | bytes 4718600 | tf_op jit(solution)/shard_map/ppermute | solution.py:82
  37.7 6.4 %collective-permute-start.6 = (bf16[4,144,128]{2,1,0:T(8,128)(2,1)S(1)}, bf16[4,144,128]{2,1,0:T(8,128)(2,1)S(1)}, u32[]{:S(2)}, u32[]{:S(2)}) collective-permute-start(bf16[4,144,128]{2,1,0:T(8,128)(2,1)S(1)} %plane_state.1), channel_id=1, source_target_pairs={{0,16},{2,18},{4,20},{6,22},{8,24},{10,26},{12,28},{14,30},{1,17},... | collective-permute-start | bytes 442376 | tf_op jit(solution)/shard_map/ppermute | solution.py:61
  44.1 2.8 %collective-permute-start.10 = (bf16[4,144,128]{2,1,0:T(8,128)(2,1)S(1)}, bf16[4,144,128]{2,1,0:T(8,128)(2,1)S(1)}, u32[]{:S(2)}, u32[]{:S(2)}) collective-permute-start(bf16[4,144,128]{2,1,0:T(8,128)(2,1)S(1)} %plane_state.1), channel_id=1, source_target_pairs={{0,24},{2,26},{4,28},{6,30},{1,25},{3,27},{5,29},{7,31}} | collective-permute-start | bytes 442376 | tf_op jit(solution)/shard_map/ppermute | solution.py:61
  46.9 5.3 %inner.3.refs_1_ = f32[512,1024]{1,0:T(8,128)S(1)} custom-call(bf16[512,2048]{1,0:T(8,128)(2,1)} %query.4, bf16[512,2048]{1,0:T(8,128)(2,1)} %key.5, bf16[512,2048]{1,0:T(8,128)(2,1)} %value.5, f32[4,4,512]{2,1,0:T(4,128)S(1)} %get-tuple-element.70.cumul.refs_2_), custom_call_target="tpu_custom_call" | custom-call | flops 1 | bytes 1 | tf_op jit(solution)/shard_map/inner/pallas_call | solution.py:350
  52.2 21.6 %collective-permute-done.6.refs_5_ = bf16[4,144,128]{2,1,0:T(8,128)(2,1)S(1)} collective-permute-done((bf16[4,144,128]{2,1,0:T(8,128)(2,1)S(1)}, bf16[4,144,128]{2,1,0:T(8,128)(2,1)S(1)}, u32[]{:S(2)}, u32[]{:S(2)}) %collective-permute-start.6) | collective-permute-done | bytes 147488 | tf_op jit(solution)/shard_map/ppermute | solution.py:61
  73.8 1.6 collective-permute-done.10.refs_6_
  75.4 0.8 entering_state.1
  76.2 0.1 collective-permute-start.12
  76.3 0.1 collective-permute-start.11
  76.4 2.0 %collective-permute-start.14 = (bf16[4,128,128]{2,1,0:T(8,128)(2,1)S(1)}, bf16[4,128,128]{2,1,0:T(8,128)(2,1)S(1)}, u32[]{:S(2)}, u32[]{:S(2)}) collective-permute-start(bf16[4,128,128]{2,1,0:T(8,128)(2,1)S(1)} %get-tuple-element.85), channel_id=1, source_target_pairs={{0,6},{2,4},{4,2},{6,0},{8,14},{10,12},{12,10},{14,8},{16,22},{18,... | collective-permute-start | bytes 393224 | tf_op jit(solution)/shard_map/ppermute | solution.py:56
  78.4 4.1 %collective-permute-done.12.refs_5_ = bf16[4,128,128]{2,1,0:T(8,128)(2,1)S(1)} collective-permute-done((bf16[4,128,128]{2,1,0:T(8,128)(2,1)S(1)}, bf16[4,128,128]{2,1,0:T(8,128)(2,1)S(1)}, u32[]{:S(2)}, u32[]{:S(2)}) %collective-permute-start.12) | collective-permute-done | bytes 131104 | tf_op jit(solution)/shard_map/ppermute | solution.py:56
  82.5 5.4 %mixed.1.refs_0_ = bf16[2,256,2048]{2,1,0:T(8,128)(2,1)S(1)} custom-call(s32[11]{0:T(128)S(1)} %stack.47.meta, bf16[512,2048]{1,0:T(8,128)(2,1)} %query.4, f32[512,1024]{1,0:T(8,128)S(1)} %inner.2.refs_0_, f32[512,1024]{1,0:T(8,128)S(1)} %inner.3.refs_1_, f32[4,4,512]{2,1,0:T(4,128)S(1)} %get-tuple-element.70.cumul.refs_2_, ...), custom_call_target="tpu_custom_call" | custom-call | flops 1 | bytes 1 | tf_op jit(solution)/shard_map/mixed/pallas_call | solution.py:468
  87.8 1.3 collective-permute-start.15
  89.1 7.0 %collective-permute-start.16 = (bf16[3072,256]{1,0:T(8,128)(2,1)S(1)}, bf16[3072,256]{1,0:T(8,128)(2,1)S(1)}, u32[]{:S(2)}, u32[]{:S(2)}) collective-permute-start(bf16[3072,256]{1,0:T(8,128)(2,1)S(1)} %collective-permute-done.9.refs_2_), channel_id=1, source_target_pairs={{0,8},{2,6},{8,16},{10,2},{16,24},{18,10},{24,28},{26,18},{28,20},... | collective-permute-start | bytes 4718600 | tf_op jit(solution)/shard_map/ppermute | solution.py:82
  96.1 0.0 collective-permute-start.18
  96.1 1.3 project.5
  97.4 1.6 collective-permute-start.17
  99.0 2.4 %project.6 = (bf16[512,1024]{1,0:T(8,128)(2,1)S(1)}, f32[512,512]{1,0:T(8,128)S(1)}, bf16[512,512]{1,0:T(8,128)(2,1)S(1)}) custom-call(bf16[2,512,2048]{2,1,0:T(8,128)(2,1)S(1)} %get-tuple-element.109.refs_0_, bf16[3072,256]{1,0:T(8,128)(2,1)S(1)} %collective-permute-done.7.refs_1_, bf16[3072,256]{1,0:T(8,128)(2,1)S(1)} %collective-permute-done.9.refs_2_), custom_call_target="tpu_custom_call" | custom-call | flops 1 | bytes 1 | tf_op jit(solution)/shard_map/project/pallas_call | solution.py:28
  101.4 12.6 %collective-permute-done.16.refs_2_ = bf16[3072,256]{1,0:T(8,128)(2,1)S(1)} collective-permute-done((bf16[3072,256]{1,0:T(8,128)(2,1)S(1)}, bf16[3072,256]{1,0:T(8,128)(2,1)S(1)}, u32[]{:S(2)}, u32[]{:S(2)}) %collective-permute-start.16) | collective-permute-done | bytes 1572896 | tf_op jit(solution)/shard_map/ppermute | solution.py:82
  114.0 2.5 %collective-permute-start.19 = (bf16[3072,256]{1,0:T(8,128)(2,1)S(1)}, bf16[3072,256]{1,0:T(8,128)(2,1)S(1)}, u32[]{:S(2)}, u32[]{:S(2)}) collective-permute-start(bf16[3072,256]{1,0:T(8,128)(2,1)S(1)} %collective-permute-done.16.refs_2_), channel_id=1, source_target_pairs={{0,8},{2,6},{8,16},{10,2},{16,24},{18,10},{24,28},{26,18},{28,20},... | collective-permute-start | bytes 4718600 | tf_op jit(solution)/shard_map/ppermute | solution.py:82
  116.5 2.4 %project.7 = (bf16[512,1024]{1,0:T(8,128)(2,1)S(1)}, f32[512,512]{1,0:T(8,128)S(1)}, bf16[512,512]{1,0:T(8,128)(2,1)S(1)}) custom-call(bf16[2,512,2048]{2,1,0:T(8,128)(2,1)S(1)} %get-tuple-element.109.refs_0_, bf16[3072,256]{1,0:T(8,128)(2,1)S(1)} %collective-permute-done.13.refs_1_, bf16[3072,256]{1,0:T(8,128)(2,1)S(1)} %collective-permute-done.16.refs_2_), custom_call_target="tpu_custom_call" | custom-call | flops 1 | bytes 1 | tf_op jit(solution)/shard_map/project/pallas_call | solution.py:28
  118.9 2.0 %cache.5 = (f32[256,1024]{1,0:T(8,128)S(1)}, f32[256,1024]{1,0:T(8,128)S(1)}, f32[256,128]{1,0:T(8,128)S(1)}, f32[256,128]{1,0:T(8,128)S(1)}) custom-call(s32[11]{0:T(128)S(1)} %stack.47.meta, f32[512,256]{1,0:T(8,128)S(1)} %get-tuple-element.93.mine, bf16[256,4096]{1,0:T(8,128)(2,1)} %refs_0_.10, bf16[256,4096]{1,0:T(8,128)(2,1)} %collective-permute-done.1.refs_1_, ...), custom_call_target="tpu_custom_call" | custom-call | flops 1 | bytes 1 | tf_op jit(solution)/shard_map/cache/pallas_call | solution.py:28
  120.9 9.9 %collective-permute-done.18.refs_1_ = bf16[3072,256]{1,0:T(8,128)(2,1)S(1)} collective-permute-done((bf16[3072,256]{1,0:T(8,128)(2,1)S(1)}, bf16[3072,256]{1,0:T(8,128)(2,1)S(1)}, u32[]{:S(2)}, u32[]{:S(2)}) %collective-permute-start.18) | collective-permute-done | bytes 1572896 | tf_op jit(solution)/shard_map/ppermute | solution.py:82
  130.8 2.5 %collective-permute-start.21 = (bf16[3072,256]{1,0:T(8,128)(2,1)S(1)}, bf16[3072,256]{1,0:T(8,128)(2,1)S(1)}, u32[]{:S(2)}, u32[]{:S(2)}) collective-permute-start(bf16[3072,256]{1,0:T(8,128)(2,1)S(1)} %collective-permute-done.18.refs_1_), channel_id=1, source_target_pairs={{0,8},{2,6},{8,16},{10,2},{16,24},{18,10},{24,28},{26,18},{28,20},... | collective-permute-start | bytes 4718600 | tf_op jit(solution)/shard_map/ppermute | solution.py:82
  133.3 1.5 collective-permute-start.20
  134.8 0.5 collective-permute-start.22
  135.3 12.3 %collective-permute-done.19.refs_2_ = bf16[3072,256]{1,0:T(8,128)(2,1)S(1)} collective-permute-done((bf16[3072,256]{1,0:T(8,128)(2,1)S(1)}, bf16[3072,256]{1,0:T(8,128)(2,1)S(1)}, u32[]{:S(2)}, u32[]{:S(2)}) %collective-permute-start.19) | collective-permute-done | bytes 1572896 | tf_op jit(solution)/shard_map/ppermute | solution.py:82
  147.7 2.4 %project.8 = (bf16[512,1024]{1,0:T(8,128)(2,1)S(1)}, f32[512,512]{1,0:T(8,128)S(1)}, bf16[512,512]{1,0:T(8,128)(2,1)S(1)}) custom-call(bf16[2,512,2048]{2,1,0:T(8,128)(2,1)S(1)} %get-tuple-element.109.refs_0_, bf16[3072,256]{1,0:T(8,128)(2,1)S(1)} %collective-permute-done.18.refs_1_, bf16[3072,256]{1,0:T(8,128)(2,1)S(1)} %collective-permute-done.19.refs_2_), custom_call_target="tpu_custom_call" | custom-call | flops 1 | bytes 1 | tf_op jit(solution)/shard_map/project/pallas_call | solution.py:28
  150.1 1.6 collective-permute-start.23
  151.7 2.5 %cache.6 = (f32[256,1024]{1,0:T(8,128)S(1)}, f32[256,1024]{1,0:T(8,128)S(1)}, f32[256,128]{1,0:T(8,128)S(1)}, f32[256,128]{1,0:T(8,128)S(1)}) custom-call(s32[11]{0:T(128)S(1)} %stack.47.meta, f32[512,512]{1,0:T(8,128)S(1)} %get-tuple-element.101.mine, bf16[256,4096]{1,0:T(8,128)(2,1)} %refs_0_.10, bf16[256,4096]{1,0:T(8,128)(2,1)} %collective-permute-done.1.refs_1_, ...), custom_call_target="tpu_custom_call" | custom-call | flops 1 | bytes 1 | tf_op jit(solution)/shard_map/cache/pallas_call | solution.py:28
  154.1 10.4 %collective-permute-done.21.refs_1_ = bf16[3072,256]{1,0:T(8,128)(2,1)S(1)} collective-permute-done((bf16[3072,256]{1,0:T(8,128)(2,1)S(1)}, bf16[3072,256]{1,0:T(8,128)(2,1)S(1)}, u32[]{:S(2)}, u32[]{:S(2)}) %collective-permute-start.21) | collective-permute-done | bytes 1572896 | tf_op jit(solution)/shard_map/ppermute | solution.py:82
  164.5 1.3 project.9
  165.8 1.6 collective-permute-start.24
  167.4 2.5 %cache.7 = (f32[256,1024]{1,0:T(8,128)S(1)}, f32[256,1024]{1,0:T(8,128)S(1)}, f32[256,128]{1,0:T(8,128)S(1)}, f32[256,128]{1,0:T(8,128)S(1)}) custom-call(s32[11]{0:T(128)S(1)} %stack.47.meta, f32[512,512]{1,0:T(8,128)S(1)} %get-tuple-element.111.mine, bf16[256,4096]{1,0:T(8,128)(2,1)} %refs_0_.10, bf16[256,4096]{1,0:T(8,128)(2,1)} %collective-permute-done.1.refs_1_, ...), custom_call_target="tpu_custom_call" | custom-call | flops 1 | bytes 1 | tf_op jit(solution)/shard_map/cache/pallas_call | solution.py:28
  169.9 2.5 %cache.8 = (f32[256,1024]{1,0:T(8,128)S(1)}, f32[256,1024]{1,0:T(8,128)S(1)}, f32[256,128]{1,0:T(8,128)S(1)}, f32[256,128]{1,0:T(8,128)S(1)}) custom-call(s32[11]{0:T(128)S(1)} %stack.47.meta, f32[512,512]{1,0:T(8,128)S(1)} %get-tuple-element.118.mine, bf16[256,4096]{1,0:T(8,128)(2,1)} %refs_0_.10, bf16[256,4096]{1,0:T(8,128)(2,1)} %collective-permute-done.1.refs_1_, ...), custom_call_target="tpu_custom_call" | custom-call | flops 1 | bytes 1 | tf_op jit(solution)/shard_map/cache/pallas_call | solution.py:28
  172.4 1.7 collective-permute-done.24.refs_4_
  174.0 2.0 %cache.9 = (f32[256,1024]{1,0:T(8,128)S(1)}, f32[256,1024]{1,0:T(8,128)S(1)}, f32[256,128]{1,0:T(8,128)S(1)}, f32[256,128]{1,0:T(8,128)S(1)}) custom-call(s32[11]{0:T(128)S(1)} %stack.47.meta, f32[512,256]{1,0:T(8,128)S(1)} %get-tuple-element.125.mine, bf16[256,4096]{1,0:T(8,128)(2,1)} %refs_0_.10, bf16[256,4096]{1,0:T(8,128)(2,1)} %collective-permute-done.1.refs_1_, ...), custom_call_target="tpu_custom_call" | custom-call | flops 1 | bytes 1 | tf_op jit(solution)/shard_map/cache/pallas_call | solution.py:28
  176.1 0.1 collective-permute-start.25
  176.1 0.5 collective-permute-start.26
  176.6 2.3 %collective-permute-done.26.square_in = f32[256,128]{1,0:T(8,128)S(1)} collective-permute-done((f32[256,128]{1,0:T(8,128)S(1)}, f32[256,128]{1,0:T(8,128)S(1)}, u32[]{:S(2)}, u32[]{:S(2)}) %collective-permute-start.26) | collective-permute-done | bytes 131104 | tf_op jit(solution)/shard_map/ppermute | solution.py:56
  179.0 0.2 finish.1.refs_2_
  179.2 1.6 collective-permute-start.27
  180.7 12.5 %collective-permute-done.27.refs_3_ = bf16[256,1024]{1,0:T(8,128)(2,1)S(1)} collective-permute-done((bf16[256,1024]{1,0:T(8,128)(2,1)S(1)}, bf16[256,1024]{1,0:T(8,128)(2,1)S(1)}, u32[]{:S(2)}, u32[]{:S(2)}) %collective-permute-start.27) | collective-permute-done | bytes 524320 | tf_op jit(solution)/shard_map/ppermute | solution.py:65
  193.2 1.7 place.1
  (22 shorter events, 0.1 us)
Async XLA Ops:
  0.0 13.4 %collective-permute-start.1 = (bf16[256,4096]{1,0:T(8,128)(2,1)}, bf16[256,4096]{1,0:T(8,128)(2,1)}, u32[]{:S(2)}, u32[]{:S(2)}) collective-permute-start(bf16[256,4096]{1,0:T(8,128)(2,1)} %refs_0_.10), channel_id=1, source_target_pairs={{0,2},{2,0},{4,6},{6,4},{8,10},{10,8},{12,14},{14,12},{16,18},{18,... | collective-permute-start | bytes 6291464 | tf_op jit(solution)/shard_map/ppermute | solution.py:56
  0.5 1.2 copy-start
  1.7 1.0 copy-start.1
  2.7 3.3 %copy-start.4 = (s32[2,2]{1,0:T(2,128)S(1)}, s32[2,2]{1,0:T(2,128)}, u32[]{:S(2)}) copy-start(s32[2,2]{1,0:T(2,128)} %refs_0_.11) | copy-start | bytes 52
  2.7 4.8 %copy-start.3 = (f32[16,512]{1,0:T(8,128)S(1)}, f32[16,512]{1,0:T(8,128)}, u32[]{:S(2)}) copy-start(f32[16,512]{1,0:T(8,128)} %decay.1) | copy-start | bytes 98308
  2.8 28.3 %collective-permute-start.8 = (bf16[3072,256]{1,0:T(8,128)(2,1)S(1)}, bf16[3072,256]{1,0:T(8,128)(2,1)}, u32[]{:S(2)}, u32[]{:S(2)}) collective-permute-start(bf16[3072,256]{1,0:T(8,128)(2,1)S(1)} %pack.1.refs_2_), channel_id=1, source_target_pairs={{0,2},{2,0},{4,6},{6,4},{8,10},{10,8},{12,14},{14,12},{16,18},{18,... | collective-permute-start | bytes 4718600 | tf_op jit(solution)/shard_map/ppermute | solution.py:56
  3.0 28.2 %collective-permute-start.7 = (bf16[3072,256]{1,0:T(8,128)(2,1)S(1)}, bf16[3072,256]{1,0:T(8,128)(2,1)S(1)}, u32[]{:S(2)}, u32[]{:S(2)}) collective-permute-start(bf16[3072,256]{1,0:T(8,128)(2,1)S(1)} %pack.1.refs_2_), channel_id=1, source_target_pairs={{0,8},{2,6},{8,16},{10,2},{16,24},{18,10},{24,28},{26,18},{28,20},... | collective-permute-start | bytes 4718600 | tf_op jit(solution)/shard_map/ppermute | solution.py:82
  6.0 7.4 %collective-permute-start = (s32[2,2]{1,0:T(2,128)S(1)}, s32[2,2]{1,0:T(2,128)S(1)}, u32[]{:S(2)}, u32[]{:S(2)}) collective-permute-start(s32[2,2]{1,0:T(2,128)S(1)} %copy-done.4), channel_id=1, source_target_pairs={{0,1},{1,0},{2,3},{3,2},{4,5},{5,4},{6,7},{7,6},{8,9},{9,8},{10,11... | collective-permute-start | bytes 56 | tf_op jit(solution)/shard_map/ppermute | solution.py:65
  13.4 7.2 %collective-permute-start.2 = (bf16[4,144,128]{2,1,0:T(8,128)(2,1)S(1)}, bf16[4,144,128]{2,1,0:T(8,128)(2,1)S(1)}, u32[]{:S(2)}, u32[]{:S(2)}) collective-permute-start(bf16[4,144,128]{2,1,0:T(8,128)(2,1)S(1)} %get-tuple-element.73), channel_id=1, source_target_pairs={{0,2},{2,0},{4,6},{6,4},{8,10},{10,8},{12,14},{14,12},{16,18},{18,... | collective-permute-start | bytes 442376 | tf_op jit(solution)/shard_map/ppermute | solution.py:56
  13.5 15.5 %collective-permute-start.3 = (bf16[4,144,128]{2,1,0:T(8,128)(2,1)S(1)}, bf16[4,144,128]{2,1,0:T(8,128)(2,1)S(1)}, u32[]{:S(2)}, u32[]{:S(2)}) collective-permute-start(bf16[4,144,128]{2,1,0:T(8,128)(2,1)S(1)} %get-tuple-element.75), channel_id=1, source_target_pairs={{0,4},{2,6},{4,0},{6,2},{8,12},{10,14},{12,8},{14,10},{16,20},{18,... | collective-permute-start | bytes 442376 | tf_op jit(solution)/shard_map/ppermute | solution.py:56
  14.5 14.5 %collective-permute-start.4 = (bf16[4,144,128]{2,1,0:T(8,128)(2,1)S(1)}, bf16[4,144,128]{2,1,0:T(8,128)(2,1)S(1)}, u32[]{:S(2)}, u32[]{:S(2)}) collective-permute-start(bf16[4,144,128]{2,1,0:T(8,128)(2,1)S(1)} %get-tuple-element.76), channel_id=1, source_target_pairs={{0,6},{2,4},{4,2},{6,0},{8,14},{10,12},{12,10},{14,8},{16,22},{18,... | collective-permute-start | bytes 442376 | tf_op jit(solution)/shard_map/ppermute | solution.py:56
  29.8 4.9 %collective-permute-start.5 = (bf16[4,144,128]{2,1,0:T(8,128)(2,1)S(1)}, bf16[4,144,128]{2,1,0:T(8,128)(2,1)S(1)}, u32[]{:S(2)}, u32[]{:S(2)}) collective-permute-start(bf16[4,144,128]{2,1,0:T(8,128)(2,1)S(1)} %plane_state.1), channel_id=1, source_target_pairs={{0,8},{2,10},{4,12},{6,14},{8,16},{10,18},{12,20},{14,22},{16,24},... | collective-permute-start | bytes 442376 | tf_op jit(solution)/shard_map/ppermute | solution.py:61
  31.1 42.7 %collective-permute-start.9 = (bf16[3072,256]{1,0:T(8,128)(2,1)}, bf16[3072,256]{1,0:T(8,128)(2,1)S(1)}, u32[]{:S(2)}, u32[]{:S(2)}) collective-permute-start(bf16[3072,256]{1,0:T(8,128)(2,1)} %collective-permute-done.8), channel_id=1, source_target_pairs={{0,8},{2,6},{8,16},{10,2},{16,24},{18,10},{24,28},{26,18},{28,20},... | collective-permute-start | bytes 4718600 | tf_op jit(solution)/shard_map/ppermute | solution.py:82
  34.6 47.8 %collective-permute-start.13 = (bf16[3072,256]{1,0:T(8,128)(2,1)S(1)}, bf16[3072,256]{1,0:T(8,128)(2,1)S(1)}, u32[]{:S(2)}, u32[]{:S(2)}) collective-permute-start(bf16[3072,256]{1,0:T(8,128)(2,1)S(1)} %collective-permute-done.7.refs_1_), channel_id=1, source_target_pairs={{0,8},{2,6},{8,16},{10,2},{16,24},{18,10},{24,28},{26,18},{28,20},... | collective-permute-start | bytes 4718600 | tf_op jit(solution)/shard_map/ppermute | solution.py:82
  37.7 36.1 %collective-permute-start.6 = (bf16[4,144,128]{2,1,0:T(8,128)(2,1)S(1)}, bf16[4,144,128]{2,1,0:T(8,128)(2,1)S(1)}, u32[]{:S(2)}, u32[]{:S(2)}) collective-permute-start(bf16[4,144,128]{2,1,0:T(8,128)(2,1)S(1)} %plane_state.1), channel_id=1, source_target_pairs={{0,16},{2,18},{4,20},{6,22},{8,24},{10,26},{12,28},{14,30},{1,17},... | collective-permute-start | bytes 442376 | tf_op jit(solution)/shard_map/ppermute | solution.py:61
  44.1 31.3 %collective-permute-start.10 = (bf16[4,144,128]{2,1,0:T(8,128)(2,1)S(1)}, bf16[4,144,128]{2,1,0:T(8,128)(2,1)S(1)}, u32[]{:S(2)}, u32[]{:S(2)}) collective-permute-start(bf16[4,144,128]{2,1,0:T(8,128)(2,1)S(1)} %plane_state.1), channel_id=1, source_target_pairs={{0,24},{2,26},{4,28},{6,30},{1,25},{3,27},{5,29},{7,31}} | collective-permute-start | bytes 442376 | tf_op jit(solution)/shard_map/ppermute | solution.py:61
  76.2 6.3 %collective-permute-start.12 = (bf16[4,128,128]{2,1,0:T(8,128)(2,1)S(1)}, bf16[4,128,128]{2,1,0:T(8,128)(2,1)S(1)}, u32[]{:S(2)}, u32[]{:S(2)}) collective-permute-start(bf16[4,128,128]{2,1,0:T(8,128)(2,1)S(1)} %get-tuple-element.82), channel_id=1, source_target_pairs={{0,4},{2,6},{4,0},{6,2},{8,12},{10,14},{12,8},{14,10},{16,20},{18,... | collective-permute-start | bytes 393224 | tf_op jit(solution)/shard_map/ppermute | solution.py:56
  76.3 6.2 %collective-permute-start.11 = (bf16[4,128,128]{2,1,0:T(8,128)(2,1)S(1)}, bf16[4,128,128]{2,1,0:T(8,128)(2,1)S(1)}, u32[]{:S(2)}, u32[]{:S(2)}) collective-permute-start(bf16[4,128,128]{2,1,0:T(8,128)(2,1)S(1)} %get-tuple-element.81), channel_id=1, source_target_pairs={{0,2},{2,0},{4,6},{6,4},{8,10},{10,8},{12,14},{14,12},{16,18},{18,... | collective-permute-start | bytes 393224 | tf_op jit(solution)/shard_map/ppermute | solution.py:56
  76.4 6.1 %collective-permute-start.14 = (bf16[4,128,128]{2,1,0:T(8,128)(2,1)S(1)}, bf16[4,128,128]{2,1,0:T(8,128)(2,1)S(1)}, u32[]{:S(2)}, u32[]{:S(2)}) collective-permute-start(bf16[4,128,128]{2,1,0:T(8,128)(2,1)S(1)} %get-tuple-element.85), channel_id=1, source_target_pairs={{0,6},{2,4},{4,2},{6,0},{8,14},{10,12},{12,10},{14,8},{16,22},{18,... | collective-permute-start | bytes 393224 | tf_op jit(solution)/shard_map/ppermute | solution.py:56
  87.8 8.3 %collective-permute-start.15 = (bf16[2,256,2048]{2,1,0:T(8,128)(2,1)S(1)}, bf16[2,256,2048]{2,1,0:T(8,128)(2,1)S(1)}, u32[]{:S(2)}, u32[]{:S(2)}) collective-permute-start(bf16[2,256,2048]{2,1,0:T(8,128)(2,1)S(1)} %mixed.1.refs_0_), channel_id=1, source_target_pairs={{0,2},{2,0},{4,6},{6,4},{8,10},{10,8},{12,14},{14,12},{16,18},{18,... | collective-permute-start | bytes 6291464 | tf_op jit(solution)/shard_map/ppermute | solution.py:56
  89.1 24.9 %collective-permute-start.16 = (bf16[3072,256]{1,0:T(8,128)(2,1)S(1)}, bf16[3072,256]{1,0:T(8,128)(2,1)S(1)}, u32[]{:S(2)}, u32[]{:S(2)}) collective-permute-start(bf16[3072,256]{1,0:T(8,128)(2,1)S(1)} %collective-permute-done.9.refs_2_), channel_id=1, source_target_pairs={{0,8},{2,6},{8,16},{10,2},{16,24},{18,10},{24,28},{26,18},{28,20},... | collective-permute-start | bytes 4718600 | tf_op jit(solution)/shard_map/ppermute | solution.py:82
  96.1 34.8 %collective-permute-start.18 = (bf16[3072,256]{1,0:T(8,128)(2,1)S(1)}, bf16[3072,256]{1,0:T(8,128)(2,1)S(1)}, u32[]{:S(2)}, u32[]{:S(2)}) collective-permute-start(bf16[3072,256]{1,0:T(8,128)(2,1)S(1)} %collective-permute-done.13.refs_1_), channel_id=1, source_target_pairs={{0,8},{2,6},{8,16},{10,2},{16,24},{18,10},{24,28},{26,18},{28,20},... | collective-permute-start | bytes 4718600 | tf_op jit(solution)/shard_map/ppermute | solution.py:82
  97.4 21.5 %collective-permute-start.17 = (bf16[512,256]{1,0:T(8,128)(2,1)S(1)}, bf16[512,256]{1,0:T(8,128)(2,1)S(1)}, u32[]{:S(2)}, u32[]{:S(2)}) collective-permute-start(bf16[512,256]{1,0:T(8,128)(2,1)S(1)} %get-tuple-element.95), channel_id=1, source_target_pairs={{0,1},{1,0},{2,3},{3,2},{4,5},{5,4},{6,7},{7,6},{8,9},{9,8},{10,11... | collective-permute-start | bytes 786440 | tf_op jit(solution)/shard_map/ppermute | solution.py:65
  114.0 4.9 %copy-start.2 = (f32[4096]{0:T(1024)S(1)}, f32[4096]{0:T(1024)}, u32[]{:S(2)}) copy-start(f32[4096]{0:T(1024)} %param.15) | copy-start | bytes 49156
  114.0 33.7 %collective-permute-start.19 = (bf16[3072,256]{1,0:T(8,128)(2,1)S(1)}, bf16[3072,256]{1,0:T(8,128)(2,1)S(1)}, u32[]{:S(2)}, u32[]{:S(2)}) collective-permute-start(bf16[3072,256]{1,0:T(8,128)(2,1)S(1)} %collective-permute-done.16.refs_2_), channel_id=1, source_target_pairs={{0,8},{2,6},{8,16},{10,2},{16,24},{18,10},{24,28},{26,18},{28,20},... | collective-permute-start | bytes 4718600 | tf_op jit(solution)/shard_map/ppermute | solution.py:82
  130.8 33.7 %collective-permute-start.21 = (bf16[3072,256]{1,0:T(8,128)(2,1)S(1)}, bf16[3072,256]{1,0:T(8,128)(2,1)S(1)}, u32[]{:S(2)}, u32[]{:S(2)}) collective-permute-start(bf16[3072,256]{1,0:T(8,128)(2,1)S(1)} %collective-permute-done.18.refs_1_), channel_id=1, source_target_pairs={{0,8},{2,6},{8,16},{10,2},{16,24},{18,10},{24,28},{26,18},{28,20},... | collective-permute-start | bytes 4718600 | tf_op jit(solution)/shard_map/ppermute | solution.py:82
  133.3 18.3 %collective-permute-start.20 = (bf16[512,512]{1,0:T(8,128)(2,1)S(1)}, bf16[512,512]{1,0:T(8,128)(2,1)S(1)}, u32[]{:S(2)}, u32[]{:S(2)}) collective-permute-start(bf16[512,512]{1,0:T(8,128)(2,1)S(1)} %get-tuple-element.103), channel_id=1, source_target_pairs={{0,1},{1,0},{2,3},{3,2},{4,5},{5,4},{6,7},{7,6},{8,9},{9,8},{10,11... | collective-permute-start | bytes 1572872 | tf_op jit(solution)/shard_map/ppermute | solution.py:65
  134.8 32.6 %collective-permute-start.22 = (bf16[512,512]{1,0:T(8,128)(2,1)S(1)}, bf16[512,512]{1,0:T(8,128)(2,1)S(1)}, u32[]{:S(2)}, u32[]{:S(2)}) collective-permute-start(bf16[512,512]{1,0:T(8,128)(2,1)S(1)} %get-tuple-element.113), channel_id=1, source_target_pairs={{0,1},{1,0},{2,3},{3,2},{4,5},{5,4},{6,7},{7,6},{8,9},{9,8},{10,11... | collective-permute-start | bytes 1572872 | tf_op jit(solution)/shard_map/ppermute | solution.py:65
  150.1 19.7 %collective-permute-start.23 = (bf16[512,512]{1,0:T(8,128)(2,1)S(1)}, bf16[512,512]{1,0:T(8,128)(2,1)S(1)}, u32[]{:S(2)}, u32[]{:S(2)}) collective-permute-start(bf16[512,512]{1,0:T(8,128)(2,1)S(1)} %get-tuple-element.120), channel_id=1, source_target_pairs={{0,1},{1,0},{2,3},{3,2},{4,5},{5,4},{6,7},{7,6},{8,9},{9,8},{10,11... | collective-permute-start | bytes 1572872 | tf_op jit(solution)/shard_map/ppermute | solution.py:65
  165.8 8.2 %collective-permute-start.24 = (bf16[512,256]{1,0:T(8,128)(2,1)S(1)}, bf16[512,256]{1,0:T(8,128)(2,1)S(1)}, u32[]{:S(2)}, u32[]{:S(2)}) collective-permute-start(bf16[512,256]{1,0:T(8,128)(2,1)S(1)} %get-tuple-element.127), channel_id=1, source_target_pairs={{0,1},{1,0},{2,3},{3,2},{4,5},{5,4},{6,7},{7,6},{8,9},{9,8},{10,11... | collective-permute-start | bytes 786440 | tf_op jit(solution)/shard_map/ppermute | solution.py:65
  176.1 2.9 %collective-permute-start.25 = (f32[256,1024]{1,0:T(8,128)S(1)}, f32[256,1024]{1,0:T(8,128)S(1)}, u32[]{:S(2)}, u32[]{:S(2)}) collective-permute-start(f32[256,1024]{1,0:T(8,128)S(1)} %get-tuple-element.133), channel_id=1, source_target_pairs={{0,2},{2,0},{4,6},{6,4},{8,10},{10,8},{12,14},{14,12},{16,18},{18,... | collective-permute-start | bytes 3145736 | tf_op jit(solution)/shard_map/ppermute | solution.py:56
  176.1 2.8 %collective-permute-start.26 = (f32[256,128]{1,0:T(8,128)S(1)}, f32[256,128]{1,0:T(8,128)S(1)}, u32[]{:S(2)}, u32[]{:S(2)}) collective-permute-start(f32[256,128]{1,0:T(8,128)S(1)} %get-tuple-element.134), channel_id=1, source_target_pairs={{0,2},{2,0},{4,6},{6,4},{8,10},{10,8},{12,14},{14,12},{16,18},{18,... | collective-permute-start | bytes 393224 | tf_op jit(solution)/shard_map/ppermute | solution.py:56
  179.2 14.0 %collective-permute-start.27 = (bf16[256,1024]{1,0:T(8,128)(2,1)S(1)}, bf16[256,1024]{1,0:T(8,128)(2,1)S(1)}, u32[]{:S(2)}, u32[]{:S(2)}) collective-permute-start(bf16[256,1024]{1,0:T(8,128)(2,1)S(1)} %finish.1.refs_2_), channel_id=1, source_target_pairs={{0,1},{1,0},{2,3},{3,2},{4,5},{5,4},{6,7},{7,6},{8,9},{9,8},{10,11... | collective-permute-start | bytes 1572872 | tf_op jit(solution)/shard_map/ppermute | solution.py:65

commit v4 on v3

--- a/solution.py
+++ b/solution.py
@@ -56,9 +56,33 @@
     return lax.ppermute(value, "seq", [(j, j ^ bits) for j in range(seq_count)])
 
 
-def seq_up(value, seq_count, planes):
-    step = planes * INNER
-    return lax.ppermute(value, "seq", [(j, j + step) for j in range(seq_count - step)])
+def seq_index(plane, row, core):
+    return plane * INNER + row * 2 + core
+
+
+def to_other_row(value, seq_count, first_plane):
+    pairs = []
+    for plane in range(first_plane, seq_count // INNER):
+        for row in range(2):
+            core = row if plane == 0 else 1 - row
+            pairs.append((seq_index(plane, row, core), seq_index(plane, 1 - row, row)))
+    return lax.ppermute(value, "seq", pairs)
+
+
+def to_later_planes(value, seq_count, reach):
+    planes = seq_count // INNER
+    return [
+        lax.ppermute(
+            value,
+            "seq",
+            [
+                (seq_index(plane, row, 1 - row), seq_index(plane + by, row, 1 - row))
+                for plane in range(reach - 1, planes - by, 2 * reach)
+                for row in range(2)
+            ],
+        )
+        for by in range(1, reach + 1)
+    ]
 
 
 def pool_shift(value, pool_count, by):
@@ -98,8 +122,7 @@
     return terms.astype(BF16)
 
 
-def update_kernel(meta, key, value, decay, cumul, *outs):
-    *pieces, held = outs
+def update_kernel(key, value, decay, cumul, out):
     _, share, rows = cumul.shape
     step = pl.program_id(0)
 
@@ -122,14 +145,8 @@
         update = lax.dot_general(
             weighted, value[:, lane], (((0,), (0,)), ((), ())), preferred_element_type=F32
         )
-        spot = step ^ meta[0]
-        held[spot, i, :HD, :] = update.astype(BF16)
-        held[spot, i, HD:, :] = tag_of(lines[i : i + 1, rows - 1 :])
-
-    @pl.when(step == INNER - 1)
-    def _():
-        for r in range(INNER):
-            pieces[r][...] = held[r]
+        out[i, :HD, :] = update.astype(BF16)
+        out[i, HD:, :] = tag_of(lines[i : i + 1, rows - 1 :])
 
 
 def state_of(ref, i):
@@ -140,44 +157,68 @@
     return jnp.sum(ref[i, HD:, :].astype(F32), axis=0, keepdims=True)
 
 
-def stack_in_order(place, got, held):
-    for r in range(INNER):
-        held[r] = got[r][...]
-    return [held.at[place ^ i] for i in range(INNER)]
-
-
-def plane_kernel(meta, *refs):
-    *got, out, held = refs
-    parts = stack_in_order(meta[0], got, held)
+def either(choice, one, two, i):
+    state = jnp.where(choice, state_of(one, i), state_of(two, i))
+    return state, jnp.where(choice, total_of(one, i), total_of(two, i))
+
+
+def chip_kernel(meta, own, other, out):
+    lead = meta[0] % 2 == 0
     for i in range(out.shape[0]):
-        state = jnp.zeros((HD, HD), F32)
-        total = jnp.zeros((1, HD), F32)
-        for part in parts:
-            one = total_of(part, i)
-            state = jnp.exp(one) * state + state_of(part, i)
-            total = total + one
-        out[i, :HD, :] = state.astype(BF16)
-        out[i, HD:, :] = tag_of(total)
-
-
-def entering_kernel(meta, *refs):
-    held, leaving = refs[-2:]
-    outs = refs[-2 - INNER : -2]
-    got = refs[:INNER]
-    earlier = refs[INNER : -2 - INNER]
-    place = meta[0]
-    parts = stack_in_order(place, got, held)
-    for i in range(leaving.shape[1]):
-        state = jnp.zeros((HD, HD), F32)
-        gap = jnp.zeros((1, HD), F32)
-        for plane in earlier:
-            state = state + jnp.exp(gap) * state_of(plane, i)
-            gap = gap + total_of(plane, i)
-        for spot, part in enumerate(parts):
-            leaving[place ^ spot, i] = state.astype(BF16)
-            state = jnp.exp(total_of(part, i)) * state + state_of(part, i)
-    for r in range(INNER):
-        outs[r][...] = leaving[r]
+        state, total = either(lead, own, other, i)
+        after_state, after_total = either(lead, other, own, i)
+        out[i, :HD, :] = (jnp.exp(after_total) * state + after_state).astype(BF16)
+        out[i, HD:, :] = tag_of(total + after_total)
+
+
+def plane_kernel(meta, own, other, out):
+    row = meta[0] // 2
+    for i in range(out.shape[0]):
+        h = row * out.shape[0] + i
+        state, total = either(row == 0, own, other, h)
+        after_state, after_total = either(row == 0, other, own, h)
+        out[i, :HD, :] = (jnp.exp(after_total) * state + after_state).astype(BF16)
+        out[i, HD:, :] = tag_of(total + after_total)
+
+
+def scan_kernel(reach, meta, *refs):
+    received, refs = refs[:reach], refs[reach:]
+    if reach > 1:
+        before, *refs = refs
+    own, *outs = refs
+    upper = meta[1] // reach % 2 == 1
+    by = meta[1] % reach
+    for i in range(own.shape[0]):
+        state, total = state_of(received[0], i), total_of(received[0], i)
+        for n in range(1, reach):
+            state = jnp.where(by == n, state_of(received[n], i), state)
+            total = jnp.where(by == n, total_of(received[n], i), total)
+        state = jnp.where(upper, state, 0.0)
+        total = jnp.where(upper, total, 0.0)
+        if reach > 1:
+            later = total_of(before, i)
+            state = jnp.exp(later) * state + state_of(before, i)
+            total = total + later
+        outs[0][i, :HD, :] = state.astype(BF16)
+        outs[0][i, HD:, :] = tag_of(total)
+        if len(outs) > 1:
+            later = total_of(own, i)
+            outs[1][i, :HD, :] = (jnp.exp(later) * state + state_of(own, i)).astype(BF16)
+            outs[1][i, HD:, :] = tag_of(total + later)
+
+
+def start_kernel(meta, own, other, row_update, prefix, other_prefix, mine, away):
+    row, lead = meta[0] // 2, meta[0] % 2 == 0
+    half = prefix.shape[0]
+    for i in range(mine.shape[0]):
+        here = row == i // half
+        state = jnp.where(here, state_of(prefix, i % half), state_of(other_prefix, i % half))
+        grown = jnp.exp(total_of(row_update, i)) * state + state_of(row_update, i)
+        state = jnp.where(row == 0, state, grown)
+        update, total = either(lead, own, other, i)
+        later = jnp.exp(total) * state + update
+        mine[i] = jnp.where(lead, state, later).astype(BF16)
+        away[i] = jnp.where(lead, later, state).astype(BF16)
 
 
 def inner_kernel(query, key, value, cumul, out):
@@ -211,27 +252,26 @@
 
 
 def mixed_kernel(meta, query, *refs):
-    inners = refs[:2]
-    cumul, *refs = refs[2:]
-    *states, out, held = refs
-    pool_count, rows, _ = out.shape
+    inners = refs[:3]
+    cumul, *refs = refs[3:]
+    own_state, other_state, *outs, held = refs
+    pool_count, rows = len(outs), outs[0].shape[0]
     step = pl.program_id(0)
-    place, me = meta[0], meta[2]
+    gathers = meta[0] // 2 + meta[0] % 2 == 1
+    me = meta[2]
     lines = cumul[0]
     grown = columns(jnp.exp(lines))
     for i in range(lines.shape[0]):
         lane = slice(i * HD, (i + 1) * HD)
-        state = states[0][i]
-        for r in range(1, INNER):
-            state = jnp.where(step ^ place == r, states[r][i], state)
+        state = jnp.where(gathers, own_state[i], other_state[i])
         outer = jnp.dot(query[:, lane], state, preferred_element_type=F32)
         held[:, lane] = outer * grown[:, i : i + 1]
     for n in range(INNER):
 
         @pl.when(step == n)
         def _():
-            part = n % (INNER // 2) * held.shape[1]
-            held[...] = held[...] + inners[n // (INNER // 2)][:, part : part + held.shape[1]]
+            part = (n if n < 2 else 0) * held.shape[1]
+            held[...] = held[...] + inners[max(0, n - 1)][:, part : part + held.shape[1]]
 
     for r in range(pool_count):
         start = pl.multiple_of(lax.rem(me + r, pool_count) * rows, rows)
@@ -239,7 +279,7 @@
             lane = slice(i * HD, (i + 1) * HD)
             retained = held[pl.ds(start, rows), lane]
             mean = jnp.mean(retained * retained, axis=-1, keepdims=True)
-            out[r, :, lane] = (retained * lax.rsqrt(mean + EPS)).astype(BF16)
+            outs[r][:, lane] = (retained * lax.rsqrt(mean + EPS)).astype(BF16)
 
 
 def pack_kernel(weight, kv, out):
@@ -253,12 +293,12 @@
 
 def project_kernel(joins, parts, *refs):
     if joins:
-        own, other = refs[:2]
         both = refs[-1]
-        refs = refs[2:-1]
-        rows = own.shape[1]
-        both[:, :rows, :] = own[...]
-        both[:, rows:, :] = other[...]
+        rows = refs[0].shape[0]
+        for r in range(joins):
+            both[r, :rows, :] = refs[r][...]
+            both[r, rows:, :] = refs[joins + r][...]
+        refs = refs[2 * joins : -1]
     else:
         both = refs[0]
         refs = refs[1:]
@@ -396,7 +436,6 @@
     pages_here = block_table.shape[0]
     slot_count = 2 * pages_here
     chip_rows = 2 * rows_here
-    tagged = (share, HD + TAG, HD)
 
     packed = shape(
         (out_weight.shape[0] + kv_weight.shape[0] * cache_width // width, width), BF16
@@ -417,70 +456,84 @@
         return [come[2 * g - 1], come[2 * g]]
 
     serve(1)
-    tables = [block_table] + [pool_shift(block_table, pool_count, r) for r in range(1, pool_count)]
-    residual_other = seq_xor(residual, seq_count, 1)
-
     by_share = pl.BlockSpec((rows, share * HD), lambda g: (0, g))
-    cumul, *pieces = pl.pallas_call(
+    cumul, update = pl.pallas_call(
         update_kernel,
         name="update",
         grid=(INNER,),
-        out_shape=[shape((INNER, share, rows), F32)] + [shape(tagged, BF16)] * INNER,
-        in_specs=[SMEM, by_share, by_share, pl.BlockSpec((heads, rows), lambda g: (0, 0))],
-        out_specs=[pl.BlockSpec((INNER, share, rows), lambda g: (0, 0, 0))]
-        + [pl.BlockSpec(tagged, lambda g: (0, 0, 0))] * INNER,
-        scratch_shapes=[pltpu.VMEM((INNER, *tagged), BF16)],
+        out_shape=[shape((INNER, share, rows), F32), shape((heads, HD + TAG, HD), BF16)],
+        in_specs=[by_share, by_share, pl.BlockSpec((heads, rows), lambda g: (0, 0))],
+        out_specs=[
+            pl.BlockSpec((INNER, share, rows), lambda g: (0, 0, 0)),
+            pl.BlockSpec((share, HD + TAG, HD), lambda g: (g, 0, 0)),
+        ],
         cost_estimate=LIGHT,
         compiler_params=params(12),
-    )(meta, in_hbm(key_rows), in_hbm(value_rows), log_decay)
-    pieces[1] = after(pieces[1], residual_other, *tables)
-    got = [pieces[0]] + [seq_xor(pieces[r], seq_count, r) for r in range(1, INNER)]
-
+    )(in_hbm(key_rows), in_hbm(value_rows), log_decay)
+    update = after(update, come[0])
+    update_other = seq_xor(update, seq_count, 1)
+    serve(2, update_other)
+    chip = call(
+        chip_kernel, "chip_state", shape(update.shape, BF16), [meta, update, update_other]
+    )
+    chip_other = to_other_row(chip, seq_count, 0)
     inners = [inner_part(0, INNER // 2, query_rows, key_rows, value_rows, cumul)]
-    serve(2, got[1])
-    got[1] = after(got[1], inners[0])
-    plane_total = call(
-        plane_kernel,
-        "plane_state",
-        shape(tagged, BF16),
-        [meta, *got],
-        [pltpu.VMEM((INNER, *tagged), BF16)],
-    )
-    earlier = [seq_up(plane_total, seq_count, d) for d in range(1, planes)]
-    inners.append(
-        inner_part(
-            INNER // 2, INNER // 2, after(query_rows, plane_total), key_rows, value_rows, cumul
+    chip_other = after(chip_other, inners[0], come[1])
+    tagged = (heads // 2, HD + TAG, HD)
+    plane_update = call(plane_kernel, "plane_state", shape(tagged, BF16), [meta, chip, chip_other])
+    serve(3, plane_update)
+    table = after(block_table, plane_update)
+    tables = [block_table] + [pool_shift(table, pool_count, r) for r in range(1, pool_count)]
+    total = plane_update
+    before = []
+    reach = 1
+    while reach < planes:
+        received = to_later_planes(total, seq_count, reach)
+        if len(inners) < 3:
+            query = after(query_rows, total)
+            inners.append(
+                inner_part(1 + len(inners), 1, query, key_rows, value_rows, cumul)
+            )
+            first = (come[2], *tables) if reach == 1 else (come[3],)
+            received[0] = after(received[0], inners[-1], *first)
+        final = 2 * reach >= planes
+        prefix, *rest = call(
+            functools.partial(scan_kernel, reach),
+            "scan_state",
+            [shape(tagged, BF16)] * (1 if final else 2),
+            [meta, *received, *before, plane_update],
         )
-    )
-    serve(3, earlier[0])
-    earlier[1] = after(earlier[1], inners[1], come[1], come[2])
-    leaving = call(
-        entering_kernel,
-        "entering_state",
-        [shape((share, HD, HD), BF16)] * INNER,
-        [meta, *got, *earlier],
-        [pltpu.VMEM((INNER, *tagged), BF16), pltpu.VMEM((INNER, share, HD, HD), BF16)],
-    )
-    states = [leaving[0]] + [seq_xor(leaving[r], seq_count, r) for r in range(1, INNER)]
-    serve(4, states[1])
-    states[2] = after(states[2], come[3])
+        if reach == 1:
+            serve(4, prefix)
+        before, total = [prefix], (rest or [None])[0]
+        reach *= 2
+    prefix_other = to_other_row(prefix, seq_count, 1)
+    residual_other = seq_xor(after(residual, prefix), seq_count, 1)
+    serve(5, prefix)
+    own_state, away_state = call(
+        start_kernel,
+        "start_state",
+        [shape((heads, HD, HD), BF16)] * 2,
+        [meta, update, update_other, chip_other, prefix, prefix_other],
+    )
+    other_state = after(seq_xor(away_state, seq_count, 1), come[4])
 
     mixed = pl.pallas_call(
         mixed_kernel,
         name="mixed",
         grid=(INNER,),
-        out_shape=shape((pool_count, rows_here, wide), BF16),
+        out_shape=[shape((rows_here, wide), BF16)] * pool_count,
         in_specs=[SMEM, by_share]
-        + [VMEM] * 2
+        + [VMEM] * 3
         + [pl.BlockSpec((1, share, rows), lambda g: (g, 0, 0))]
-        + [VMEM] * INNER,
-        out_specs=pl.BlockSpec((pool_count, rows_here, share * HD), lambda g: (0, 0, g)),
+        + [pl.BlockSpec((share, HD, HD), lambda g: (g, 0, 0))] * 2,
+        out_specs=[pl.BlockSpec((rows_here, share * HD), lambda g: (0, g))] * pool_count,
         scratch_shapes=[pltpu.VMEM((rows, share * HD), F32)],
         cost_estimate=LIGHT,
         compiler_params=params(12),
-    )(meta, in_hbm(query_rows), *inners, cumul, *states)
-    mixed_other = seq_xor(mixed, seq_count, 1)
-    serve(5, mixed)
+    )(meta, in_hbm(query_rows), *inners, cumul, own_state, other_state)
+    mixed_other = [seq_xor(part, seq_count, 1) for part in mixed]
+    serve(6, mixed[0])
     both = []
 
     def project(g, *first):
@@ -488,10 +541,10 @@
         count = len(blocks)
         out_wide = count * width
         joins = not both
-        sources = [after(both[0], *first)] if both else [mixed, mixed_other]
+        sources = [after(both[0], *first)] if both else [*mixed, *mixed_other]
         joined = [shape((pool_count, chip_rows, wide), BF16)] if joins else []
         kv, mine, *away = call(
-            functools.partial(project_kernel, joins, count),
+            functools.partial(project_kernel, pool_count if joins else 0, count),
             "project",
             [shape((out_wide, cache_width), BF16), shape((chip_rows, out_wide), F32)]
             + [shape((chip_rows, out_wide), BF16)] * (pool_count - 1)
@@ -550,15 +603,20 @@
         cached += 1
 
     for g in range(1, steps + 1):
-        if g >= 2:
-            for n in (2 * g - 1, 2 * g):
-                if n <= last:
-                    if 5 < n + 2 <= last:
-                        serve(n + 2, come[n], *done)
-                    done = (*done, come[n])
+        if g > 2:
+            done = (*done, *[come[m] for m in (2 * g - 1, 2 * g) if m <= last])
         projected[g] = project(g, *done)
         done = (projected[g][0],)
-        if 2 <= g < steps:
+        if g == 1:
+            continue
+        if g == 2:
+            done = (*done, residual_other)
+            reduce_one()
+        for n in (2 * g + 3, 2 * g + 4):
+            if n not in come and n <= last:
+                serve(n, come[n - 2], *done)
+                done = (*done, come[n - 2])
+        while g < steps and cached <= g - 1:
             reduce_one()
     while cached <= steps:
         reduce_one()

time: 195 us -> 169 us (0.87)
  waiting for transfers between devices: 101 us -> 79.5 us
  starting transfers between devices: 44.8 us -> 31.9 us
  Pallas kernels: 46.5 us -> 52.1 us
    ppermute x7, waiting for transfers between devices: 14.2 us -> 38.8 us  [pool_shift(): lax.ppermute(value, 'pool', [(i, (i + by) % pool_count) for i in range(po...]
    ppermute x3 -> x5, waiting for transfers between devices: 26.6 us -> 4.44 us  [the longest x2 4.43 us: to_other_row(): return lax.ppermute(value, 'seq', pairs)]
    ppermute x7, waiting for transfers between devices: 45.3 us -> 28.3 us  [ring_step(): return lax.ppermute(value, 'seq', pairs)]
    ppermute x11 -> x8, waiting for transfers between devices: 14.8 us -> 7.89 us  [seq_xor(): return lax.ppermute(value, 'seq', [(j, j ^ bits) for j in range(seq_count)])]
    ppermute x3 -> x5, starting transfers between devices: 10.5 us -> 5.24 us  [the longest x2 3.07 us: to_other_row(): return lax.ppermute(value, 'seq', pairs)]
    pallas_call x15 -> x18, Pallas kernels: 24.7 us -> 29.2 us  [call(): pl.pallas_call(body, name=name, out_shape=out_shape, in_specs=[SMEM if a....]
    ppermute x11 -> x8, starting transfers between devices: 6.53 us -> 2.45 us  [seq_xor(): return lax.ppermute(value, 'seq', [(j, j ^ bits) for j in range(seq_count)])]
    ppermute x7, starting transfers between devices: 9.73 us -> 7.45 us  [pool_shift(): lax.ppermute(value, 'pool', [(i, (i + by) % pool_count) for i in range(po...]
  transfers between devices with their start and end apart: 28 -> 27, of which waited for: 12 -> 14; matrix products, arithmetic and copies ran while one was open for 0% -> 0% of each run, Pallas kernels for 19% -> 29%
where the time goes in v4:
time: 169 us; the launch traced here: 168 us
  waiting for transfers between devices  79.5 us (47%)
  Pallas kernels  52.1 us (31%)
  starting transfers between devices  31.9 us (19%)
  local copies, waits for them, and re-layouts  3.7 us (2%)
    ppermute x7, waiting for transfers between devices, pool_shift(): lax.ppermute(value, 'pool', [(i, (i + by) % pool_count) for i in range(po...  38.8 us
    pallas_call x18, Pallas kernels, call(): pl.pallas_call(body, name=name, out_shape=out_shape, in_specs=[SMEM if a....  29.2 us
    ppermute x7, waiting for transfers between devices, ring_step(): return lax.ppermute(value, 'seq', pairs)  28.3 us
    ppermute x7, starting transfers between devices, ring_step(): return lax.ppermute(value, 'seq', pairs)  16.8 us
    pallas_call x3, Pallas kernels, inner_part(): pl.pallas_call(inner_kernel, name='inner', grid=(count,), out_shape=shape...  11.8 us
    ppermute x8, waiting for transfers between devices, seq_xor(): return lax.ppermute(value, 'seq', [(j, j ^ bits) for j in range(seq_count)])  7.89 us
    ppermute x7, starting transfers between devices, pool_shift(): lax.ppermute(value, 'pool', [(i, (i + by) % pool_count) for i in range(po...  7.45 us
    pallas_call x1, Pallas kernels, on_device(): pl.pallas_call(update_kernel, name='update', grid=(INNER,), out_shape=[sh...  5.74 us
  transfers between devices with their start and end apart: 27, of which 14 were waited for; matrix products, arithmetic and copies ran while one was open for 0% of the time, Pallas kernels for 29%

profile of v4, /device:TPU:0, one launch (start us, length us, event | category | flops | bytes accessed | tf_op | source)
XLA Modules:
  0.0 167.5 jit_solution(10403569836744143513)
XLA Ops:
  0.0 1.2 copy-done
  1.2 1.0 copy-done.1
  2.3 0.1 pack.1.refs_4_
  2.4 0.5 collective-permute-start
  2.9 2.6 %collective-permute-start.3 = (bf16[3072,256]{1,0:T(8,128)(2,1)S(1)}, bf16[3072,256]{1,0:T(8,128)(2,1)}, u32[]{:S(2)}, u32[]{:S(2)}) collective-permute-start(bf16[3072,256]{1,0:T(8,128)(2,1)S(1)} %pack.1.refs_4_), channel_id=1, source_target_pairs={{0,8},{2,6},{8,16},{10,2},{16,24},{18,10},{24,28},{26,18},{28,20},... | collective-permute-start | bytes 4718600 | tf_op jit(solution)/shard_map/ppermute | solution.py:106
  5.5 5.7 %update.1 = (f32[4,4,512]{2,1,0:T(4,128)S(1)}, bf16[16,144,128]{2,1,0:T(8,128)(2,1)S(1)}) custom-call(bf16[512,2048]{1,0:T(8,128)(2,1)} %key.7, bf16[512,2048]{1,0:T(8,128)(2,1)} %value.7, f32[16,512]{1,0:T(8,128)S(1)} %copy-done.3), custom_call_target="tpu_custom_call" | custom-call | flops 1 | bytes 1 | tf_op jit(solution)/shard_map/update/pallas_call | solution.py:460
  11.3 0.2 collective-permute-start.1
  11.5 1.9 %collective-permute-done.1.other = bf16[16,144,128]{2,1,0:T(8,128)(2,1)S(1)} collective-permute-done((bf16[16,144,128]{2,1,0:T(8,128)(2,1)S(1)}, bf16[16,144,128]{2,1,0:T(8,128)(2,1)S(1)}, u32[]{:S(2)}, u32[]{:S(2)}) %collective-permute-start.1) | collective-permute-done | bytes 589856 | tf_op jit(solution)/shard_map/ppermute | solution.py:56
  13.4 1.6 collective-permute-start.6
  14.9 0.1 stack.47.meta
  15.0 0.8 chip_state.1.own
  15.9 2.4 %collective-permute-start.2 = (bf16[16,144,128]{2,1,0:T(8,128)(2,1)S(1)}, bf16[16,144,128]{2,1,0:T(8,128)(2,1)S(1)}, u32[]{:S(2)}, u32[]{:S(2)}) collective-permute-start(bf16[16,144,128]{2,1,0:T(8,128)(2,1)S(1)} %chip_state.1.own), channel_id=1, source_target_pairs={{0,4},{6,2},{10,12},{12,10},{18,20},{20,18},{26,28},{28,26},{1,5},... | collective-permute-start | bytes 1769480 | tf_op jit(solution)/shard_map/ppermute | solution.py:69
  18.3 5.3 %inner.3.refs_0_ = f32[512,1024]{1,0:T(8,128)S(1)} custom-call(bf16[512,2048]{1,0:T(8,128)(2,1)} %query.5, bf16[512,2048]{1,0:T(8,128)(2,1)} %key.7, bf16[512,2048]{1,0:T(8,128)(2,1)} %value.7, f32[4,4,512]{2,1,0:T(4,128)S(1)} %get-tuple-element.75.cumul.refs_3_), custom_call_target="tpu_custom_call" | custom-call | flops 1 | bytes 1 | tf_op jit(solution)/shard_map/inner/pallas_call | solution.py:390
  23.6 4.0 %collective-permute-done.3.refs_1_ = bf16[3072,256]{1,0:T(8,128)(2,1)} collective-permute-done((bf16[3072,256]{1,0:T(8,128)(2,1)S(1)}, bf16[3072,256]{1,0:T(8,128)(2,1)}, u32[]{:S(2)}, u32[]{:S(2)}) %collective-permute-start.3) | collective-permute-done | bytes 1572896 | tf_op jit(solution)/shard_map/ppermute | solution.py:106
  27.6 4.4 %collective-permute-done.2.other.row_update = bf16[16,144,128]{2,1,0:T(8,128)(2,1)S(1)} collective-permute-done((bf16[16,144,128]{2,1,0:T(8,128)(2,1)S(1)}, bf16[16,144,128]{2,1,0:T(8,128)(2,1)S(1)}, u32[]{:S(2)}, u32[]{:S(2)}) %collective-permute-start.2) | collective-permute-done | bytes 589856 | tf_op jit(solution)/shard_map/ppermute | solution.py:69
  32.0 0.7 plane_state.1.refs_1_.refs_3_
  32.8 0.7 collective-permute-start.5
  33.5 1.6 collective-permute-start.4
  35.0 3.3 %inner.4.refs_1_ = f32[512,512]{1,0:T(8,128)S(1)} custom-call(bf16[512,2048]{1,0:T(8,128)(2,1)} %query.5, bf16[512,2048]{1,0:T(8,128)(2,1)} %key.7, bf16[512,2048]{1,0:T(8,128)(2,1)} %value.7, f32[4,4,512]{2,1,0:T(4,128)S(1)} %get-tuple-element.75.cumul.refs_3_), custom_call_target="tpu_custom_call" | custom-call | flops 1 | bytes 1 | tf_op jit(solution)/shard_map/inner/pallas_call | solution.py:390
  38.3 8.8 %collective-permute-done.6.refs_2_ = bf16[3072,256]{1,0:T(8,128)(2,1)} collective-permute-done((bf16[3072,256]{1,0:T(8,128)(2,1)}, bf16[3072,256]{1,0:T(8,128)(2,1)}, u32[]{:S(2)}, u32[]{:S(2)}) %collective-permute-start.6) | collective-permute-done | bytes 1572896 | tf_op jit(solution)/shard_map/ppermute | solution.py:106
  47.2 0.7 scan_state.2
  47.9 0.8 collective-permute-start.7
  48.8 0.7 collective-permute-start.9
  49.4 3.3 %inner.5.refs_2_ = f32[512,512]{1,0:T(8,128)S(1)} custom-call(bf16[512,2048]{1,0:T(8,128)(2,1)} %query.5, bf16[512,2048]{1,0:T(8,128)(2,1)} %key.7, bf16[512,2048]{1,0:T(8,128)(2,1)} %value.7, f32[4,4,512]{2,1,0:T(4,128)S(1)} %get-tuple-element.75.cumul.refs_3_), custom_call_target="tpu_custom_call" | custom-call | flops 1 | bytes 1 | tf_op jit(solution)/shard_map/inner/pallas_call | solution.py:390
  52.7 11.2 %collective-permute-done.8.refs_1_ = bf16[3072,256]{1,0:T(8,128)(2,1)S(1)} collective-permute-done((bf16[3072,256]{1,0:T(8,128)(2,1)}, bf16[3072,256]{1,0:T(8,128)(2,1)S(1)}, u32[]{:S(2)}, u32[]{:S(2)}) %collective-permute-start.8) | collective-permute-done | bytes 1572896 | tf_op jit(solution)/shard_map/ppermute | solution.py:106
  63.9 0.7 scan_state.3.prefix
  64.6 0.7 collective-permute-start.10
  65.3 0.1 collective-permute-start.15
  65.4 1.1 start_state.1
  66.6 0.6 collective-permute-start.11
  67.1 9.2 %collective-permute-start.17 = (bf16[3072,256]{1,0:T(8,128)(2,1)S(1)}, bf16[3072,256]{1,0:T(8,128)(2,1)S(1)}, u32[]{:S(2)}, u32[]{:S(2)}) collective-permute-start(bf16[3072,256]{1,0:T(8,128)(2,1)S(1)} %collective-permute-done.8.refs_1_), channel_id=1, source_target_pairs={{0,8},{2,6},{8,16},{10,2},{16,24},{18,10},{24,28},{26,18},{28,20},... | collective-permute-start | bytes 4718600 | tf_op jit(solution)/shard_map/ppermute | solution.py:106
  76.4 4.4 %collective-permute-done.12.refs_2_ = bf16[3072,256]{1,0:T(8,128)(2,1)S(1)} collective-permute-done((bf16[3072,256]{1,0:T(8,128)(2,1)}, bf16[3072,256]{1,0:T(8,128)(2,1)S(1)}, u32[]{:S(2)}, u32[]{:S(2)}) %collective-permute-start.12) | collective-permute-done | bytes 1572896 | tf_op jit(solution)/shard_map/ppermute | solution.py:106
  80.8 5.3 %mixed.1 = (bf16[256,2048]{1,0:T(8,128)(2,1)S(1)}, bf16[256,2048]{1,0:T(8,128)(2,1)S(1)}) custom-call(s32[11]{0:T(128)S(1)} %stack.47.meta, bf16[512,2048]{1,0:T(8,128)(2,1)} %query.5, f32[512,1024]{1,0:T(8,128)S(1)} %inner.3.refs_0_, f32[512,512]{1,0:T(8,128)S(1)} %inner.4.refs_1_, f32[512,512]{1,0:T(8,128)S(1)} %inner.5.refs_2_, ...), custom_call_target="tpu_custom_call" | custom-call | flops 1 | bytes 1 | tf_op jit(solution)/shard_map/mixed/pallas_call | solution.py:521
  86.1 0.5 collective-permute-start.13
  86.6 2.1 %collective-permute-done.14.refs_3_ = bf16[256,2048]{1,0:T(8,128)(2,1)S(1)} collective-permute-done((bf16[256,2048]{1,0:T(8,128)(2,1)S(1)}, bf16[256,2048]{1,0:T(8,128)(2,1)S(1)}, u32[]{:S(2)}, u32[]{:S(2)}) %collective-permute-start.14) | collective-permute-done | bytes 1048608 | tf_op jit(solution)/shard_map/ppermute | solution.py:56
  88.7 1.5 collective-permute-done.13.refs_2_
  90.2 1.3 project.5
  91.6 2.1 %collective-permute-start.16 = (bf16[512,256]{1,0:T(8,128)(2,1)S(1)}, bf16[512,256]{1,0:T(8,128)(2,1)S(1)}, u32[]{:S(2)}, u32[]{:S(2)}) collective-permute-start(bf16[512,256]{1,0:T(8,128)(2,1)S(1)} %get-tuple-element.101), channel_id=1, source_target_pairs={{0,1},{1,0},{2,3},{3,2},{4,5},{5,4},{6,7},{7,6},{8,9},{9,8},{10,11... | collective-permute-start | bytes 786440 | tf_op jit(solution)/shard_map/ppermute | solution.py:89
  93.6 0.8 collective-permute-start.19
  94.4 4.3 %project.6 = (bf16[512,1024]{1,0:T(8,128)(2,1)S(1)}, f32[512,512]{1,0:T(8,128)S(1)}, bf16[512,512]{1,0:T(8,128)(2,1)S(1)}) custom-call(bf16[2,512,2048]{2,1,0:T(8,128)(2,1)S(1)} %get-tuple-element.122.refs_0_, bf16[3072,256]{1,0:T(8,128)(2,1)} %collective-permute-done.3.refs_1_, bf16[3072,256]{1,0:T(8,128)(2,1)} %collective-permute-done.6.refs_2_), custom_call_target="tpu_custom_call" | custom-call | flops 1 | bytes 1 | tf_op jit(solution)/shard_map/project/pallas_call | solution.py:28
  98.8 2.4 %project.7 = (bf16[512,1024]{1,0:T(8,128)(2,1)S(1)}, f32[512,512]{1,0:T(8,128)S(1)}, bf16[512,512]{1,0:T(8,128)(2,1)S(1)}) custom-call(bf16[2,512,2048]{2,1,0:T(8,128)(2,1)S(1)} %get-tuple-element.122.refs_0_, bf16[3072,256]{1,0:T(8,128)(2,1)S(1)} %collective-permute-done.8.refs_1_, bf16[3072,256]{1,0:T(8,128)(2,1)S(1)} %collective-permute-done.12.refs_2_), custom_call_target="tpu_custom_call" | custom-call | flops 1 | bytes 1 | tf_op jit(solution)/shard_map/project/pallas_call | solution.py:28
  101.2 1.3 copy-done.6
  102.5 2.0 %cache.5 = (f32[256,1024]{1,0:T(8,128)S(1)}, f32[256,1024]{1,0:T(8,128)S(1)}, f32[256,128]{1,0:T(8,128)S(1)}, f32[256,128]{1,0:T(8,128)S(1)}) custom-call(s32[11]{0:T(128)S(1)} %stack.47.meta, f32[512,256]{1,0:T(8,128)S(1)} %get-tuple-element.99.mine, bf16[256,4096]{1,0:T(8,128)(2,1)} %refs_0_.10, bf16[256,4096]{1,0:T(8,128)(2,1)} %copy-done.6, ...), custom_call_target="tpu_custom_call" | custom-call | flops 1 | bytes 1 | tf_op jit(solution)/shard_map/cache/pallas_call | solution.py:28
  104.5 2.4 %collective-permute-start.21 = (bf16[3072,256]{1,0:T(8,128)(2,1)S(1)}, bf16[3072,256]{1,0:T(8,128)(2,1)S(1)}, u32[]{:S(2)}, u32[]{:S(2)}) collective-permute-start(bf16[3072,256]{1,0:T(8,128)(2,1)S(1)} %collective-permute-done.17.refs_1_), channel_id=1, source_target_pairs={{0,8},{2,6},{8,16},{10,2},{16,24},{18,10},{24,28},{26,18},{28,20},... | collective-permute-start | bytes 4718600 | tf_op jit(solution)/shard_map/ppermute | solution.py:106
  107.0 0.5 collective-permute-start.18
  107.5 1.5 collective-permute-start.20
  109.0 12.8 %collective-permute-done.18.refs_4_ = bf16[512,512]{1,0:T(8,128)(2,1)S(1)} collective-permute-done((bf16[512,512]{1,0:T(8,128)(2,1)S(1)}, bf16[512,512]{1,0:T(8,128)(2,1)S(1)}, u32[]{:S(2)}, u32[]{:S(2)}) %collective-permute-start.18) | collective-permute-done | bytes 524320 | tf_op jit(solution)/shard_map/ppermute | solution.py:89
  121.8 2.5 %cache.6 = (f32[256,1024]{1,0:T(8,128)S(1)}, f32[256,1024]{1,0:T(8,128)S(1)}, f32[256,128]{1,0:T(8,128)S(1)}, f32[256,128]{1,0:T(8,128)S(1)}) custom-call(s32[11]{0:T(128)S(1)} %stack.47.meta, f32[512,512]{1,0:T(8,128)S(1)} %get-tuple-element.104.mine, bf16[256,4096]{1,0:T(8,128)(2,1)} %refs_0_.10, bf16[256,4096]{1,0:T(8,128)(2,1)} %copy-done.6, ...), custom_call_target="tpu_custom_call" | custom-call | flops 1 | bytes 1 | tf_op jit(solution)/shard_map/cache/pallas_call | solution.py:28
  124.3 2.4 %project.8 = (bf16[512,1024]{1,0:T(8,128)(2,1)S(1)}, f32[512,512]{1,0:T(8,128)S(1)}, bf16[512,512]{1,0:T(8,128)(2,1)S(1)}) custom-call(bf16[2,512,2048]{2,1,0:T(8,128)(2,1)S(1)} %get-tuple-element.122.refs_0_, bf16[3072,256]{1,0:T(8,128)(2,1)S(1)} %collective-permute-done.17.refs_1_, bf16[3072,256]{1,0:T(8,128)(2,1)S(1)} %collective-permute-done.19.refs_2_), custom_call_target="tpu_custom_call" | custom-call | flops 1 | bytes 1 | tf_op jit(solution)/shard_map/project/pallas_call | solution.py:28
  126.8 0.6 collective-permute-start.22
  127.4 5.7 %collective-permute-done.20.refs_4_ = bf16[512,512]{1,0:T(8,128)(2,1)S(1)} collective-permute-done((bf16[512,512]{1,0:T(8,128)(2,1)S(1)}, bf16[512,512]{1,0:T(8,128)(2,1)S(1)}, u32[]{:S(2)}, u32[]{:S(2)}) %collective-permute-start.20) | collective-permute-done | bytes 524320 | tf_op jit(solution)/shard_map/ppermute | solution.py:89
  133.1 2.5 %cache.7 = (f32[256,1024]{1,0:T(8,128)S(1)}, f32[256,1024]{1,0:T(8,128)S(1)}, f32[256,128]{1,0:T(8,128)S(1)}, f32[256,128]{1,0:T(8,128)S(1)}) custom-call(s32[11]{0:T(128)S(1)} %stack.47.meta, f32[512,512]{1,0:T(8,128)S(1)} %get-tuple-element.114.mine, bf16[256,4096]{1,0:T(8,128)(2,1)} %refs_0_.10, bf16[256,4096]{1,0:T(8,128)(2,1)} %copy-done.6, ...), custom_call_target="tpu_custom_call" | custom-call | flops 1 | bytes 1 | tf_op jit(solution)/shard_map/cache/pallas_call | solution.py:28
  135.6 1.3 project.9
  136.8 0.6 collective-permute-start.23
  137.4 6.5 %collective-permute-done.22.refs_4_ = bf16[512,512]{1,0:T(8,128)(2,1)S(1)} collective-permute-done((bf16[512,512]{1,0:T(8,128)(2,1)S(1)}, bf16[512,512]{1,0:T(8,128)(2,1)S(1)}, u32[]{:S(2)}, u32[]{:S(2)}) %collective-permute-start.22) | collective-permute-done | bytes 524320 | tf_op jit(solution)/shard_map/ppermute | solution.py:89
  144.0 2.5 %cache.8 = (f32[256,1024]{1,0:T(8,128)S(1)}, f32[256,1024]{1,0:T(8,128)S(1)}, f32[256,128]{1,0:T(8,128)S(1)}, f32[256,128]{1,0:T(8,128)S(1)}) custom-call(s32[11]{0:T(128)S(1)} %stack.47.meta, f32[512,512]{1,0:T(8,128)S(1)} %get-tuple-element.124.mine, bf16[256,4096]{1,0:T(8,128)(2,1)} %refs_0_.10, bf16[256,4096]{1,0:T(8,128)(2,1)} %copy-done.6, ...), custom_call_target="tpu_custom_call" | custom-call | flops 1 | bytes 1 | tf_op jit(solution)/shard_map/cache/pallas_call | solution.py:28
  146.5 0.3 collective-permute-done.23.refs_4_
  146.8 2.0 %cache.9 = (f32[256,1024]{1,0:T(8,128)S(1)}, f32[256,1024]{1,0:T(8,128)S(1)}, f32[256,128]{1,0:T(8,128)S(1)}, f32[256,128]{1,0:T(8,128)S(1)}) custom-call(s32[11]{0:T(128)S(1)} %stack.47.meta, f32[512,256]{1,0:T(8,128)S(1)} %get-tuple-element.131.mine, bf16[256,4096]{1,0:T(8,128)(2,1)} %refs_0_.10, bf16[256,4096]{1,0:T(8,128)(2,1)} %copy-done.6, ...), custom_call_target="tpu_custom_call" | custom-call | flops 1 | bytes 1 | tf_op jit(solution)/shard_map/cache/pallas_call | solution.py:28
  148.9 0.5 collective-permute-start.25
  149.4 2.3 %collective-permute-done.25.square_in = f32[256,128]{1,0:T(8,128)S(1)} collective-permute-done((f32[256,128]{1,0:T(8,128)S(1)}, f32[256,128]{1,0:T(8,128)S(1)}, u32[]{:S(2)}, u32[]{:S(2)}) %collective-permute-start.25) | collective-permute-done | bytes 131104 | tf_op jit(solution)/shard_map/ppermute | solution.py:56
  151.7 0.2 finish.1.refs_2_
  151.9 0.6 collective-permute-start.26
  152.5 13.4 %collective-permute-done.26.refs_3_ = bf16[256,1024]{1,0:T(8,128)(2,1)S(1)} collective-permute-done((bf16[256,1024]{1,0:T(8,128)(2,1)S(1)}, bf16[256,1024]{1,0:T(8,128)(2,1)S(1)}, u32[]{:S(2)}, u32[]{:S(2)}) %collective-permute-start.26) | collective-permute-done | bytes 524320 | tf_op jit(solution)/shard_map/ppermute | solution.py:89
  165.9 1.6 place.1
  (28 shorter events, 0.3 us)
Async XLA Ops:
  0.0 1.2 copy-start
  1.2 1.0 copy-start.1
  2.3 3.3 %copy-start.3 = (f32[16,512]{1,0:T(8,128)S(1)}, f32[16,512]{1,0:T(8,128)}, u32[]{:S(2)}) copy-start(f32[16,512]{1,0:T(8,128)} %decay.1) | copy-start | bytes 98308
  2.4 8.9 %collective-permute-start = (bf16[3072,256]{1,0:T(8,128)(2,1)S(1)}, bf16[3072,256]{1,0:T(8,128)(2,1)}, u32[]{:S(2)}, u32[]{:S(2)}) collective-permute-start(bf16[3072,256]{1,0:T(8,128)(2,1)S(1)} %pack.1.refs_4_), channel_id=1, source_target_pairs={{0,2},{2,0},{4,6},{6,4},{8,10},{10,8},{12,14},{14,12},{16,18},{18,... | collective-permute-start | bytes 4718600 | tf_op jit(solution)/shard_map/ppermute | solution.py:56
  2.9 24.7 %collective-permute-start.3 = (bf16[3072,256]{1,0:T(8,128)(2,1)S(1)}, bf16[3072,256]{1,0:T(8,128)(2,1)}, u32[]{:S(2)}, u32[]{:S(2)}) collective-permute-start(bf16[3072,256]{1,0:T(8,128)(2,1)S(1)} %pack.1.refs_4_), channel_id=1, source_target_pairs={{0,8},{2,6},{8,16},{10,2},{16,24},{18,10},{24,28},{26,18},{28,20},... | collective-permute-start | bytes 4718600 | tf_op jit(solution)/shard_map/ppermute | solution.py:106
  11.3 2.1 %collective-permute-start.1 = (bf16[16,144,128]{2,1,0:T(8,128)(2,1)S(1)}, bf16[16,144,128]{2,1,0:T(8,128)(2,1)S(1)}, u32[]{:S(2)}, u32[]{:S(2)}) collective-permute-start(bf16[16,144,128]{2,1,0:T(8,128)(2,1)S(1)} %get-tuple-element.74.own), channel_id=1, source_target_pairs={{0,2},{2,0},{4,6},{6,4},{8,10},{10,8},{12,14},{14,12},{16,18},{18,... | collective-permute-start | bytes 1769480 | tf_op jit(solution)/shard_map/ppermute | solution.py:56
  13.4 33.8 %collective-permute-start.6 = (bf16[3072,256]{1,0:T(8,128)(2,1)}, bf16[3072,256]{1,0:T(8,128)(2,1)}, u32[]{:S(2)}, u32[]{:S(2)}) collective-permute-start(bf16[3072,256]{1,0:T(8,128)(2,1)} %collective-permute-done), channel_id=1, source_target_pairs={{0,8},{2,6},{8,16},{10,2},{16,24},{18,10},{24,28},{26,18},{28,20},... | collective-permute-start | bytes 4718600 | tf_op jit(solution)/shard_map/ppermute | solution.py:106
  15.9 16.1 %collective-permute-start.2 = (bf16[16,144,128]{2,1,0:T(8,128)(2,1)S(1)}, bf16[16,144,128]{2,1,0:T(8,128)(2,1)S(1)}, u32[]{:S(2)}, u32[]{:S(2)}) collective-permute-start(bf16[16,144,128]{2,1,0:T(8,128)(2,1)S(1)} %chip_state.1.own), channel_id=1, source_target_pairs={{0,4},{6,2},{10,12},{12,10},{18,20},{20,18},{26,28},{28,26},{1,5},... | collective-permute-start | bytes 1769480 | tf_op jit(solution)/shard_map/ppermute | solution.py:69
  18.3 15.2 %copy-start.4 = (s32[2,2]{1,0:T(2,128)S(1)}, s32[2,2]{1,0:T(2,128)}, u32[]{:S(2)}) copy-start(s32[2,2]{1,0:T(2,128)} %refs_0_.11) | copy-start | bytes 52
  32.7 31.2 %collective-permute-start.8 = (bf16[3072,256]{1,0:T(8,128)(2,1)}, bf16[3072,256]{1,0:T(8,128)(2,1)S(1)}, u32[]{:S(2)}, u32[]{:S(2)}) collective-permute-start(bf16[3072,256]{1,0:T(8,128)(2,1)} %collective-permute-done.3.refs_1_), channel_id=1, source_target_pairs={{0,8},{2,6},{8,16},{10,2},{16,24},{18,10},{24,28},{26,18},{28,20},... | collective-permute-start | bytes 4718600 | tf_op jit(solution)/shard_map/ppermute | solution.py:106
  32.8 5.5 %collective-permute-start.5 = (bf16[8,144,128]{2,1,0:T(8,128)(2,1)S(1)}, bf16[8,144,128]{2,1,0:T(8,128)(2,1)S(1)}, u32[]{:S(2)}, u32[]{:S(2)}) collective-permute-start(bf16[8,144,128]{2,1,0:T(8,128)(2,1)S(1)} %plane_state.1.refs_1_.refs_3_), channel_id=1, source_target_pairs={{2,10},{4,12},{18,26},{20,28},{3,11},{5,13},{19,27},{21,29}} | collective-permute-start | bytes 884744 | tf_op jit(solution)/shard_map/ppermute | solution.py:75
  33.5 4.8 %collective-permute-start.4 = (s32[2,2]{1,0:T(2,128)S(1)}, s32[2,2]{1,0:T(2,128)S(1)}, u32[]{:S(2)}, u32[]{:S(2)}) collective-permute-start(s32[2,2]{1,0:T(2,128)S(1)} %copy-done.4), channel_id=1, source_target_pairs={{0,1},{1,0},{2,3},{3,2},{4,5},{5,4},{6,7},{7,6},{8,9},{9,8},{10,11... | collective-permute-start | bytes 56 | tf_op jit(solution)/shard_map/ppermute | solution.py:89
  47.9 32.9 %collective-permute-start.12 = (bf16[3072,256]{1,0:T(8,128)(2,1)}, bf16[3072,256]{1,0:T(8,128)(2,1)S(1)}, u32[]{:S(2)}, u32[]{:S(2)}) collective-permute-start(bf16[3072,256]{1,0:T(8,128)(2,1)} %collective-permute-done.6.refs_2_), channel_id=1, source_target_pairs={{0,8},{2,6},{8,16},{10,2},{16,24},{18,10},{24,28},{26,18},{28,20},... | collective-permute-start | bytes 4718600 | tf_op jit(solution)/shard_map/ppermute | solution.py:106
  47.9 17.4 %copy-start.5 = (bf16[256,4096]{1,0:T(8,128)(2,1)S(1)}, bf16[256,4096]{1,0:T(8,128)(2,1)}, u32[]{:S(2)}) copy-start(bf16[256,4096]{1,0:T(8,128)(2,1)} %refs_0_.10) | copy-start | bytes 6291460
  47.9 4.8 %collective-permute-start.7 = (bf16[8,144,128]{2,1,0:T(8,128)(2,1)S(1)}, bf16[8,144,128]{2,1,0:T(8,128)(2,1)S(1)}, u32[]{:S(2)}, u32[]{:S(2)}) collective-permute-start(bf16[8,144,128]{2,1,0:T(8,128)(2,1)S(1)} %get-tuple-element.81), channel_id=1, source_target_pairs={{10,18},{12,20},{11,19},{13,21}} | collective-permute-start | bytes 884744 | tf_op jit(solution)/shard_map/ppermute | solution.py:75
  48.8 15.1 %collective-permute-start.9 = (bf16[8,144,128]{2,1,0:T(8,128)(2,1)S(1)}, bf16[8,144,128]{2,1,0:T(8,128)(2,1)S(1)}, u32[]{:S(2)}, u32[]{:S(2)}) collective-permute-start(bf16[8,144,128]{2,1,0:T(8,128)(2,1)S(1)} %get-tuple-element.81), channel_id=1, source_target_pairs={{10,26},{12,28},{11,27},{13,29}} | collective-permute-start | bytes 884744 | tf_op jit(solution)/shard_map/ppermute | solution.py:75
  64.6 0.8 collective-permute-start.10
  65.3 35.8 %collective-permute-start.15 = (bf16[256,4096]{1,0:T(8,128)(2,1)S(1)}, bf16[256,4096]{1,0:T(8,128)(2,1)S(1)}, u32[]{:S(2)}, u32[]{:S(2)}) collective-permute-start(bf16[256,4096]{1,0:T(8,128)(2,1)S(1)} %copy-done.5), channel_id=1, source_target_pairs={{0,2},{2,0},{4,6},{6,4},{8,10},{10,8},{12,14},{14,12},{16,18},{18,... | collective-permute-start | bytes 6291464 | tf_op jit(solution)/shard_map/ppermute | solution.py:56
  66.6 9.8 %collective-permute-start.11 = (bf16[16,128,128]{2,1,0:T(8,128)(2,1)S(1)}, bf16[16,128,128]{2,1,0:T(8,128)(2,1)S(1)}, u32[]{:S(2)}, u32[]{:S(2)}) collective-permute-start(bf16[16,128,128]{2,1,0:T(8,128)(2,1)S(1)} %get-tuple-element.87), channel_id=1, source_target_pairs={{0,2},{2,0},{4,6},{6,4},{8,10},{10,8},{12,14},{14,12},{16,18},{18,... | collective-permute-start | bytes 1572872 | tf_op jit(solution)/shard_map/ppermute | solution.py:56
  67.1 37.4 %collective-permute-start.17 = (bf16[3072,256]{1,0:T(8,128)(2,1)S(1)}, bf16[3072,256]{1,0:T(8,128)(2,1)S(1)}, u32[]{:S(2)}, u32[]{:S(2)}) collective-permute-start(bf16[3072,256]{1,0:T(8,128)(2,1)S(1)} %collective-permute-done.8.refs_1_), channel_id=1, source_target_pairs={{0,8},{2,6},{8,16},{10,2},{16,24},{18,10},{24,28},{26,18},{28,20},... | collective-permute-start | bytes 4718600 | tf_op jit(solution)/shard_map/ppermute | solution.py:106
  86.0 2.7 %collective-permute-start.14 = (bf16[256,2048]{1,0:T(8,128)(2,1)S(1)}, bf16[256,2048]{1,0:T(8,128)(2,1)S(1)}, u32[]{:S(2)}, u32[]{:S(2)}) collective-permute-start(bf16[256,2048]{1,0:T(8,128)(2,1)S(1)} %get-tuple-element.91.refs_1_), channel_id=1, source_target_pairs={{0,2},{2,0},{4,6},{6,4},{8,10},{10,8},{12,14},{14,12},{16,18},{18,... | collective-permute-start | bytes 3145736 | tf_op jit(solution)/shard_map/ppermute | solution.py:56
  86.1 4.1 %collective-permute-start.13 = (bf16[256,2048]{1,0:T(8,128)(2,1)S(1)}, bf16[256,2048]{1,0:T(8,128)(2,1)S(1)}, u32[]{:S(2)}, u32[]{:S(2)}) collective-permute-start(bf16[256,2048]{1,0:T(8,128)(2,1)S(1)} %get-tuple-element.90.refs_0_), channel_id=1, source_target_pairs={{0,2},{2,0},{4,6},{6,4},{8,10},{10,8},{12,14},{14,12},{16,18},{18,... | collective-permute-start | bytes 3145736 | tf_op jit(solution)/shard_map/ppermute | solution.py:56
  91.6 9.6 %collective-permute-start.16 = (bf16[512,256]{1,0:T(8,128)(2,1)S(1)}, bf16[512,256]{1,0:T(8,128)(2,1)S(1)}, u32[]{:S(2)}, u32[]{:S(2)}) collective-permute-start(bf16[512,256]{1,0:T(8,128)(2,1)S(1)} %get-tuple-element.101), channel_id=1, source_target_pairs={{0,1},{1,0},{2,3},{3,2},{4,5},{5,4},{6,7},{7,6},{8,9},{9,8},{10,11... | collective-permute-start | bytes 786440 | tf_op jit(solution)/shard_map/ppermute | solution.py:89
  93.6 30.7 %collective-permute-start.19 = (bf16[3072,256]{1,0:T(8,128)(2,1)S(1)}, bf16[3072,256]{1,0:T(8,128)(2,1)S(1)}, u32[]{:S(2)}, u32[]{:S(2)}) collective-permute-start(bf16[3072,256]{1,0:T(8,128)(2,1)S(1)} %collective-permute-done.12.refs_2_), channel_id=1, source_target_pairs={{0,8},{2,6},{8,16},{10,2},{16,24},{18,10},{24,28},{26,18},{28,20},... | collective-permute-start | bytes 4718600 | tf_op jit(solution)/shard_map/ppermute | solution.py:106
  98.8 3.8 %copy-start.2 = (f32[4096]{0:T(1024)S(1)}, f32[4096]{0:T(1024)}, u32[]{:S(2)}) copy-start(f32[4096]{0:T(1024)} %param.15) | copy-start | bytes 49156
  101.2 1.3 copy-start.6
  104.5 31.0 %collective-permute-start.21 = (bf16[3072,256]{1,0:T(8,128)(2,1)S(1)}, bf16[3072,256]{1,0:T(8,128)(2,1)S(1)}, u32[]{:S(2)}, u32[]{:S(2)}) collective-permute-start(bf16[3072,256]{1,0:T(8,128)(2,1)S(1)} %collective-permute-done.17.refs_1_), channel_id=1, source_target_pairs={{0,8},{2,6},{8,16},{10,2},{16,24},{18,10},{24,28},{26,18},{28,20},... | collective-permute-start | bytes 4718600 | tf_op jit(solution)/shard_map/ppermute | solution.py:106
  107.0 14.9 %collective-permute-start.18 = (bf16[512,512]{1,0:T(8,128)(2,1)S(1)}, bf16[512,512]{1,0:T(8,128)(2,1)S(1)}, u32[]{:S(2)}, u32[]{:S(2)}) collective-permute-start(bf16[512,512]{1,0:T(8,128)(2,1)S(1)} %get-tuple-element.106), channel_id=1, source_target_pairs={{0,1},{1,0},{2,3},{3,2},{4,5},{5,4},{6,7},{7,6},{8,9},{9,8},{10,11... | collective-permute-start | bytes 1572872 | tf_op jit(solution)/shard_map/ppermute | solution.py:89
  107.5 25.6 %collective-permute-start.20 = (bf16[512,512]{1,0:T(8,128)(2,1)S(1)}, bf16[512,512]{1,0:T(8,128)(2,1)S(1)}, u32[]{:S(2)}, u32[]{:S(2)}) collective-permute-start(bf16[512,512]{1,0:T(8,128)(2,1)S(1)} %get-tuple-element.116), channel_id=1, source_target_pairs={{0,1},{1,0},{2,3},{3,2},{4,5},{5,4},{6,7},{7,6},{8,9},{9,8},{10,11... | collective-permute-start | bytes 1572872 | tf_op jit(solution)/shard_map/ppermute | solution.py:89
  126.8 17.2 %collective-permute-start.22 = (bf16[512,512]{1,0:T(8,128)(2,1)S(1)}, bf16[512,512]{1,0:T(8,128)(2,1)S(1)}, u32[]{:S(2)}, u32[]{:S(2)}) collective-permute-start(bf16[512,512]{1,0:T(8,128)(2,1)S(1)} %get-tuple-element.126), channel_id=1, source_target_pairs={{0,1},{1,0},{2,3},{3,2},{4,5},{5,4},{6,7},{7,6},{8,9},{9,8},{10,11... | collective-permute-start | bytes 1572872 | tf_op jit(solution)/shard_map/ppermute | solution.py:89
  136.8 9.9 %collective-permute-start.23 = (bf16[512,256]{1,0:T(8,128)(2,1)S(1)}, bf16[512,256]{1,0:T(8,128)(2,1)S(1)}, u32[]{:S(2)}, u32[]{:S(2)}) collective-permute-start(bf16[512,256]{1,0:T(8,128)(2,1)S(1)} %get-tuple-element.133), channel_id=1, source_target_pairs={{0,1},{1,0},{2,3},{3,2},{4,5},{5,4},{6,7},{7,6},{8,9},{9,8},{10,11... | collective-permute-start | bytes 786440 | tf_op jit(solution)/shard_map/ppermute | solution.py:89
  148.8 2.9 %collective-permute-start.24 = (f32[256,1024]{1,0:T(8,128)S(1)}, f32[256,1024]{1,0:T(8,128)S(1)}, u32[]{:S(2)}, u32[]{:S(2)}) collective-permute-start(f32[256,1024]{1,0:T(8,128)S(1)} %get-tuple-element.139), channel_id=1, source_target_pairs={{0,2},{2,0},{4,6},{6,4},{8,10},{10,8},{12,14},{14,12},{16,18},{18,... | collective-permute-start | bytes 3145736 | tf_op jit(solution)/shard_map/ppermute | solution.py:56
  148.9 2.8 %collective-permute-start.25 = (f32[256,128]{1,0:T(8,128)S(1)}, f32[256,128]{1,0:T(8,128)S(1)}, u32[]{:S(2)}, u32[]{:S(2)}) collective-permute-start(f32[256,128]{1,0:T(8,128)S(1)} %get-tuple-element.140), channel_id=1, source_target_pairs={{0,2},{2,0},{4,6},{6,4},{8,10},{10,8},{12,14},{14,12},{16,18},{18,... | collective-permute-start | bytes 393224 | tf_op jit(solution)/shard_map/ppermute | solution.py:56
  151.9 14.0 %collective-permute-start.26 = (bf16[256,1024]{1,0:T(8,128)(2,1)S(1)}, bf16[256,1024]{1,0:T(8,128)(2,1)S(1)}, u32[]{:S(2)}, u32[]{:S(2)}) collective-permute-start(bf16[256,1024]{1,0:T(8,128)(2,1)S(1)} %finish.1.refs_2_), channel_id=1, source_target_pairs={{0,1},{1,0},{2,3},{3,2},{4,5},{5,4},{6,7},{7,6},{8,9},{9,8},{10,11... | collective-permute-start | bytes 1572872 | tf_op jit(solution)/shard_map/ppermute | solution.py:89

commit v5 on v4

--- a/solution.py
+++ b/solution.py
@@ -291,6 +291,21 @@
         out[depth + c * rows : depth + (c + 1) * rows, :] = kv[:, here]
 
 
+def cut_kernel(block, out):
+    out[...] = block[block.shape[0] - out.shape[0] :, :]
+
+
+def widen_kernel(meta, block, *refs):
+    *shares, out = refs
+    rows = shares[0].shape[0]
+    depth = block.shape[0] - rows
+    out[:depth, :] = block[:depth, :]
+    for r, part in enumerate(shares):
+        share = lax.rem(meta[2] + len(shares) - r, len(shares))
+        start = pl.multiple_of(depth + share * rows, rows)
+        out[pl.ds(start, rows), :] = part[...]
+
+
 def project_kernel(joins, parts, *refs):
     if joins:
         both = refs[-1]
@@ -303,10 +318,9 @@
         both = refs[0]
         refs = refs[1:]
     blocks = refs[:parts]
-    kv, mine, *away = refs[parts:]
+    mine, *away = refs[parts:]
     pool_count, _, depth = both.shape
     width = blocks[0].shape[1]
-    rows = kv.shape[0] // parts
     for r in list(range(1, pool_count)) + [0]:
         for p in range(parts):
             here = slice(p * width, (p + 1) * width)
@@ -315,15 +329,12 @@
                 mine[:, here] = total
             else:
                 away[r - 1][:, here] = total.astype(BF16)
-    for p in range(parts):
-        for c in range(kv.shape[1] // width):
-            below = slice(depth + c * rows, depth + (c + 1) * rows)
-            kv[p * rows : (p + 1) * rows, c * width : (c + 1) * width] = blocks[p][below, :]
-
-
-def cache_kernel(first, parts, width, at, meta, mine, *refs):
-    own_rows, other_rows, kv, gain, *refs = refs
-    *arrived, scaled, near, sems = refs
+
+
+def cache_kernel(first, parts, shares, kv_count, width, at, meta, mine, *refs):
+    own_rows, other_rows, gain, *refs = refs
+    kv, refs = refs[:kv_count], refs[kv_count:]
+    *arrived, held, scaled, near, sems = refs
     arrived, sums = arrived[:-4], arrived[-4:]
     if not first:
         arrived, old = arrived[:-4], arrived[-4:]
@@ -339,6 +350,24 @@
                 pltpu.make_async_copy(source.at[:, there], target, sems.at[2 * p + n])
             )
             copies[-1].start()
+    depth = width // shares
+    chunks = held.shape[1] // width
+    if kv_count == 1 and parts == 1 and kv[0].shape == held.shape:
+        held[...] = kv[0][...]
+    else:
+        each = kv_count // parts
+        for p in range(parts):
+            for r in range(shares):
+                source = kv[p * each + (r if each > 1 else 0)]
+                share = lax.rem(meta[2] + shares - r, shares) if each > 1 else r
+                start = p * width + share * depth
+                if each > 1:
+                    start = pl.multiple_of(start, depth)
+                base = source.shape[0] - chunks * depth * (1 if each > 1 else shares - r)
+                for c in range(chunks):
+                    held[pl.ds(start, depth), c * width : (c + 1) * width] = source[
+                        base + c * depth : base + (c + 1) * depth, :
+                    ]
     for copy in copies:
         copy.wait()
     if whole:
@@ -355,7 +384,7 @@
         scaled[:, here] = (values * gain[:, there]).astype(BF16)
     for n in range(2):
         here = slice(n * rows, (n + 1) * rows)
-        product = jnp.dot(scaled[here, :], kv[...], preferred_element_type=F32)
+        product = jnp.dot(scaled[here, :], held[...], preferred_element_type=F32)
         if first:
             sums[n][...] = product
             sums[2 + n][...] = jnp.broadcast_to(squares[here], (rows, HD))
@@ -437,15 +466,31 @@
     slot_count = 2 * pages_here
     chip_rows = 2 * rows_here
 
-    packed = shape(
-        (out_weight.shape[0] + kv_weight.shape[0] * cache_width // width, width), BF16
-    )
-    weights = call(pack_kernel, "pack", packed, [out_weight, kv_weight])
+    kv_share = kv_weight.shape[0] // pool_count
+    kv_rows = kv_share * cache_width // width
+    kv_own = lax.dynamic_slice_in_dim(kv_weight, me * kv_share, kv_share, 0)
+    packed = shape((out_weight.shape[0] + kv_rows, width), BF16)
+    weights = call(pack_kernel, "pack", packed, [out_weight, kv_own])
     last = 2 * steps - 1
     come = {-1: weights, 0: seq_xor(weights, seq_count, 1)}
+    shares = {}
+
+    def spread(n, *first):
+        part = call(
+            cut_kernel,
+            "cut",
+            shape((kv_rows, width), BF16),
+            [after(come[n], *first) if first else come[n]],
+        )
+        shares[n] = [part] + [pool_shift(part, pool_count, r) for r in range(1, pool_count)]
+        return shares[n]
 
     def serve(n, *first):
-        come[n] = ring_step(after(come[n - 2], *first) if first else come[n - 2], seq_count)
+        block = after(come[n - 2], *first) if first else come[n - 2]
+        if n - 2 in (3, 4):
+            whole = shape((out_weight.shape[0] + kv_rows * pool_count, width), BF16)
+            block = call(widen_kernel, "widen", whole, [meta, block, *shares[n - 2]])
+        come[n] = ring_step(block, seq_count)
         return come[n]
 
     def arrivals(g):
@@ -455,7 +500,15 @@
             return [come[last]]
         return [come[2 * g - 1], come[2 * g]]
 
+    def kv_of(g):
+        if g == 0:
+            return [kv_weight]
+        if g < 3:
+            return [part for n in (2 * g - 1, 2 * g) for part in shares[n]]
+        return arrivals(g)
+
     serve(1)
+
     by_share = pl.BlockSpec((rows, share * HD), lambda g: (0, g))
     cumul, update = pl.pallas_call(
         update_kernel,
@@ -482,6 +535,7 @@
     tagged = (heads // 2, HD + TAG, HD)
     plane_update = call(plane_kernel, "plane_state", shape(tagged, BF16), [meta, chip, chip_other])
     serve(3, plane_update)
+    spread(1, plane_update)
     table = after(block_table, plane_update)
     tables = [block_table] + [pool_shift(table, pool_count, r) for r in range(1, pool_count)]
     total = plane_update
@@ -494,7 +548,7 @@
             inners.append(
                 inner_part(1 + len(inners), 1, query, key_rows, value_rows, cumul)
             )
-            first = (come[2], *tables) if reach == 1 else (come[3],)
+            first = (come[2], *shares[1], *tables) if reach == 1 else (*shares[3], *shares[2])
             received[0] = after(received[0], inners[-1], *first)
         final = 2 * reach >= planes
         prefix, *rest = call(
@@ -505,6 +559,8 @@
         )
         if reach == 1:
             serve(4, prefix)
+            spread(2, prefix)
+            spread(3, prefix)
         before, total = [prefix], (rest or [None])[0]
         reach *= 2
     prefix_other = to_other_row(prefix, seq_count, 1)
@@ -516,7 +572,9 @@
         [shape((heads, HD, HD), BF16)] * 2,
         [meta, update, update_other, chip_other, prefix, prefix_other],
     )
-    other_state = after(seq_xor(away_state, seq_count, 1), come[4])
+    other_state = seq_xor(away_state, seq_count, 1)
+    spread(4, own_state)
+    other_state = after(other_state, come[4])
 
     mixed = pl.pallas_call(
         mixed_kernel,
@@ -533,7 +591,6 @@
         compiler_params=params(12),
     )(meta, in_hbm(query_rows), *inners, cumul, own_state, other_state)
     mixed_other = [seq_xor(part, seq_count, 1) for part in mixed]
-    serve(6, mixed[0])
     both = []
 
     def project(g, *first):
@@ -543,10 +600,10 @@
         joins = not both
         sources = [after(both[0], *first)] if both else [*mixed, *mixed_other]
         joined = [shape((pool_count, chip_rows, wide), BF16)] if joins else []
-        kv, mine, *away = call(
+        mine, *away = call(
             functools.partial(project_kernel, pool_count if joins else 0, count),
             "project",
-            [shape((out_wide, cache_width), BF16), shape((chip_rows, out_wide), F32)]
+            [shape((chip_rows, out_wide), F32)]
             + [shape((chip_rows, out_wide), BF16)] * (pool_count - 1)
             + joined,
             [*sources, *blocks],
@@ -555,10 +612,11 @@
         if joins:
             both.append(away.pop())
         arrived = [pool_shift(away[r - 1], pool_count, r) for r in range(1, pool_count)]
-        return mine, kv, arrived
+        return mine, arrived
 
     def cache(g, projected, sums, *first):
-        mine, kv, arrived = projected
+        mine, arrived = projected
+        kv = kv_of(g)
         count = len(starts[g])
         out_wide = count * width
         around = [residual, residual_other, norm_gain.reshape(1, -1)]
@@ -569,20 +627,26 @@
             ]
         return call(
             functools.partial(
-                cache_kernel, not sums, count, width, 3 + sum(len(x) for x in starts[:g])
+                cache_kernel,
+                not sums,
+                count,
+                pool_count,
+                len(kv),
+                width,
+                3 + sum(len(x) for x in starts[:g]),
             ),
             "cache",
             [shape((rows_here, cache_width), F32)] * 2 + [shape((rows_here, HD), F32)] * 2,
             [
                 meta,
                 after(mine, *first),
-                *around[:2],
-                kv,
-                around[2],
+                *around,
+                *kv,
                 *arrived,
                 *sums,
             ],
             [
+                pltpu.VMEM((out_wide, cache_width), BF16),
                 pltpu.VMEM((chip_rows, out_wide), BF16),
                 pltpu.VMEM((chip_rows, out_wide), BF16),
                 pltpu.SemaphoreType.DMA((2 * count,)),
@@ -608,6 +672,7 @@
         projected[g] = project(g, *done)
         done = (projected[g][0],)
         if g == 1:
+            serve(6, *done)
             continue
         if g == 2:
             done = (*done, residual_other)

time: 169 us -> 165 us (0.976)
  waiting for transfers between devices: 79.5 us -> 66.2 us
  starting transfers between devices: 31.9 us -> 41.7 us
    ppermute x7, waiting for transfers between devices: 28.3 us -> 9.83 us  [ring_step(): return lax.ppermute(value, 'seq', pairs)]
    ppermute x7 -> x11, starting transfers between devices: 7.45 us -> 15.3 us  [pool_shift(): lax.ppermute(value, 'pool', [(i, (i + by) % pool_count) for i in range(po...]
    ppermute x2, waiting for transfers between devices: 4.43 us -> 8.33 us  [to_other_row(): return lax.ppermute(value, 'seq', pairs)]
    ppermute x7 -> x11, waiting for transfers between devices: 38.8 us -> 41.6 us  [pool_shift(): lax.ppermute(value, 'pool', [(i, (i + by) % pool_count) for i in range(po...]
    unnamed x14 -> x18, local copies, waits for them, and re-layouts: 3.61 us -> 2.62 us
    pallas_call x18 -> x24, Pallas kernels: 29.2 us -> 29.3 us  [call(): pl.pallas_call(body, name=name, out_shape=out_shape, in_specs=[SMEM if a....]
  transfers between devices with their start and end apart: 27 -> 31, of which waited for: 14 -> 15; matrix products, arithmetic and copies ran while one was open for 0% -> 0% of each run, Pallas kernels for 29% -> 29%
where the time goes in v5:
time: 165 us; the launch traced here: 164 us
  waiting for transfers between devices  66.2 us (40%)
  Pallas kernels  52.2 us (32%)
  starting transfers between devices  41.7 us (25%)
  local copies, waits for them, and re-layouts  3.68 us (2%)
    ppermute x11, waiting for transfers between devices, pool_shift(): lax.ppermute(value, 'pool', [(i, (i + by) % pool_count) for i in range(po...  41.6 us
    pallas_call x24, Pallas kernels, call(): pl.pallas_call(body, name=name, out_shape=out_shape, in_specs=[SMEM if a....  29.3 us
    ppermute x7, starting transfers between devices, ring_step(): return lax.ppermute(value, 'seq', pairs)  18 us
    ppermute x11, starting transfers between devices, pool_shift(): lax.ppermute(value, 'pool', [(i, (i + by) % pool_count) for i in range(po...  15.3 us
    pallas_call x3, Pallas kernels, inner_part(): pl.pallas_call(inner_kernel, name='inner', grid=(count,), out_shape=shape...  11.8 us
    ppermute x7, waiting for transfers between devices, ring_step(): return lax.ppermute(value, 'seq', pairs)  9.83 us
    ppermute x2, waiting for transfers between devices, to_other_row(): return lax.ppermute(value, 'seq', pairs)  8.33 us
    ppermute x8, waiting for transfers between devices, seq_xor(): return lax.ppermute(value, 'seq', [(j, j ^ bits) for j in range(seq_count)])  6.36 us
  transfers between devices with their start and end apart: 31, of which 15 were waited for; matrix products, arithmetic and copies ran while one was open for 0% of the time, Pallas kernels for 29%

profile of v5, /device:TPU:0, one launch (start us, length us, event | category | flops | bytes accessed | tf_op | source)
XLA Modules:
  0.0 164.2 jit_solution(8280193476224633881)
XLA Ops:
  0.0 1.0 constant_dynamic-slice_fusion.kv
  1.0 1.2 copy-done.1
  2.3 0.5 collective-permute-start
  2.8 2.6 %collective-permute-start.3 = (bf16[2560,256]{1,0:T(8,128)(2,1)S(1)}, bf16[2560,256]{1,0:T(8,128)(2,1)S(1)}, u32[]{:S(2)}, u32[]{:S(2)}) collective-permute-start(bf16[2560,256]{1,0:T(8,128)(2,1)S(1)} %pack.1.refs_4_), channel_id=1, source_target_pairs={{0,8},{2,6},{8,16},{10,2},{16,24},{18,10},{24,28},{26,18},{28,20},... | collective-permute-start | bytes 3932168 | tf_op jit(solution)/shard_map/ppermute | solution.py:106
  5.5 5.7 %update.1 = (f32[4,4,512]{2,1,0:T(4,128)S(1)}, bf16[16,144,128]{2,1,0:T(8,128)(2,1)S(1)}) custom-call(bf16[512,2048]{1,0:T(8,128)(2,1)} %key.7, bf16[512,2048]{1,0:T(8,128)(2,1)} %value.7, f32[16,512]{1,0:T(8,128)S(1)} %copy-done.3), custom_call_target="tpu_custom_call" | custom-call | flops 1 | bytes 1 | tf_op jit(solution)/shard_map/update/pallas_call | solution.py:513
  11.2 1.1 copy-done.7
  12.5 1.9 %collective-permute-done.1.other = bf16[16,144,128]{2,1,0:T(8,128)(2,1)} collective-permute-done((bf16[16,144,128]{2,1,0:T(8,128)(2,1)S(1)}, bf16[16,144,128]{2,1,0:T(8,128)(2,1)}, u32[]{:S(2)}, u32[]{:S(2)}) %collective-permute-start.1) | collective-permute-done | bytes 589856 | tf_op jit(solution)/shard_map/ppermute | solution.py:56
  14.5 1.4 chip_state.1.own
  15.8 3.3 %collective-permute-start.2 = (bf16[16,144,128]{2,1,0:T(8,128)(2,1)S(1)}, bf16[16,144,128]{2,1,0:T(8,128)(2,1)S(1)}, u32[]{:S(2)}, u32[]{:S(2)}) collective-permute-start(bf16[16,144,128]{2,1,0:T(8,128)(2,1)S(1)} %chip_state.1.own), channel_id=1, source_target_pairs={{0,4},{6,2},{10,12},{12,10},{18,20},{20,18},{26,28},{28,26},{1,5},... | collective-permute-start | bytes 1769480 | tf_op jit(solution)/shard_map/ppermute | solution.py:69
  19.2 5.3 %inner.3.refs_0_ = f32[512,1024]{1,0:T(8,128)S(1)} custom-call(bf16[512,2048]{1,0:T(8,128)(2,1)} %query.5, bf16[512,2048]{1,0:T(8,128)(2,1)} %key.7, bf16[512,2048]{1,0:T(8,128)(2,1)} %value.7, f32[4,4,512]{2,1,0:T(4,128)S(1)} %get-tuple-element.72.cumul.refs_3_), custom_call_target="tpu_custom_call" | custom-call | flops 1 | bytes 1 | tf_op jit(solution)/shard_map/inner/pallas_call | solution.py:419
  24.5 8.3 %collective-permute-done.2.other.row_update = bf16[16,144,128]{2,1,0:T(8,128)(2,1)S(1)} collective-permute-done((bf16[16,144,128]{2,1,0:T(8,128)(2,1)S(1)}, bf16[16,144,128]{2,1,0:T(8,128)(2,1)S(1)}, u32[]{:S(2)}, u32[]{:S(2)}) %collective-permute-start.2) | collective-permute-done | bytes 589856 | tf_op jit(solution)/shard_map/ppermute | solution.py:69
  32.8 0.7 plane_state.1.refs_1_.refs_3_
  33.6 0.7 collective-permute-start.5
  34.3 1.6 collective-permute-start.7
  35.9 0.5 collective-permute-start.4
  36.4 3.3 %inner.4.refs_1_ = f32[512,512]{1,0:T(8,128)S(1)} custom-call(bf16[512,2048]{1,0:T(8,128)(2,1)} %query.5, bf16[512,2048]{1,0:T(8,128)(2,1)} %key.7, bf16[512,2048]{1,0:T(8,128)(2,1)} %value.7, f32[4,4,512]{2,1,0:T(4,128)S(1)} %get-tuple-element.72.cumul.refs_3_), custom_call_target="tpu_custom_call" | custom-call | flops 1 | bytes 1 | tf_op jit(solution)/shard_map/inner/pallas_call | solution.py:419
  39.7 2.3 %collective-permute-done.4.refs_1_ = s32[2,2]{1,0:T(2,128)S(1)} collective-permute-done((s32[2,2]{1,0:T(2,128)S(1)}, s32[2,2]{1,0:T(2,128)S(1)}, u32[]{:S(2)}, u32[]{:S(2)}) %collective-permute-start.4) | collective-permute-done | bytes 48 | tf_op jit(solution)/shard_map/ppermute | solution.py:89
  42.0 0.7 scan_state.2
  42.8 0.7 collective-permute-start.8
  43.5 0.7 collective-permute-start.12
  44.2 1.4 collective-permute-start.11
  45.6 9.8 %collective-permute-done.9.block.refs_1_ = bf16[2560,256]{1,0:T(8,128)(2,1)S(1)} collective-permute-done((bf16[2560,256]{1,0:T(8,128)(2,1)S(1)}, bf16[2560,256]{1,0:T(8,128)(2,1)S(1)}, u32[]{:S(2)}, u32[]{:S(2)}) %collective-permute-start.9) | collective-permute-done | bytes 1310752 | tf_op jit(solution)/shard_map/ppermute | solution.py:106
  55.4 2.1 %collective-permute-start.10 = (bf16[512,256]{1,0:T(8,128)(2,1)S(1)}, bf16[512,256]{1,0:T(8,128)(2,1)S(1)}, u32[]{:S(2)}, u32[]{:S(2)}) collective-permute-start(bf16[512,256]{1,0:T(8,128)(2,1)S(1)} %cut.5.refs_0_.refs_3_), channel_id=1, source_target_pairs={{0,1},{1,0},{2,3},{3,2},{4,5},{5,4},{6,7},{7,6},{8,9},{9,8},{10,11... | collective-permute-start | bytes 786440 | tf_op jit(solution)/shard_map/ppermute | solution.py:89
  57.5 3.3 %inner.5.refs_2_ = f32[512,512]{1,0:T(8,128)S(1)} custom-call(bf16[512,2048]{1,0:T(8,128)(2,1)} %query.5, bf16[512,2048]{1,0:T(8,128)(2,1)} %key.7, bf16[512,2048]{1,0:T(8,128)(2,1)} %value.7, f32[4,4,512]{2,1,0:T(4,128)S(1)} %get-tuple-element.72.cumul.refs_3_), custom_call_target="tpu_custom_call" | custom-call | flops 1 | bytes 1 | tf_op jit(solution)/shard_map/inner/pallas_call | solution.py:419
  60.8 2.1 %collective-permute-done.10.refs_1_.refs_4_ = bf16[512,256]{1,0:T(8,128)(2,1)S(1)} collective-permute-done((bf16[512,256]{1,0:T(8,128)(2,1)S(1)}, bf16[512,256]{1,0:T(8,128)(2,1)S(1)}, u32[]{:S(2)}, u32[]{:S(2)}) %collective-permute-start.10) | collective-permute-done | bytes 262176 | tf_op jit(solution)/shard_map/ppermute | solution.py:89
  62.8 0.7 scan_state.3.prefix
  63.6 0.7 collective-permute-start.13
  64.4 1.7 %start_state.1 = (bf16[16,128,128]{2,1,0:T(8,128)(2,1)S(1)}, bf16[16,128,128]{2,1,0:T(8,128)(2,1)S(1)}) custom-call(s32[11]{0:T(128)S(1)} %stack.47.meta, bf16[16,144,128]{2,1,0:T(8,128)(2,1)S(1)} %get-tuple-element.71.own, bf16[16,144,128]{2,1,0:T(8,128)(2,1)} %collective-permute-done.1.other, ...), custom_call_target="tpu_custom_call" | custom-call | flops 1 | bytes 1 | tf_op jit(solution)/shard_map/start_state/pallas_call | solution.py:28
  66.0 0.6 collective-permute-start.14
  66.6 0.6 widen.2
  67.2 10.9 %collective-permute-start.20 = (bf16[3072,256]{1,0:T(8,128)(2,1)S(1)}, bf16[3072,256]{1,0:T(8,128)(2,1)S(1)}, u32[]{:S(2)}, u32[]{:S(2)}) collective-permute-start(bf16[3072,256]{1,0:T(8,128)(2,1)S(1)} %widen.2), channel_id=1, source_target_pairs={{0,8},{2,6},{8,16},{10,2},{16,24},{18,10},{24,28},{26,18},{28,20},... | collective-permute-start | bytes 4718600 | tf_op jit(solution)/shard_map/ppermute | solution.py:106
  78.2 5.3 %mixed.1 = (bf16[256,2048]{1,0:T(8,128)(2,1)S(1)}, bf16[256,2048]{1,0:T(8,128)(2,1)S(1)}) custom-call(s32[11]{0:T(128)S(1)} %stack.47.meta, bf16[512,2048]{1,0:T(8,128)(2,1)} %query.5, f32[512,1024]{1,0:T(8,128)S(1)} %inner.3.refs_0_, f32[512,512]{1,0:T(8,128)S(1)} %inner.4.refs_1_, f32[512,512]{1,0:T(8,128)S(1)} %inner.5.refs_2_, ...), custom_call_target="tpu_custom_call" | custom-call | flops 1 | bytes 1 | tf_op jit(solution)/shard_map/mixed/pallas_call | solution.py:579
  83.5 0.5 collective-permute-start.17
  84.1 1.6 collective-permute-start.22
  85.6 0.6 collective-permute-done.16.refs_2_
  86.2 1.5 collective-permute-done.17.refs_3_
  87.7 1.3 project.5
  89.0 1.6 collective-permute-start.19
  90.5 2.3 %project.6 = (f32[512,512]{1,0:T(8,128)S(1)}, bf16[512,512]{1,0:T(8,128)(2,1)S(1)}) custom-call(bf16[2,512,2048]{2,1,0:T(8,128)(2,1)S(1)} %get-tuple-element.118.refs_0_, bf16[2560,256]{1,0:T(8,128)(2,1)S(1)} %collective-permute-done.3.block.refs_1_, bf16[2560,256]{1,0:T(8,128)(2,1)S(1)} %collective-permute-done.6.block.refs_2_), custom_call_target="tpu_custom_call" | custom-call | flops 1 | bytes 1 | tf_op jit(solution)/shard_map/project/pallas_call | solution.py:28
  93.0 0.6 widen.3
  93.6 1.0 collective-permute-start.23
  94.6 2.3 %project.7 = (f32[512,512]{1,0:T(8,128)S(1)}, bf16[512,512]{1,0:T(8,128)(2,1)S(1)}) custom-call(bf16[2,512,2048]{2,1,0:T(8,128)(2,1)S(1)} %get-tuple-element.118.refs_0_, bf16[2560,256]{1,0:T(8,128)(2,1)S(1)} %collective-permute-done.9.block.refs_1_, bf16[2560,256]{1,0:T(8,128)(2,1)S(1)} %collective-permute-done.15.refs_2_.block), custom_call_target="tpu_custom_call" | custom-call | flops 1 | bytes 1 | tf_op jit(solution)/shard_map/project/pallas_call | solution.py:28
  97.0 1.1 collective-permute-done.19.refs_4_
  98.3 2.0 %cache.5 = (f32[256,1024]{1,0:T(8,128)S(1)}, f32[256,1024]{1,0:T(8,128)S(1)}, f32[256,128]{1,0:T(8,128)S(1)}, f32[256,128]{1,0:T(8,128)S(1)}) custom-call(s32[11]{0:T(128)S(1)} %stack.47.meta, f32[512,256]{1,0:T(8,128)S(1)} %get-tuple-element.97.mine, bf16[256,4096]{1,0:T(8,128)(2,1)} %refs_0_.10, bf16[256,4096]{1,0:T(8,128)(2,1)} %copy-done.6, ...), custom_call_target="tpu_custom_call" | custom-call | flops 1 | bytes 1 | tf_op jit(solution)/shard_map/cache/pallas_call | solution.py:28
  100.3 3.3 %collective-permute-start.25 = (bf16[3072,256]{1,0:T(8,128)(2,1)S(1)}, bf16[3072,256]{1,0:T(8,128)(2,1)S(1)}, u32[]{:S(2)}, u32[]{:S(2)}) collective-permute-start(bf16[3072,256]{1,0:T(8,128)(2,1)S(1)} %collective-permute-done.20.refs_1_.refs_3_), channel_id=1, source_target_pairs={{0,8},{2,6},{8,16},{10,2},{16,24},{18,10},{24,28},{26,18},{28,20},... | collective-permute-start | bytes 4718600 | tf_op jit(solution)/shard_map/ppermute | solution.py:106
  103.6 1.5 collective-permute-start.21
  105.1 0.5 collective-permute-start.24
  105.6 12.8 %collective-permute-done.21.refs_7_ = bf16[512,512]{1,0:T(8,128)(2,1)S(1)} collective-permute-done((bf16[512,512]{1,0:T(8,128)(2,1)S(1)}, bf16[512,512]{1,0:T(8,128)(2,1)S(1)}, u32[]{:S(2)}, u32[]{:S(2)}) %collective-permute-start.21) | collective-permute-done | bytes 524320 | tf_op jit(solution)/shard_map/ppermute | solution.py:89
  118.5 2.5 %cache.6 = (f32[256,1024]{1,0:T(8,128)S(1)}, f32[256,1024]{1,0:T(8,128)S(1)}, f32[256,128]{1,0:T(8,128)S(1)}, f32[256,128]{1,0:T(8,128)S(1)}) custom-call(s32[11]{0:T(128)S(1)} %stack.47.meta, f32[512,512]{1,0:T(8,128)S(1)} %get-tuple-element.101.mine, bf16[256,4096]{1,0:T(8,128)(2,1)} %refs_0_.10, bf16[256,4096]{1,0:T(8,128)(2,1)} %copy-done.6, ...), custom_call_target="tpu_custom_call" | custom-call | flops 1 | bytes 1 | tf_op jit(solution)/shard_map/cache/pallas_call | solution.py:28
  121.0 2.3 %project.8 = (f32[512,512]{1,0:T(8,128)S(1)}, bf16[512,512]{1,0:T(8,128)(2,1)S(1)}) custom-call(bf16[2,512,2048]{2,1,0:T(8,128)(2,1)S(1)} %get-tuple-element.118.refs_0_, bf16[3072,256]{1,0:T(8,128)(2,1)S(1)} %collective-permute-done.20.refs_1_.refs_3_, bf16[3072,256]{1,0:T(8,128)(2,1)S(1)} %collective-permute-done.23.refs_2_.refs_4_), custom_call_target="tpu_custom_call" | custom-call | flops 1 | bytes 1 | tf_op jit(solution)/shard_map/project/pallas_call | solution.py:28
  123.3 1.6 collective-permute-start.26
  124.8 4.9 %collective-permute-done.24.refs_7_ = bf16[512,512]{1,0:T(8,128)(2,1)S(1)} collective-permute-done((bf16[512,512]{1,0:T(8,128)(2,1)S(1)}, bf16[512,512]{1,0:T(8,128)(2,1)S(1)}, u32[]{:S(2)}, u32[]{:S(2)}) %collective-permute-start.24) | collective-permute-done | bytes 524320 | tf_op jit(solution)/shard_map/ppermute | solution.py:89
  129.7 2.5 %cache.7 = (f32[256,1024]{1,0:T(8,128)S(1)}, f32[256,1024]{1,0:T(8,128)S(1)}, f32[256,128]{1,0:T(8,128)S(1)}, f32[256,128]{1,0:T(8,128)S(1)}) custom-call(s32[11]{0:T(128)S(1)} %stack.47.meta, f32[512,512]{1,0:T(8,128)S(1)} %get-tuple-element.111.mine, bf16[256,4096]{1,0:T(8,128)(2,1)} %refs_0_.10, bf16[256,4096]{1,0:T(8,128)(2,1)} %copy-done.6, ...), custom_call_target="tpu_custom_call" | custom-call | flops 1 | bytes 1 | tf_op jit(solution)/shard_map/cache/pallas_call | solution.py:28
  132.2 1.2 project.9
  133.4 1.6 collective-permute-start.27
  135.0 5.6 %collective-permute-done.26.refs_5_ = bf16[512,512]{1,0:T(8,128)(2,1)S(1)} collective-permute-done((bf16[512,512]{1,0:T(8,128)(2,1)S(1)}, bf16[512,512]{1,0:T(8,128)(2,1)S(1)}, u32[]{:S(2)}, u32[]{:S(2)}) %collective-permute-start.26) | collective-permute-done | bytes 524320 | tf_op jit(solution)/shard_map/ppermute | solution.py:89
  140.6 2.5 %cache.8 = (f32[256,1024]{1,0:T(8,128)S(1)}, f32[256,1024]{1,0:T(8,128)S(1)}, f32[256,128]{1,0:T(8,128)S(1)}, f32[256,128]{1,0:T(8,128)S(1)}) custom-call(s32[11]{0:T(128)S(1)} %stack.47.meta, f32[512,512]{1,0:T(8,128)S(1)} %get-tuple-element.120.mine, bf16[256,4096]{1,0:T(8,128)(2,1)} %refs_0_.10, bf16[256,4096]{1,0:T(8,128)(2,1)} %copy-done.6, ...), custom_call_target="tpu_custom_call" | custom-call | flops 1 | bytes 1 | tf_op jit(solution)/shard_map/cache/pallas_call | solution.py:28
  143.1 0.3 collective-permute-done.27.refs_4_
  143.4 2.0 %cache.9 = (f32[256,1024]{1,0:T(8,128)S(1)}, f32[256,1024]{1,0:T(8,128)S(1)}, f32[256,128]{1,0:T(8,128)S(1)}, f32[256,128]{1,0:T(8,128)S(1)}) custom-call(s32[11]{0:T(128)S(1)} %stack.47.meta, f32[512,256]{1,0:T(8,128)S(1)} %get-tuple-element.126.mine, bf16[256,4096]{1,0:T(8,128)(2,1)} %refs_0_.10, bf16[256,4096]{1,0:T(8,128)(2,1)} %copy-done.6, ...), custom_call_target="tpu_custom_call" | custom-call | flops 1 | bytes 1 | tf_op jit(solution)/shard_map/cache/pallas_call | solution.py:28
  145.5 0.5 collective-permute-start.29
  146.0 2.3 %collective-permute-done.29.square_in = f32[256,128]{1,0:T(8,128)S(1)} collective-permute-done((f32[256,128]{1,0:T(8,128)S(1)}, f32[256,128]{1,0:T(8,128)S(1)}, u32[]{:S(2)}, u32[]{:S(2)}) %collective-permute-start.29) | collective-permute-done | bytes 131104 | tf_op jit(solution)/shard_map/ppermute | solution.py:56
  148.5 1.5 collective-permute-start.30
  150.1 12.5 %collective-permute-done.30.refs_3_ = bf16[256,1024]{1,0:T(8,128)(2,1)S(1)} collective-permute-done((bf16[256,1024]{1,0:T(8,128)(2,1)S(1)}, bf16[256,1024]{1,0:T(8,128)(2,1)S(1)}, u32[]{:S(2)}, u32[]{:S(2)}) %collective-permute-start.30) | collective-permute-done | bytes 524320 | tf_op jit(solution)/shard_map/ppermute | solution.py:89
  162.6 1.6 place.1
  (47 shorter events, 1.4 us)
Async XLA Ops:
  0.0 5.5 %copy-start.3 = (f32[16,512]{1,0:T(8,128)S(1)}, f32[16,512]{1,0:T(8,128)}, u32[]{:S(2)}) copy-start(f32[16,512]{1,0:T(8,128)} %decay.1) | copy-start | bytes 98308
  1.0 1.2 copy-start.1
  2.3 8.9 %collective-permute-start = (bf16[2560,256]{1,0:T(8,128)(2,1)S(1)}, bf16[2560,256]{1,0:T(8,128)(2,1)S(1)}, u32[]{:S(2)}, u32[]{:S(2)}) collective-permute-start(bf16[2560,256]{1,0:T(8,128)(2,1)S(1)} %pack.1.refs_4_), channel_id=1, source_target_pairs={{0,2},{2,0},{4,6},{6,4},{8,10},{10,8},{12,14},{14,12},{16,18},{18,... | collective-permute-start | bytes 3932168 | tf_op jit(solution)/shard_map/ppermute | solution.py:56
  2.8 21.7 %collective-permute-start.3 = (bf16[2560,256]{1,0:T(8,128)(2,1)S(1)}, bf16[2560,256]{1,0:T(8,128)(2,1)S(1)}, u32[]{:S(2)}, u32[]{:S(2)}) collective-permute-start(bf16[2560,256]{1,0:T(8,128)(2,1)S(1)} %pack.1.refs_4_), channel_id=1, source_target_pairs={{0,8},{2,6},{8,16},{10,2},{16,24},{18,10},{24,28},{26,18},{28,20},... | collective-permute-start | bytes 3932168 | tf_op jit(solution)/shard_map/ppermute | solution.py:106
  11.2 1.1 copy-start.7
  12.3 2.1 %collective-permute-start.1 = (bf16[16,144,128]{2,1,0:T(8,128)(2,1)S(1)}, bf16[16,144,128]{2,1,0:T(8,128)(2,1)}, u32[]{:S(2)}, u32[]{:S(2)}) collective-permute-start(bf16[16,144,128]{2,1,0:T(8,128)(2,1)S(1)} %get-tuple-element.71.own), channel_id=1, source_target_pairs={{0,2},{2,0},{4,6},{6,4},{8,10},{10,8},{12,14},{14,12},{16,18},{18,... | collective-permute-start | bytes 1769480 | tf_op jit(solution)/shard_map/ppermute | solution.py:56
  12.5 6.6 %copy-start.8 = (bf16[2560,256]{1,0:T(8,128)(2,1)S(1)}, bf16[2560,256]{1,0:T(8,128)(2,1)}, u32[]{:S(2)}) copy-start(bf16[2560,256]{1,0:T(8,128)(2,1)} %copy-done.7) | copy-start | bytes 3932164
  15.8 17.0 %collective-permute-start.2 = (bf16[16,144,128]{2,1,0:T(8,128)(2,1)S(1)}, bf16[16,144,128]{2,1,0:T(8,128)(2,1)S(1)}, u32[]{:S(2)}, u32[]{:S(2)}) collective-permute-start(bf16[16,144,128]{2,1,0:T(8,128)(2,1)S(1)} %chip_state.1.own), channel_id=1, source_target_pairs={{0,4},{6,2},{10,12},{12,10},{18,20},{20,18},{26,28},{28,26},{1,5},... | collective-permute-start | bytes 1769480 | tf_op jit(solution)/shard_map/ppermute | solution.py:69
  19.1 22.9 %collective-permute-start.6 = (bf16[2560,256]{1,0:T(8,128)(2,1)S(1)}, bf16[2560,256]{1,0:T(8,128)(2,1)S(1)}, u32[]{:S(2)}, u32[]{:S(2)}) collective-permute-start(bf16[2560,256]{1,0:T(8,128)(2,1)S(1)} %copy-done.8), channel_id=1, source_target_pairs={{0,8},{2,6},{8,16},{10,2},{16,24},{18,10},{24,28},{26,18},{28,20},... | collective-permute-start | bytes 3932168 | tf_op jit(solution)/shard_map/ppermute | solution.py:106
  24.5 11.4 %copy-start.4 = (s32[2,2]{1,0:T(2,128)S(1)}, s32[2,2]{1,0:T(2,128)}, u32[]{:S(2)}) copy-start(s32[2,2]{1,0:T(2,128)} %refs_0_.11) | copy-start | bytes 52
  33.5 21.8 %collective-permute-start.9 = (bf16[2560,256]{1,0:T(8,128)(2,1)S(1)}, bf16[2560,256]{1,0:T(8,128)(2,1)S(1)}, u32[]{:S(2)}, u32[]{:S(2)}) collective-permute-start(bf16[2560,256]{1,0:T(8,128)(2,1)S(1)} %collective-permute-done.3.block.refs_1_), channel_id=1, source_target_pairs={{0,8},{2,6},{8,16},{10,2},{16,24},{18,10},{24,28},{26,18},{28,20},... | collective-permute-start | bytes 3932168 | tf_op jit(solution)/shard_map/ppermute | solution.py:106
  33.6 8.4 %collective-permute-start.5 = (bf16[8,144,128]{2,1,0:T(8,128)(2,1)S(1)}, bf16[8,144,128]{2,1,0:T(8,128)(2,1)S(1)}, u32[]{:S(2)}, u32[]{:S(2)}) collective-permute-start(bf16[8,144,128]{2,1,0:T(8,128)(2,1)S(1)} %plane_state.1.refs_1_.refs_3_), channel_id=1, source_target_pairs={{2,10},{4,12},{18,26},{20,28},{3,11},{5,13},{19,27},{21,29}} | collective-permute-start | bytes 884744 | tf_op jit(solution)/shard_map/ppermute | solution.py:75
  34.3 7.7 %collective-permute-start.7 = (bf16[512,256]{1,0:T(8,128)(2,1)S(1)}, bf16[512,256]{1,0:T(8,128)(2,1)S(1)}, u32[]{:S(2)}, u32[]{:S(2)}) collective-permute-start(bf16[512,256]{1,0:T(8,128)(2,1)S(1)} %cut.4.refs_3_), channel_id=1, source_target_pairs={{0,1},{1,0},{2,3},{3,2},{4,5},{5,4},{6,7},{7,6},{8,9},{9,8},{10,11... | collective-permute-start | bytes 786440 | tf_op jit(solution)/shard_map/ppermute | solution.py:89
  35.9 6.1 %collective-permute-start.4 = (s32[2,2]{1,0:T(2,128)S(1)}, s32[2,2]{1,0:T(2,128)S(1)}, u32[]{:S(2)}, u32[]{:S(2)}) collective-permute-start(s32[2,2]{1,0:T(2,128)S(1)} %copy-done.4), channel_id=1, source_target_pairs={{0,1},{1,0},{2,3},{3,2},{4,5},{5,4},{6,7},{7,6},{8,9},{9,8},{10,11... | collective-permute-start | bytes 56 | tf_op jit(solution)/shard_map/ppermute | solution.py:89
  42.7 35.5 %collective-permute-start.15 = (bf16[2560,256]{1,0:T(8,128)(2,1)S(1)}, bf16[2560,256]{1,0:T(8,128)(2,1)S(1)}, u32[]{:S(2)}, u32[]{:S(2)}) collective-permute-start(bf16[2560,256]{1,0:T(8,128)(2,1)S(1)} %collective-permute-done.6.block.refs_2_), channel_id=1, source_target_pairs={{0,8},{2,6},{8,16},{10,2},{16,24},{18,10},{24,28},{26,18},{28,20},... | collective-permute-start | bytes 3932168 | tf_op jit(solution)/shard_map/ppermute | solution.py:106
  42.8 18.0 %collective-permute-start.8 = (bf16[8,144,128]{2,1,0:T(8,128)(2,1)S(1)}, bf16[8,144,128]{2,1,0:T(8,128)(2,1)S(1)}, u32[]{:S(2)}, u32[]{:S(2)}) collective-permute-start(bf16[8,144,128]{2,1,0:T(8,128)(2,1)S(1)} %get-tuple-element.79), channel_id=1, source_target_pairs={{10,18},{12,20},{11,19},{13,21}} | collective-permute-start | bytes 884744 | tf_op jit(solution)/shard_map/ppermute | solution.py:75
  43.5 19.4 %collective-permute-start.12 = (bf16[8,144,128]{2,1,0:T(8,128)(2,1)S(1)}, bf16[8,144,128]{2,1,0:T(8,128)(2,1)S(1)}, u32[]{:S(2)}, u32[]{:S(2)}) collective-permute-start(bf16[8,144,128]{2,1,0:T(8,128)(2,1)S(1)} %get-tuple-element.79), channel_id=1, source_target_pairs={{10,26},{12,28},{11,27},{13,29}} | collective-permute-start | bytes 884744 | tf_op jit(solution)/shard_map/ppermute | solution.py:75
  44.2 16.6 %collective-permute-start.11 = (bf16[512,256]{1,0:T(8,128)(2,1)S(1)}, bf16[512,256]{1,0:T(8,128)(2,1)S(1)}, u32[]{:S(2)}, u32[]{:S(2)}) collective-permute-start(bf16[512,256]{1,0:T(8,128)(2,1)S(1)} %cut.6.refs_5_), channel_id=1, source_target_pairs={{0,1},{1,0},{2,3},{3,2},{4,5},{5,4},{6,7},{7,6},{8,9},{9,8},{10,11... | collective-permute-start | bytes 786440 | tf_op jit(solution)/shard_map/ppermute | solution.py:89
  55.4 8.9 %copy-start.5 = (bf16[256,4096]{1,0:T(8,128)(2,1)S(1)}, bf16[256,4096]{1,0:T(8,128)(2,1)}, u32[]{:S(2)}) copy-start(bf16[256,4096]{1,0:T(8,128)(2,1)} %refs_0_.10) | copy-start | bytes 6291460
  55.4 7.4 %collective-permute-start.10 = (bf16[512,256]{1,0:T(8,128)(2,1)S(1)}, bf16[512,256]{1,0:T(8,128)(2,1)S(1)}, u32[]{:S(2)}, u32[]{:S(2)}) collective-permute-start(bf16[512,256]{1,0:T(8,128)(2,1)S(1)} %cut.5.refs_0_.refs_3_), channel_id=1, source_target_pairs={{0,1},{1,0},{2,3},{3,2},{4,5},{5,4},{6,7},{7,6},{8,9},{9,8},{10,11... | collective-permute-start | bytes 786440 | tf_op jit(solution)/shard_map/ppermute | solution.py:89
  63.6 0.8 collective-permute-start.13
  64.3 32.7 %collective-permute-start.18 = (bf16[256,4096]{1,0:T(8,128)(2,1)S(1)}, bf16[256,4096]{1,0:T(8,128)(2,1)S(1)}, u32[]{:S(2)}, u32[]{:S(2)}) collective-permute-start(bf16[256,4096]{1,0:T(8,128)(2,1)S(1)} %copy-done.5), channel_id=1, source_target_pairs={{0,2},{2,0},{4,6},{6,4},{8,10},{10,8},{12,14},{14,12},{16,18},{18,... | collective-permute-start | bytes 6291464 | tf_op jit(solution)/shard_map/ppermute | solution.py:56
  66.0 12.1 %collective-permute-start.14 = (bf16[16,128,128]{2,1,0:T(8,128)(2,1)S(1)}, bf16[16,128,128]{2,1,0:T(8,128)(2,1)S(1)}, u32[]{:S(2)}, u32[]{:S(2)}) collective-permute-start(bf16[16,128,128]{2,1,0:T(8,128)(2,1)S(1)} %get-tuple-element.86), channel_id=1, source_target_pairs={{0,2},{2,0},{4,6},{6,4},{8,10},{10,8},{12,14},{14,12},{16,18},{18,... | collective-permute-start | bytes 1572872 | tf_op jit(solution)/shard_map/ppermute | solution.py:56
  67.2 33.1 %collective-permute-start.20 = (bf16[3072,256]{1,0:T(8,128)(2,1)S(1)}, bf16[3072,256]{1,0:T(8,128)(2,1)S(1)}, u32[]{:S(2)}, u32[]{:S(2)}) collective-permute-start(bf16[3072,256]{1,0:T(8,128)(2,1)S(1)} %widen.2), channel_id=1, source_target_pairs={{0,8},{2,6},{8,16},{10,2},{16,24},{18,10},{24,28},{26,18},{28,20},... | collective-permute-start | bytes 4718600 | tf_op jit(solution)/shard_map/ppermute | solution.py:106
  83.5 2.7 %collective-permute-start.16 = (bf16[256,2048]{1,0:T(8,128)(2,1)S(1)}, bf16[256,2048]{1,0:T(8,128)(2,1)S(1)}, u32[]{:S(2)}, u32[]{:S(2)}) collective-permute-start(bf16[256,2048]{1,0:T(8,128)(2,1)S(1)} %get-tuple-element.88.refs_0_), channel_id=1, source_target_pairs={{0,2},{2,0},{4,6},{6,4},{8,10},{10,8},{12,14},{14,12},{16,18},{18,... | collective-permute-start | bytes 3145736 | tf_op jit(solution)/shard_map/ppermute | solution.py:56
  83.5 4.1 %collective-permute-start.17 = (bf16[256,2048]{1,0:T(8,128)(2,1)S(1)}, bf16[256,2048]{1,0:T(8,128)(2,1)S(1)}, u32[]{:S(2)}, u32[]{:S(2)}) collective-permute-start(bf16[256,2048]{1,0:T(8,128)(2,1)S(1)} %get-tuple-element.89.refs_1_), channel_id=1, source_target_pairs={{0,2},{2,0},{4,6},{6,4},{8,10},{10,8},{12,14},{14,12},{16,18},{18,... | collective-permute-start | bytes 3145736 | tf_op jit(solution)/shard_map/ppermute | solution.py:56
  84.1 8.9 %collective-permute-start.22 = (bf16[512,256]{1,0:T(8,128)(2,1)S(1)}, bf16[512,256]{1,0:T(8,128)(2,1)S(1)}, u32[]{:S(2)}, u32[]{:S(2)}) collective-permute-start(bf16[512,256]{1,0:T(8,128)(2,1)S(1)} %cut.7.refs_0_.refs_5_), channel_id=1, source_target_pairs={{0,1},{1,0},{2,3},{3,2},{4,5},{5,4},{6,7},{7,6},{8,9},{9,8},{10,11... | collective-permute-start | bytes 786440 | tf_op jit(solution)/shard_map/ppermute | solution.py:89
  89.0 9.1 %collective-permute-start.19 = (bf16[512,256]{1,0:T(8,128)(2,1)S(1)}, bf16[512,256]{1,0:T(8,128)(2,1)S(1)}, u32[]{:S(2)}, u32[]{:S(2)}) collective-permute-start(bf16[512,256]{1,0:T(8,128)(2,1)S(1)} %get-tuple-element.98), channel_id=1, source_target_pairs={{0,1},{1,0},{2,3},{3,2},{4,5},{5,4},{6,7},{7,6},{8,9},{9,8},{10,11... | collective-permute-start | bytes 786440 | tf_op jit(solution)/shard_map/ppermute | solution.py:89
  93.6 4.7 %copy-start = (bf16[256,1024]{1,0:T(8,128)(2,1)S(1)}, bf16[256,1024]{1,0:T(8,128)(2,1)}, u32[]{:S(2)}) copy-start(bf16[256,1024]{1,0:T(8,128)(2,1)} %refs_3_.1) | copy-start | bytes 1572868
  93.6 4.7 %copy-start.2 = (f32[4096]{0:T(1024)S(1)}, f32[4096]{0:T(1024)}, u32[]{:S(2)}) copy-start(f32[4096]{0:T(1024)} %param.15) | copy-start | bytes 49156
  93.6 27.3 %collective-permute-start.23 = (bf16[3072,256]{1,0:T(8,128)(2,1)S(1)}, bf16[3072,256]{1,0:T(8,128)(2,1)S(1)}, u32[]{:S(2)}, u32[]{:S(2)}) collective-permute-start(bf16[3072,256]{1,0:T(8,128)(2,1)S(1)} %widen.3), channel_id=1, source_target_pairs={{0,8},{2,6},{8,16},{10,2},{16,24},{18,10},{24,28},{26,18},{28,20},... | collective-permute-start | bytes 4718600 | tf_op jit(solution)/shard_map/ppermute | solution.py:106
  97.0 1.3 copy-start.6
  100.3 31.9 %collective-permute-start.25 = (bf16[3072,256]{1,0:T(8,128)(2,1)S(1)}, bf16[3072,256]{1,0:T(8,128)(2,1)S(1)}, u32[]{:S(2)}, u32[]{:S(2)}) collective-permute-start(bf16[3072,256]{1,0:T(8,128)(2,1)S(1)} %collective-permute-done.20.refs_1_.refs_3_), channel_id=1, source_target_pairs={{0,8},{2,6},{8,16},{10,2},{16,24},{18,10},{24,28},{26,18},{28,20},... | collective-permute-start | bytes 4718600 | tf_op jit(solution)/shard_map/ppermute | solution.py:106
  103.6 14.9 %collective-permute-start.21 = (bf16[512,512]{1,0:T(8,128)(2,1)S(1)}, bf16[512,512]{1,0:T(8,128)(2,1)S(1)}, u32[]{:S(2)}, u32[]{:S(2)}) collective-permute-start(bf16[512,512]{1,0:T(8,128)(2,1)S(1)} %get-tuple-element.102), channel_id=1, source_target_pairs={{0,1},{1,0},{2,3},{3,2},{4,5},{5,4},{6,7},{7,6},{8,9},{9,8},{10,11... | collective-permute-start | bytes 1572872 | tf_op jit(solution)/shard_map/ppermute | solution.py:89
  105.1 24.6 %collective-permute-start.24 = (bf16[512,512]{1,0:T(8,128)(2,1)S(1)}, bf16[512,512]{1,0:T(8,128)(2,1)S(1)}, u32[]{:S(2)}, u32[]{:S(2)}) collective-permute-start(bf16[512,512]{1,0:T(8,128)(2,1)S(1)} %get-tuple-element.112), channel_id=1, source_target_pairs={{0,1},{1,0},{2,3},{3,2},{4,5},{5,4},{6,7},{7,6},{8,9},{9,8},{10,11... | collective-permute-start | bytes 1572872 | tf_op jit(solution)/shard_map/ppermute | solution.py:89
  123.3 17.3 %collective-permute-start.26 = (bf16[512,512]{1,0:T(8,128)(2,1)S(1)}, bf16[512,512]{1,0:T(8,128)(2,1)S(1)}, u32[]{:S(2)}, u32[]{:S(2)}) collective-permute-start(bf16[512,512]{1,0:T(8,128)(2,1)S(1)} %get-tuple-element.121), channel_id=1, source_target_pairs={{0,1},{1,0},{2,3},{3,2},{4,5},{5,4},{6,7},{7,6},{8,9},{9,8},{10,11... | collective-permute-start | bytes 1572872 | tf_op jit(solution)/shard_map/ppermute | solution.py:89
  133.4 10.0 %collective-permute-start.27 = (bf16[512,256]{1,0:T(8,128)(2,1)S(1)}, bf16[512,256]{1,0:T(8,128)(2,1)S(1)}, u32[]{:S(2)}, u32[]{:S(2)}) collective-permute-start(bf16[512,256]{1,0:T(8,128)(2,1)S(1)} %get-tuple-element.127), channel_id=1, source_target_pairs={{0,1},{1,0},{2,3},{3,2},{4,5},{5,4},{6,7},{7,6},{8,9},{9,8},{10,11... | collective-permute-start | bytes 786440 | tf_op jit(solution)/shard_map/ppermute | solution.py:89
  145.4 2.9 %collective-permute-start.28 = (f32[256,1024]{1,0:T(8,128)S(1)}, f32[256,1024]{1,0:T(8,128)S(1)}, u32[]{:S(2)}, u32[]{:S(2)}) collective-permute-start(f32[256,1024]{1,0:T(8,128)S(1)} %get-tuple-element.133), channel_id=1, source_target_pairs={{0,2},{2,0},{4,6},{6,4},{8,10},{10,8},{12,14},{14,12},{16,18},{18,... | collective-permute-start | bytes 3145736 | tf_op jit(solution)/shard_map/ppermute | solution.py:56
  145.5 2.8 %collective-permute-start.29 = (f32[256,128]{1,0:T(8,128)S(1)}, f32[256,128]{1,0:T(8,128)S(1)}, u32[]{:S(2)}, u32[]{:S(2)}) collective-permute-start(f32[256,128]{1,0:T(8,128)S(1)} %get-tuple-element.134), channel_id=1, source_target_pairs={{0,2},{2,0},{4,6},{6,4},{8,10},{10,8},{12,14},{14,12},{16,18},{18,... | collective-permute-start | bytes 393224 | tf_op jit(solution)/shard_map/ppermute | solution.py:56
  148.5 14.0 %collective-permute-start.30 = (bf16[256,1024]{1,0:T(8,128)(2,1)S(1)}, bf16[256,1024]{1,0:T(8,128)(2,1)S(1)}, u32[]{:S(2)}, u32[]{:S(2)}) collective-permute-start(bf16[256,1024]{1,0:T(8,128)(2,1)S(1)} %finish.1.refs_2_), channel_id=1, source_target_pairs={{0,1},{1,0},{2,3},{3,2},{4,5},{5,4},{6,7},{7,6},{8,9},{9,8},{10,11... | collective-permute-start | bytes 1572872 | tf_op jit(solution)/shard_map/ppermute | solution.py:89

commit v6 on v5

--- a/solution.py
+++ b/solution.py
@@ -672,15 +672,15 @@
         projected[g] = project(g, *done)
         done = (projected[g][0],)
         if g == 1:
-            serve(6, *done)
+            serve(6)
             continue
         if g == 2:
             done = (*done, residual_other)
             reduce_one()
+            reduce_one()
         for n in (2 * g + 3, 2 * g + 4):
             if n not in come and n <= last:
-                serve(n, come[n - 2], *done)
-                done = (*done, come[n - 2])
+                serve(n)
         while g < steps and cached <= g - 1:
             reduce_one()
     while cached <= steps:

time: 165 us -> 161 us (0.976)
  starting transfers between devices: 41.7 us -> 36.2 us
    ppermute x7, starting transfers between devices: 18 us -> 12 us  [ring_step(): return lax.ppermute(value, 'seq', pairs)]
    ppermute x7, waiting for transfers between devices: 9.83 us -> 12.3 us  [ring_step(): return lax.ppermute(value, 'seq', pairs)]
    ppermute x8, waiting for transfers between devices: 6.36 us -> 4.29 us  [seq_xor(): return lax.ppermute(value, 'seq', [(j, j ^ bits) for j in range(seq_count)])]
  transfers between devices with their start and end apart: 31 -> 31, of which waited for: 15 -> 13; matrix products, arithmetic and copies ran while one was open for 0% -> 0% of each run, Pallas kernels for 29% -> 30%
where the time goes in v6:
time: 161 us; the launch traced here: 159 us
  waiting for transfers between devices  67.1 us (42%)
  Pallas kernels  52.3 us (32%)
  starting transfers between devices  36.2 us (22%)
  local copies, waits for them, and re-layouts  3.41 us (2%)
    ppermute x11, waiting for transfers between devices, pool_shift(): lax.ppermute(value, 'pool', [(i, (i + by) % pool_count) for i in range(po...  42.1 us
    pallas_call x24, Pallas kernels, call(): pl.pallas_call(body, name=name, out_shape=out_shape, in_specs=[SMEM if a....  29.4 us
    ppermute x11, starting transfers between devices, pool_shift(): lax.ppermute(value, 'pool', [(i, (i + by) % pool_count) for i in range(po...  15.9 us
    ppermute x7, waiting for transfers between devices, ring_step(): return lax.ppermute(value, 'seq', pairs)  12.3 us
    ppermute x7, starting transfers between devices, ring_step(): return lax.ppermute(value, 'seq', pairs)  12 us
    pallas_call x3, Pallas kernels, inner_part(): pl.pallas_call(inner_kernel, name='inner', grid=(count,), out_shape=shape...  11.8 us
    ppermute x2, waiting for transfers between devices, to_other_row(): return lax.ppermute(value, 'seq', pairs)  8.33 us
    pallas_call x1, Pallas kernels, on_device(): pl.pallas_call(update_kernel, name='update', grid=(INNER,), out_shape=[sh...  5.74 us
  transfers between devices with their start and end apart: 31, of which 13 were waited for; matrix products, arithmetic and copies ran while one was open for 0% of the time, Pallas kernels for 30%

profile of v6, /device:TPU:0, one launch (start us, length us, event | category | flops | bytes accessed | tf_op | source)
XLA Modules:
  0.0 159.4 jit_solution(7703886563022686376)
XLA Ops:
  0.0 1.0 constant_dynamic-slice_fusion.kv
  1.0 1.2 copy-done.1
  2.3 0.5 collective-permute-start
  2.8 2.6 %collective-permute-start.3 = (bf16[2560,256]{1,0:T(8,128)(2,1)S(1)}, bf16[2560,256]{1,0:T(8,128)(2,1)S(1)}, u32[]{:S(2)}, u32[]{:S(2)}) collective-permute-start(bf16[2560,256]{1,0:T(8,128)(2,1)S(1)} %pack.1.refs_4_), channel_id=1, source_target_pairs={{0,8},{2,6},{8,16},{10,2},{16,24},{18,10},{24,28},{26,18},{28,20},... | collective-permute-start | bytes 3932168 | tf_op jit(solution)/shard_map/ppermute | solution.py:106
  5.5 5.7 %update.1 = (f32[4,4,512]{2,1,0:T(4,128)S(1)}, bf16[16,144,128]{2,1,0:T(8,128)(2,1)S(1)}) custom-call(bf16[512,2048]{1,0:T(8,128)(2,1)} %key.7, bf16[512,2048]{1,0:T(8,128)(2,1)} %value.7, f32[16,512]{1,0:T(8,128)S(1)} %copy-done.3), custom_call_target="tpu_custom_call" | custom-call | flops 1 | bytes 1 | tf_op jit(solution)/shard_map/update/pallas_call | solution.py:513
  11.2 1.1 copy-done.7
  12.5 1.9 %collective-permute-done.1.other = bf16[16,144,128]{2,1,0:T(8,128)(2,1)} collective-permute-done((bf16[16,144,128]{2,1,0:T(8,128)(2,1)S(1)}, bf16[16,144,128]{2,1,0:T(8,128)(2,1)}, u32[]{:S(2)}, u32[]{:S(2)}) %collective-permute-start.1) | collective-permute-done | bytes 589856 | tf_op jit(solution)/shard_map/ppermute | solution.py:56
  14.5 1.4 chip_state.1.own
  15.8 3.3 %collective-permute-start.2 = (bf16[16,144,128]{2,1,0:T(8,128)(2,1)S(1)}, bf16[16,144,128]{2,1,0:T(8,128)(2,1)S(1)}, u32[]{:S(2)}, u32[]{:S(2)}) collective-permute-start(bf16[16,144,128]{2,1,0:T(8,128)(2,1)S(1)} %chip_state.1.own), channel_id=1, source_target_pairs={{0,4},{6,2},{10,12},{12,10},{18,20},{20,18},{26,28},{28,26},{1,5},... | collective-permute-start | bytes 1769480 | tf_op jit(solution)/shard_map/ppermute | solution.py:69
  19.2 5.3 %inner.3.refs_0_ = f32[512,1024]{1,0:T(8,128)S(1)} custom-call(bf16[512,2048]{1,0:T(8,128)(2,1)} %query.5, bf16[512,2048]{1,0:T(8,128)(2,1)} %key.7, bf16[512,2048]{1,0:T(8,128)(2,1)} %value.7, f32[4,4,512]{2,1,0:T(4,128)S(1)} %get-tuple-element.70.cumul.refs_3_), custom_call_target="tpu_custom_call" | custom-call | flops 1 | bytes 1 | tf_op jit(solution)/shard_map/inner/pallas_call | solution.py:419
  24.5 8.3 %collective-permute-done.2.other.row_update = bf16[16,144,128]{2,1,0:T(8,128)(2,1)S(1)} collective-permute-done((bf16[16,144,128]{2,1,0:T(8,128)(2,1)S(1)}, bf16[16,144,128]{2,1,0:T(8,128)(2,1)S(1)}, u32[]{:S(2)}, u32[]{:S(2)}) %collective-permute-start.2) | collective-permute-done | bytes 589856 | tf_op jit(solution)/shard_map/ppermute | solution.py:69
  32.8 0.7 plane_state.1.refs_1_.refs_3_
  33.6 0.7 collective-permute-start.5
  34.3 1.6 collective-permute-start.7
  35.9 0.5 collective-permute-start.4
  36.4 3.3 %inner.4.refs_1_ = f32[512,512]{1,0:T(8,128)S(1)} custom-call(bf16[512,2048]{1,0:T(8,128)(2,1)} %query.5, bf16[512,2048]{1,0:T(8,128)(2,1)} %key.7, bf16[512,2048]{1,0:T(8,128)(2,1)} %value.7, f32[4,4,512]{2,1,0:T(4,128)S(1)} %get-tuple-element.70.cumul.refs_3_), custom_call_target="tpu_custom_call" | custom-call | flops 1 | bytes 1 | tf_op jit(solution)/shard_map/inner/pallas_call | solution.py:419
  39.7 2.3 %collective-permute-done.4.refs_1_ = s32[2,2]{1,0:T(2,128)S(1)} collective-permute-done((s32[2,2]{1,0:T(2,128)S(1)}, s32[2,2]{1,0:T(2,128)S(1)}, u32[]{:S(2)}, u32[]{:S(2)}) %collective-permute-start.4) | collective-permute-done | bytes 48 | tf_op jit(solution)/shard_map/ppermute | solution.py:89
  42.0 0.7 scan_state.2
  42.7 0.7 collective-permute-start.8
  43.4 0.7 collective-permute-start.12
  44.2 1.4 collective-permute-start.11
  45.6 9.8 %collective-permute-done.9.block.refs_1_ = bf16[2560,256]{1,0:T(8,128)(2,1)S(1)} collective-permute-done((bf16[2560,256]{1,0:T(8,128)(2,1)S(1)}, bf16[2560,256]{1,0:T(8,128)(2,1)S(1)}, u32[]{:S(2)}, u32[]{:S(2)}) %collective-permute-start.9) | collective-permute-done | bytes 1310752 | tf_op jit(solution)/shard_map/ppermute | solution.py:106
  55.4 2.1 %collective-permute-start.10 = (bf16[512,256]{1,0:T(8,128)(2,1)S(1)}, bf16[512,256]{1,0:T(8,128)(2,1)S(1)}, u32[]{:S(2)}, u32[]{:S(2)}) collective-permute-start(bf16[512,256]{1,0:T(8,128)(2,1)S(1)} %cut.5.refs_0_.refs_3_), channel_id=1, source_target_pairs={{0,1},{1,0},{2,3},{3,2},{4,5},{5,4},{6,7},{7,6},{8,9},{9,8},{10,11... | collective-permute-start | bytes 786440 | tf_op jit(solution)/shard_map/ppermute | solution.py:89
  57.5 3.3 %inner.5.refs_2_ = f32[512,512]{1,0:T(8,128)S(1)} custom-call(bf16[512,2048]{1,0:T(8,128)(2,1)} %query.5, bf16[512,2048]{1,0:T(8,128)(2,1)} %key.7, bf16[512,2048]{1,0:T(8,128)(2,1)} %value.7, f32[4,4,512]{2,1,0:T(4,128)S(1)} %get-tuple-element.70.cumul.refs_3_), custom_call_target="tpu_custom_call" | custom-call | flops 1 | bytes 1 | tf_op jit(solution)/shard_map/inner/pallas_call | solution.py:419
  60.8 2.1 %collective-permute-done.10.refs_1_.refs_4_ = bf16[512,256]{1,0:T(8,128)(2,1)S(1)} collective-permute-done((bf16[512,256]{1,0:T(8,128)(2,1)S(1)}, bf16[512,256]{1,0:T(8,128)(2,1)S(1)}, u32[]{:S(2)}, u32[]{:S(2)}) %collective-permute-start.10) | collective-permute-done | bytes 262176 | tf_op jit(solution)/shard_map/ppermute | solution.py:89
  62.8 0.7 scan_state.3.prefix
  63.6 0.6 widen.2
  64.2 0.9 collective-permute-start.21
  65.2 0.7 collective-permute-start.13
  65.8 0.4 collective-permute-start.18
  66.3 1.7 %start_state.1 = (bf16[16,128,128]{2,1,0:T(8,128)(2,1)S(1)}, bf16[16,128,128]{2,1,0:T(8,128)(2,1)S(1)}) custom-call(s32[11]{0:T(128)S(1)} %stack.47.meta, bf16[16,144,128]{2,1,0:T(8,128)(2,1)S(1)} %get-tuple-element.69.own, bf16[16,144,128]{2,1,0:T(8,128)(2,1)} %collective-permute-done.1.other, ...), custom_call_target="tpu_custom_call" | custom-call | flops 1 | bytes 1 | tf_op jit(solution)/shard_map/start_state/pallas_call | solution.py:28
  67.9 0.2 collective-permute-start.14
  68.2 1.3 collective-permute-done.15.refs_2_.block
  69.5 2.1 %collective-permute-start.22 = (bf16[512,256]{1,0:T(8,128)(2,1)S(1)}, bf16[512,256]{1,0:T(8,128)(2,1)S(1)}, u32[]{:S(2)}, u32[]{:S(2)}) collective-permute-start(bf16[512,256]{1,0:T(8,128)(2,1)S(1)} %cut.7.refs_0_.refs_5_), channel_id=1, source_target_pairs={{0,1},{1,0},{2,3},{3,2},{4,5},{5,4},{6,7},{7,6},{8,9},{9,8},{10,11... | collective-permute-start | bytes 786440 | tf_op jit(solution)/shard_map/ppermute | solution.py:89
  71.5 5.3 %mixed.1 = (bf16[256,2048]{1,0:T(8,128)(2,1)S(1)}, bf16[256,2048]{1,0:T(8,128)(2,1)S(1)}) custom-call(s32[11]{0:T(128)S(1)} %stack.47.meta, bf16[512,2048]{1,0:T(8,128)(2,1)} %query.5, f32[512,1024]{1,0:T(8,128)S(1)} %inner.3.refs_0_, f32[512,512]{1,0:T(8,128)S(1)} %inner.4.refs_1_, f32[512,512]{1,0:T(8,128)S(1)} %inner.5.refs_2_, ...), custom_call_target="tpu_custom_call" | custom-call | flops 1 | bytes 1 | tf_op jit(solution)/shard_map/mixed/pallas_call | solution.py:579
  76.9 0.5 collective-permute-start.17
  77.4 0.6 widen.3
  78.0 7.0 %collective-permute-start.23 = (bf16[3072,256]{1,0:T(8,128)(2,1)S(1)}, bf16[3072,256]{1,0:T(8,128)(2,1)S(1)}, u32[]{:S(2)}, u32[]{:S(2)}) collective-permute-start(bf16[3072,256]{1,0:T(8,128)(2,1)S(1)} %widen.3), channel_id=1, source_target_pairs={{0,8},{2,6},{8,16},{10,2},{16,24},{18,10},{24,28},{26,18},{28,20},... | collective-permute-start | bytes 4718600 | tf_op jit(solution)/shard_map/ppermute | solution.py:106
  85.1 1.2 collective-permute-done.21.refs_1_.refs_3_
  86.3 1.2 collective-permute-start.25
  87.5 1.3 project.5
  88.8 2.3 %project.6 = (f32[512,512]{1,0:T(8,128)S(1)}, bf16[512,512]{1,0:T(8,128)(2,1)S(1)}) custom-call(bf16[2,512,2048]{2,1,0:T(8,128)(2,1)S(1)} %get-tuple-element.114.refs_0_, bf16[2560,256]{1,0:T(8,128)(2,1)S(1)} %collective-permute-done.3.block.refs_1_, bf16[2560,256]{1,0:T(8,128)(2,1)S(1)} %collective-permute-done.6.block.refs_2_), custom_call_target="tpu_custom_call" | custom-call | flops 1 | bytes 1 | tf_op jit(solution)/shard_map/project/pallas_call | solution.py:28
  91.1 1.6 collective-permute-start.20
  92.7 0.5 collective-permute-start.19
  93.2 2.3 %project.7 = (f32[512,512]{1,0:T(8,128)S(1)}, bf16[512,512]{1,0:T(8,128)(2,1)S(1)}) custom-call(bf16[2,512,2048]{2,1,0:T(8,128)(2,1)S(1)} %get-tuple-element.114.refs_0_, bf16[2560,256]{1,0:T(8,128)(2,1)S(1)} %collective-permute-done.9.block.refs_1_, bf16[2560,256]{1,0:T(8,128)(2,1)S(1)} %collective-permute-done.15.refs_2_.block), custom_call_target="tpu_custom_call" | custom-call | flops 1 | bytes 1 | tf_op jit(solution)/shard_map/project/pallas_call | solution.py:28
  95.5 1.6 collective-permute-start.24
  97.1 14.5 %collective-permute-done.19.refs_4_ = bf16[512,256]{1,0:T(8,128)(2,1)S(1)} collective-permute-done((bf16[512,256]{1,0:T(8,128)(2,1)S(1)}, bf16[512,256]{1,0:T(8,128)(2,1)S(1)}, u32[]{:S(2)}, u32[]{:S(2)}) %collective-permute-start.19) | collective-permute-done | bytes 262176 | tf_op jit(solution)/shard_map/ppermute | solution.py:89
  111.6 2.0 %cache.5 = (f32[256,1024]{1,0:T(8,128)S(1)}, f32[256,1024]{1,0:T(8,128)S(1)}, f32[256,128]{1,0:T(8,128)S(1)}, f32[256,128]{1,0:T(8,128)S(1)}) custom-call(s32[11]{0:T(128)S(1)} %stack.47.meta, f32[512,256]{1,0:T(8,128)S(1)} %get-tuple-element.95.mine, bf16[256,4096]{1,0:T(8,128)(2,1)} %refs_0_.10, bf16[256,4096]{1,0:T(8,128)(2,1)} %copy-done.6, ...), custom_call_target="tpu_custom_call" | custom-call | flops 1 | bytes 1 | tf_op jit(solution)/shard_map/cache/pallas_call | solution.py:28
  113.6 2.5 %cache.6 = (f32[256,1024]{1,0:T(8,128)S(1)}, f32[256,1024]{1,0:T(8,128)S(1)}, f32[256,128]{1,0:T(8,128)S(1)}, f32[256,128]{1,0:T(8,128)S(1)}) custom-call(s32[11]{0:T(128)S(1)} %stack.47.meta, f32[512,512]{1,0:T(8,128)S(1)} %get-tuple-element.98.mine, bf16[256,4096]{1,0:T(8,128)(2,1)} %refs_0_.10, bf16[256,4096]{1,0:T(8,128)(2,1)} %copy-done.6, ...), custom_call_target="tpu_custom_call" | custom-call | flops 1 | bytes 1 | tf_op jit(solution)/shard_map/cache/pallas_call | solution.py:28
  116.1 2.3 %project.8 = (f32[512,512]{1,0:T(8,128)S(1)}, bf16[512,512]{1,0:T(8,128)(2,1)S(1)}) custom-call(bf16[2,512,2048]{2,1,0:T(8,128)(2,1)S(1)} %get-tuple-element.114.refs_0_, bf16[3072,256]{1,0:T(8,128)(2,1)S(1)} %collective-permute-done.21.refs_1_.refs_3_, bf16[3072,256]{1,0:T(8,128)(2,1)S(1)} %collective-permute-done.23.refs_2_.refs_4_), custom_call_target="tpu_custom_call" | custom-call | flops 1 | bytes 1 | tf_op jit(solution)/shard_map/project/pallas_call | solution.py:28
  118.5 1.6 collective-permute-start.26
  120.0 2.8 %collective-permute-done.24.refs_7_ = bf16[512,512]{1,0:T(8,128)(2,1)S(1)} collective-permute-done((bf16[512,512]{1,0:T(8,128)(2,1)S(1)}, bf16[512,512]{1,0:T(8,128)(2,1)S(1)}, u32[]{:S(2)}, u32[]{:S(2)}) %collective-permute-start.24) | collective-permute-done | bytes 524320 | tf_op jit(solution)/shard_map/ppermute | solution.py:89
  122.8 2.4 %cache.7 = (f32[256,1024]{1,0:T(8,128)S(1)}, f32[256,1024]{1,0:T(8,128)S(1)}, f32[256,128]{1,0:T(8,128)S(1)}, f32[256,128]{1,0:T(8,128)S(1)}) custom-call(s32[11]{0:T(128)S(1)} %stack.47.meta, f32[512,512]{1,0:T(8,128)S(1)} %get-tuple-element.108.mine, bf16[256,4096]{1,0:T(8,128)(2,1)} %refs_0_.10, bf16[256,4096]{1,0:T(8,128)(2,1)} %copy-done.6, ...), custom_call_target="tpu_custom_call" | custom-call | flops 1 | bytes 1 | tf_op jit(solution)/shard_map/cache/pallas_call | solution.py:28
  125.3 1.2 project.9
  126.5 1.6 collective-permute-start.27
  128.1 6.0 %collective-permute-done.26.refs_5_ = bf16[512,512]{1,0:T(8,128)(2,1)S(1)} collective-permute-done((bf16[512,512]{1,0:T(8,128)(2,1)S(1)}, bf16[512,512]{1,0:T(8,128)(2,1)S(1)}, u32[]{:S(2)}, u32[]{:S(2)}) %collective-permute-start.26) | collective-permute-done | bytes 524320 | tf_op jit(solution)/shard_map/ppermute | solution.py:89
  134.1 2.5 %cache.8 = (f32[256,1024]{1,0:T(8,128)S(1)}, f32[256,1024]{1,0:T(8,128)S(1)}, f32[256,128]{1,0:T(8,128)S(1)}, f32[256,128]{1,0:T(8,128)S(1)}) custom-call(s32[11]{0:T(128)S(1)} %stack.47.meta, f32[512,512]{1,0:T(8,128)S(1)} %get-tuple-element.116.mine, bf16[256,4096]{1,0:T(8,128)(2,1)} %refs_0_.10, bf16[256,4096]{1,0:T(8,128)(2,1)} %copy-done.6, ...), custom_call_target="tpu_custom_call" | custom-call | flops 1 | bytes 1 | tf_op jit(solution)/shard_map/cache/pallas_call | solution.py:28
  136.5 2.0 %collective-permute-done.27.refs_4_ = bf16[512,256]{1,0:T(8,128)(2,1)S(1)} collective-permute-done((bf16[512,256]{1,0:T(8,128)(2,1)S(1)}, bf16[512,256]{1,0:T(8,128)(2,1)S(1)}, u32[]{:S(2)}, u32[]{:S(2)}) %collective-permute-start.27) | collective-permute-done | bytes 262176 | tf_op jit(solution)/shard_map/ppermute | solution.py:89
  138.6 2.0 %cache.9 = (f32[256,1024]{1,0:T(8,128)S(1)}, f32[256,1024]{1,0:T(8,128)S(1)}, f32[256,128]{1,0:T(8,128)S(1)}, f32[256,128]{1,0:T(8,128)S(1)}) custom-call(s32[11]{0:T(128)S(1)} %stack.47.meta, f32[512,256]{1,0:T(8,128)S(1)} %get-tuple-element.122.mine, bf16[256,4096]{1,0:T(8,128)(2,1)} %refs_0_.10, bf16[256,4096]{1,0:T(8,128)(2,1)} %copy-done.6, ...), custom_call_target="tpu_custom_call" | custom-call | flops 1 | bytes 1 | tf_op jit(solution)/shard_map/cache/pallas_call | solution.py:28
  140.7 0.5 collective-permute-start.29
  141.2 2.3 %collective-permute-done.29.square_in = f32[256,128]{1,0:T(8,128)S(1)} collective-permute-done((f32[256,128]{1,0:T(8,128)S(1)}, f32[256,128]{1,0:T(8,128)S(1)}, u32[]{:S(2)}, u32[]{:S(2)}) %collective-permute-start.29) | collective-permute-done | bytes 131104 | tf_op jit(solution)/shard_map/ppermute | solution.py:56
  143.7 1.6 collective-permute-start.30
  145.2 12.5 %collective-permute-done.30.refs_3_ = bf16[256,1024]{1,0:T(8,128)(2,1)S(1)} collective-permute-done((bf16[256,1024]{1,0:T(8,128)(2,1)S(1)}, bf16[256,1024]{1,0:T(8,128)(2,1)S(1)}, u32[]{:S(2)}, u32[]{:S(2)}) %collective-permute-start.30) | collective-permute-done | bytes 524320 | tf_op jit(solution)/shard_map/ppermute | solution.py:89
  157.7 1.7 %place.1 = bf16[4,128,1024]{2,1,0:T(8,128)(2,1)} custom-call(s32[11]{0:T(128)S(1)} %stack.47.meta, s32[2,2]{1,0:T(2,128)S(1)} %copy-done.4, s32[2,2]{1,0:T(2,128)S(1)} %collective-permute-done.4.refs_1_, bf16[256,1024]{1,0:T(8,128)(2,1)S(1)} %finish.1.refs_2_, bf16[256,1024]{1,0:T(8,128)(2,1)S(1)} %collective-permute-done.30.refs_3_), custom_call_target="tpu_custom_call" | custom-call | flops 1 | bytes 1 | tf_op jit(solution)/shard_map/place/pallas_call | solution.py:28
  (47 shorter events, 0.9 us)
Async XLA Ops:
  0.0 5.5 %copy-start.3 = (f32[16,512]{1,0:T(8,128)S(1)}, f32[16,512]{1,0:T(8,128)}, u32[]{:S(2)}) copy-start(f32[16,512]{1,0:T(8,128)} %decay.1) | copy-start | bytes 98308
  1.0 1.2 copy-start.1
  2.3 8.9 %collective-permute-start = (bf16[2560,256]{1,0:T(8,128)(2,1)S(1)}, bf16[2560,256]{1,0:T(8,128)(2,1)S(1)}, u32[]{:S(2)}, u32[]{:S(2)}) collective-permute-start(bf16[2560,256]{1,0:T(8,128)(2,1)S(1)} %pack.1.refs_4_), channel_id=1, source_target_pairs={{0,2},{2,0},{4,6},{6,4},{8,10},{10,8},{12,14},{14,12},{16,18},{18,... | collective-permute-start | bytes 3932168 | tf_op jit(solution)/shard_map/ppermute | solution.py:56
  2.8 21.7 %collective-permute-start.3 = (bf16[2560,256]{1,0:T(8,128)(2,1)S(1)}, bf16[2560,256]{1,0:T(8,128)(2,1)S(1)}, u32[]{:S(2)}, u32[]{:S(2)}) collective-permute-start(bf16[2560,256]{1,0:T(8,128)(2,1)S(1)} %pack.1.refs_4_), channel_id=1, source_target_pairs={{0,8},{2,6},{8,16},{10,2},{16,24},{18,10},{24,28},{26,18},{28,20},... | collective-permute-start | bytes 3932168 | tf_op jit(solution)/shard_map/ppermute | solution.py:106
  11.2 1.1 copy-start.7
  12.3 2.1 %collective-permute-start.1 = (bf16[16,144,128]{2,1,0:T(8,128)(2,1)S(1)}, bf16[16,144,128]{2,1,0:T(8,128)(2,1)}, u32[]{:S(2)}, u32[]{:S(2)}) collective-permute-start(bf16[16,144,128]{2,1,0:T(8,128)(2,1)S(1)} %get-tuple-element.69.own), channel_id=1, source_target_pairs={{0,2},{2,0},{4,6},{6,4},{8,10},{10,8},{12,14},{14,12},{16,18},{18,... | collective-permute-start | bytes 1769480 | tf_op jit(solution)/shard_map/ppermute | solution.py:56
  12.5 6.6 %copy-start.8 = (bf16[2560,256]{1,0:T(8,128)(2,1)S(1)}, bf16[2560,256]{1,0:T(8,128)(2,1)}, u32[]{:S(2)}) copy-start(bf16[2560,256]{1,0:T(8,128)(2,1)} %copy-done.7) | copy-start | bytes 3932164
  15.8 17.0 %collective-permute-start.2 = (bf16[16,144,128]{2,1,0:T(8,128)(2,1)S(1)}, bf16[16,144,128]{2,1,0:T(8,128)(2,1)S(1)}, u32[]{:S(2)}, u32[]{:S(2)}) collective-permute-start(bf16[16,144,128]{2,1,0:T(8,128)(2,1)S(1)} %chip_state.1.own), channel_id=1, source_target_pairs={{0,4},{6,2},{10,12},{12,10},{18,20},{20,18},{26,28},{28,26},{1,5},... | collective-permute-start | bytes 1769480 | tf_op jit(solution)/shard_map/ppermute | solution.py:69
  19.1 22.9 %collective-permute-start.6 = (bf16[2560,256]{1,0:T(8,128)(2,1)S(1)}, bf16[2560,256]{1,0:T(8,128)(2,1)S(1)}, u32[]{:S(2)}, u32[]{:S(2)}) collective-permute-start(bf16[2560,256]{1,0:T(8,128)(2,1)S(1)} %copy-done.8), channel_id=1, source_target_pairs={{0,8},{2,6},{8,16},{10,2},{16,24},{18,10},{24,28},{26,18},{28,20},... | collective-permute-start | bytes 3932168 | tf_op jit(solution)/shard_map/ppermute | solution.py:106
  24.5 11.4 %copy-start.4 = (s32[2,2]{1,0:T(2,128)S(1)}, s32[2,2]{1,0:T(2,128)}, u32[]{:S(2)}) copy-start(s32[2,2]{1,0:T(2,128)} %refs_0_.11) | copy-start | bytes 52
  33.5 21.8 %collective-permute-start.9 = (bf16[2560,256]{1,0:T(8,128)(2,1)S(1)}, bf16[2560,256]{1,0:T(8,128)(2,1)S(1)}, u32[]{:S(2)}, u32[]{:S(2)}) collective-permute-start(bf16[2560,256]{1,0:T(8,128)(2,1)S(1)} %collective-permute-done.3.block.refs_1_), channel_id=1, source_target_pairs={{0,8},{2,6},{8,16},{10,2},{16,24},{18,10},{24,28},{26,18},{28,20},... | collective-permute-start | bytes 3932168 | tf_op jit(solution)/shard_map/ppermute | solution.py:106
  33.6 8.4 %collective-permute-start.5 = (bf16[8,144,128]{2,1,0:T(8,128)(2,1)S(1)}, bf16[8,144,128]{2,1,0:T(8,128)(2,1)S(1)}, u32[]{:S(2)}, u32[]{:S(2)}) collective-permute-start(bf16[8,144,128]{2,1,0:T(8,128)(2,1)S(1)} %plane_state.1.refs_1_.refs_3_), channel_id=1, source_target_pairs={{2,10},{4,12},{18,26},{20,28},{3,11},{5,13},{19,27},{21,29}} | collective-permute-start | bytes 884744 | tf_op jit(solution)/shard_map/ppermute | solution.py:75
  34.3 7.7 %collective-permute-start.7 = (bf16[512,256]{1,0:T(8,128)(2,1)S(1)}, bf16[512,256]{1,0:T(8,128)(2,1)S(1)}, u32[]{:S(2)}, u32[]{:S(2)}) collective-permute-start(bf16[512,256]{1,0:T(8,128)(2,1)S(1)} %cut.4.refs_3_), channel_id=1, source_target_pairs={{0,1},{1,0},{2,3},{3,2},{4,5},{5,4},{6,7},{7,6},{8,9},{9,8},{10,11... | collective-permute-start | bytes 786440 | tf_op jit(solution)/shard_map/ppermute | solution.py:89
  35.9 6.1 %collective-permute-start.4 = (s32[2,2]{1,0:T(2,128)S(1)}, s32[2,2]{1,0:T(2,128)S(1)}, u32[]{:S(2)}, u32[]{:S(2)}) collective-permute-start(s32[2,2]{1,0:T(2,128)S(1)} %copy-done.4), channel_id=1, source_target_pairs={{0,1},{1,0},{2,3},{3,2},{4,5},{5,4},{6,7},{7,6},{8,9},{9,8},{10,11... | collective-permute-start | bytes 56 | tf_op jit(solution)/shard_map/ppermute | solution.py:89
  42.7 18.0 %collective-permute-start.8 = (bf16[8,144,128]{2,1,0:T(8,128)(2,1)S(1)}, bf16[8,144,128]{2,1,0:T(8,128)(2,1)S(1)}, u32[]{:S(2)}, u32[]{:S(2)}) collective-permute-start(bf16[8,144,128]{2,1,0:T(8,128)(2,1)S(1)} %get-tuple-element.77), channel_id=1, source_target_pairs={{10,18},{12,20},{11,19},{13,21}} | collective-permute-start | bytes 884744 | tf_op jit(solution)/shard_map/ppermute | solution.py:75
  43.4 19.4 %collective-permute-start.12 = (bf16[8,144,128]{2,1,0:T(8,128)(2,1)S(1)}, bf16[8,144,128]{2,1,0:T(8,128)(2,1)S(1)}, u32[]{:S(2)}, u32[]{:S(2)}) collective-permute-start(bf16[8,144,128]{2,1,0:T(8,128)(2,1)S(1)} %get-tuple-element.77), channel_id=1, source_target_pairs={{10,26},{12,28},{11,27},{13,29}} | collective-permute-start | bytes 884744 | tf_op jit(solution)/shard_map/ppermute | solution.py:75
  44.1 25.3 %collective-permute-start.15 = (bf16[2560,256]{1,0:T(8,128)(2,1)S(1)}, bf16[2560,256]{1,0:T(8,128)(2,1)S(1)}, u32[]{:S(2)}, u32[]{:S(2)}) collective-permute-start(bf16[2560,256]{1,0:T(8,128)(2,1)S(1)} %collective-permute-done.6.block.refs_2_), channel_id=1, source_target_pairs={{0,8},{2,6},{8,16},{10,2},{16,24},{18,10},{24,28},{26,18},{28,20},... | collective-permute-start | bytes 3932168 | tf_op jit(solution)/shard_map/ppermute | solution.py:106
  44.2 16.6 %collective-permute-start.11 = (bf16[512,256]{1,0:T(8,128)(2,1)S(1)}, bf16[512,256]{1,0:T(8,128)(2,1)S(1)}, u32[]{:S(2)}, u32[]{:S(2)}) collective-permute-start(bf16[512,256]{1,0:T(8,128)(2,1)S(1)} %cut.6.refs_5_), channel_id=1, source_target_pairs={{0,1},{1,0},{2,3},{3,2},{4,5},{5,4},{6,7},{7,6},{8,9},{9,8},{10,11... | collective-permute-start | bytes 786440 | tf_op jit(solution)/shard_map/ppermute | solution.py:89
  55.4 7.4 %collective-permute-start.10 = (bf16[512,256]{1,0:T(8,128)(2,1)S(1)}, bf16[512,256]{1,0:T(8,128)(2,1)S(1)}, u32[]{:S(2)}, u32[]{:S(2)}) collective-permute-start(bf16[512,256]{1,0:T(8,128)(2,1)S(1)} %cut.5.refs_0_.refs_3_), channel_id=1, source_target_pairs={{0,1},{1,0},{2,3},{3,2},{4,5},{5,4},{6,7},{7,6},{8,9},{9,8},{10,11... | collective-permute-start | bytes 786440 | tf_op jit(solution)/shard_map/ppermute | solution.py:89
  63.6 2.3 %copy-start.5 = (bf16[256,4096]{1,0:T(8,128)(2,1)S(1)}, bf16[256,4096]{1,0:T(8,128)(2,1)}, u32[]{:S(2)}) copy-start(bf16[256,4096]{1,0:T(8,128)(2,1)} %refs_0_.10) | copy-start | bytes 6291460
  64.2 22.1 %collective-permute-start.21 = (bf16[3072,256]{1,0:T(8,128)(2,1)S(1)}, bf16[3072,256]{1,0:T(8,128)(2,1)S(1)}, u32[]{:S(2)}, u32[]{:S(2)}) collective-permute-start(bf16[3072,256]{1,0:T(8,128)(2,1)S(1)} %widen.2), channel_id=1, source_target_pairs={{0,8},{2,6},{8,16},{10,2},{16,24},{18,10},{24,28},{26,18},{28,20},... | collective-permute-start | bytes 4718600 | tf_op jit(solution)/shard_map/ppermute | solution.py:106
  65.2 1.1 collective-permute-start.13
  65.8 29.7 %collective-permute-start.18 = (bf16[256,4096]{1,0:T(8,128)(2,1)S(1)}, bf16[256,4096]{1,0:T(8,128)(2,1)S(1)}, u32[]{:S(2)}, u32[]{:S(2)}) collective-permute-start(bf16[256,4096]{1,0:T(8,128)(2,1)S(1)} %copy-done.5), channel_id=1, source_target_pairs={{0,2},{2,0},{4,6},{6,4},{8,10},{10,8},{12,14},{14,12},{16,18},{18,... | collective-permute-start | bytes 6291464 | tf_op jit(solution)/shard_map/ppermute | solution.py:56
  67.9 3.6 %collective-permute-start.14 = (bf16[16,128,128]{2,1,0:T(8,128)(2,1)S(1)}, bf16[16,128,128]{2,1,0:T(8,128)(2,1)S(1)}, u32[]{:S(2)}, u32[]{:S(2)}) collective-permute-start(bf16[16,128,128]{2,1,0:T(8,128)(2,1)S(1)} %get-tuple-element.84), channel_id=1, source_target_pairs={{0,2},{2,0},{4,6},{6,4},{8,10},{10,8},{12,14},{14,12},{16,18},{18,... | collective-permute-start | bytes 1572872 | tf_op jit(solution)/shard_map/ppermute | solution.py:56
  69.5 7.9 %collective-permute-start.22 = (bf16[512,256]{1,0:T(8,128)(2,1)S(1)}, bf16[512,256]{1,0:T(8,128)(2,1)S(1)}, u32[]{:S(2)}, u32[]{:S(2)}) collective-permute-start(bf16[512,256]{1,0:T(8,128)(2,1)S(1)} %cut.7.refs_0_.refs_5_), channel_id=1, source_target_pairs={{0,1},{1,0},{2,3},{3,2},{4,5},{5,4},{6,7},{7,6},{8,9},{9,8},{10,11... | collective-permute-start | bytes 786440 | tf_op jit(solution)/shard_map/ppermute | solution.py:89
  76.8 10.7 %collective-permute-start.16 = (bf16[256,2048]{1,0:T(8,128)(2,1)S(1)}, bf16[256,2048]{1,0:T(8,128)(2,1)S(1)}, u32[]{:S(2)}, u32[]{:S(2)}) collective-permute-start(bf16[256,2048]{1,0:T(8,128)(2,1)S(1)} %get-tuple-element.86.refs_0_), channel_id=1, source_target_pairs={{0,2},{2,0},{4,6},{6,4},{8,10},{10,8},{12,14},{14,12},{16,18},{18,... | collective-permute-start | bytes 3145736 | tf_op jit(solution)/shard_map/ppermute | solution.py:56
  76.9 10.6 %collective-permute-start.17 = (bf16[256,2048]{1,0:T(8,128)(2,1)S(1)}, bf16[256,2048]{1,0:T(8,128)(2,1)S(1)}, u32[]{:S(2)}, u32[]{:S(2)}) collective-permute-start(bf16[256,2048]{1,0:T(8,128)(2,1)S(1)} %get-tuple-element.87.refs_1_), channel_id=1, source_target_pairs={{0,2},{2,0},{4,6},{6,4},{8,10},{10,8},{12,14},{14,12},{16,18},{18,... | collective-permute-start | bytes 3145736 | tf_op jit(solution)/shard_map/ppermute | solution.py:56
  78.0 38.1 %collective-permute-start.23 = (bf16[3072,256]{1,0:T(8,128)(2,1)S(1)}, bf16[3072,256]{1,0:T(8,128)(2,1)S(1)}, u32[]{:S(2)}, u32[]{:S(2)}) collective-permute-start(bf16[3072,256]{1,0:T(8,128)(2,1)S(1)} %widen.3), channel_id=1, source_target_pairs={{0,8},{2,6},{8,16},{10,2},{16,24},{18,10},{24,28},{26,18},{28,20},... | collective-permute-start | bytes 4718600 | tf_op jit(solution)/shard_map/ppermute | solution.py:106
  86.3 39.0 %collective-permute-start.25 = (bf16[3072,256]{1,0:T(8,128)(2,1)S(1)}, bf16[3072,256]{1,0:T(8,128)(2,1)S(1)}, u32[]{:S(2)}, u32[]{:S(2)}) collective-permute-start(bf16[3072,256]{1,0:T(8,128)(2,1)S(1)} %collective-permute-done.21.refs_1_.refs_3_), channel_id=1, source_target_pairs={{0,8},{2,6},{8,16},{10,2},{16,24},{18,10},{24,28},{26,18},{28,20},... | collective-permute-start | bytes 4718600 | tf_op jit(solution)/shard_map/ppermute | solution.py:106
  91.1 22.5 %collective-permute-start.20 = (bf16[512,512]{1,0:T(8,128)(2,1)S(1)}, bf16[512,512]{1,0:T(8,128)(2,1)S(1)}, u32[]{:S(2)}, u32[]{:S(2)}) collective-permute-start(bf16[512,512]{1,0:T(8,128)(2,1)S(1)} %get-tuple-element.99), channel_id=1, source_target_pairs={{0,1},{1,0},{2,3},{3,2},{4,5},{5,4},{6,7},{7,6},{8,9},{9,8},{10,11... | collective-permute-start | bytes 1572872 | tf_op jit(solution)/shard_map/ppermute | solution.py:89
  92.7 18.9 %collective-permute-start.19 = (bf16[512,256]{1,0:T(8,128)(2,1)S(1)}, bf16[512,256]{1,0:T(8,128)(2,1)S(1)}, u32[]{:S(2)}, u32[]{:S(2)}) collective-permute-start(bf16[512,256]{1,0:T(8,128)(2,1)S(1)} %get-tuple-element.96), channel_id=1, source_target_pairs={{0,1},{1,0},{2,3},{3,2},{4,5},{5,4},{6,7},{7,6},{8,9},{9,8},{10,11... | collective-permute-start | bytes 786440 | tf_op jit(solution)/shard_map/ppermute | solution.py:89
  93.2 18.4 %copy-start = (bf16[256,1024]{1,0:T(8,128)(2,1)S(1)}, bf16[256,1024]{1,0:T(8,128)(2,1)}, u32[]{:S(2)}) copy-start(bf16[256,1024]{1,0:T(8,128)(2,1)} %refs_3_.1) | copy-start | bytes 1572868
  93.2 18.4 %copy-start.2 = (f32[4096]{0:T(1024)S(1)}, f32[4096]{0:T(1024)}, u32[]{:S(2)}) copy-start(f32[4096]{0:T(1024)} %param.15) | copy-start | bytes 49156
  95.5 16.1 %copy-start.6 = (bf16[256,4096]{1,0:T(8,128)(2,1)}, bf16[256,4096]{1,0:T(8,128)(2,1)S(1)}, u32[]{:S(2)}) copy-start(bf16[256,4096]{1,0:T(8,128)(2,1)S(1)} %collective-permute-done.18.refs_1_) | copy-start | bytes 6291460
  95.5 27.3 %collective-permute-start.24 = (bf16[512,512]{1,0:T(8,128)(2,1)S(1)}, bf16[512,512]{1,0:T(8,128)(2,1)S(1)}, u32[]{:S(2)}, u32[]{:S(2)}) collective-permute-start(bf16[512,512]{1,0:T(8,128)(2,1)S(1)} %get-tuple-element.109), channel_id=1, source_target_pairs={{0,1},{1,0},{2,3},{3,2},{4,5},{5,4},{6,7},{7,6},{8,9},{9,8},{10,11... | collective-permute-start | bytes 1572872 | tf_op jit(solution)/shard_map/ppermute | solution.py:89
  118.5 15.6 %collective-permute-start.26 = (bf16[512,512]{1,0:T(8,128)(2,1)S(1)}, bf16[512,512]{1,0:T(8,128)(2,1)S(1)}, u32[]{:S(2)}, u32[]{:S(2)}) collective-permute-start(bf16[512,512]{1,0:T(8,128)(2,1)S(1)} %get-tuple-element.117), channel_id=1, source_target_pairs={{0,1},{1,0},{2,3},{3,2},{4,5},{5,4},{6,7},{7,6},{8,9},{9,8},{10,11... | collective-permute-start | bytes 1572872 | tf_op jit(solution)/shard_map/ppermute | solution.py:89
  126.5 12.0 %collective-permute-start.27 = (bf16[512,256]{1,0:T(8,128)(2,1)S(1)}, bf16[512,256]{1,0:T(8,128)(2,1)S(1)}, u32[]{:S(2)}, u32[]{:S(2)}) collective-permute-start(bf16[512,256]{1,0:T(8,128)(2,1)S(1)} %get-tuple-element.123), channel_id=1, source_target_pairs={{0,1},{1,0},{2,3},{3,2},{4,5},{5,4},{6,7},{7,6},{8,9},{9,8},{10,11... | collective-permute-start | bytes 786440 | tf_op jit(solution)/shard_map/ppermute | solution.py:89
  140.6 2.9 %collective-permute-start.28 = (f32[256,1024]{1,0:T(8,128)S(1)}, f32[256,1024]{1,0:T(8,128)S(1)}, u32[]{:S(2)}, u32[]{:S(2)}) collective-permute-start(f32[256,1024]{1,0:T(8,128)S(1)} %get-tuple-element.129), channel_id=1, source_target_pairs={{0,2},{2,0},{4,6},{6,4},{8,10},{10,8},{12,14},{14,12},{16,18},{18,... | collective-permute-start | bytes 3145736 | tf_op jit(solution)/shard_map/ppermute | solution.py:56
  140.7 2.8 %collective-permute-start.29 = (f32[256,128]{1,0:T(8,128)S(1)}, f32[256,128]{1,0:T(8,128)S(1)}, u32[]{:S(2)}, u32[]{:S(2)}) collective-permute-start(f32[256,128]{1,0:T(8,128)S(1)} %get-tuple-element.130), channel_id=1, source_target_pairs={{0,2},{2,0},{4,6},{6,4},{8,10},{10,8},{12,14},{14,12},{16,18},{18,... | collective-permute-start | bytes 393224 | tf_op jit(solution)/shard_map/ppermute | solution.py:56
  143.7 14.0 %collective-permute-start.30 = (bf16[256,1024]{1,0:T(8,128)(2,1)S(1)}, bf16[256,1024]{1,0:T(8,128)(2,1)S(1)}, u32[]{:S(2)}, u32[]{:S(2)}) collective-permute-start(bf16[256,1024]{1,0:T(8,128)(2,1)S(1)} %finish.1.refs_2_), channel_id=1, source_target_pairs={{0,1},{1,0},{2,3},{3,2},{4,5},{5,4},{6,7},{7,6},{8,9},{9,8},{10,11... | collective-permute-start | bytes 1572872 | tf_op jit(solution)/shard_map/ppermute | solution.py:89

commit v7 on v6

--- a/solution.py
+++ b/solution.py
@@ -386,16 +386,16 @@
         here = slice(n * rows, (n + 1) * rows)
         product = jnp.dot(scaled[here, :], held[...], preferred_element_type=F32)
         if first:
-            sums[n][...] = product
+            sums[n][...] = product.astype(sums[n].dtype)
             sums[2 + n][...] = jnp.broadcast_to(squares[here], (rows, HD))
         else:
-            sums[n][...] = old[n][...] + product
+            sums[n][...] = (old[n][...] + product).astype(sums[n].dtype)
             sums[2 + n][...] = old[2 + n][...] + squares[here]
 
 
 def finish_kernel(features, total, square, total_in, square_in, out):
     mean = (square[:, :1] + square_in[:, :1]) / features
-    out[...] = ((total[...] + total_in[...]) * lax.rsqrt(mean + EPS)).astype(BF16)
+    out[...] = ((total[...] + total_in[...].astype(F32)) * lax.rsqrt(mean + EPS)).astype(BF16)
 
 
 def place_kernel(pool_count, meta, *refs):
@@ -636,7 +636,11 @@
                 3 + sum(len(x) for x in starts[:g]),
             ),
             "cache",
-            [shape((rows_here, cache_width), F32)] * 2 + [shape((rows_here, HD), F32)] * 2,
+            [
+                shape((rows_here, cache_width), F32),
+                shape((rows_here, cache_width), BF16 if g == steps else F32),
+            ]
+            + [shape((rows_here, HD), F32)] * 2,
             [
                 meta,
                 after(mine, *first),

time: 161 us -> 160 us (level)
  no operation moved by 1% of the time
where the time goes in v7:
time: 160 us; the launch traced here: 159 us
  waiting for transfers between devices  66.3 us (41%)
  Pallas kernels  52.2 us (33%)
  starting transfers between devices  36.2 us (23%)
  local copies, waits for them, and re-layouts  3.41 us (2%)
    ppermute x11, waiting for transfers between devices, pool_shift(): lax.ppermute(value, 'pool', [(i, (i + by) % pool_count) for i in range(po...  42.1 us
    pallas_call x24, Pallas kernels, call(): pl.pallas_call(body, name=name, out_shape=out_shape, in_specs=[SMEM if a....  29.4 us
    ppermute x11, starting transfers between devices, pool_shift(): lax.ppermute(value, 'pool', [(i, (i + by) % pool_count) for i in range(po...  15.9 us
    ppermute x7, waiting for transfers between devices, ring_step(): return lax.ppermute(value, 'seq', pairs)  12.3 us
    ppermute x7, starting transfers between devices, ring_step(): return lax.ppermute(value, 'seq', pairs)  12 us
    pallas_call x3, Pallas kernels, inner_part(): pl.pallas_call(inner_kernel, name='inner', grid=(count,), out_shape=shape...  11.8 us
    ppermute x2, waiting for transfers between devices, to_other_row(): return lax.ppermute(value, 'seq', pairs)  8.33 us
    pallas_call x1, Pallas kernels, on_device(): pl.pallas_call(update_kernel, name='update', grid=(INNER,), out_shape=[sh...  5.74 us
  transfers between devices with their start and end apart: 31, of which 13 were waited for; matrix products, arithmetic and copies ran while one was open for 0% of the time, Pallas kernels for 30%

profile of v7, /device:TPU:0, one launch (start us, length us, event | category | flops | bytes accessed | tf_op | source)
XLA Modules:
  0.0 158.6 jit_solution(1693773230689000280)
XLA Ops:
  0.0 1.0 constant_dynamic-slice_fusion.kv
  1.0 1.2 copy-done.1
  2.3 0.5 collective-permute-start
  2.8 2.6 %collective-permute-start.3 = (bf16[2560,256]{1,0:T(8,128)(2,1)S(1)}, bf16[2560,256]{1,0:T(8,128)(2,1)S(1)}, u32[]{:S(2)}, u32[]{:S(2)}) collective-permute-start(bf16[2560,256]{1,0:T(8,128)(2,1)S(1)} %pack.1.refs_4_), channel_id=1, source_target_pairs={{0,8},{2,6},{8,16},{10,2},{16,24},{18,10},{24,28},{26,18},{28,20},... | collective-permute-start | bytes 3932168 | tf_op jit(solution)/shard_map/ppermute | solution.py:106
  5.5 5.7 %update.1 = (f32[4,4,512]{2,1,0:T(4,128)S(1)}, bf16[16,144,128]{2,1,0:T(8,128)(2,1)S(1)}) custom-call(bf16[512,2048]{1,0:T(8,128)(2,1)} %key.7, bf16[512,2048]{1,0:T(8,128)(2,1)} %value.7, f32[16,512]{1,0:T(8,128)S(1)} %copy-done.3), custom_call_target="tpu_custom_call" | custom-call | flops 1 | bytes 1 | tf_op jit(solution)/shard_map/update/pallas_call | solution.py:513
  11.2 1.1 copy-done.7
  12.5 1.9 %collective-permute-done.1.other = bf16[16,144,128]{2,1,0:T(8,128)(2,1)} collective-permute-done((bf16[16,144,128]{2,1,0:T(8,128)(2,1)S(1)}, bf16[16,144,128]{2,1,0:T(8,128)(2,1)}, u32[]{:S(2)}, u32[]{:S(2)}) %collective-permute-start.1) | collective-permute-done | bytes 589856 | tf_op jit(solution)/shard_map/ppermute | solution.py:56
  14.5 1.4 chip_state.1.own
  15.8 3.3 %collective-permute-start.2 = (bf16[16,144,128]{2,1,0:T(8,128)(2,1)S(1)}, bf16[16,144,128]{2,1,0:T(8,128)(2,1)S(1)}, u32[]{:S(2)}, u32[]{:S(2)}) collective-permute-start(bf16[16,144,128]{2,1,0:T(8,128)(2,1)S(1)} %chip_state.1.own), channel_id=1, source_target_pairs={{0,4},{6,2},{10,12},{12,10},{18,20},{20,18},{26,28},{28,26},{1,5},... | collective-permute-start | bytes 1769480 | tf_op jit(solution)/shard_map/ppermute | solution.py:69
  19.2 5.3 %inner.3.refs_0_ = f32[512,1024]{1,0:T(8,128)S(1)} custom-call(bf16[512,2048]{1,0:T(8,128)(2,1)} %query.5, bf16[512,2048]{1,0:T(8,128)(2,1)} %key.7, bf16[512,2048]{1,0:T(8,128)(2,1)} %value.7, f32[4,4,512]{2,1,0:T(4,128)S(1)} %get-tuple-element.70.cumul.refs_3_), custom_call_target="tpu_custom_call" | custom-call | flops 1 | bytes 1 | tf_op jit(solution)/shard_map/inner/pallas_call | solution.py:419
  24.5 8.3 %collective-permute-done.2.other.row_update = bf16[16,144,128]{2,1,0:T(8,128)(2,1)S(1)} collective-permute-done((bf16[16,144,128]{2,1,0:T(8,128)(2,1)S(1)}, bf16[16,144,128]{2,1,0:T(8,128)(2,1)S(1)}, u32[]{:S(2)}, u32[]{:S(2)}) %collective-permute-start.2) | collective-permute-done | bytes 589856 | tf_op jit(solution)/shard_map/ppermute | solution.py:69
  32.8 0.7 plane_state.1.refs_1_.refs_3_
  33.6 0.7 collective-permute-start.5
  34.3 1.6 collective-permute-start.7
  35.9 0.5 collective-permute-start.4
  36.4 3.3 %inner.4.refs_1_ = f32[512,512]{1,0:T(8,128)S(1)} custom-call(bf16[512,2048]{1,0:T(8,128)(2,1)} %query.5, bf16[512,2048]{1,0:T(8,128)(2,1)} %key.7, bf16[512,2048]{1,0:T(8,128)(2,1)} %value.7, f32[4,4,512]{2,1,0:T(4,128)S(1)} %get-tuple-element.70.cumul.refs_3_), custom_call_target="tpu_custom_call" | custom-call | flops 1 | bytes 1 | tf_op jit(solution)/shard_map/inner/pallas_call | solution.py:419
  39.7 2.3 %collective-permute-done.4.refs_1_ = s32[2,2]{1,0:T(2,128)S(1)} collective-permute-done((s32[2,2]{1,0:T(2,128)S(1)}, s32[2,2]{1,0:T(2,128)S(1)}, u32[]{:S(2)}, u32[]{:S(2)}) %collective-permute-start.4) | collective-permute-done | bytes 48 | tf_op jit(solution)/shard_map/ppermute | solution.py:89
  42.0 0.7 scan_state.2
  42.7 0.7 collective-permute-start.8
  43.4 0.7 collective-permute-start.12
  44.2 1.4 collective-permute-start.11
  45.6 9.8 %collective-permute-done.9.block.refs_1_ = bf16[2560,256]{1,0:T(8,128)(2,1)S(1)} collective-permute-done((bf16[2560,256]{1,0:T(8,128)(2,1)S(1)}, bf16[2560,256]{1,0:T(8,128)(2,1)S(1)}, u32[]{:S(2)}, u32[]{:S(2)}) %collective-permute-start.9) | collective-permute-done | bytes 1310752 | tf_op jit(solution)/shard_map/ppermute | solution.py:106
  55.4 2.1 %collective-permute-start.10 = (bf16[512,256]{1,0:T(8,128)(2,1)S(1)}, bf16[512,256]{1,0:T(8,128)(2,1)S(1)}, u32[]{:S(2)}, u32[]{:S(2)}) collective-permute-start(bf16[512,256]{1,0:T(8,128)(2,1)S(1)} %cut.5.refs_0_.refs_3_), channel_id=1, source_target_pairs={{0,1},{1,0},{2,3},{3,2},{4,5},{5,4},{6,7},{7,6},{8,9},{9,8},{10,11... | collective-permute-start | bytes 786440 | tf_op jit(solution)/shard_map/ppermute | solution.py:89
  57.5 3.3 %inner.5.refs_2_ = f32[512,512]{1,0:T(8,128)S(1)} custom-call(bf16[512,2048]{1,0:T(8,128)(2,1)} %query.5, bf16[512,2048]{1,0:T(8,128)(2,1)} %key.7, bf16[512,2048]{1,0:T(8,128)(2,1)} %value.7, f32[4,4,512]{2,1,0:T(4,128)S(1)} %get-tuple-element.70.cumul.refs_3_), custom_call_target="tpu_custom_call" | custom-call | flops 1 | bytes 1 | tf_op jit(solution)/shard_map/inner/pallas_call | solution.py:419
  60.8 2.1 %collective-permute-done.10.refs_1_.refs_4_ = bf16[512,256]{1,0:T(8,128)(2,1)S(1)} collective-permute-done((bf16[512,256]{1,0:T(8,128)(2,1)S(1)}, bf16[512,256]{1,0:T(8,128)(2,1)S(1)}, u32[]{:S(2)}, u32[]{:S(2)}) %collective-permute-start.10) | collective-permute-done | bytes 262176 | tf_op jit(solution)/shard_map/ppermute | solution.py:89
  62.8 0.7 scan_state.3.prefix
  63.6 0.6 widen.2
  64.2 0.9 collective-permute-start.21
  65.2 0.7 collective-permute-start.13
  65.8 0.4 collective-permute-start.18
  66.3 1.7 %start_state.1 = (bf16[16,128,128]{2,1,0:T(8,128)(2,1)S(1)}, bf16[16,128,128]{2,1,0:T(8,128)(2,1)S(1)}) custom-call(s32[11]{0:T(128)S(1)} %stack.47.meta, bf16[16,144,128]{2,1,0:T(8,128)(2,1)S(1)} %get-tuple-element.69.own, bf16[16,144,128]{2,1,0:T(8,128)(2,1)} %collective-permute-done.1.other, ...), custom_call_target="tpu_custom_call" | custom-call | flops 1 | bytes 1 | tf_op jit(solution)/shard_map/start_state/pallas_call | solution.py:28
  67.9 0.2 collective-permute-start.14
  68.2 1.3 collective-permute-done.15.refs_2_.block
  69.5 2.1 %collective-permute-start.22 = (bf16[512,256]{1,0:T(8,128)(2,1)S(1)}, bf16[512,256]{1,0:T(8,128)(2,1)S(1)}, u32[]{:S(2)}, u32[]{:S(2)}) collective-permute-start(bf16[512,256]{1,0:T(8,128)(2,1)S(1)} %cut.7.refs_0_.refs_5_), channel_id=1, source_target_pairs={{0,1},{1,0},{2,3},{3,2},{4,5},{5,4},{6,7},{7,6},{8,9},{9,8},{10,11... | collective-permute-start | bytes 786440 | tf_op jit(solution)/shard_map/ppermute | solution.py:89
  71.5 5.3 %mixed.1 = (bf16[256,2048]{1,0:T(8,128)(2,1)S(1)}, bf16[256,2048]{1,0:T(8,128)(2,1)S(1)}) custom-call(s32[11]{0:T(128)S(1)} %stack.47.meta, bf16[512,2048]{1,0:T(8,128)(2,1)} %query.5, f32[512,1024]{1,0:T(8,128)S(1)} %inner.3.refs_0_, f32[512,512]{1,0:T(8,128)S(1)} %inner.4.refs_1_, f32[512,512]{1,0:T(8,128)S(1)} %inner.5.refs_2_, ...), custom_call_target="tpu_custom_call" | custom-call | flops 1 | bytes 1 | tf_op jit(solution)/shard_map/mixed/pallas_call | solution.py:579
  76.9 0.5 collective-permute-start.17
  77.4 0.6 widen.3
  78.0 7.0 %collective-permute-start.23 = (bf16[3072,256]{1,0:T(8,128)(2,1)S(1)}, bf16[3072,256]{1,0:T(8,128)(2,1)S(1)}, u32[]{:S(2)}, u32[]{:S(2)}) collective-permute-start(bf16[3072,256]{1,0:T(8,128)(2,1)S(1)} %widen.3), channel_id=1, source_target_pairs={{0,8},{2,6},{8,16},{10,2},{16,24},{18,10},{24,28},{26,18},{28,20},... | collective-permute-start | bytes 4718600 | tf_op jit(solution)/shard_map/ppermute | solution.py:106
  85.1 1.2 collective-permute-done.21.refs_1_.refs_3_
  86.3 1.2 collective-permute-start.25
  87.5 1.3 project.5
  88.8 2.3 %project.6 = (f32[512,512]{1,0:T(8,128)S(1)}, bf16[512,512]{1,0:T(8,128)(2,1)S(1)}) custom-call(bf16[2,512,2048]{2,1,0:T(8,128)(2,1)S(1)} %get-tuple-element.114.refs_0_, bf16[2560,256]{1,0:T(8,128)(2,1)S(1)} %collective-permute-done.3.block.refs_1_, bf16[2560,256]{1,0:T(8,128)(2,1)S(1)} %collective-permute-done.6.block.refs_2_), custom_call_target="tpu_custom_call" | custom-call | flops 1 | bytes 1 | tf_op jit(solution)/shard_map/project/pallas_call | solution.py:28
  91.1 1.6 collective-permute-start.20
  92.7 0.5 collective-permute-start.19
  93.2 2.3 %project.7 = (f32[512,512]{1,0:T(8,128)S(1)}, bf16[512,512]{1,0:T(8,128)(2,1)S(1)}) custom-call(bf16[2,512,2048]{2,1,0:T(8,128)(2,1)S(1)} %get-tuple-element.114.refs_0_, bf16[2560,256]{1,0:T(8,128)(2,1)S(1)} %collective-permute-done.9.block.refs_1_, bf16[2560,256]{1,0:T(8,128)(2,1)S(1)} %collective-permute-done.15.refs_2_.block), custom_call_target="tpu_custom_call" | custom-call | flops 1 | bytes 1 | tf_op jit(solution)/shard_map/project/pallas_call | solution.py:28
  95.5 1.6 collective-permute-start.24
  97.1 14.5 %collective-permute-done.19.refs_4_ = bf16[512,256]{1,0:T(8,128)(2,1)S(1)} collective-permute-done((bf16[512,256]{1,0:T(8,128)(2,1)S(1)}, bf16[512,256]{1,0:T(8,128)(2,1)S(1)}, u32[]{:S(2)}, u32[]{:S(2)}) %collective-permute-start.19) | collective-permute-done | bytes 262176 | tf_op jit(solution)/shard_map/ppermute | solution.py:89
  111.6 2.0 %cache.5 = (f32[256,1024]{1,0:T(8,128)S(1)}, f32[256,1024]{1,0:T(8,128)S(1)}, f32[256,128]{1,0:T(8,128)S(1)}, f32[256,128]{1,0:T(8,128)S(1)}) custom-call(s32[11]{0:T(128)S(1)} %stack.47.meta, f32[512,256]{1,0:T(8,128)S(1)} %get-tuple-element.95.mine, bf16[256,4096]{1,0:T(8,128)(2,1)} %refs_0_.10, bf16[256,4096]{1,0:T(8,128)(2,1)} %copy-done.6, ...), custom_call_target="tpu_custom_call" | custom-call | flops 1 | bytes 1 | tf_op jit(solution)/shard_map/cache/pallas_call | solution.py:28
  113.6 2.5 %cache.6 = (f32[256,1024]{1,0:T(8,128)S(1)}, f32[256,1024]{1,0:T(8,128)S(1)}, f32[256,128]{1,0:T(8,128)S(1)}, f32[256,128]{1,0:T(8,128)S(1)}) custom-call(s32[11]{0:T(128)S(1)} %stack.47.meta, f32[512,512]{1,0:T(8,128)S(1)} %get-tuple-element.98.mine, bf16[256,4096]{1,0:T(8,128)(2,1)} %refs_0_.10, bf16[256,4096]{1,0:T(8,128)(2,1)} %copy-done.6, ...), custom_call_target="tpu_custom_call" | custom-call | flops 1 | bytes 1 | tf_op jit(solution)/shard_map/cache/pallas_call | solution.py:28
  116.1 2.3 %project.8 = (f32[512,512]{1,0:T(8,128)S(1)}, bf16[512,512]{1,0:T(8,128)(2,1)S(1)}) custom-call(bf16[2,512,2048]{2,1,0:T(8,128)(2,1)S(1)} %get-tuple-element.114.refs_0_, bf16[3072,256]{1,0:T(8,128)(2,1)S(1)} %collective-permute-done.21.refs_1_.refs_3_, bf16[3072,256]{1,0:T(8,128)(2,1)S(1)} %collective-permute-done.23.refs_2_.refs_4_), custom_call_target="tpu_custom_call" | custom-call | flops 1 | bytes 1 | tf_op jit(solution)/shard_map/project/pallas_call | solution.py:28
  118.5 1.6 collective-permute-start.26
  120.0 2.8 %collective-permute-done.24.refs_7_ = bf16[512,512]{1,0:T(8,128)(2,1)S(1)} collective-permute-done((bf16[512,512]{1,0:T(8,128)(2,1)S(1)}, bf16[512,512]{1,0:T(8,128)(2,1)S(1)}, u32[]{:S(2)}, u32[]{:S(2)}) %collective-permute-start.24) | collective-permute-done | bytes 524320 | tf_op jit(solution)/shard_map/ppermute | solution.py:89
  122.8 2.4 %cache.7 = (f32[256,1024]{1,0:T(8,128)S(1)}, f32[256,1024]{1,0:T(8,128)S(1)}, f32[256,128]{1,0:T(8,128)S(1)}, f32[256,128]{1,0:T(8,128)S(1)}) custom-call(s32[11]{0:T(128)S(1)} %stack.47.meta, f32[512,512]{1,0:T(8,128)S(1)} %get-tuple-element.108.mine, bf16[256,4096]{1,0:T(8,128)(2,1)} %refs_0_.10, bf16[256,4096]{1,0:T(8,128)(2,1)} %copy-done.6, ...), custom_call_target="tpu_custom_call" | custom-call | flops 1 | bytes 1 | tf_op jit(solution)/shard_map/cache/pallas_call | solution.py:28
  125.3 1.2 project.9
  126.5 1.6 collective-permute-start.27
  128.1 6.0 %collective-permute-done.26.refs_5_ = bf16[512,512]{1,0:T(8,128)(2,1)S(1)} collective-permute-done((bf16[512,512]{1,0:T(8,128)(2,1)S(1)}, bf16[512,512]{1,0:T(8,128)(2,1)S(1)}, u32[]{:S(2)}, u32[]{:S(2)}) %collective-permute-start.26) | collective-permute-done | bytes 524320 | tf_op jit(solution)/shard_map/ppermute | solution.py:89
  134.1 2.5 %cache.8 = (f32[256,1024]{1,0:T(8,128)S(1)}, f32[256,1024]{1,0:T(8,128)S(1)}, f32[256,128]{1,0:T(8,128)S(1)}, f32[256,128]{1,0:T(8,128)S(1)}) custom-call(s32[11]{0:T(128)S(1)} %stack.47.meta, f32[512,512]{1,0:T(8,128)S(1)} %get-tuple-element.116.mine, bf16[256,4096]{1,0:T(8,128)(2,1)} %refs_0_.10, bf16[256,4096]{1,0:T(8,128)(2,1)} %copy-done.6, ...), custom_call_target="tpu_custom_call" | custom-call | flops 1 | bytes 1 | tf_op jit(solution)/shard_map/cache/pallas_call | solution.py:28
  136.5 2.0 %collective-permute-done.27.refs_4_ = bf16[512,256]{1,0:T(8,128)(2,1)S(1)} collective-permute-done((bf16[512,256]{1,0:T(8,128)(2,1)S(1)}, bf16[512,256]{1,0:T(8,128)(2,1)S(1)}, u32[]{:S(2)}, u32[]{:S(2)}) %collective-permute-start.27) | collective-permute-done | bytes 262176 | tf_op jit(solution)/shard_map/ppermute | solution.py:89
  138.6 2.0 %cache.9 = (f32[256,1024]{1,0:T(8,128)S(1)}, bf16[256,1024]{1,0:T(8,128)(2,1)S(1)}, f32[256,128]{1,0:T(8,128)S(1)}, f32[256,128]{1,0:T(8,128)S(1)}) custom-call(s32[11]{0:T(128)S(1)} %stack.47.meta, f32[512,256]{1,0:T(8,128)S(1)} %get-tuple-element.122.mine, bf16[256,4096]{1,0:T(8,128)(2,1)} %refs_0_.10, bf16[256,4096]{1,0:T(8,128)(2,1)} %copy-done.6, ...), custom_call_target="tpu_custom_call" | custom-call | flops 1 | bytes 1 | tf_op jit(solution)/shard_map/cache/pallas_call | solution.py:28
  140.7 0.5 collective-permute-start.29
  141.2 1.6 %collective-permute-done.29.square_in = f32[256,128]{1,0:T(8,128)S(1)} collective-permute-done((f32[256,128]{1,0:T(8,128)S(1)}, f32[256,128]{1,0:T(8,128)S(1)}, u32[]{:S(2)}, u32[]{:S(2)}) %collective-permute-start.29) | collective-permute-done | bytes 131104 | tf_op jit(solution)/shard_map/ppermute | solution.py:56
  142.9 1.6 collective-permute-start.30
  144.5 12.5 %collective-permute-done.30.refs_3_ = bf16[256,1024]{1,0:T(8,128)(2,1)S(1)} collective-permute-done((bf16[256,1024]{1,0:T(8,128)(2,1)S(1)}, bf16[256,1024]{1,0:T(8,128)(2,1)S(1)}, u32[]{:S(2)}, u32[]{:S(2)}) %collective-permute-start.30) | collective-permute-done | bytes 524320 | tf_op jit(solution)/shard_map/ppermute | solution.py:89
  157.0 1.6 %place.1 = bf16[4,128,1024]{2,1,0:T(8,128)(2,1)} custom-call(s32[11]{0:T(128)S(1)} %stack.47.meta, s32[2,2]{1,0:T(2,128)S(1)} %copy-done.4, s32[2,2]{1,0:T(2,128)S(1)} %collective-permute-done.4.refs_1_, bf16[256,1024]{1,0:T(8,128)(2,1)S(1)} %finish.1.refs_2_, bf16[256,1024]{1,0:T(8,128)(2,1)S(1)} %collective-permute-done.30.refs_3_), custom_call_target="tpu_custom_call" | custom-call | flops 1 | bytes 1 | tf_op jit(solution)/shard_map/place/pallas_call | solution.py:28
  (47 shorter events, 0.9 us)
Async XLA Ops:
  0.0 5.5 %copy-start.3 = (f32[16,512]{1,0:T(8,128)S(1)}, f32[16,512]{1,0:T(8,128)}, u32[]{:S(2)}) copy-start(f32[16,512]{1,0:T(8,128)} %decay.1) | copy-start | bytes 98308
  1.0 1.2 copy-start.1
  2.3 8.9 %collective-permute-start = (bf16[2560,256]{1,0:T(8,128)(2,1)S(1)}, bf16[2560,256]{1,0:T(8,128)(2,1)S(1)}, u32[]{:S(2)}, u32[]{:S(2)}) collective-permute-start(bf16[2560,256]{1,0:T(8,128)(2,1)S(1)} %pack.1.refs_4_), channel_id=1, source_target_pairs={{0,2},{2,0},{4,6},{6,4},{8,10},{10,8},{12,14},{14,12},{16,18},{18,... | collective-permute-start | bytes 3932168 | tf_op jit(solution)/shard_map/ppermute | solution.py:56
  2.8 21.7 %collective-permute-start.3 = (bf16[2560,256]{1,0:T(8,128)(2,1)S(1)}, bf16[2560,256]{1,0:T(8,128)(2,1)S(1)}, u32[]{:S(2)}, u32[]{:S(2)}) collective-permute-start(bf16[2560,256]{1,0:T(8,128)(2,1)S(1)} %pack.1.refs_4_), channel_id=1, source_target_pairs={{0,8},{2,6},{8,16},{10,2},{16,24},{18,10},{24,28},{26,18},{28,20},... | collective-permute-start | bytes 3932168 | tf_op jit(solution)/shard_map/ppermute | solution.py:106
  11.2 1.1 copy-start.7
  12.3 2.1 %collective-permute-start.1 = (bf16[16,144,128]{2,1,0:T(8,128)(2,1)S(1)}, bf16[16,144,128]{2,1,0:T(8,128)(2,1)}, u32[]{:S(2)}, u32[]{:S(2)}) collective-permute-start(bf16[16,144,128]{2,1,0:T(8,128)(2,1)S(1)} %get-tuple-element.69.own), channel_id=1, source_target_pairs={{0,2},{2,0},{4,6},{6,4},{8,10},{10,8},{12,14},{14,12},{16,18},{18,... | collective-permute-start | bytes 1769480 | tf_op jit(solution)/shard_map/ppermute | solution.py:56
  12.5 6.6 %copy-start.8 = (bf16[2560,256]{1,0:T(8,128)(2,1)S(1)}, bf16[2560,256]{1,0:T(8,128)(2,1)}, u32[]{:S(2)}) copy-start(bf16[2560,256]{1,0:T(8,128)(2,1)} %copy-done.7) | copy-start | bytes 3932164
  15.8 17.0 %collective-permute-start.2 = (bf16[16,144,128]{2,1,0:T(8,128)(2,1)S(1)}, bf16[16,144,128]{2,1,0:T(8,128)(2,1)S(1)}, u32[]{:S(2)}, u32[]{:S(2)}) collective-permute-start(bf16[16,144,128]{2,1,0:T(8,128)(2,1)S(1)} %chip_state.1.own), channel_id=1, source_target_pairs={{0,4},{6,2},{10,12},{12,10},{18,20},{20,18},{26,28},{28,26},{1,5},... | collective-permute-start | bytes 1769480 | tf_op jit(solution)/shard_map/ppermute | solution.py:69
  19.1 22.9 %collective-permute-start.6 = (bf16[2560,256]{1,0:T(8,128)(2,1)S(1)}, bf16[2560,256]{1,0:T(8,128)(2,1)S(1)}, u32[]{:S(2)}, u32[]{:S(2)}) collective-permute-start(bf16[2560,256]{1,0:T(8,128)(2,1)S(1)} %copy-done.8), channel_id=1, source_target_pairs={{0,8},{2,6},{8,16},{10,2},{16,24},{18,10},{24,28},{26,18},{28,20},... | collective-permute-start | bytes 3932168 | tf_op jit(solution)/shard_map/ppermute | solution.py:106
  24.5 11.4 %copy-start.4 = (s32[2,2]{1,0:T(2,128)S(1)}, s32[2,2]{1,0:T(2,128)}, u32[]{:S(2)}) copy-start(s32[2,2]{1,0:T(2,128)} %refs_0_.11) | copy-start | bytes 52
  33.5 21.8 %collective-permute-start.9 = (bf16[2560,256]{1,0:T(8,128)(2,1)S(1)}, bf16[2560,256]{1,0:T(8,128)(2,1)S(1)}, u32[]{:S(2)}, u32[]{:S(2)}) collective-permute-start(bf16[2560,256]{1,0:T(8,128)(2,1)S(1)} %collective-permute-done.3.block.refs_1_), channel_id=1, source_target_pairs={{0,8},{2,6},{8,16},{10,2},{16,24},{18,10},{24,28},{26,18},{28,20},... | collective-permute-start | bytes 3932168 | tf_op jit(solution)/shard_map/ppermute | solution.py:106
  33.6 8.4 %collective-permute-start.5 = (bf16[8,144,128]{2,1,0:T(8,128)(2,1)S(1)}, bf16[8,144,128]{2,1,0:T(8,128)(2,1)S(1)}, u32[]{:S(2)}, u32[]{:S(2)}) collective-permute-start(bf16[8,144,128]{2,1,0:T(8,128)(2,1)S(1)} %plane_state.1.refs_1_.refs_3_), channel_id=1, source_target_pairs={{2,10},{4,12},{18,26},{20,28},{3,11},{5,13},{19,27},{21,29}} | collective-permute-start | bytes 884744 | tf_op jit(solution)/shard_map/ppermute | solution.py:75
  34.3 7.7 %collective-permute-start.7 = (bf16[512,256]{1,0:T(8,128)(2,1)S(1)}, bf16[512,256]{1,0:T(8,128)(2,1)S(1)}, u32[]{:S(2)}, u32[]{:S(2)}) collective-permute-start(bf16[512,256]{1,0:T(8,128)(2,1)S(1)} %cut.4.refs_3_), channel_id=1, source_target_pairs={{0,1},{1,0},{2,3},{3,2},{4,5},{5,4},{6,7},{7,6},{8,9},{9,8},{10,11... | collective-permute-start | bytes 786440 | tf_op jit(solution)/shard_map/ppermute | solution.py:89
  35.9 6.1 %collective-permute-start.4 = (s32[2,2]{1,0:T(2,128)S(1)}, s32[2,2]{1,0:T(2,128)S(1)}, u32[]{:S(2)}, u32[]{:S(2)}) collective-permute-start(s32[2,2]{1,0:T(2,128)S(1)} %copy-done.4), channel_id=1, source_target_pairs={{0,1},{1,0},{2,3},{3,2},{4,5},{5,4},{6,7},{7,6},{8,9},{9,8},{10,11... | collective-permute-start | bytes 56 | tf_op jit(solution)/shard_map/ppermute | solution.py:89
  42.7 18.0 %collective-permute-start.8 = (bf16[8,144,128]{2,1,0:T(8,128)(2,1)S(1)}, bf16[8,144,128]{2,1,0:T(8,128)(2,1)S(1)}, u32[]{:S(2)}, u32[]{:S(2)}) collective-permute-start(bf16[8,144,128]{2,1,0:T(8,128)(2,1)S(1)} %get-tuple-element.77), channel_id=1, source_target_pairs={{10,18},{12,20},{11,19},{13,21}} | collective-permute-start | bytes 884744 | tf_op jit(solution)/shard_map/ppermute | solution.py:75
  43.4 19.4 %collective-permute-start.12 = (bf16[8,144,128]{2,1,0:T(8,128)(2,1)S(1)}, bf16[8,144,128]{2,1,0:T(8,128)(2,1)S(1)}, u32[]{:S(2)}, u32[]{:S(2)}) collective-permute-start(bf16[8,144,128]{2,1,0:T(8,128)(2,1)S(1)} %get-tuple-element.77), channel_id=1, source_target_pairs={{10,26},{12,28},{11,27},{13,29}} | collective-permute-start | bytes 884744 | tf_op jit(solution)/shard_map/ppermute | solution.py:75
  44.1 25.3 %collective-permute-start.15 = (bf16[2560,256]{1,0:T(8,128)(2,1)S(1)}, bf16[2560,256]{1,0:T(8,128)(2,1)S(1)}, u32[]{:S(2)}, u32[]{:S(2)}) collective-permute-start(bf16[2560,256]{1,0:T(8,128)(2,1)S(1)} %collective-permute-done.6.block.refs_2_), channel_id=1, source_target_pairs={{0,8},{2,6},{8,16},{10,2},{16,24},{18,10},{24,28},{26,18},{28,20},... | collective-permute-start | bytes 3932168 | tf_op jit(solution)/shard_map/ppermute | solution.py:106
  44.2 16.6 %collective-permute-start.11 = (bf16[512,256]{1,0:T(8,128)(2,1)S(1)}, bf16[512,256]{1,0:T(8,128)(2,1)S(1)}, u32[]{:S(2)}, u32[]{:S(2)}) collective-permute-start(bf16[512,256]{1,0:T(8,128)(2,1)S(1)} %cut.6.refs_5_), channel_id=1, source_target_pairs={{0,1},{1,0},{2,3},{3,2},{4,5},{5,4},{6,7},{7,6},{8,9},{9,8},{10,11... | collective-permute-start | bytes 786440 | tf_op jit(solution)/shard_map/ppermute | solution.py:89
  55.4 7.4 %collective-permute-start.10 = (bf16[512,256]{1,0:T(8,128)(2,1)S(1)}, bf16[512,256]{1,0:T(8,128)(2,1)S(1)}, u32[]{:S(2)}, u32[]{:S(2)}) collective-permute-start(bf16[512,256]{1,0:T(8,128)(2,1)S(1)} %cut.5.refs_0_.refs_3_), channel_id=1, source_target_pairs={{0,1},{1,0},{2,3},{3,2},{4,5},{5,4},{6,7},{7,6},{8,9},{9,8},{10,11... | collective-permute-start | bytes 786440 | tf_op jit(solution)/shard_map/ppermute | solution.py:89
  63.6 2.3 %copy-start.5 = (bf16[256,4096]{1,0:T(8,128)(2,1)S(1)}, bf16[256,4096]{1,0:T(8,128)(2,1)}, u32[]{:S(2)}) copy-start(bf16[256,4096]{1,0:T(8,128)(2,1)} %refs_0_.10) | copy-start | bytes 6291460
  64.2 22.1 %collective-permute-start.21 = (bf16[3072,256]{1,0:T(8,128)(2,1)S(1)}, bf16[3072,256]{1,0:T(8,128)(2,1)S(1)}, u32[]{:S(2)}, u32[]{:S(2)}) collective-permute-start(bf16[3072,256]{1,0:T(8,128)(2,1)S(1)} %widen.2), channel_id=1, source_target_pairs={{0,8},{2,6},{8,16},{10,2},{16,24},{18,10},{24,28},{26,18},{28,20},... | collective-permute-start | bytes 4718600 | tf_op jit(solution)/shard_map/ppermute | solution.py:106
  65.2 1.1 collective-permute-start.13
  65.8 29.7 %collective-permute-start.18 = (bf16[256,4096]{1,0:T(8,128)(2,1)S(1)}, bf16[256,4096]{1,0:T(8,128)(2,1)S(1)}, u32[]{:S(2)}, u32[]{:S(2)}) collective-permute-start(bf16[256,4096]{1,0:T(8,128)(2,1)S(1)} %copy-done.5), channel_id=1, source_target_pairs={{0,2},{2,0},{4,6},{6,4},{8,10},{10,8},{12,14},{14,12},{16,18},{18,... | collective-permute-start | bytes 6291464 | tf_op jit(solution)/shard_map/ppermute | solution.py:56
  67.9 3.6 %collective-permute-start.14 = (bf16[16,128,128]{2,1,0:T(8,128)(2,1)S(1)}, bf16[16,128,128]{2,1,0:T(8,128)(2,1)S(1)}, u32[]{:S(2)}, u32[]{:S(2)}) collective-permute-start(bf16[16,128,128]{2,1,0:T(8,128)(2,1)S(1)} %get-tuple-element.84), channel_id=1, source_target_pairs={{0,2},{2,0},{4,6},{6,4},{8,10},{10,8},{12,14},{14,12},{16,18},{18,... | collective-permute-start | bytes 1572872 | tf_op jit(solution)/shard_map/ppermute | solution.py:56
  69.5 7.9 %collective-permute-start.22 = (bf16[512,256]{1,0:T(8,128)(2,1)S(1)}, bf16[512,256]{1,0:T(8,128)(2,1)S(1)}, u32[]{:S(2)}, u32[]{:S(2)}) collective-permute-start(bf16[512,256]{1,0:T(8,128)(2,1)S(1)} %cut.7.refs_0_.refs_5_), channel_id=1, source_target_pairs={{0,1},{1,0},{2,3},{3,2},{4,5},{5,4},{6,7},{7,6},{8,9},{9,8},{10,11... | collective-permute-start | bytes 786440 | tf_op jit(solution)/shard_map/ppermute | solution.py:89
  76.8 10.7 %collective-permute-start.16 = (bf16[256,2048]{1,0:T(8,128)(2,1)S(1)}, bf16[256,2048]{1,0:T(8,128)(2,1)S(1)}, u32[]{:S(2)}, u32[]{:S(2)}) collective-permute-start(bf16[256,2048]{1,0:T(8,128)(2,1)S(1)} %get-tuple-element.86.refs_0_), channel_id=1, source_target_pairs={{0,2},{2,0},{4,6},{6,4},{8,10},{10,8},{12,14},{14,12},{16,18},{18,... | collective-permute-start | bytes 3145736 | tf_op jit(solution)/shard_map/ppermute | solution.py:56
  76.9 10.6 %collective-permute-start.17 = (bf16[256,2048]{1,0:T(8,128)(2,1)S(1)}, bf16[256,2048]{1,0:T(8,128)(2,1)S(1)}, u32[]{:S(2)}, u32[]{:S(2)}) collective-permute-start(bf16[256,2048]{1,0:T(8,128)(2,1)S(1)} %get-tuple-element.87.refs_1_), channel_id=1, source_target_pairs={{0,2},{2,0},{4,6},{6,4},{8,10},{10,8},{12,14},{14,12},{16,18},{18,... | collective-permute-start | bytes 3145736 | tf_op jit(solution)/shard_map/ppermute | solution.py:56
  78.0 38.1 %collective-permute-start.23 = (bf16[3072,256]{1,0:T(8,128)(2,1)S(1)}, bf16[3072,256]{1,0:T(8,128)(2,1)S(1)}, u32[]{:S(2)}, u32[]{:S(2)}) collective-permute-start(bf16[3072,256]{1,0:T(8,128)(2,1)S(1)} %widen.3), channel_id=1, source_target_pairs={{0,8},{2,6},{8,16},{10,2},{16,24},{18,10},{24,28},{26,18},{28,20},... | collective-permute-start | bytes 4718600 | tf_op jit(solution)/shard_map/ppermute | solution.py:106
  86.3 39.0 %collective-permute-start.25 = (bf16[3072,256]{1,0:T(8,128)(2,1)S(1)}, bf16[3072,256]{1,0:T(8,128)(2,1)S(1)}, u32[]{:S(2)}, u32[]{:S(2)}) collective-permute-start(bf16[3072,256]{1,0:T(8,128)(2,1)S(1)} %collective-permute-done.21.refs_1_.refs_3_), channel_id=1, source_target_pairs={{0,8},{2,6},{8,16},{10,2},{16,24},{18,10},{24,28},{26,18},{28,20},... | collective-permute-start | bytes 4718600 | tf_op jit(solution)/shard_map/ppermute | solution.py:106
  91.1 22.5 %collective-permute-start.20 = (bf16[512,512]{1,0:T(8,128)(2,1)S(1)}, bf16[512,512]{1,0:T(8,128)(2,1)S(1)}, u32[]{:S(2)}, u32[]{:S(2)}) collective-permute-start(bf16[512,512]{1,0:T(8,128)(2,1)S(1)} %get-tuple-element.99), channel_id=1, source_target_pairs={{0,1},{1,0},{2,3},{3,2},{4,5},{5,4},{6,7},{7,6},{8,9},{9,8},{10,11... | collective-permute-start | bytes 1572872 | tf_op jit(solution)/shard_map/ppermute | solution.py:89
  92.7 18.9 %collective-permute-start.19 = (bf16[512,256]{1,0:T(8,128)(2,1)S(1)}, bf16[512,256]{1,0:T(8,128)(2,1)S(1)}, u32[]{:S(2)}, u32[]{:S(2)}) collective-permute-start(bf16[512,256]{1,0:T(8,128)(2,1)S(1)} %get-tuple-element.96), channel_id=1, source_target_pairs={{0,1},{1,0},{2,3},{3,2},{4,5},{5,4},{6,7},{7,6},{8,9},{9,8},{10,11... | collective-permute-start | bytes 786440 | tf_op jit(solution)/shard_map/ppermute | solution.py:89
  93.2 18.4 %copy-start = (bf16[256,1024]{1,0:T(8,128)(2,1)S(1)}, bf16[256,1024]{1,0:T(8,128)(2,1)}, u32[]{:S(2)}) copy-start(bf16[256,1024]{1,0:T(8,128)(2,1)} %refs_3_.1) | copy-start | bytes 1572868
  93.2 18.4 %copy-start.2 = (f32[4096]{0:T(1024)S(1)}, f32[4096]{0:T(1024)}, u32[]{:S(2)}) copy-start(f32[4096]{0:T(1024)} %param.15) | copy-start | bytes 49156
  95.5 16.1 %copy-start.6 = (bf16[256,4096]{1,0:T(8,128)(2,1)}, bf16[256,4096]{1,0:T(8,128)(2,1)S(1)}, u32[]{:S(2)}) copy-start(bf16[256,4096]{1,0:T(8,128)(2,1)S(1)} %collective-permute-done.18.refs_1_) | copy-start | bytes 6291460
  95.5 27.3 %collective-permute-start.24 = (bf16[512,512]{1,0:T(8,128)(2,1)S(1)}, bf16[512,512]{1,0:T(8,128)(2,1)S(1)}, u32[]{:S(2)}, u32[]{:S(2)}) collective-permute-start(bf16[512,512]{1,0:T(8,128)(2,1)S(1)} %get-tuple-element.109), channel_id=1, source_target_pairs={{0,1},{1,0},{2,3},{3,2},{4,5},{5,4},{6,7},{7,6},{8,9},{9,8},{10,11... | collective-permute-start | bytes 1572872 | tf_op jit(solution)/shard_map/ppermute | solution.py:89
  118.5 15.6 %collective-permute-start.26 = (bf16[512,512]{1,0:T(8,128)(2,1)S(1)}, bf16[512,512]{1,0:T(8,128)(2,1)S(1)}, u32[]{:S(2)}, u32[]{:S(2)}) collective-permute-start(bf16[512,512]{1,0:T(8,128)(2,1)S(1)} %get-tuple-element.117), channel_id=1, source_target_pairs={{0,1},{1,0},{2,3},{3,2},{4,5},{5,4},{6,7},{7,6},{8,9},{9,8},{10,11... | collective-permute-start | bytes 1572872 | tf_op jit(solution)/shard_map/ppermute | solution.py:89
  126.5 12.0 %collective-permute-start.27 = (bf16[512,256]{1,0:T(8,128)(2,1)S(1)}, bf16[512,256]{1,0:T(8,128)(2,1)S(1)}, u32[]{:S(2)}, u32[]{:S(2)}) collective-permute-start(bf16[512,256]{1,0:T(8,128)(2,1)S(1)} %get-tuple-element.123), channel_id=1, source_target_pairs={{0,1},{1,0},{2,3},{3,2},{4,5},{5,4},{6,7},{7,6},{8,9},{9,8},{10,11... | collective-permute-start | bytes 786440 | tf_op jit(solution)/shard_map/ppermute | solution.py:89
  140.6 2.2 %collective-permute-start.28 = (bf16[256,1024]{1,0:T(8,128)(2,1)S(1)}, bf16[256,1024]{1,0:T(8,128)(2,1)S(1)}, u32[]{:S(2)}, u32[]{:S(2)}) collective-permute-start(bf16[256,1024]{1,0:T(8,128)(2,1)S(1)} %get-tuple-element.129), channel_id=1, source_target_pairs={{0,2},{2,0},{4,6},{6,4},{8,10},{10,8},{12,14},{14,12},{16,18},{18,... | collective-permute-start | bytes 1572872 | tf_op jit(solution)/shard_map/ppermute | solution.py:56
  140.7 2.1 %collective-permute-start.29 = (f32[256,128]{1,0:T(8,128)S(1)}, f32[256,128]{1,0:T(8,128)S(1)}, u32[]{:S(2)}, u32[]{:S(2)}) collective-permute-start(f32[256,128]{1,0:T(8,128)S(1)} %get-tuple-element.130), channel_id=1, source_target_pairs={{0,2},{2,0},{4,6},{6,4},{8,10},{10,8},{12,14},{14,12},{16,18},{18,... | collective-permute-start | bytes 393224 | tf_op jit(solution)/shard_map/ppermute | solution.py:56
  142.9 14.0 %collective-permute-start.30 = (bf16[256,1024]{1,0:T(8,128)(2,1)S(1)}, bf16[256,1024]{1,0:T(8,128)(2,1)S(1)}, u32[]{:S(2)}, u32[]{:S(2)}) collective-permute-start(bf16[256,1024]{1,0:T(8,128)(2,1)S(1)} %finish.1.refs_2_), channel_id=1, source_target_pairs={{0,1},{1,0},{2,3},{3,2},{4,5},{5,4},{6,7},{7,6},{8,9},{9,8},{10,11... | collective-permute-start | bytes 1572872 | tf_op jit(solution)/shard_map/ppermute | solution.py:89
